TPU v7x, 32 devices: a whole 2x2x4 slice. The times are simulated.
32 devices in a mesh: lm: 4 (over z), sl: 8 (over y, x, core).
Axes of the slice: x: 2, y: 2, z: 4, core: 2. Of those that a mesh axis runs over, the one named last changes fastest.
Arguments:
- slab: bfloat16 [8192, 1024], P('sl'), may hold values from -6 to 6
- landmarks: bfloat16 [8192, 1024], P(('lm', 'sl')), may hold values from -6 to 6
- codes: bfloat16 [8192, 96], P(('lm', 'sl')), may hold values from -4 to 4
- exponents: int32 [64], P(('lm', 'sl')), may hold values from -3 to 3
- eigvec: bfloat16 [96, 64], replicated, may hold values from -0.625 to 0.625
- ritz: float32 [64], replicated, may hold values from 0.5 to 4
Outputs:
- extended: float32 [8192, 64], P('sl')
All inputs are finite; a program needn't handle non-finite values.
Results may differ from a plain program's by a relative error of at most 0.004.
Values may be sent and summed in bfloat16 or wider, within the bound.
No kernel may reach another device: no remote copies, remote signals or barrier semaphores. Data moves between devices by JAX's collectives and lax.ppermute only.
A program may use at most 128 MiB of HBM per device.

v0:
```python
import functools
import math

import jax
import jax.numpy as jnp
from jax import lax
from jax.experimental import pallas as pl
from jax.experimental.pallas import tpu as pltpu
from jax.sharding import PartitionSpec as P

BLOCK = 128
CHUNK = 512
HALVES = 2
MIB = 2**20


def core_send(value, n):
    return lax.ppermute(value, "sl", [(i, i ^ 1) for i in range(n)])


def chip_send(value, k, n):
    bits = [1 << b for b in range(1, n.bit_length() - 1)]
    return lax.ppermute(value, "sl", [(i, i ^ bits[(k + i % 2) % len(bits)]) for i in range(n)])


def lm_send(value, k, n_lm, n_sl):
    bits = [1 << b for b in range(n_lm.bit_length() - 1)]
    perm = [
        (i * n_sl + j, (i ^ bits[(k + j % 2) % len(bits)]) * n_sl + j)
        for i in range(n_lm)
        for j in range(n_sl)
    ]
    return lax.ppermute(value, ("lm", "sl"), perm)


def prepare_kernel(
    land_ref, codes_ref, exponents_ref, eig_ref, first_ref, second_ref, codes, eig, exponents, sems
):
    rows, feat = land_ref.shape
    half = rows - second_ref.shape[0]
    ritz = eig_ref.shape[0]
    pairs = [
        (codes_ref, codes),
        (eig_ref, eig),
        (exponents_ref, exponents),
        (land_ref.at[:half], first_ref.at[:half]),
        (land_ref.at[half:], second_ref),
    ]
    copies = [pltpu.make_async_copy(src, dst, sems.at[k]) for k, (src, dst) in enumerate(pairs)]
    for copy in copies:
        copy.start()
    for copy in copies[:3]:
        copy.wait()
    pieces = []
    for b in range(rows // BLOCK):
        scale = lax.shift_left(jnp.int32(1), exponents[b] + 15).astype(jnp.float32) * 2.0**-15
        pieces.append(codes[:, b * BLOCK : (b + 1) * BLOCK].astype(jnp.float32) * scale)
    basis = jnp.concatenate(pieces, axis=1).astype(jnp.bfloat16)
    vectors = jnp.dot(eig[...], basis, preferred_element_type=jnp.float32).astype(jnp.bfloat16)
    chunks = feat // rows
    depth = ritz // chunks
    for c in range(chunks):
        first_ref[half:, c * rows : (c + 1) * rows] = vectors[c * depth : (c + 1) * depth, :]
    for copy in copies[3:]:
        copy.wait()


def prepare(landmarks, codes_t, exponents, eig_t):
    rows, feat = landmarks.shape
    extra = eig_t.shape[0] * rows // feat
    head = rows // 2
    return pl.pallas_call(
        prepare_kernel,
        out_shape=[
            jax.ShapeDtypeStruct((head + extra, feat), jnp.bfloat16),
            jax.ShapeDtypeStruct((rows - head, feat), jnp.bfloat16),
        ],
        in_specs=[pl.BlockSpec(memory_space=pltpu.HBM)] * 4,
        scratch_shapes=[
            pltpu.VMEM(codes_t.shape, codes_t.dtype),
            pltpu.VMEM(eig_t.shape, eig_t.dtype),
            pltpu.SMEM(exponents.shape, exponents.dtype),
            pltpu.SemaphoreType.DMA((5,)),
        ],
        compiler_params=pltpu.CompilerParams(vmem_limit_bytes=8 * MIB),
    )(*(pltpu.with_memory_space_constraint(x, pltpu.HBM) for x in (landmarks, codes_t, exponents, eig_t)))


def transpose_kernel(in_ref, out_ref):
    for k in range(in_ref.shape[0] // CHUNK):
        rows = slice(k * CHUNK, (k + 1) * CHUNK)
        out_ref[:, rows] = in_ref[rows, :].T


def stage_kernel(count, coeff, ritz, has_acc, span, *refs):
    start, stop = span
    slabs = refs[:count]
    first_ref, second_ref = refs[count : count + 2]
    accs = refs[count + 2 : 2 * count + 2] if has_acc else [None] * count
    outs = refs[-count:]
    tail, feat = second_ref.shape
    rows = (first_ref.shape[0] + tail) * feat // (feat + ritz)
    head = rows - tail
    land = jnp.concatenate([first_ref[:head, :], second_ref[...]], axis=0)
    vec = jnp.concatenate(
        [first_ref[head:, c * rows : (c + 1) * rows] for c in range(feat // rows)], axis=0
    )
    work = [
        (k, slice(c, min(c + CHUNK, stop))) for k in range(count) for c in range(start, stop, CHUNK)
    ]

    def scores(k, cols):
        return jnp.dot(land, slabs[k][:, cols], preferred_element_type=jnp.float32)

    ahead = scores(*work[0])
    for n, (k, cols) in enumerate(work):
        now, ahead = ahead, scores(*work[n + 1]) if n + 1 < len(work) else None
        affinity = jnp.exp(now * coeff).astype(jnp.bfloat16)
        term = jnp.dot(vec, affinity, preferred_element_type=jnp.float32)
        place = slice(cols.start - start, cols.stop - start)
        outs[k][:, place] = term if accs[k] is None else accs[k][:, cols] + term


def stage(slabs, first, second, accs, coeff, ritz, span=None):
    feat, rows = slabs[0].shape
    span = span or (0, rows)
    rows = span[1] - span[0]
    land = (first.shape[0] + second.shape[0]) * feat // (feat + ritz)
    count = len(slabs)
    return pl.pallas_call(
        functools.partial(stage_kernel, count, coeff, ritz, accs is not None, span),
        out_shape=[jax.ShapeDtypeStruct((ritz, rows), jnp.float32)] * count,
        compiler_params=pltpu.CompilerParams(vmem_limit_bytes=32 * MIB),
        cost_estimate=pl.CostEstimate(
            flops=2 * count * rows * land * (feat + 4 * ritz),
            bytes_accessed=2 * (count * rows + land) * feat,
            transcendentals=count * rows * land,
        ),
    )(*slabs, first, second, *(accs or []))


def add_kernel(a_ref, b_ref, out_ref):
    total = a_ref[...].astype(jnp.float32) + b_ref[...].astype(jnp.float32)
    out_ref[...] = total.astype(out_ref.dtype)


def scale_kernel(*refs, total_land):
    ritz_ref, out_ref = refs[-2:]
    factor = 1.0 / (ritz_ref[...] * math.sqrt(total_land))
    start = 0
    for a_ref, b_ref in zip(refs[0:-2:2], refs[1:-2:2]):
        stop = start + a_ref.shape[1]
        total = a_ref[...].astype(jnp.float32) + b_ref[...].astype(jnp.float32)
        out_ref[:, start:stop] = total * factor
        start = stop


def small_call(kernel, out, *args):
    return pl.pallas_call(
        kernel,
        out_shape=jax.ShapeDtypeStruct(out.shape, out.dtype),
        compiler_params=pltpu.CompilerParams(vmem_limit_bytes=8 * MIB),
    )(*args)


def local(slab, landmarks, codes, exponents, eigvec, ritz):
    n_lm, n_sl = lax.axis_size("lm"), lax.axis_size("sl")
    total_land = codes.shape[0] * n_lm * n_sl
    coeff = 1.0 / math.sqrt(slab.shape[1])
    cols = ritz.shape[0]
    rows = slab.shape[0]
    ways = n_sl.bit_length() - 2

    first, second = prepare(landmarks, codes.T, exponents, eigvec.T)
    blocks = {0: [first, second]}
    for k in range(ways):
        blocks[1 << k] = [None, None]
    for turn in (0, 1):
        for k in range(ways):
            piece = (k + turn) % 2
            blocks[1 << k][piece] = chip_send(blocks[0][piece], k, n_sl)
    late_slab, _ = lax.optimization_barrier((slab, first))
    turned = jax.ShapeDtypeStruct(slab.shape[::-1], slab.dtype)
    other = small_call(transpose_kernel, turned, core_send(late_slab, n_sl))
    slab = small_call(transpose_kernel, turned, slab)
    (acc,) = stage([slab], first, second, None, coeff, cols)
    held = [blocks[1 << k][k % 2] for k in range(ways)]
    held, acc = lax.optimization_barrier((held, acc))
    for k in range(ways):
        blocks[1 << k][k % 2] = held[k]
    (other_acc,) = stage([other], first, second, None, coeff, cols)
    accs = [acc, other_acc]
    for t in range(1, 1 << ways):
        if t in blocks:
            continue
        low, high = (t & -t).bit_length() - 1, t.bit_length() - 1
        blocks[t] = [
            chip_send(blocks[t ^ (1 << high)][0], high, n_sl),
            chip_send(blocks[t ^ (1 << low)][1], low, n_sl),
        ]

    for t in range(1, (1 << ways) - 1):
        accs = stage([slab, other], *blocks[t], accs, coeff, cols)
    end = blocks[(1 << ways) - 1]
    width = rows // HALVES
    spans = [(h * width, (h + 1) * width) for h in range(HALVES)]
    theirs = [stage([other], *end, accs[1:], coeff, cols, span)[0] for span in spans]
    received = [core_send(value, n_sl) for value in theirs]
    half = jax.ShapeDtypeStruct((cols, width), jnp.bfloat16)
    totals, acc = [], accs[0]
    for span, part in zip(spans, received):
        (mine,) = stage([slab], *end, [acc], coeff, cols, span)
        total = small_call(add_kernel, half, mine, part)
        acc, total = lax.optimization_barrier((acc, total))
        totals.append(total)
    turns = n_lm.bit_length() - 1
    for k in range(turns - 1):
        arrived = [lm_send(total, k, n_lm, n_sl) for total in totals]
        totals = [small_call(add_kernel, half, a, b) for a, b in zip(totals, arrived)]
    pairs = [(total, lm_send(total, turns - 1, n_lm, n_sl)) for total in totals]
    scale = functools.partial(scale_kernel, total_land=total_land)
    out = jax.ShapeDtypeStruct((cols, rows), jnp.float32)
    return small_call(scale, out, *(x for pair in pairs for x in pair), ritz[:, None]).T


def solution(mesh):
    return jax.shard_map(
        local,
        mesh=mesh,
        in_specs=(
            P("sl", None),
            P(("lm", "sl"), None),
            P(("lm", "sl"), None),
            P(("lm", "sl")),
            P(),
            P(),
        ),
        out_specs=P("sl", None),
        check_vma=False,
    )
```

profile of v0, /device:TPU:0, one launch (start us, length us, event | category | flops | bytes accessed | tf_op | source)
XLA Modules:
  0.0 39.7 jit_solution(1332070044477134016)
XLA Ops:
  0.0 1.1 %shard_map.65 = (bf16[144,1024]{1,0:T(8,128)(2,1)S(1)}, bf16[128,1024]{1,0:T(8,128)(2,1)S(1)}) custom-call(bf16[256,1024]{1,0:T(8,128)(2,1)} %land_ref.1, bf16[96,256]{1,0:T(8,128)(2,1)} %bitcast.4, s32[2]{0:T(128)} %exponents_ref.1, bf16[64,96]{1,0:T(8,128)(2,1)} %bitcast.5), custom_call_target="tpu_custom_call" | custom-call | tf_op jit(solution)/shard_map/pallas_call | solution.py:72
  1.6 2.6 %collective-permute-start.2 = (bf16[144,1024]{1,0:T(8,128)(2,1)S(1)}, bf16[144,1024]{1,0:T(8,128)(2,1)S(1)}, u32[]{:S(2)}, u32[]{:S(2)}) collective-permute-start(bf16[144,1024]{1,0:T(8,128)(2,1)S(1)} %get-tuple-element.18.refs_1_), channel_id=1, source_target_pairs={{0,2},{1,5},{2,0},{3,7},{4,6},{5,1},{6,4},{7,3},{8,10},{9,13},{10,... | collective-permute-start | bytes 884744 | tf_op jit(solution)/shard_map/ppermute | solution.py:23
  4.2 1.5 %collective-permute-start.3 = (bf16[128,1024]{1,0:T(8,128)(2,1)S(1)}, bf16[128,1024]{1,0:T(8,128)(2,1)S(1)}, u32[]{:S(2)}, u32[]{:S(2)}) collective-permute-start(bf16[128,1024]{1,0:T(8,128)(2,1)S(1)} %get-tuple-element.20.refs_2_), channel_id=1, source_target_pairs={{0,4},{1,3},{2,6},{3,1},{4,0},{5,7},{6,2},{7,5},{8,12},{9,11},{10,... | collective-permute-start | bytes 786440 | tf_op jit(solution)/shard_map/ppermute | solution.py:23
  6.3 1.6 %copy-done = bf16[1024,1024]{1,0:T(8,128)(2,1)S(1)} copy-done((bf16[1024,1024]{1,0:T(8,128)(2,1)S(1)}, bf16[1024,1024]{1,0:T(8,128)(2,1)}, u32[]{:S(2)}) %copy-start) | copy-done | bytes 2097176
  7.9 0.6 %shard_map.64.refs_0_ = bf16[1024,1024]{1,0:T(8,128)(2,1)S(1)} custom-call(bf16[1024,1024]{1,0:T(8,128)(2,1)S(1)} %copy-done), custom_call_target="tpu_custom_call" | custom-call | tf_op jit(solution)/shard_map/pallas_call | solution.py:159
  8.6 0.9 %shard_map.67.refs_4_ = f32[64,1024]{1,0:T(8,128)S(1)} custom-call(bf16[1024,1024]{1,0:T(8,128)(2,1)S(1)} %shard_map.64.refs_0_, bf16[144,1024]{1,0:T(8,128)(2,1)S(1)} %get-tuple-element.18.refs_1_, bf16[128,1024]{1,0:T(8,128)(2,1)S(1)} %get-tuple-element.20.refs_2_), custom_call_target="tpu_custom_call" | custom-call | flops 671088640 | bytes 2621440 | tf_op jit(solution)/shard_map/pallas_call | solution.py:130
  9.4 4.0 %collective-permute-done.3.refs_3_ = bf16[128,1024]{1,0:T(8,128)(2,1)S(1)} collective-permute-done((bf16[128,1024]{1,0:T(8,128)(2,1)S(1)}, bf16[128,1024]{1,0:T(8,128)(2,1)S(1)}, u32[]{:S(2)}, u32[]{:S(2)}) %collective-permute-start.3) | collective-permute-done | bytes 262176 | tf_op jit(solution)/shard_map/ppermute | solution.py:23
  13.5 1.5 %collective-permute-start.5 = (bf16[144,1024]{1,0:T(8,128)(2,1)S(1)}, bf16[144,1024]{1,0:T(8,128)(2,1)S(1)}, u32[]{:S(2)}, u32[]{:S(2)}) collective-permute-start(bf16[144,1024]{1,0:T(8,128)(2,1)S(1)} %collective-permute-done.2.refs_2_), channel_id=1, source_target_pairs={{0,4},{1,3},{2,6},{3,1},{4,0},{5,7},{6,2},{7,5},{8,12},{9,11},{10,... | collective-permute-start | bytes 884744 | tf_op jit(solution)/shard_map/ppermute | solution.py:23
  15.0 0.6 %collective-permute-start.6 = (bf16[128,1024]{1,0:T(8,128)(2,1)S(1)}, bf16[128,1024]{1,0:T(8,128)(2,1)S(1)}, u32[]{:S(2)}, u32[]{:S(2)}) collective-permute-start(bf16[128,1024]{1,0:T(8,128)(2,1)S(1)} %collective-permute-done.3.refs_3_), channel_id=1, source_target_pairs={{0,2},{1,5},{2,0},{3,7},{4,6},{5,1},{6,4},{7,3},{8,10},{9,13},{10,... | collective-permute-start | bytes 786440 | tf_op jit(solution)/shard_map/ppermute | solution.py:23
  15.6 0.6 %shard_map.66.refs_0_.refs_1_ = bf16[1024,1024]{1,0:T(8,128)(2,1)S(1)} custom-call(bf16[1024,1024]{1,0:T(8,128)(2,1)S(1)} %collective-permute-done.in_ref), custom_call_target="tpu_custom_call" | custom-call | tf_op jit(solution)/shard_map/pallas_call | solution.py:159
  16.3 0.9 %shard_map.68.refs_5_ = f32[64,1024]{1,0:T(8,128)S(1)} custom-call(bf16[1024,1024]{1,0:T(8,128)(2,1)S(1)} %shard_map.66.refs_0_.refs_1_, bf16[144,1024]{1,0:T(8,128)(2,1)S(1)} %get-tuple-element.18.refs_1_, bf16[128,1024]{1,0:T(8,128)(2,1)S(1)} %get-tuple-element.20.refs_2_), custom_call_target="tpu_custom_call" | custom-call | flops 671088640 | bytes 2621440 | tf_op jit(solution)/shard_map/pallas_call | solution.py:130
  17.1 1.5 %shard_map.69 = (f32[64,1024]{1,0:T(8,128)S(1)}, f32[64,1024]{1,0:T(8,128)S(1)}) custom-call(bf16[1024,1024]{1,0:T(8,128)(2,1)S(1)} %shard_map.64.refs_0_, bf16[1024,1024]{1,0:T(8,128)(2,1)S(1)} %shard_map.66.refs_0_.refs_1_, bf16[144,1024]{1,0:T(8,128)(2,1)S(1)} %collective-permute-done.2.refs_2_, bf16[128,1024]{1,0:T(8,128)(2,1)S(1)} %collective-permute-done.4.refs_3_, ...), custom_call_target="tpu_custom_call" | custom-call | flops 1342177280 | bytes 4718592 | tf_op jit(solution)/shard_map/pallas_call | solution.py:130
  18.8 1.5 %shard_map.70 = (f32[64,1024]{1,0:T(8,128)S(1)}, f32[64,1024]{1,0:T(8,128)S(1)}) custom-call(bf16[1024,1024]{1,0:T(8,128)(2,1)S(1)} %shard_map.64.refs_0_, bf16[1024,1024]{1,0:T(8,128)(2,1)S(1)} %shard_map.66.refs_0_.refs_1_, bf16[144,1024]{1,0:T(8,128)(2,1)S(1)} %collective-permute-done.1.refs_2_, bf16[128,1024]{1,0:T(8,128)(2,1)S(1)} %collective-permute-done.3.refs_3_, ...), custom_call_target="tpu_custom_call" | custom-call | flops 1342177280 | bytes 4718592 | tf_op jit(solution)/shard_map/pallas_call | solution.py:130
  20.4 3.3 %collective-permute-done.6.refs_2_ = bf16[128,1024]{1,0:T(8,128)(2,1)S(1)} collective-permute-done((bf16[128,1024]{1,0:T(8,128)(2,1)S(1)}, bf16[128,1024]{1,0:T(8,128)(2,1)S(1)}, u32[]{:S(2)}, u32[]{:S(2)}) %collective-permute-start.6) | collective-permute-done | bytes 262176 | tf_op jit(solution)/shard_map/ppermute | solution.py:23
  23.7 0.6 %shard_map.72 = f32[64,512]{1,0:T(8,128)S(1)} custom-call(bf16[1024,1024]{1,0:T(8,128)(2,1)S(1)} %shard_map.66.refs_0_.refs_1_, bf16[144,1024]{1,0:T(8,128)(2,1)S(1)} %collective-permute-done.5.refs_1_, bf16[128,1024]{1,0:T(8,128)(2,1)S(1)} %collective-permute-done.6.refs_2_, f32[64,1024]{1,0:T(8,128)S(1)} %get-tuple-element.27.refs_3_), custom_call_target="tpu_custom_call" | custom-call | flops 335544320 | bytes 1572864 | tf_op jit(solution)/shard_map/pallas_call | solution.py:130
  24.3 0.6 %shard_map.76 = f32[64,512]{1,0:T(8,128)S(1)} custom-call(bf16[1024,1024]{1,0:T(8,128)(2,1)S(1)} %shard_map.66.refs_0_.refs_1_, bf16[144,1024]{1,0:T(8,128)(2,1)S(1)} %collective-permute-done.5.refs_1_, bf16[128,1024]{1,0:T(8,128)(2,1)S(1)} %collective-permute-done.6.refs_2_, f32[64,1024]{1,0:T(8,128)S(1)} %get-tuple-element.27.refs_3_), custom_call_target="tpu_custom_call" | custom-call | flops 335544320 | bytes 1572864 | tf_op jit(solution)/shard_map/pallas_call | solution.py:130
  25.5 0.6 %shard_map.71.a_ref = f32[64,512]{1,0:T(8,128)S(1)} custom-call(bf16[1024,1024]{1,0:T(8,128)(2,1)S(1)} %shard_map.64.refs_0_, bf16[144,1024]{1,0:T(8,128)(2,1)S(1)} %collective-permute-done.5.refs_1_, bf16[128,1024]{1,0:T(8,128)(2,1)S(1)} %collective-permute-done.6.refs_2_, f32[64,1024]{1,0:T(8,128)S(1)} %get-tuple-element.29.refs_3_), custom_call_target="tpu_custom_call" | custom-call | flops 335544320 | bytes 1572864 | tf_op jit(solution)/shard_map/pallas_call | solution.py:130
  26.1 2.2 %collective-permute-start.8 = (bf16[64,512]{1,0:T(8,128)(2,1)S(1)}, bf16[64,512]{1,0:T(8,128)(2,1)S(1)}, u32[]{:S(2)}, u32[]{:S(2)}) collective-permute-start(bf16[64,512]{1,0:T(8,128)(2,1)S(1)} %shard_map.73.a_ref), channel_id=1, source_target_pairs={{0,8},{1,17},{2,10},{3,19},{4,12},{5,21},{6,14},{7,23},{8,0},{9,25... | collective-permute-start | bytes 196616 | tf_op jit(solution)/shard_map/ppermute | solution.py:33
  28.3 0.6 %shard_map.75.a_ref = f32[64,512]{1,0:T(8,128)S(1)} custom-call(bf16[1024,1024]{1,0:T(8,128)(2,1)S(1)} %shard_map.64.refs_0_, bf16[144,1024]{1,0:T(8,128)(2,1)S(1)} %collective-permute-done.5.refs_1_, bf16[128,1024]{1,0:T(8,128)(2,1)S(1)} %collective-permute-done.6.refs_2_, f32[64,1024]{1,0:T(8,128)S(1)} %get-tuple-element.29.refs_3_), custom_call_target="tpu_custom_call" | custom-call | flops 335544320 | bytes 1572864 | tf_op jit(solution)/shard_map/pallas_call | solution.py:130
  29.0 2.2 %collective-permute-done.8.b_ref = bf16[64,512]{1,0:T(8,128)(2,1)S(1)} collective-permute-done((bf16[64,512]{1,0:T(8,128)(2,1)S(1)}, bf16[64,512]{1,0:T(8,128)(2,1)S(1)}, u32[]{:S(2)}, u32[]{:S(2)}) %collective-permute-start.8) | collective-permute-done | bytes 65568 | tf_op jit(solution)/shard_map/ppermute | solution.py:33
  31.2 2.4 %collective-permute-start.9 = (bf16[64,512]{1,0:T(8,128)(2,1)S(1)}, bf16[64,512]{1,0:T(8,128)(2,1)S(1)}, u32[]{:S(2)}, u32[]{:S(2)}) collective-permute-start(bf16[64,512]{1,0:T(8,128)(2,1)S(1)} %shard_map.74.refs_0_), channel_id=1, source_target_pairs={{0,16},{1,9},{2,18},{3,11},{4,20},{5,13},{6,22},{7,15},{8,24},{9,1... | collective-permute-start | bytes 196616 | tf_op jit(solution)/shard_map/ppermute | solution.py:33
  33.7 2.6 %collective-permute-start.12 = (bf16[64,512]{1,0:T(8,128)(2,1)S(1)}, bf16[64,512]{1,0:T(8,128)(2,1)S(1)}, u32[]{:S(2)}, u32[]{:S(2)}) collective-permute-start(bf16[64,512]{1,0:T(8,128)(2,1)S(1)} %shard_map.78.refs_2_), channel_id=1, source_target_pairs={{0,16},{1,9},{2,18},{3,11},{4,20},{5,13},{6,22},{7,15},{8,24},{9,1... | collective-permute-start | bytes 196616 | tf_op jit(solution)/shard_map/ppermute | solution.py:33
  36.5 2.4 %collective-permute-done.12.refs_3_ = bf16[64,512]{1,0:T(8,128)(2,1)S(1)} collective-permute-done((bf16[64,512]{1,0:T(8,128)(2,1)S(1)}, bf16[64,512]{1,0:T(8,128)(2,1)S(1)}, u32[]{:S(2)}, u32[]{:S(2)}) %collective-permute-start.12) | collective-permute-done | bytes 65568 | tf_op jit(solution)/shard_map/ppermute | solution.py:33
  38.9 0.8 %shard_map.79 = f32[64,1024]{1,0:T(8,128)} custom-call(bf16[64,512]{1,0:T(8,128)(2,1)S(1)} %shard_map.74.refs_0_, bf16[64,512]{1,0:T(8,128)(2,1)S(1)} %collective-permute-done.9.refs_1_, bf16[64,512]{1,0:T(8,128)(2,1)S(1)} %shard_map.78.refs_2_, bf16[64,512]{1,0:T(8,128)(2,1)S(1)} %collective-permute-done.12.refs_3_, f32[64,1]{1,0:T(8,128)S(1)} %copy.7.refs_4_), custom_call_target="tpu_custom_call" | custom-call | tf_op jit(solution)/shard_map/pallas_call | solution.py:159
  (23 shorter events, 2.2 us)
Async XLA Ops:
  1.1 14.5 %collective-permute-start = (bf16[1024,1024]{1,0:T(8,128)(2,1)}, bf16[1024,1024]{1,0:T(8,128)(2,1)S(1)}, u32[]{:S(2)}, u32[]{:S(2)}) collective-permute-start(bf16[1024,1024]{1,0:T(8,128)(2,1)} %in_ref.1), channel_id=1, source_target_pairs={{0,1},{1,0},{2,3},{3,2},{4,5},{5,4},{6,7},{7,6},{8,9},{9,8},{10,11... | collective-permute-start | bytes 6291464 | tf_op jit(solution)/shard_map/ppermute | solution.py:18
  1.6 11.8 %collective-permute-start.2 = (bf16[144,1024]{1,0:T(8,128)(2,1)S(1)}, bf16[144,1024]{1,0:T(8,128)(2,1)S(1)}, u32[]{:S(2)}, u32[]{:S(2)}) collective-permute-start(bf16[144,1024]{1,0:T(8,128)(2,1)S(1)} %get-tuple-element.18.refs_1_), channel_id=1, source_target_pairs={{0,2},{1,5},{2,0},{3,7},{4,6},{5,1},{6,4},{7,3},{8,10},{9,13},{10,... | collective-permute-start | bytes 884744 | tf_op jit(solution)/shard_map/ppermute | solution.py:23
  4.2 9.2 %collective-permute-start.3 = (bf16[128,1024]{1,0:T(8,128)(2,1)S(1)}, bf16[128,1024]{1,0:T(8,128)(2,1)S(1)}, u32[]{:S(2)}, u32[]{:S(2)}) collective-permute-start(bf16[128,1024]{1,0:T(8,128)(2,1)S(1)} %get-tuple-element.20.refs_2_), channel_id=1, source_target_pairs={{0,4},{1,3},{2,6},{3,1},{4,0},{5,7},{6,2},{7,5},{8,12},{9,11},{10,... | collective-permute-start | bytes 786440 | tf_op jit(solution)/shard_map/ppermute | solution.py:23
  5.7 11.4 %collective-permute-start.4 = (bf16[128,1024]{1,0:T(8,128)(2,1)S(1)}, bf16[128,1024]{1,0:T(8,128)(2,1)S(1)}, u32[]{:S(2)}, u32[]{:S(2)}) collective-permute-start(bf16[128,1024]{1,0:T(8,128)(2,1)S(1)} %get-tuple-element.20.refs_2_), channel_id=1, source_target_pairs={{0,2},{1,5},{2,0},{3,7},{4,6},{5,1},{6,4},{7,3},{8,10},{9,13},{10,... | collective-permute-start | bytes 786440 | tf_op jit(solution)/shard_map/ppermute | solution.py:23
  6.3 12.6 %collective-permute-start.1 = (bf16[144,1024]{1,0:T(8,128)(2,1)S(1)}, bf16[144,1024]{1,0:T(8,128)(2,1)S(1)}, u32[]{:S(2)}, u32[]{:S(2)}) collective-permute-start(bf16[144,1024]{1,0:T(8,128)(2,1)S(1)} %get-tuple-element.18.refs_1_), channel_id=1, source_target_pairs={{0,4},{1,3},{2,6},{3,1},{4,0},{5,7},{6,2},{7,5},{8,12},{9,11},{10,... | collective-permute-start | bytes 884744 | tf_op jit(solution)/shard_map/ppermute | solution.py:23
  6.3 1.6 %copy-start = (bf16[1024,1024]{1,0:T(8,128)(2,1)S(1)}, bf16[1024,1024]{1,0:T(8,128)(2,1)}, u32[]{:S(2)}) copy-start(bf16[1024,1024]{1,0:T(8,128)(2,1)} %in_ref.1) | copy-start | bytes 6291460
  13.5 10.2 %collective-permute-start.5 = (bf16[144,1024]{1,0:T(8,128)(2,1)S(1)}, bf16[144,1024]{1,0:T(8,128)(2,1)S(1)}, u32[]{:S(2)}, u32[]{:S(2)}) collective-permute-start(bf16[144,1024]{1,0:T(8,128)(2,1)S(1)} %collective-permute-done.2.refs_2_), channel_id=1, source_target_pairs={{0,4},{1,3},{2,6},{3,1},{4,0},{5,7},{6,2},{7,5},{8,12},{9,11},{10,... | collective-permute-start | bytes 884744 | tf_op jit(solution)/shard_map/ppermute | solution.py:23
  15.0 8.7 %collective-permute-start.6 = (bf16[128,1024]{1,0:T(8,128)(2,1)S(1)}, bf16[128,1024]{1,0:T(8,128)(2,1)S(1)}, u32[]{:S(2)}, u32[]{:S(2)}) collective-permute-start(bf16[128,1024]{1,0:T(8,128)(2,1)S(1)} %collective-permute-done.3.refs_3_), channel_id=1, source_target_pairs={{0,2},{1,5},{2,0},{3,7},{4,6},{5,1},{6,4},{7,3},{8,10},{9,13},{10,... | collective-permute-start | bytes 786440 | tf_op jit(solution)/shard_map/ppermute | solution.py:23
  24.3 1.8 %collective-permute-start.7 = (f32[64,512]{1,0:T(8,128)S(1)}, f32[64,512]{1,0:T(8,128)S(1)}, u32[]{:S(2)}, u32[]{:S(2)}) collective-permute-start(f32[64,512]{1,0:T(8,128)S(1)} %shard_map.72), channel_id=1, source_target_pairs={{0,1},{1,0},{2,3},{3,2},{4,5},{5,4},{6,7},{7,6},{8,9},{9,8},{10,11... | collective-permute-start | bytes 393224 | tf_op jit(solution)/shard_map/ppermute | solution.py:18
  24.9 3.9 %collective-permute-start.10 = (f32[64,512]{1,0:T(8,128)S(1)}, f32[64,512]{1,0:T(8,128)S(1)}, u32[]{:S(2)}, u32[]{:S(2)}) collective-permute-start(f32[64,512]{1,0:T(8,128)S(1)} %shard_map.76), channel_id=1, source_target_pairs={{0,1},{1,0},{2,3},{3,2},{4,5},{5,4},{6,7},{7,6},{8,9},{9,8},{10,11... | collective-permute-start | bytes 393224 | tf_op jit(solution)/shard_map/ppermute | solution.py:18
  26.1 10.3 %copy-start.1 = (f32[64]{0:T(128)S(1)}, f32[64]{0:T(128)}, u32[]{:S(2)}) copy-start(f32[64]{0:T(128)} %param.11) | copy-start | bytes 772
  26.1 5.1 %collective-permute-start.8 = (bf16[64,512]{1,0:T(8,128)(2,1)S(1)}, bf16[64,512]{1,0:T(8,128)(2,1)S(1)}, u32[]{:S(2)}, u32[]{:S(2)}) collective-permute-start(bf16[64,512]{1,0:T(8,128)(2,1)S(1)} %shard_map.73.a_ref), channel_id=1, source_target_pairs={{0,8},{1,17},{2,10},{3,19},{4,12},{5,21},{6,14},{7,23},{8,0},{9,25... | collective-permute-start | bytes 196616 | tf_op jit(solution)/shard_map/ppermute | solution.py:33
  28.9 4.7 %collective-permute-start.11 = (bf16[64,512]{1,0:T(8,128)(2,1)S(1)}, bf16[64,512]{1,0:T(8,128)(2,1)S(1)}, u32[]{:S(2)}, u32[]{:S(2)}) collective-permute-start(bf16[64,512]{1,0:T(8,128)(2,1)S(1)} %shard_map.77.a_ref), channel_id=1, source_target_pairs={{0,8},{1,17},{2,10},{3,19},{4,12},{5,21},{6,14},{7,23},{8,0},{9,25... | collective-permute-start | bytes 196616 | tf_op jit(solution)/shard_map/ppermute | solution.py:33
  31.2 5.2 %collective-permute-start.9 = (bf16[64,512]{1,0:T(8,128)(2,1)S(1)}, bf16[64,512]{1,0:T(8,128)(2,1)S(1)}, u32[]{:S(2)}, u32[]{:S(2)}) collective-permute-start(bf16[64,512]{1,0:T(8,128)(2,1)S(1)} %shard_map.74.refs_0_), channel_id=1, source_target_pairs={{0,16},{1,9},{2,18},{3,11},{4,20},{5,13},{6,22},{7,15},{8,24},{9,1... | collective-permute-start | bytes 196616 | tf_op jit(solution)/shard_map/ppermute | solution.py:33
  33.7 5.2 %collective-permute-start.12 = (bf16[64,512]{1,0:T(8,128)(2,1)S(1)}, bf16[64,512]{1,0:T(8,128)(2,1)S(1)}, u32[]{:S(2)}, u32[]{:S(2)}) collective-permute-start(bf16[64,512]{1,0:T(8,128)(2,1)S(1)} %shard_map.78.refs_2_), channel_id=1, source_target_pairs={{0,16},{1,9},{2,18},{3,11},{4,20},{5,13},{6,22},{7,15},{8,24},{9,1... | collective-permute-start | bytes 196616 | tf_op jit(solution)/shard_map/ppermute | solution.py:33
where the time goes:
time: 39.9 us; the launch traced here: 39.7 us
  starting transfers between devices  15.3 us (38%)
  waiting for transfers between devices  12.3 us (31%)
  Pallas kernels  10.4 us (26%)
  local copies, waits for them, and re-layouts  1.69 us (4%)
    ppermute x6, waiting for transfers between devices, chip_send(): lax.ppermute(value, 'sl', [(i, i ^ bits[(k + i % 2) % len(bits)]) for i i...  7.51 us
    ppermute x4, starting transfers between devices, lm_send(): return lax.ppermute(value, ('lm', 'sl'), perm)  7.29 us
    pallas_call x8, Pallas kernels, stage(): pl.pallas_call(functools.partial(stage_kernel, count, coeff, ritz, accs i...  7.14 us
    ppermute x6, starting transfers between devices, chip_send(): lax.ppermute(value, 'sl', [(i, i ^ bits[(k + i % 2) % len(bits)]) for i i...  6.82 us
    ppermute x4, waiting for transfers between devices, lm_send(): return lax.ppermute(value, ('lm', 'sl'), perm)  4.74 us
    pallas_call x7, Pallas kernels, small_call(): pl.pallas_call(kernel, out_shape=jax.ShapeDtypeStruct(out.shape, out.dtyp...  2.13 us
    unnamed x4, local copies, waits for them, and re-layouts  1.6 us
    ppermute x3, starting transfers between devices, core_send(): return lax.ppermute(value, 'sl', [(i, i ^ 1) for i in range(n)])  1.14 us
  transfers between devices with their start and end apart: 13, of which 6 were waited for; matrix products, arithmetic and copies ran while one was open for 0% of the time, Pallas kernels for 20%

commit v1 on v0

--- a/solution.py
+++ b/solution.py
@@ -9,8 +9,8 @@
 from jax.sharding import PartitionSpec as P
 
 BLOCK = 128
+SHIFT = 16
 CHUNK = 512
-HALVES = 2
 MIB = 2**20
 
 
@@ -34,17 +34,16 @@
 
 
 def prepare_kernel(
-    land_ref, codes_ref, exponents_ref, eig_ref, first_ref, second_ref, codes, eig, exponents, sems
+    land_ref, codes_ref, exponents_ref, eig_ref, first_ref, codes, eig, exponents, sems
 ):
     rows, feat = land_ref.shape
-    half = rows - second_ref.shape[0]
+    half = rows // 2 - SHIFT
     ritz = eig_ref.shape[0]
     pairs = [
         (codes_ref, codes),
         (eig_ref, eig),
         (exponents_ref, exponents),
         (land_ref.at[:half], first_ref.at[:half]),
-        (land_ref.at[half:], second_ref),
     ]
     copies = [pltpu.make_async_copy(src, dst, sems.at[k]) for k, (src, dst) in enumerate(pairs)]
     for copy in copies:
@@ -65,22 +64,35 @@
         copy.wait()
 
 
+def tail_kernel(land_ref, out_ref, sem):
+    copy = pltpu.make_async_copy(land_ref.at[land_ref.shape[0] - out_ref.shape[0] :], out_ref, sem)
+    copy.start()
+    copy.wait()
+
+
+def second_half(landmarks):
+    rows, feat = landmarks.shape
+    return pl.pallas_call(
+        tail_kernel,
+        out_shape=jax.ShapeDtypeStruct((rows // 2 + SHIFT, feat), jnp.bfloat16),
+        in_specs=[pl.BlockSpec(memory_space=pltpu.HBM)],
+        scratch_shapes=[pltpu.SemaphoreType.DMA],
+        compiler_params=pltpu.CompilerParams(vmem_limit_bytes=8 * MIB),
+    )(pltpu.with_memory_space_constraint(landmarks, pltpu.HBM))
+
+
 def prepare(landmarks, codes_t, exponents, eig_t):
     rows, feat = landmarks.shape
     extra = eig_t.shape[0] * rows // feat
-    head = rows // 2
     return pl.pallas_call(
         prepare_kernel,
-        out_shape=[
-            jax.ShapeDtypeStruct((head + extra, feat), jnp.bfloat16),
-            jax.ShapeDtypeStruct((rows - head, feat), jnp.bfloat16),
-        ],
+        out_shape=jax.ShapeDtypeStruct((rows // 2 - SHIFT + extra, feat), jnp.bfloat16),
         in_specs=[pl.BlockSpec(memory_space=pltpu.HBM)] * 4,
         scratch_shapes=[
             pltpu.VMEM(codes_t.shape, codes_t.dtype),
             pltpu.VMEM(eig_t.shape, eig_t.dtype),
             pltpu.SMEM(exponents.shape, exponents.dtype),
-            pltpu.SemaphoreType.DMA((5,)),
+            pltpu.SemaphoreType.DMA((4,)),
         ],
         compiler_params=pltpu.CompilerParams(vmem_limit_bytes=8 * MIB),
     )(*(pltpu.with_memory_space_constraint(x, pltpu.HBM) for x in (landmarks, codes_t, exponents, eig_t)))
@@ -92,8 +104,7 @@
         out_ref[:, rows] = in_ref[rows, :].T
 
 
-def stage_kernel(count, coeff, ritz, has_acc, span, *refs):
-    start, stop = span
+def stage_kernel(count, coeff, ritz, has_acc, spans, *refs):
     slabs = refs[:count]
     first_ref, second_ref = refs[count : count + 2]
     accs = refs[count + 2 : 2 * count + 2] if has_acc else [None] * count
@@ -106,7 +117,9 @@
         [first_ref[head:, c * rows : (c + 1) * rows] for c in range(feat // rows)], axis=0
     )
     work = [
-        (k, slice(c, min(c + CHUNK, stop))) for k in range(count) for c in range(start, stop, CHUNK)
+        (k, slice(c, min(c + CHUNK, stop)))
+        for k, (start, stop) in enumerate(spans)
+        for c in range(start, stop, CHUNK)
     ]
 
     def scores(k, cols):
@@ -117,18 +130,18 @@
         now, ahead = ahead, scores(*work[n + 1]) if n + 1 < len(work) else None
         affinity = jnp.exp(now * coeff).astype(jnp.bfloat16)
         term = jnp.dot(vec, affinity, preferred_element_type=jnp.float32)
-        place = slice(cols.start - start, cols.stop - start)
+        place = slice(cols.start - spans[k][0], cols.stop - spans[k][0])
         outs[k][:, place] = term if accs[k] is None else accs[k][:, cols] + term
 
 
-def stage(slabs, first, second, accs, coeff, ritz, span=None):
+def stage(slabs, first, second, accs, coeff, ritz, spans=None):
     feat, rows = slabs[0].shape
-    span = span or (0, rows)
-    rows = span[1] - span[0]
     land = (first.shape[0] + second.shape[0]) * feat // (feat + ritz)
     count = len(slabs)
-    return pl.pallas_call(
-        functools.partial(stage_kernel, count, coeff, ritz, accs is not None, span),
+    spans = spans or [(0, rows)] * count
+    rows = spans[0][1] - spans[0][0]
+    return pl.pallas_call(
+        functools.partial(stage_kernel, count, coeff, ritz, accs is not None, spans),
         out_shape=[jax.ShapeDtypeStruct((ritz, rows), jnp.float32)] * count,
         compiler_params=pltpu.CompilerParams(vmem_limit_bytes=32 * MIB),
         cost_estimate=pl.CostEstimate(
@@ -171,7 +184,8 @@
     rows = slab.shape[0]
     ways = n_sl.bit_length() - 2
 
-    first, second = prepare(landmarks, codes.T, exponents, eigvec.T)
+    second = second_half(landmarks)
+    first = prepare(landmarks, codes.T, exponents, eigvec.T)
     blocks = {0: [first, second]}
     for k in range(ways):
         blocks[1 << k] = [None, None]
@@ -179,7 +193,7 @@
         for k in range(ways):
             piece = (k + turn) % 2
             blocks[1 << k][piece] = chip_send(blocks[0][piece], k, n_sl)
-    late_slab, _ = lax.optimization_barrier((slab, first))
+    late_slab, _ = lax.optimization_barrier((slab, second))
     turned = jax.ShapeDtypeStruct(slab.shape[::-1], slab.dtype)
     other = small_call(transpose_kernel, turned, core_send(late_slab, n_sl))
     slab = small_call(transpose_kernel, turned, slab)
@@ -202,17 +216,17 @@
     for t in range(1, (1 << ways) - 1):
         accs = stage([slab, other], *blocks[t], accs, coeff, cols)
     end = blocks[(1 << ways) - 1]
-    width = rows // HALVES
-    spans = [(h * width, (h + 1) * width) for h in range(HALVES)]
-    theirs = [stage([other], *end, accs[1:], coeff, cols, span)[0] for span in spans]
-    received = [core_send(value, n_sl) for value in theirs]
+    width = rows // 2
+    spans = [(0, width), (width, rows)]
     half = jax.ShapeDtypeStruct((cols, width), jnp.bfloat16)
-    totals, acc = [], accs[0]
-    for span, part in zip(spans, received):
-        (mine,) = stage([slab], *end, [acc], coeff, cols, span)
-        total = small_call(add_kernel, half, mine, part)
-        acc, total = lax.optimization_barrier((acc, total))
-        totals.append(total)
+    (early,) = stage([other], *end, accs[1:], coeff, cols, spans[:1])
+    received = [core_send(early, n_sl)]
+    late, mine = stage([other, slab], *end, accs[::-1], coeff, cols, spans[::-1])
+    received.append(core_send(late, n_sl))
+    total = small_call(add_kernel, half, mine, received[0])
+    acc, total = lax.optimization_barrier((accs[0], total))
+    (mine,) = stage([slab], *end, [acc], coeff, cols, spans[1:])
+    totals = [total, small_call(add_kernel, half, mine, received[1])]
     turns = n_lm.bit_length() - 1
     for k in range(turns - 1):
         arrived = [lm_send(total, k, n_lm, n_sl) for total in totals]

time: 39.9 us -> 38.9 us (0.975)
  waiting for transfers between devices: 12.3 us -> 10.3 us
  Pallas kernels: 10.4 us -> 11 us
    ppermute x6, waiting for transfers between devices: 7.51 us -> 5.92 us  [chip_send(): lax.ppermute(value, 'sl', [(i, i ^ bits[(k + i % 2) % len(bits)]) for i i...]
    pallas_call x1 -> x2, Pallas kernels: 1.12 us -> 1.99 us  [the longest x1 1.02 us: prepare(): pl.pallas_call(prepare_kernel, out_shape=jax.ShapeDtypeStruct((rows // 2...]
    ppermute x6, starting transfers between devices: 6.82 us -> 7.36 us  [chip_send(): lax.ppermute(value, 'sl', [(i, i ^ bits[(k + i % 2) % len(bits)]) for i i...]
    pallas_call x8 -> x7, Pallas kernels: 7.14 us -> 6.83 us  [stage(): pl.pallas_call(functools.partial(stage_kernel, count, coeff, ritz, accs i...]
  transfers between devices with their start and end apart: 13 -> 13, of which waited for: 6 -> 7; matrix products, arithmetic and copies ran while one was open for 0% -> 0% of each run, Pallas kernels for 20% -> 22%
where the time goes in v1:
time: 38.9 us; the launch traced here: 38.7 us
  starting transfers between devices  15.6 us (40%)
  Pallas kernels  11 us (28%)
  waiting for transfers between devices  10.3 us (26%)
  local copies, waits for them, and re-layouts  1.69 us (4%)
    ppermute x6, starting transfers between devices, chip_send(): lax.ppermute(value, 'sl', [(i, i ^ bits[(k + i % 2) % len(bits)]) for i i...  7.36 us
    ppermute x4, starting transfers between devices, lm_send(): return lax.ppermute(value, ('lm', 'sl'), perm)  7.11 us
    pallas_call x7, Pallas kernels, stage(): pl.pallas_call(functools.partial(stage_kernel, count, coeff, ritz, accs i...  6.83 us
    ppermute x6, waiting for transfers between devices, chip_send(): lax.ppermute(value, 'sl', [(i, i ^ bits[(k + i % 2) % len(bits)]) for i i...  5.92 us
    ppermute x4, waiting for transfers between devices, lm_send(): return lax.ppermute(value, ('lm', 'sl'), perm)  4.4 us
    pallas_call x7, Pallas kernels, small_call(): pl.pallas_call(kernel, out_shape=jax.ShapeDtypeStruct(out.shape, out.dtyp...  2.13 us
    unnamed x4, local copies, waits for them, and re-layouts  1.59 us
    ppermute x3, starting transfers between devices, core_send(): return lax.ppermute(value, 'sl', [(i, i ^ 1) for i in range(n)])  1.16 us
  transfers between devices with their start and end apart: 13, of which 7 were waited for; matrix products, arithmetic and copies ran while one was open for 0% of the time, Pallas kernels for 22%

profile of v1, /device:TPU:0, one launch (start us, length us, event | category | flops | bytes accessed | tf_op | source)
XLA Modules:
  0.0 38.7 jit_solution(8002944153154378134)
XLA Ops:
  0.0 1.0 %shard_map.65.refs_2_ = bf16[144,1024]{1,0:T(8,128)(2,1)S(1)} custom-call(bf16[256,1024]{1,0:T(8,128)(2,1)} %land_ref.3), custom_call_target="tpu_custom_call" | custom-call | tf_op jit(solution)/shard_map/pallas_call | solution.py:75
  1.5 2.6 %collective-permute-start.3 = (bf16[144,1024]{1,0:T(8,128)(2,1)S(1)}, bf16[144,1024]{1,0:T(8,128)(2,1)S(1)}, u32[]{:S(2)}, u32[]{:S(2)}) collective-permute-start(bf16[144,1024]{1,0:T(8,128)(2,1)S(1)} %shard_map.65.refs_2_), channel_id=1, source_target_pairs={{0,4},{1,3},{2,6},{3,1},{4,0},{5,7},{6,2},{7,5},{8,12},{9,11},{10,... | collective-permute-start | bytes 884744 | tf_op jit(solution)/shard_map/ppermute | solution.py:23
  4.1 1.0 %shard_map.67.refs_1_ = bf16[128,1024]{1,0:T(8,128)(2,1)S(1)} custom-call(bf16[256,1024]{1,0:T(8,128)(2,1)} %land_ref.3, bf16[96,256]{1,0:T(8,128)(2,1)} %bitcast.4, s32[2]{0:T(128)} %exponents_ref.1, bf16[64,96]{1,0:T(8,128)(2,1)} %bitcast.5), custom_call_target="tpu_custom_call" | custom-call | tf_op jit(solution)/shard_map/pallas_call | solution.py:87
  5.1 1.6 %collective-permute-start.2 = (bf16[128,1024]{1,0:T(8,128)(2,1)S(1)}, bf16[128,1024]{1,0:T(8,128)(2,1)S(1)}, u32[]{:S(2)}, u32[]{:S(2)}) collective-permute-start(bf16[128,1024]{1,0:T(8,128)(2,1)S(1)} %shard_map.67.refs_1_), channel_id=1, source_target_pairs={{0,2},{1,5},{2,0},{3,7},{4,6},{5,1},{6,4},{7,3},{8,10},{9,13},{10,... | collective-permute-start | bytes 786440 | tf_op jit(solution)/shard_map/ppermute | solution.py:23
  7.3 1.6 %copy-done = bf16[1024,1024]{1,0:T(8,128)(2,1)S(1)} copy-done((bf16[1024,1024]{1,0:T(8,128)(2,1)S(1)}, bf16[1024,1024]{1,0:T(8,128)(2,1)}, u32[]{:S(2)}) %copy-start) | copy-done | bytes 2097176
  8.9 0.6 %shard_map.64.refs_0_.refs_1_ = bf16[1024,1024]{1,0:T(8,128)(2,1)S(1)} custom-call(bf16[1024,1024]{1,0:T(8,128)(2,1)S(1)} %copy-done), custom_call_target="tpu_custom_call" | custom-call | tf_op jit(solution)/shard_map/pallas_call | solution.py:172
  9.5 0.9 %shard_map.68.refs_4_ = f32[64,1024]{1,0:T(8,128)S(1)} custom-call(bf16[1024,1024]{1,0:T(8,128)(2,1)S(1)} %shard_map.64.refs_0_.refs_1_, bf16[128,1024]{1,0:T(8,128)(2,1)S(1)} %shard_map.67.refs_1_, bf16[144,1024]{1,0:T(8,128)(2,1)S(1)} %shard_map.65.refs_2_), custom_call_target="tpu_custom_call" | custom-call | flops 671088640 | bytes 2621440 | tf_op jit(solution)/shard_map/pallas_call | solution.py:143
  10.4 3.4 %collective-permute-done.2.refs_2_ = bf16[128,1024]{1,0:T(8,128)(2,1)S(1)} collective-permute-done((bf16[128,1024]{1,0:T(8,128)(2,1)S(1)}, bf16[128,1024]{1,0:T(8,128)(2,1)S(1)}, u32[]{:S(2)}, u32[]{:S(2)}) %collective-permute-start.2) | collective-permute-done | bytes 262176 | tf_op jit(solution)/shard_map/ppermute | solution.py:23
  13.8 0.6 %collective-permute-start.5 = (bf16[128,1024]{1,0:T(8,128)(2,1)S(1)}, bf16[128,1024]{1,0:T(8,128)(2,1)S(1)}, u32[]{:S(2)}, u32[]{:S(2)}) collective-permute-start(bf16[128,1024]{1,0:T(8,128)(2,1)S(1)} %collective-permute-done.2.refs_2_), channel_id=1, source_target_pairs={{0,4},{1,3},{2,6},{3,1},{4,0},{5,7},{6,2},{7,5},{8,12},{9,11},{10,... | collective-permute-start | bytes 786440 | tf_op jit(solution)/shard_map/ppermute | solution.py:23
  14.4 2.0 %collective-permute-start.6 = (bf16[144,1024]{1,0:T(8,128)(2,1)S(1)}, bf16[144,1024]{1,0:T(8,128)(2,1)S(1)}, u32[]{:S(2)}, u32[]{:S(2)}) collective-permute-start(bf16[144,1024]{1,0:T(8,128)(2,1)S(1)} %collective-permute-done.3.refs_3_), channel_id=1, source_target_pairs={{0,2},{1,5},{2,0},{3,7},{4,6},{5,1},{6,4},{7,3},{8,10},{9,13},{10,... | collective-permute-start | bytes 884744 | tf_op jit(solution)/shard_map/ppermute | solution.py:23
  16.4 0.6 %shard_map.66.refs_0_.refs_1_ = bf16[1024,1024]{1,0:T(8,128)(2,1)S(1)} custom-call(bf16[1024,1024]{1,0:T(8,128)(2,1)S(1)} %collective-permute-done.in_ref), custom_call_target="tpu_custom_call" | custom-call | tf_op jit(solution)/shard_map/pallas_call | solution.py:172
  17.1 0.9 %shard_map.69.refs_5_ = f32[64,1024]{1,0:T(8,128)S(1)} custom-call(bf16[1024,1024]{1,0:T(8,128)(2,1)S(1)} %shard_map.66.refs_0_.refs_1_, bf16[128,1024]{1,0:T(8,128)(2,1)S(1)} %shard_map.67.refs_1_, bf16[144,1024]{1,0:T(8,128)(2,1)S(1)} %shard_map.65.refs_2_), custom_call_target="tpu_custom_call" | custom-call | flops 671088640 | bytes 2621440 | tf_op jit(solution)/shard_map/pallas_call | solution.py:143
  17.9 1.7 %collective-permute-done.4.refs_3_ = bf16[144,1024]{1,0:T(8,128)(2,1)S(1)} collective-permute-done((bf16[144,1024]{1,0:T(8,128)(2,1)S(1)}, bf16[144,1024]{1,0:T(8,128)(2,1)S(1)}, u32[]{:S(2)}, u32[]{:S(2)}) %collective-permute-start.4) | collective-permute-done | bytes 294944 | tf_op jit(solution)/shard_map/ppermute | solution.py:23
  19.6 1.5 %shard_map.70 = (f32[64,1024]{1,0:T(8,128)S(1)}, f32[64,1024]{1,0:T(8,128)S(1)}) custom-call(bf16[1024,1024]{1,0:T(8,128)(2,1)S(1)} %shard_map.64.refs_0_.refs_1_, bf16[1024,1024]{1,0:T(8,128)(2,1)S(1)} %shard_map.66.refs_0_.refs_1_, bf16[128,1024]{1,0:T(8,128)(2,1)S(1)} %collective-permute-done.2.refs_2_, ...), custom_call_target="tpu_custom_call" | custom-call | flops 1342177280 | bytes 4718592 | tf_op jit(solution)/shard_map/pallas_call | solution.py:143
  21.2 1.5 %shard_map.71 = (f32[64,1024]{1,0:T(8,128)S(1)}, f32[64,1024]{1,0:T(8,128)S(1)}) custom-call(bf16[1024,1024]{1,0:T(8,128)(2,1)S(1)} %shard_map.64.refs_0_.refs_1_, bf16[1024,1024]{1,0:T(8,128)(2,1)S(1)} %shard_map.66.refs_0_.refs_1_, bf16[128,1024]{1,0:T(8,128)(2,1)S(1)} %collective-permute-done.1.refs_2_, ...), custom_call_target="tpu_custom_call" | custom-call | flops 1342177280 | bytes 4718592 | tf_op jit(solution)/shard_map/pallas_call | solution.py:143
  23.5 0.6 %shard_map.73 = f32[64,512]{1,0:T(8,128)S(1)} custom-call(bf16[1024,1024]{1,0:T(8,128)(2,1)S(1)} %shard_map.66.refs_0_.refs_1_, bf16[128,1024]{1,0:T(8,128)(2,1)S(1)} %collective-permute-done.5.refs_2_.refs_1_, bf16[144,1024]{1,0:T(8,128)(2,1)S(1)} %collective-permute-done.6.refs_3_.refs_2_, f32[64,1024]{1,0:T(8,128)S(1)} %get-tuple-element.24.refs_4_.refs_3_), custom_call_target="tpu_custom_call" | custom-call | flops 335544320 | bytes 1572864 | tf_op jit(solution)/shard_map/pallas_call | solution.py:143
  24.3 0.9 %shard_map.72 = (f32[64,512]{1,0:T(8,128)S(1)}, f32[64,512]{1,0:T(8,128)S(1)}) custom-call(bf16[1024,1024]{1,0:T(8,128)(2,1)S(1)} %shard_map.66.refs_0_.refs_1_, bf16[1024,1024]{1,0:T(8,128)(2,1)S(1)} %shard_map.64.refs_0_.refs_1_, bf16[128,1024]{1,0:T(8,128)(2,1)S(1)} %collective-permute-done.5.refs_2_.refs_1_, ...), custom_call_target="tpu_custom_call" | custom-call | flops 671088640 | bytes 2621440 | tf_op jit(solution)/shard_map/pallas_call | solution.py:143
  25.6 1.6 %collective-permute-start.8 = (bf16[64,512]{1,0:T(8,128)(2,1)S(1)}, bf16[64,512]{1,0:T(8,128)(2,1)S(1)}, u32[]{:S(2)}, u32[]{:S(2)}) collective-permute-start(bf16[64,512]{1,0:T(8,128)(2,1)S(1)} %shard_map.74.a_ref), channel_id=1, source_target_pairs={{0,8},{1,17},{2,10},{3,19},{4,12},{5,21},{6,14},{7,23},{8,0},{9,25... | collective-permute-start | bytes 196616 | tf_op jit(solution)/shard_map/ppermute | solution.py:33
  27.3 0.6 %shard_map.76.a_ref = f32[64,512]{1,0:T(8,128)S(1)} custom-call(bf16[1024,1024]{1,0:T(8,128)(2,1)S(1)} %shard_map.64.refs_0_.refs_1_, bf16[128,1024]{1,0:T(8,128)(2,1)S(1)} %collective-permute-done.5.refs_2_.refs_1_, bf16[144,1024]{1,0:T(8,128)(2,1)S(1)} %collective-permute-done.6.refs_3_.refs_2_, f32[64,1024]{1,0:T(8,128)S(1)} %get-tuple-element.27.refs_5_.refs_3_), custom_call_target="tpu_custom_call" | custom-call | flops 335544320 | bytes 1572864 | tf_op jit(solution)/shard_map/pallas_call | solution.py:143
  28.5 2.2 %collective-permute-done.8.b_ref = bf16[64,512]{1,0:T(8,128)(2,1)S(1)} collective-permute-done((bf16[64,512]{1,0:T(8,128)(2,1)S(1)}, bf16[64,512]{1,0:T(8,128)(2,1)S(1)}, u32[]{:S(2)}, u32[]{:S(2)}) %collective-permute-start.8) | collective-permute-done | bytes 65568 | tf_op jit(solution)/shard_map/ppermute | solution.py:33
  30.7 2.0 %collective-permute-start.9 = (bf16[64,512]{1,0:T(8,128)(2,1)S(1)}, bf16[64,512]{1,0:T(8,128)(2,1)S(1)}, u32[]{:S(2)}, u32[]{:S(2)}) collective-permute-start(bf16[64,512]{1,0:T(8,128)(2,1)S(1)} %shard_map.75.refs_0_), channel_id=1, source_target_pairs={{0,16},{1,9},{2,18},{3,11},{4,20},{5,13},{6,22},{7,15},{8,24},{9,1... | collective-permute-start | bytes 196616 | tf_op jit(solution)/shard_map/ppermute | solution.py:33
  32.7 2.9 %collective-permute-start.12 = (bf16[64,512]{1,0:T(8,128)(2,1)S(1)}, bf16[64,512]{1,0:T(8,128)(2,1)S(1)}, u32[]{:S(2)}, u32[]{:S(2)}) collective-permute-start(bf16[64,512]{1,0:T(8,128)(2,1)S(1)} %shard_map.78.refs_2_), channel_id=1, source_target_pairs={{0,16},{1,9},{2,18},{3,11},{4,20},{5,13},{6,22},{7,15},{8,24},{9,1... | collective-permute-start | bytes 196616 | tf_op jit(solution)/shard_map/ppermute | solution.py:33
  35.9 2.0 %collective-permute-done.12.refs_3_ = bf16[64,512]{1,0:T(8,128)(2,1)S(1)} collective-permute-done((bf16[64,512]{1,0:T(8,128)(2,1)S(1)}, bf16[64,512]{1,0:T(8,128)(2,1)S(1)}, u32[]{:S(2)}, u32[]{:S(2)}) %collective-permute-start.12) | collective-permute-done | bytes 65568 | tf_op jit(solution)/shard_map/ppermute | solution.py:33
  37.9 0.8 %shard_map.79 = f32[64,1024]{1,0:T(8,128)} custom-call(bf16[64,512]{1,0:T(8,128)(2,1)S(1)} %shard_map.75.refs_0_, bf16[64,512]{1,0:T(8,128)(2,1)S(1)} %collective-permute-done.9.refs_1_, bf16[64,512]{1,0:T(8,128)(2,1)S(1)} %shard_map.78.refs_2_, bf16[64,512]{1,0:T(8,128)(2,1)S(1)} %collective-permute-done.12.refs_3_, f32[64,1]{1,0:T(8,128)S(1)} %copy.7.refs_4_), custom_call_target="tpu_custom_call" | custom-call | tf_op jit(solution)/shard_map/pallas_call | solution.py:172
  (23 shorter events, 3.5 us)
Async XLA Ops:
  1.0 15.5 %collective-permute-start = (bf16[1024,1024]{1,0:T(8,128)(2,1)}, bf16[1024,1024]{1,0:T(8,128)(2,1)S(1)}, u32[]{:S(2)}, u32[]{:S(2)}) collective-permute-start(bf16[1024,1024]{1,0:T(8,128)(2,1)} %in_ref.1), channel_id=1, source_target_pairs={{0,1},{1,0},{2,3},{3,2},{4,5},{5,4},{6,7},{7,6},{8,9},{9,8},{10,11... | collective-permute-start | bytes 6291464 | tf_op jit(solution)/shard_map/ppermute | solution.py:18
  1.5 12.3 %collective-permute-start.3 = (bf16[144,1024]{1,0:T(8,128)(2,1)S(1)}, bf16[144,1024]{1,0:T(8,128)(2,1)S(1)}, u32[]{:S(2)}, u32[]{:S(2)}) collective-permute-start(bf16[144,1024]{1,0:T(8,128)(2,1)S(1)} %shard_map.65.refs_2_), channel_id=1, source_target_pairs={{0,4},{1,3},{2,6},{3,1},{4,0},{5,7},{6,2},{7,5},{8,12},{9,11},{10,... | collective-permute-start | bytes 884744 | tf_op jit(solution)/shard_map/ppermute | solution.py:23
  5.1 8.7 %collective-permute-start.2 = (bf16[128,1024]{1,0:T(8,128)(2,1)S(1)}, bf16[128,1024]{1,0:T(8,128)(2,1)S(1)}, u32[]{:S(2)}, u32[]{:S(2)}) collective-permute-start(bf16[128,1024]{1,0:T(8,128)(2,1)S(1)} %shard_map.67.refs_1_), channel_id=1, source_target_pairs={{0,2},{1,5},{2,0},{3,7},{4,6},{5,1},{6,4},{7,3},{8,10},{9,13},{10,... | collective-permute-start | bytes 786440 | tf_op jit(solution)/shard_map/ppermute | solution.py:23
  6.7 13.0 %collective-permute-start.4 = (bf16[144,1024]{1,0:T(8,128)(2,1)S(1)}, bf16[144,1024]{1,0:T(8,128)(2,1)S(1)}, u32[]{:S(2)}, u32[]{:S(2)}) collective-permute-start(bf16[144,1024]{1,0:T(8,128)(2,1)S(1)} %shard_map.65.refs_2_), channel_id=1, source_target_pairs={{0,2},{1,5},{2,0},{3,7},{4,6},{5,1},{6,4},{7,3},{8,10},{9,13},{10,... | collective-permute-start | bytes 884744 | tf_op jit(solution)/shard_map/ppermute | solution.py:23
  7.2 14.0 %collective-permute-start.1 = (bf16[128,1024]{1,0:T(8,128)(2,1)S(1)}, bf16[128,1024]{1,0:T(8,128)(2,1)S(1)}, u32[]{:S(2)}, u32[]{:S(2)}) collective-permute-start(bf16[128,1024]{1,0:T(8,128)(2,1)S(1)} %shard_map.67.refs_1_), channel_id=1, source_target_pairs={{0,4},{1,3},{2,6},{3,1},{4,0},{5,7},{6,2},{7,5},{8,12},{9,11},{10,... | collective-permute-start | bytes 786440 | tf_op jit(solution)/shard_map/ppermute | solution.py:23
  7.3 1.6 %copy-start = (bf16[1024,1024]{1,0:T(8,128)(2,1)S(1)}, bf16[1024,1024]{1,0:T(8,128)(2,1)}, u32[]{:S(2)}) copy-start(bf16[1024,1024]{1,0:T(8,128)(2,1)} %in_ref.1) | copy-start | bytes 6291460
  13.8 9.2 %collective-permute-start.5 = (bf16[128,1024]{1,0:T(8,128)(2,1)S(1)}, bf16[128,1024]{1,0:T(8,128)(2,1)S(1)}, u32[]{:S(2)}, u32[]{:S(2)}) collective-permute-start(bf16[128,1024]{1,0:T(8,128)(2,1)S(1)} %collective-permute-done.2.refs_2_), channel_id=1, source_target_pairs={{0,4},{1,3},{2,6},{3,1},{4,0},{5,7},{6,2},{7,5},{8,12},{9,11},{10,... | collective-permute-start | bytes 786440 | tf_op jit(solution)/shard_map/ppermute | solution.py:23
  14.4 9.0 %collective-permute-start.6 = (bf16[144,1024]{1,0:T(8,128)(2,1)S(1)}, bf16[144,1024]{1,0:T(8,128)(2,1)S(1)}, u32[]{:S(2)}, u32[]{:S(2)}) collective-permute-start(bf16[144,1024]{1,0:T(8,128)(2,1)S(1)} %collective-permute-done.3.refs_3_), channel_id=1, source_target_pairs={{0,2},{1,5},{2,0},{3,7},{4,6},{5,1},{6,4},{7,3},{8,10},{9,13},{10,... | collective-permute-start | bytes 884744 | tf_op jit(solution)/shard_map/ppermute | solution.py:23
  24.1 1.5 %collective-permute-start.7 = (f32[64,512]{1,0:T(8,128)S(1)}, f32[64,512]{1,0:T(8,128)S(1)}, u32[]{:S(2)}, u32[]{:S(2)}) collective-permute-start(f32[64,512]{1,0:T(8,128)S(1)} %shard_map.73), channel_id=1, source_target_pairs={{0,1},{1,0},{2,3},{3,2},{4,5},{5,4},{6,7},{7,6},{8,9},{9,8},{10,11... | collective-permute-start | bytes 393224 | tf_op jit(solution)/shard_map/ppermute | solution.py:18
  25.1 10.5 %copy-start.1 = (f32[64]{0:T(128)S(1)}, f32[64]{0:T(128)}, u32[]{:S(2)}) copy-start(f32[64]{0:T(128)} %param.11) | copy-start | bytes 772
  25.1 2.7 %collective-permute-start.10 = (f32[64,512]{1,0:T(8,128)S(1)}, f32[64,512]{1,0:T(8,128)S(1)}, u32[]{:S(2)}, u32[]{:S(2)}) collective-permute-start(f32[64,512]{1,0:T(8,128)S(1)} %get-tuple-element.28), channel_id=1, source_target_pairs={{0,1},{1,0},{2,3},{3,2},{4,5},{5,4},{6,7},{7,6},{8,9},{9,8},{10,11... | collective-permute-start | bytes 393224 | tf_op jit(solution)/shard_map/ppermute | solution.py:18
  25.6 5.0 %collective-permute-start.8 = (bf16[64,512]{1,0:T(8,128)(2,1)S(1)}, bf16[64,512]{1,0:T(8,128)(2,1)S(1)}, u32[]{:S(2)}, u32[]{:S(2)}) collective-permute-start(bf16[64,512]{1,0:T(8,128)(2,1)S(1)} %shard_map.74.a_ref), channel_id=1, source_target_pairs={{0,8},{1,17},{2,10},{3,19},{4,12},{5,21},{6,14},{7,23},{8,0},{9,25... | collective-permute-start | bytes 196616 | tf_op jit(solution)/shard_map/ppermute | solution.py:33
  27.9 4.7 %collective-permute-start.11 = (bf16[64,512]{1,0:T(8,128)(2,1)S(1)}, bf16[64,512]{1,0:T(8,128)(2,1)S(1)}, u32[]{:S(2)}, u32[]{:S(2)}) collective-permute-start(bf16[64,512]{1,0:T(8,128)(2,1)S(1)} %shard_map.77.a_ref), channel_id=1, source_target_pairs={{0,8},{1,17},{2,10},{3,19},{4,12},{5,21},{6,14},{7,23},{8,0},{9,25... | collective-permute-start | bytes 196616 | tf_op jit(solution)/shard_map/ppermute | solution.py:33
  30.7 5.2 %collective-permute-start.9 = (bf16[64,512]{1,0:T(8,128)(2,1)S(1)}, bf16[64,512]{1,0:T(8,128)(2,1)S(1)}, u32[]{:S(2)}, u32[]{:S(2)}) collective-permute-start(bf16[64,512]{1,0:T(8,128)(2,1)S(1)} %shard_map.75.refs_0_), channel_id=1, source_target_pairs={{0,16},{1,9},{2,18},{3,11},{4,20},{5,13},{6,22},{7,15},{8,24},{9,1... | collective-permute-start | bytes 196616 | tf_op jit(solution)/shard_map/ppermute | solution.py:33
  32.7 5.2 %collective-permute-start.12 = (bf16[64,512]{1,0:T(8,128)(2,1)S(1)}, bf16[64,512]{1,0:T(8,128)(2,1)S(1)}, u32[]{:S(2)}, u32[]{:S(2)}) collective-permute-start(bf16[64,512]{1,0:T(8,128)(2,1)S(1)} %shard_map.78.refs_2_), channel_id=1, source_target_pairs={{0,16},{1,9},{2,18},{3,11},{4,20},{5,13},{6,22},{7,15},{8,24},{9,1... | collective-permute-start | bytes 196616 | tf_op jit(solution)/shard_map/ppermute | solution.py:33

commit v2 on v1

--- a/solution.py
+++ b/solution.py
@@ -112,7 +112,6 @@
     tail, feat = second_ref.shape
     rows = (first_ref.shape[0] + tail) * feat // (feat + ritz)
     head = rows - tail
-    land = jnp.concatenate([first_ref[:head, :], second_ref[...]], axis=0)
     vec = jnp.concatenate(
         [first_ref[head:, c * rows : (c + 1) * rows] for c in range(feat // rows)], axis=0
     )
@@ -123,12 +122,17 @@
     ]
 
     def scores(k, cols):
-        return jnp.dot(land, slabs[k][:, cols], preferred_element_type=jnp.float32)
+        weights = slabs[k][:, cols]
+        return [
+            jnp.dot(land, weights, preferred_element_type=jnp.float32)
+            for land in (second_ref[...], first_ref[:head, :])
+        ]
 
     ahead = scores(*work[0])
     for n, (k, cols) in enumerate(work):
         now, ahead = ahead, scores(*work[n + 1]) if n + 1 < len(work) else None
-        affinity = jnp.exp(now * coeff).astype(jnp.bfloat16)
+        late, early = [jnp.exp(part * coeff).astype(jnp.bfloat16) for part in now]
+        affinity = jnp.concatenate([early, late], axis=0)
         term = jnp.dot(vec, affinity, preferred_element_type=jnp.float32)
         place = slice(cols.start - spans[k][0], cols.stop - spans[k][0])
         outs[k][:, place] = term if accs[k] is None else accs[k][:, cols] + term

time: 38.9 us -> 39 us (level)
  Pallas kernels: 11 us -> 11.6 us
  waiting for transfers between devices: 10.3 us -> 9.82 us
    pallas_call x7, Pallas kernels: 6.83 us -> 7.48 us  [stage(): pl.pallas_call(functools.partial(stage_kernel, count, coeff, ritz, accs i...]
    ppermute x6, waiting for transfers between devices: 5.92 us -> 5.46 us  [chip_send(): lax.ppermute(value, 'sl', [(i, i ^ bits[(k + i % 2) % len(bits)]) for i i...]
  transfers between devices with their start and end apart: 13 -> 13, of which waited for: 7 -> 6; matrix products, arithmetic and copies ran while one was open for 0% -> 0% of each run, Pallas kernels for 22% -> 24%
where the time goes in v2:
time: 39 us; the launch traced here: 38.8 us
  starting transfers between devices  15.6 us (40%)
  Pallas kernels  11.6 us (30%)
  waiting for transfers between devices  9.82 us (25%)
  local copies, waits for them, and re-layouts  1.69 us (4%)
    pallas_call x7, Pallas kernels, stage(): pl.pallas_call(functools.partial(stage_kernel, count, coeff, ritz, accs i...  7.48 us
    ppermute x6, starting transfers between devices, chip_send(): lax.ppermute(value, 'sl', [(i, i ^ bits[(k + i % 2) % len(bits)]) for i i...  7.36 us
    ppermute x4, starting transfers between devices, lm_send(): return lax.ppermute(value, ('lm', 'sl'), perm)  7.12 us
    ppermute x6, waiting for transfers between devices, chip_send(): lax.ppermute(value, 'sl', [(i, i ^ bits[(k + i % 2) % len(bits)]) for i i...  5.46 us
    ppermute x4, waiting for transfers between devices, lm_send(): return lax.ppermute(value, ('lm', 'sl'), perm)  4.35 us
    pallas_call x7, Pallas kernels, small_call(): pl.pallas_call(kernel, out_shape=jax.ShapeDtypeStruct(out.shape, out.dtyp...  2.13 us
    unnamed x4, local copies, waits for them, and re-layouts  1.59 us
    ppermute x3, starting transfers between devices, core_send(): return lax.ppermute(value, 'sl', [(i, i ^ 1) for i in range(n)])  1.15 us
  transfers between devices with their start and end apart: 13, of which 6 were waited for; matrix products, arithmetic and copies ran while one was open for 0% of the time, Pallas kernels for 24%

profile of v2, /device:TPU:0, one launch (start us, length us, event | category | flops | bytes accessed | tf_op | source)
XLA Modules:
  0.0 38.8 jit_solution(17857443067393094257)
XLA Ops:
  0.0 1.0 %shard_map.65.refs_2_ = bf16[144,1024]{1,0:T(8,128)(2,1)S(1)} custom-call(bf16[256,1024]{1,0:T(8,128)(2,1)} %land_ref.3), custom_call_target="tpu_custom_call" | custom-call | tf_op jit(solution)/shard_map/pallas_call | solution.py:75
  1.5 2.6 %collective-permute-start.3 = (bf16[144,1024]{1,0:T(8,128)(2,1)S(1)}, bf16[144,1024]{1,0:T(8,128)(2,1)S(1)}, u32[]{:S(2)}, u32[]{:S(2)}) collective-permute-start(bf16[144,1024]{1,0:T(8,128)(2,1)S(1)} %shard_map.65.refs_2_), channel_id=1, source_target_pairs={{0,4},{1,3},{2,6},{3,1},{4,0},{5,7},{6,2},{7,5},{8,12},{9,11},{10,... | collective-permute-start | bytes 884744 | tf_op jit(solution)/shard_map/ppermute | solution.py:23
  4.1 1.0 %shard_map.67.refs_1_ = bf16[128,1024]{1,0:T(8,128)(2,1)S(1)} custom-call(bf16[256,1024]{1,0:T(8,128)(2,1)} %land_ref.3, bf16[96,256]{1,0:T(8,128)(2,1)} %bitcast.4, s32[2]{0:T(128)} %exponents_ref.1, bf16[64,96]{1,0:T(8,128)(2,1)} %bitcast.5), custom_call_target="tpu_custom_call" | custom-call | tf_op jit(solution)/shard_map/pallas_call | solution.py:87
  5.1 1.6 %collective-permute-start.2 = (bf16[128,1024]{1,0:T(8,128)(2,1)S(1)}, bf16[128,1024]{1,0:T(8,128)(2,1)S(1)}, u32[]{:S(2)}, u32[]{:S(2)}) collective-permute-start(bf16[128,1024]{1,0:T(8,128)(2,1)S(1)} %shard_map.67.refs_1_), channel_id=1, source_target_pairs={{0,2},{1,5},{2,0},{3,7},{4,6},{5,1},{6,4},{7,3},{8,10},{9,13},{10,... | collective-permute-start | bytes 786440 | tf_op jit(solution)/shard_map/ppermute | solution.py:23
  7.3 1.6 %copy-done = bf16[1024,1024]{1,0:T(8,128)(2,1)S(1)} copy-done((bf16[1024,1024]{1,0:T(8,128)(2,1)S(1)}, bf16[1024,1024]{1,0:T(8,128)(2,1)}, u32[]{:S(2)}) %copy-start) | copy-done | bytes 2097176
  8.9 0.6 %shard_map.64.refs_0_.refs_1_ = bf16[1024,1024]{1,0:T(8,128)(2,1)S(1)} custom-call(bf16[1024,1024]{1,0:T(8,128)(2,1)S(1)} %copy-done), custom_call_target="tpu_custom_call" | custom-call | tf_op jit(solution)/shard_map/pallas_call | solution.py:176
  9.5 0.9 %shard_map.68.refs_4_ = f32[64,1024]{1,0:T(8,128)S(1)} custom-call(bf16[1024,1024]{1,0:T(8,128)(2,1)S(1)} %shard_map.64.refs_0_.refs_1_, bf16[128,1024]{1,0:T(8,128)(2,1)S(1)} %shard_map.67.refs_1_, bf16[144,1024]{1,0:T(8,128)(2,1)S(1)} %shard_map.65.refs_2_), custom_call_target="tpu_custom_call" | custom-call | flops 671088640 | bytes 2621440 | tf_op jit(solution)/shard_map/pallas_call | solution.py:147
  10.4 3.4 %collective-permute-done.2.refs_2_ = bf16[128,1024]{1,0:T(8,128)(2,1)S(1)} collective-permute-done((bf16[128,1024]{1,0:T(8,128)(2,1)S(1)}, bf16[128,1024]{1,0:T(8,128)(2,1)S(1)}, u32[]{:S(2)}, u32[]{:S(2)}) %collective-permute-start.2) | collective-permute-done | bytes 262176 | tf_op jit(solution)/shard_map/ppermute | solution.py:23
  13.8 0.6 %collective-permute-start.5 = (bf16[128,1024]{1,0:T(8,128)(2,1)S(1)}, bf16[128,1024]{1,0:T(8,128)(2,1)S(1)}, u32[]{:S(2)}, u32[]{:S(2)}) collective-permute-start(bf16[128,1024]{1,0:T(8,128)(2,1)S(1)} %collective-permute-done.2.refs_2_), channel_id=1, source_target_pairs={{0,4},{1,3},{2,6},{3,1},{4,0},{5,7},{6,2},{7,5},{8,12},{9,11},{10,... | collective-permute-start | bytes 786440 | tf_op jit(solution)/shard_map/ppermute | solution.py:23
  14.4 2.0 %collective-permute-start.6 = (bf16[144,1024]{1,0:T(8,128)(2,1)S(1)}, bf16[144,1024]{1,0:T(8,128)(2,1)S(1)}, u32[]{:S(2)}, u32[]{:S(2)}) collective-permute-start(bf16[144,1024]{1,0:T(8,128)(2,1)S(1)} %collective-permute-done.3.refs_3_), channel_id=1, source_target_pairs={{0,2},{1,5},{2,0},{3,7},{4,6},{5,1},{6,4},{7,3},{8,10},{9,13},{10,... | collective-permute-start | bytes 884744 | tf_op jit(solution)/shard_map/ppermute | solution.py:23
  16.4 0.6 %shard_map.66.refs_0_.refs_1_ = bf16[1024,1024]{1,0:T(8,128)(2,1)S(1)} custom-call(bf16[1024,1024]{1,0:T(8,128)(2,1)S(1)} %collective-permute-done.in_ref), custom_call_target="tpu_custom_call" | custom-call | tf_op jit(solution)/shard_map/pallas_call | solution.py:176
  17.1 1.0 %shard_map.69.refs_5_ = f32[64,1024]{1,0:T(8,128)S(1)} custom-call(bf16[1024,1024]{1,0:T(8,128)(2,1)S(1)} %shard_map.66.refs_0_.refs_1_, bf16[128,1024]{1,0:T(8,128)(2,1)S(1)} %shard_map.67.refs_1_, bf16[144,1024]{1,0:T(8,128)(2,1)S(1)} %shard_map.65.refs_2_), custom_call_target="tpu_custom_call" | custom-call | flops 671088640 | bytes 2621440 | tf_op jit(solution)/shard_map/pallas_call | solution.py:147
  18.0 1.6 %collective-permute-done.4.refs_3_ = bf16[144,1024]{1,0:T(8,128)(2,1)S(1)} collective-permute-done((bf16[144,1024]{1,0:T(8,128)(2,1)S(1)}, bf16[144,1024]{1,0:T(8,128)(2,1)S(1)}, u32[]{:S(2)}, u32[]{:S(2)}) %collective-permute-start.4) | collective-permute-done | bytes 294944 | tf_op jit(solution)/shard_map/ppermute | solution.py:23
  19.6 1.7 %shard_map.70 = (f32[64,1024]{1,0:T(8,128)S(1)}, f32[64,1024]{1,0:T(8,128)S(1)}) custom-call(bf16[1024,1024]{1,0:T(8,128)(2,1)S(1)} %shard_map.64.refs_0_.refs_1_, bf16[1024,1024]{1,0:T(8,128)(2,1)S(1)} %shard_map.66.refs_0_.refs_1_, bf16[128,1024]{1,0:T(8,128)(2,1)S(1)} %collective-permute-done.2.refs_2_, ...), custom_call_target="tpu_custom_call" | custom-call | flops 1342177280 | bytes 4718592 | tf_op jit(solution)/shard_map/pallas_call | solution.py:147
  21.3 1.7 %shard_map.71 = (f32[64,1024]{1,0:T(8,128)S(1)}, f32[64,1024]{1,0:T(8,128)S(1)}) custom-call(bf16[1024,1024]{1,0:T(8,128)(2,1)S(1)} %shard_map.64.refs_0_.refs_1_, bf16[1024,1024]{1,0:T(8,128)(2,1)S(1)} %shard_map.66.refs_0_.refs_1_, bf16[128,1024]{1,0:T(8,128)(2,1)S(1)} %collective-permute-done.1.refs_2_, ...), custom_call_target="tpu_custom_call" | custom-call | flops 1342177280 | bytes 4718592 | tf_op jit(solution)/shard_map/pallas_call | solution.py:147
  23.5 0.6 %shard_map.73 = f32[64,512]{1,0:T(8,128)S(1)} custom-call(bf16[1024,1024]{1,0:T(8,128)(2,1)S(1)} %shard_map.66.refs_0_.refs_1_, bf16[128,1024]{1,0:T(8,128)(2,1)S(1)} %collective-permute-done.5.refs_2_.refs_1_, bf16[144,1024]{1,0:T(8,128)(2,1)S(1)} %collective-permute-done.6.refs_3_.refs_2_, f32[64,1024]{1,0:T(8,128)S(1)} %get-tuple-element.24.refs_4_.refs_3_), custom_call_target="tpu_custom_call" | custom-call | flops 335544320 | bytes 1572864 | tf_op jit(solution)/shard_map/pallas_call | solution.py:147
  24.3 0.9 %shard_map.72 = (f32[64,512]{1,0:T(8,128)S(1)}, f32[64,512]{1,0:T(8,128)S(1)}) custom-call(bf16[1024,1024]{1,0:T(8,128)(2,1)S(1)} %shard_map.66.refs_0_.refs_1_, bf16[1024,1024]{1,0:T(8,128)(2,1)S(1)} %shard_map.64.refs_0_.refs_1_, bf16[128,1024]{1,0:T(8,128)(2,1)S(1)} %collective-permute-done.5.refs_2_.refs_1_, ...), custom_call_target="tpu_custom_call" | custom-call | flops 671088640 | bytes 2621440 | tf_op jit(solution)/shard_map/pallas_call | solution.py:147
  25.7 1.6 %collective-permute-start.8 = (bf16[64,512]{1,0:T(8,128)(2,1)S(1)}, bf16[64,512]{1,0:T(8,128)(2,1)S(1)}, u32[]{:S(2)}, u32[]{:S(2)}) collective-permute-start(bf16[64,512]{1,0:T(8,128)(2,1)S(1)} %shard_map.74.a_ref), channel_id=1, source_target_pairs={{0,8},{1,17},{2,10},{3,19},{4,12},{5,21},{6,14},{7,23},{8,0},{9,25... | collective-permute-start | bytes 196616 | tf_op jit(solution)/shard_map/ppermute | solution.py:33
  27.4 0.6 %shard_map.76.a_ref = f32[64,512]{1,0:T(8,128)S(1)} custom-call(bf16[1024,1024]{1,0:T(8,128)(2,1)S(1)} %shard_map.64.refs_0_.refs_1_, bf16[128,1024]{1,0:T(8,128)(2,1)S(1)} %collective-permute-done.5.refs_2_.refs_1_, bf16[144,1024]{1,0:T(8,128)(2,1)S(1)} %collective-permute-done.6.refs_3_.refs_2_, f32[64,1024]{1,0:T(8,128)S(1)} %get-tuple-element.27.refs_5_.refs_3_), custom_call_target="tpu_custom_call" | custom-call | flops 335544320 | bytes 1572864 | tf_op jit(solution)/shard_map/pallas_call | solution.py:147
  28.6 2.2 %collective-permute-done.8.b_ref = bf16[64,512]{1,0:T(8,128)(2,1)S(1)} collective-permute-done((bf16[64,512]{1,0:T(8,128)(2,1)S(1)}, bf16[64,512]{1,0:T(8,128)(2,1)S(1)}, u32[]{:S(2)}, u32[]{:S(2)}) %collective-permute-start.8) | collective-permute-done | bytes 65568 | tf_op jit(solution)/shard_map/ppermute | solution.py:33
  30.8 2.0 %collective-permute-start.9 = (bf16[64,512]{1,0:T(8,128)(2,1)S(1)}, bf16[64,512]{1,0:T(8,128)(2,1)S(1)}, u32[]{:S(2)}, u32[]{:S(2)}) collective-permute-start(bf16[64,512]{1,0:T(8,128)(2,1)S(1)} %shard_map.75.refs_0_), channel_id=1, source_target_pairs={{0,16},{1,9},{2,18},{3,11},{4,20},{5,13},{6,22},{7,15},{8,24},{9,1... | collective-permute-start | bytes 196616 | tf_op jit(solution)/shard_map/ppermute | solution.py:33
  32.8 3.0 %collective-permute-start.12 = (bf16[64,512]{1,0:T(8,128)(2,1)S(1)}, bf16[64,512]{1,0:T(8,128)(2,1)S(1)}, u32[]{:S(2)}, u32[]{:S(2)}) collective-permute-start(bf16[64,512]{1,0:T(8,128)(2,1)S(1)} %shard_map.78.refs_2_), channel_id=1, source_target_pairs={{0,16},{1,9},{2,18},{3,11},{4,20},{5,13},{6,22},{7,15},{8,24},{9,1... | collective-permute-start | bytes 196616 | tf_op jit(solution)/shard_map/ppermute | solution.py:33
  36.0 2.0 %collective-permute-done.12.refs_3_ = bf16[64,512]{1,0:T(8,128)(2,1)S(1)} collective-permute-done((bf16[64,512]{1,0:T(8,128)(2,1)S(1)}, bf16[64,512]{1,0:T(8,128)(2,1)S(1)}, u32[]{:S(2)}, u32[]{:S(2)}) %collective-permute-start.12) | collective-permute-done | bytes 65568 | tf_op jit(solution)/shard_map/ppermute | solution.py:33
  38.0 0.8 %shard_map.79 = f32[64,1024]{1,0:T(8,128)} custom-call(bf16[64,512]{1,0:T(8,128)(2,1)S(1)} %shard_map.75.refs_0_, bf16[64,512]{1,0:T(8,128)(2,1)S(1)} %collective-permute-done.9.refs_1_, bf16[64,512]{1,0:T(8,128)(2,1)S(1)} %shard_map.78.refs_2_, bf16[64,512]{1,0:T(8,128)(2,1)S(1)} %collective-permute-done.12.refs_3_, f32[64,1]{1,0:T(8,128)S(1)} %copy.7.refs_4_), custom_call_target="tpu_custom_call" | custom-call | tf_op jit(solution)/shard_map/pallas_call | solution.py:176
  (23 shorter events, 3.1 us)
Async XLA Ops:
  1.0 15.5 %collective-permute-start = (bf16[1024,1024]{1,0:T(8,128)(2,1)}, bf16[1024,1024]{1,0:T(8,128)(2,1)S(1)}, u32[]{:S(2)}, u32[]{:S(2)}) collective-permute-start(bf16[1024,1024]{1,0:T(8,128)(2,1)} %in_ref.1), channel_id=1, source_target_pairs={{0,1},{1,0},{2,3},{3,2},{4,5},{5,4},{6,7},{7,6},{8,9},{9,8},{10,11... | collective-permute-start | bytes 6291464 | tf_op jit(solution)/shard_map/ppermute | solution.py:18
  1.5 12.3 %collective-permute-start.3 = (bf16[144,1024]{1,0:T(8,128)(2,1)S(1)}, bf16[144,1024]{1,0:T(8,128)(2,1)S(1)}, u32[]{:S(2)}, u32[]{:S(2)}) collective-permute-start(bf16[144,1024]{1,0:T(8,128)(2,1)S(1)} %shard_map.65.refs_2_), channel_id=1, source_target_pairs={{0,4},{1,3},{2,6},{3,1},{4,0},{5,7},{6,2},{7,5},{8,12},{9,11},{10,... | collective-permute-start | bytes 884744 | tf_op jit(solution)/shard_map/ppermute | solution.py:23
  5.1 8.7 %collective-permute-start.2 = (bf16[128,1024]{1,0:T(8,128)(2,1)S(1)}, bf16[128,1024]{1,0:T(8,128)(2,1)S(1)}, u32[]{:S(2)}, u32[]{:S(2)}) collective-permute-start(bf16[128,1024]{1,0:T(8,128)(2,1)S(1)} %shard_map.67.refs_1_), channel_id=1, source_target_pairs={{0,2},{1,5},{2,0},{3,7},{4,6},{5,1},{6,4},{7,3},{8,10},{9,13},{10,... | collective-permute-start | bytes 786440 | tf_op jit(solution)/shard_map/ppermute | solution.py:23
  6.7 13.0 %collective-permute-start.4 = (bf16[144,1024]{1,0:T(8,128)(2,1)S(1)}, bf16[144,1024]{1,0:T(8,128)(2,1)S(1)}, u32[]{:S(2)}, u32[]{:S(2)}) collective-permute-start(bf16[144,1024]{1,0:T(8,128)(2,1)S(1)} %shard_map.65.refs_2_), channel_id=1, source_target_pairs={{0,2},{1,5},{2,0},{3,7},{4,6},{5,1},{6,4},{7,3},{8,10},{9,13},{10,... | collective-permute-start | bytes 884744 | tf_op jit(solution)/shard_map/ppermute | solution.py:23
  7.2 14.1 %collective-permute-start.1 = (bf16[128,1024]{1,0:T(8,128)(2,1)S(1)}, bf16[128,1024]{1,0:T(8,128)(2,1)S(1)}, u32[]{:S(2)}, u32[]{:S(2)}) collective-permute-start(bf16[128,1024]{1,0:T(8,128)(2,1)S(1)} %shard_map.67.refs_1_), channel_id=1, source_target_pairs={{0,4},{1,3},{2,6},{3,1},{4,0},{5,7},{6,2},{7,5},{8,12},{9,11},{10,... | collective-permute-start | bytes 786440 | tf_op jit(solution)/shard_map/ppermute | solution.py:23
  7.3 1.6 %copy-start = (bf16[1024,1024]{1,0:T(8,128)(2,1)S(1)}, bf16[1024,1024]{1,0:T(8,128)(2,1)}, u32[]{:S(2)}) copy-start(bf16[1024,1024]{1,0:T(8,128)(2,1)} %in_ref.1) | copy-start | bytes 6291460
  13.8 9.2 %collective-permute-start.5 = (bf16[128,1024]{1,0:T(8,128)(2,1)S(1)}, bf16[128,1024]{1,0:T(8,128)(2,1)S(1)}, u32[]{:S(2)}, u32[]{:S(2)}) collective-permute-start(bf16[128,1024]{1,0:T(8,128)(2,1)S(1)} %collective-permute-done.2.refs_2_), channel_id=1, source_target_pairs={{0,4},{1,3},{2,6},{3,1},{4,0},{5,7},{6,2},{7,5},{8,12},{9,11},{10,... | collective-permute-start | bytes 786440 | tf_op jit(solution)/shard_map/ppermute | solution.py:23
  14.4 9.0 %collective-permute-start.6 = (bf16[144,1024]{1,0:T(8,128)(2,1)S(1)}, bf16[144,1024]{1,0:T(8,128)(2,1)S(1)}, u32[]{:S(2)}, u32[]{:S(2)}) collective-permute-start(bf16[144,1024]{1,0:T(8,128)(2,1)S(1)} %collective-permute-done.3.refs_3_), channel_id=1, source_target_pairs={{0,2},{1,5},{2,0},{3,7},{4,6},{5,1},{6,4},{7,3},{8,10},{9,13},{10,... | collective-permute-start | bytes 884744 | tf_op jit(solution)/shard_map/ppermute | solution.py:23
  24.1 1.6 %collective-permute-start.7 = (f32[64,512]{1,0:T(8,128)S(1)}, f32[64,512]{1,0:T(8,128)S(1)}, u32[]{:S(2)}, u32[]{:S(2)}) collective-permute-start(f32[64,512]{1,0:T(8,128)S(1)} %shard_map.73), channel_id=1, source_target_pairs={{0,1},{1,0},{2,3},{3,2},{4,5},{5,4},{6,7},{7,6},{8,9},{9,8},{10,11... | collective-permute-start | bytes 393224 | tf_op jit(solution)/shard_map/ppermute | solution.py:18
  25.3 10.5 %copy-start.1 = (f32[64]{0:T(128)S(1)}, f32[64]{0:T(128)}, u32[]{:S(2)}) copy-start(f32[64]{0:T(128)} %param.11) | copy-start | bytes 772
  25.3 2.8 %collective-permute-start.10 = (f32[64,512]{1,0:T(8,128)S(1)}, f32[64,512]{1,0:T(8,128)S(1)}, u32[]{:S(2)}, u32[]{:S(2)}) collective-permute-start(f32[64,512]{1,0:T(8,128)S(1)} %get-tuple-element.28), channel_id=1, source_target_pairs={{0,1},{1,0},{2,3},{3,2},{4,5},{5,4},{6,7},{7,6},{8,9},{9,8},{10,11... | collective-permute-start | bytes 393224 | tf_op jit(solution)/shard_map/ppermute | solution.py:18
  25.7 5.0 %collective-permute-start.8 = (bf16[64,512]{1,0:T(8,128)(2,1)S(1)}, bf16[64,512]{1,0:T(8,128)(2,1)S(1)}, u32[]{:S(2)}, u32[]{:S(2)}) collective-permute-start(bf16[64,512]{1,0:T(8,128)(2,1)S(1)} %shard_map.74.a_ref), channel_id=1, source_target_pairs={{0,8},{1,17},{2,10},{3,19},{4,12},{5,21},{6,14},{7,23},{8,0},{9,25... | collective-permute-start | bytes 196616 | tf_op jit(solution)/shard_map/ppermute | solution.py:33
  28.1 4.7 %collective-permute-start.11 = (bf16[64,512]{1,0:T(8,128)(2,1)S(1)}, bf16[64,512]{1,0:T(8,128)(2,1)S(1)}, u32[]{:S(2)}, u32[]{:S(2)}) collective-permute-start(bf16[64,512]{1,0:T(8,128)(2,1)S(1)} %shard_map.77.a_ref), channel_id=1, source_target_pairs={{0,8},{1,17},{2,10},{3,19},{4,12},{5,21},{6,14},{7,23},{8,0},{9,25... | collective-permute-start | bytes 196616 | tf_op jit(solution)/shard_map/ppermute | solution.py:33
  30.8 5.2 %collective-permute-start.9 = (bf16[64,512]{1,0:T(8,128)(2,1)S(1)}, bf16[64,512]{1,0:T(8,128)(2,1)S(1)}, u32[]{:S(2)}, u32[]{:S(2)}) collective-permute-start(bf16[64,512]{1,0:T(8,128)(2,1)S(1)} %shard_map.75.refs_0_), channel_id=1, source_target_pairs={{0,16},{1,9},{2,18},{3,11},{4,20},{5,13},{6,22},{7,15},{8,24},{9,1... | collective-permute-start | bytes 196616 | tf_op jit(solution)/shard_map/ppermute | solution.py:33
  32.8 5.2 %collective-permute-start.12 = (bf16[64,512]{1,0:T(8,128)(2,1)S(1)}, bf16[64,512]{1,0:T(8,128)(2,1)S(1)}, u32[]{:S(2)}, u32[]{:S(2)}) collective-permute-start(bf16[64,512]{1,0:T(8,128)(2,1)S(1)} %shard_map.78.refs_2_), channel_id=1, source_target_pairs={{0,16},{1,9},{2,18},{3,11},{4,20},{5,13},{6,22},{7,15},{8,24},{9,1... | collective-permute-start | bytes 196616 | tf_op jit(solution)/shard_map/ppermute | solution.py:33

commit v3 on v1

--- a/solution.py
+++ b/solution.py
@@ -64,23 +64,6 @@
         copy.wait()
 
 
-def tail_kernel(land_ref, out_ref, sem):
-    copy = pltpu.make_async_copy(land_ref.at[land_ref.shape[0] - out_ref.shape[0] :], out_ref, sem)
-    copy.start()
-    copy.wait()
-
-
-def second_half(landmarks):
-    rows, feat = landmarks.shape
-    return pl.pallas_call(
-        tail_kernel,
-        out_shape=jax.ShapeDtypeStruct((rows // 2 + SHIFT, feat), jnp.bfloat16),
-        in_specs=[pl.BlockSpec(memory_space=pltpu.HBM)],
-        scratch_shapes=[pltpu.SemaphoreType.DMA],
-        compiler_params=pltpu.CompilerParams(vmem_limit_bytes=8 * MIB),
-    )(pltpu.with_memory_space_constraint(landmarks, pltpu.HBM))
-
-
 def prepare(landmarks, codes_t, exponents, eig_t):
     rows, feat = landmarks.shape
     extra = eig_t.shape[0] * rows // feat
@@ -184,7 +167,7 @@
     rows = slab.shape[0]
     ways = n_sl.bit_length() - 2
 
-    second = second_half(landmarks)
+    second = landmarks[landmarks.shape[0] // 2 - SHIFT :]
     first = prepare(landmarks, codes.T, exponents, eigvec.T)
     blocks = {0: [first, second]}
     for k in range(ways):

time: 38.9 us -> 38.9 us (level)
  Pallas kernels: 11 us -> 9.97 us
  local copies, waits for them, and re-layouts: 1.69 us -> 2.67 us
    slice x0 -> x1, local copies, waits for them, and re-layouts: none -> 0.98 us  [local(): second = landmarks[landmarks.shape[0] // 2 - SHIFT:]]
    pallas_call x1 -> x0, Pallas kernels: 0.97 us -> none  [second_half(): pl.pallas_call(tail_kernel, out_shape=jax.ShapeDtypeStruct((rows // 2 + S...]
where the time goes in v3:
time: 38.9 us; the launch traced here: 38.7 us
  starting transfers between devices  15.6 us (40%)
  waiting for transfers between devices  10.3 us (26%)
  Pallas kernels  9.97 us (26%)
  local copies, waits for them, and re-layouts  2.67 us (7%)
    ppermute x6, starting transfers between devices, chip_send(): lax.ppermute(value, 'sl', [(i, i ^ bits[(k + i % 2) % len(bits)]) for i i...  7.36 us
    ppermute x4, starting transfers between devices, lm_send(): return lax.ppermute(value, ('lm', 'sl'), perm)  7.11 us
    pallas_call x7, Pallas kernels, stage(): pl.pallas_call(functools.partial(stage_kernel, count, coeff, ritz, accs i...  6.82 us
    ppermute x6, waiting for transfers between devices, chip_send(): lax.ppermute(value, 'sl', [(i, i ^ bits[(k + i % 2) % len(bits)]) for i i...  5.93 us
    ppermute x4, waiting for transfers between devices, lm_send(): return lax.ppermute(value, ('lm', 'sl'), perm)  4.39 us
    pallas_call x7, Pallas kernels, small_call(): pl.pallas_call(kernel, out_shape=jax.ShapeDtypeStruct(out.shape, out.dtyp...  2.13 us
    unnamed x4, local copies, waits for them, and re-layouts  1.59 us
    ppermute x3, starting transfers between devices, core_send(): return lax.ppermute(value, 'sl', [(i, i ^ 1) for i in range(n)])  1.16 us
  transfers between devices with their start and end apart: 13, of which 7 were waited for; matrix products, arithmetic and copies ran while one was open for 0% of the time, Pallas kernels for 22%

profile of v3, /device:TPU:0, one launch (start us, length us, event | category | flops | bytes accessed | tf_op | source)
XLA Modules:
  0.0 38.7 jit_solution(2309774302384979631)
XLA Ops:
  0.0 1.0 %slice.3.refs_2_ = bf16[144,1024]{1,0:T(8,128)(2,1)S(1)} slice(bf16[256,1024]{1,0:T(8,128)(2,1)} %land_ref.1), slice={[112:256], [0:1024]} | slice | bytes 589824 | tf_op jit(solution)/shard_map/slice | solution.py:170
  1.5 2.6 %collective-permute-start.3 = (bf16[144,1024]{1,0:T(8,128)(2,1)S(1)}, bf16[144,1024]{1,0:T(8,128)(2,1)S(1)}, u32[]{:S(2)}, u32[]{:S(2)}) collective-permute-start(bf16[144,1024]{1,0:T(8,128)(2,1)S(1)} %slice.3.refs_2_), channel_id=1, source_target_pairs={{0,4},{1,3},{2,6},{3,1},{4,0},{5,7},{6,2},{7,5},{8,12},{9,11},{10,... | collective-permute-start | bytes 884744 | tf_op jit(solution)/shard_map/ppermute | solution.py:23
  4.1 1.0 %shard_map.66.refs_1_ = bf16[128,1024]{1,0:T(8,128)(2,1)S(1)} custom-call(bf16[256,1024]{1,0:T(8,128)(2,1)} %land_ref.1, bf16[96,256]{1,0:T(8,128)(2,1)} %bitcast.4, s32[2]{0:T(128)} %exponents_ref.1, bf16[64,96]{1,0:T(8,128)(2,1)} %bitcast.5), custom_call_target="tpu_custom_call" | custom-call | tf_op jit(solution)/shard_map/pallas_call | solution.py:70
  5.1 1.6 %collective-permute-start.2 = (bf16[128,1024]{1,0:T(8,128)(2,1)S(1)}, bf16[128,1024]{1,0:T(8,128)(2,1)S(1)}, u32[]{:S(2)}, u32[]{:S(2)}) collective-permute-start(bf16[128,1024]{1,0:T(8,128)(2,1)S(1)} %shard_map.66.refs_1_), channel_id=1, source_target_pairs={{0,2},{1,5},{2,0},{3,7},{4,6},{5,1},{6,4},{7,3},{8,10},{9,13},{10,... | collective-permute-start | bytes 786440 | tf_op jit(solution)/shard_map/ppermute | solution.py:23
  7.3 1.6 %copy-done = bf16[1024,1024]{1,0:T(8,128)(2,1)S(1)} copy-done((bf16[1024,1024]{1,0:T(8,128)(2,1)S(1)}, bf16[1024,1024]{1,0:T(8,128)(2,1)}, u32[]{:S(2)}) %copy-start) | copy-done | bytes 2097176
  8.9 0.6 %shard_map.64.refs_0_.refs_1_ = bf16[1024,1024]{1,0:T(8,128)(2,1)S(1)} custom-call(bf16[1024,1024]{1,0:T(8,128)(2,1)S(1)} %copy-done), custom_call_target="tpu_custom_call" | custom-call | tf_op jit(solution)/shard_map/pallas_call | solution.py:155
  9.5 0.9 %shard_map.67.refs_4_ = f32[64,1024]{1,0:T(8,128)S(1)} custom-call(bf16[1024,1024]{1,0:T(8,128)(2,1)S(1)} %shard_map.64.refs_0_.refs_1_, bf16[128,1024]{1,0:T(8,128)(2,1)S(1)} %shard_map.66.refs_1_, bf16[144,1024]{1,0:T(8,128)(2,1)S(1)} %slice.3.refs_2_), custom_call_target="tpu_custom_call" | custom-call | flops 671088640 | bytes 2621440 | tf_op jit(solution)/shard_map/pallas_call | solution.py:126
  10.4 3.4 %collective-permute-done.2.refs_2_ = bf16[128,1024]{1,0:T(8,128)(2,1)S(1)} collective-permute-done((bf16[128,1024]{1,0:T(8,128)(2,1)S(1)}, bf16[128,1024]{1,0:T(8,128)(2,1)S(1)}, u32[]{:S(2)}, u32[]{:S(2)}) %collective-permute-start.2) | collective-permute-done | bytes 262176 | tf_op jit(solution)/shard_map/ppermute | solution.py:23
  13.8 0.6 %collective-permute-start.5 = (bf16[128,1024]{1,0:T(8,128)(2,1)S(1)}, bf16[128,1024]{1,0:T(8,128)(2,1)S(1)}, u32[]{:S(2)}, u32[]{:S(2)}) collective-permute-start(bf16[128,1024]{1,0:T(8,128)(2,1)S(1)} %collective-permute-done.2.refs_2_), channel_id=1, source_target_pairs={{0,4},{1,3},{2,6},{3,1},{4,0},{5,7},{6,2},{7,5},{8,12},{9,11},{10,... | collective-permute-start | bytes 786440 | tf_op jit(solution)/shard_map/ppermute | solution.py:23
  14.5 2.0 %collective-permute-start.6 = (bf16[144,1024]{1,0:T(8,128)(2,1)S(1)}, bf16[144,1024]{1,0:T(8,128)(2,1)S(1)}, u32[]{:S(2)}, u32[]{:S(2)}) collective-permute-start(bf16[144,1024]{1,0:T(8,128)(2,1)S(1)} %collective-permute-done.3.refs_3_), channel_id=1, source_target_pairs={{0,2},{1,5},{2,0},{3,7},{4,6},{5,1},{6,4},{7,3},{8,10},{9,13},{10,... | collective-permute-start | bytes 884744 | tf_op jit(solution)/shard_map/ppermute | solution.py:23
  16.4 0.6 %shard_map.65.refs_0_.refs_1_ = bf16[1024,1024]{1,0:T(8,128)(2,1)S(1)} custom-call(bf16[1024,1024]{1,0:T(8,128)(2,1)S(1)} %collective-permute-done.in_ref), custom_call_target="tpu_custom_call" | custom-call | tf_op jit(solution)/shard_map/pallas_call | solution.py:155
  17.1 0.9 %shard_map.68.refs_5_ = f32[64,1024]{1,0:T(8,128)S(1)} custom-call(bf16[1024,1024]{1,0:T(8,128)(2,1)S(1)} %shard_map.65.refs_0_.refs_1_, bf16[128,1024]{1,0:T(8,128)(2,1)S(1)} %shard_map.66.refs_1_, bf16[144,1024]{1,0:T(8,128)(2,1)S(1)} %slice.3.refs_2_), custom_call_target="tpu_custom_call" | custom-call | flops 671088640 | bytes 2621440 | tf_op jit(solution)/shard_map/pallas_call | solution.py:126
  17.9 1.7 %collective-permute-done.4.refs_3_ = bf16[144,1024]{1,0:T(8,128)(2,1)S(1)} collective-permute-done((bf16[144,1024]{1,0:T(8,128)(2,1)S(1)}, bf16[144,1024]{1,0:T(8,128)(2,1)S(1)}, u32[]{:S(2)}, u32[]{:S(2)}) %collective-permute-start.4) | collective-permute-done | bytes 294944 | tf_op jit(solution)/shard_map/ppermute | solution.py:23
  19.7 1.5 %shard_map.69 = (f32[64,1024]{1,0:T(8,128)S(1)}, f32[64,1024]{1,0:T(8,128)S(1)}) custom-call(bf16[1024,1024]{1,0:T(8,128)(2,1)S(1)} %shard_map.64.refs_0_.refs_1_, bf16[1024,1024]{1,0:T(8,128)(2,1)S(1)} %shard_map.65.refs_0_.refs_1_, bf16[128,1024]{1,0:T(8,128)(2,1)S(1)} %collective-permute-done.2.refs_2_, ...), custom_call_target="tpu_custom_call" | custom-call | flops 1342177280 | bytes 4718592 | tf_op jit(solution)/shard_map/pallas_call | solution.py:126
  21.2 1.5 %shard_map.70 = (f32[64,1024]{1,0:T(8,128)S(1)}, f32[64,1024]{1,0:T(8,128)S(1)}) custom-call(bf16[1024,1024]{1,0:T(8,128)(2,1)S(1)} %shard_map.64.refs_0_.refs_1_, bf16[1024,1024]{1,0:T(8,128)(2,1)S(1)} %shard_map.65.refs_0_.refs_1_, bf16[128,1024]{1,0:T(8,128)(2,1)S(1)} %collective-permute-done.1.refs_2_, ...), custom_call_target="tpu_custom_call" | custom-call | flops 1342177280 | bytes 4718592 | tf_op jit(solution)/shard_map/pallas_call | solution.py:126
  23.5 0.6 %shard_map.72 = f32[64,512]{1,0:T(8,128)S(1)} custom-call(bf16[1024,1024]{1,0:T(8,128)(2,1)S(1)} %shard_map.65.refs_0_.refs_1_, bf16[128,1024]{1,0:T(8,128)(2,1)S(1)} %collective-permute-done.5.refs_2_.refs_1_, bf16[144,1024]{1,0:T(8,128)(2,1)S(1)} %collective-permute-done.6.refs_3_.refs_2_, f32[64,1024]{1,0:T(8,128)S(1)} %get-tuple-element.24.refs_4_.refs_3_), custom_call_target="tpu_custom_call" | custom-call | flops 335544320 | bytes 1572864 | tf_op jit(solution)/shard_map/pallas_call | solution.py:126
  24.3 0.9 %shard_map.71 = (f32[64,512]{1,0:T(8,128)S(1)}, f32[64,512]{1,0:T(8,128)S(1)}) custom-call(bf16[1024,1024]{1,0:T(8,128)(2,1)S(1)} %shard_map.65.refs_0_.refs_1_, bf16[1024,1024]{1,0:T(8,128)(2,1)S(1)} %shard_map.64.refs_0_.refs_1_, bf16[128,1024]{1,0:T(8,128)(2,1)S(1)} %collective-permute-done.5.refs_2_.refs_1_, ...), custom_call_target="tpu_custom_call" | custom-call | flops 671088640 | bytes 2621440 | tf_op jit(solution)/shard_map/pallas_call | solution.py:126
  25.6 1.6 %collective-permute-start.8 = (bf16[64,512]{1,0:T(8,128)(2,1)S(1)}, bf16[64,512]{1,0:T(8,128)(2,1)S(1)}, u32[]{:S(2)}, u32[]{:S(2)}) collective-permute-start(bf16[64,512]{1,0:T(8,128)(2,1)S(1)} %shard_map.73.a_ref), channel_id=1, source_target_pairs={{0,8},{1,17},{2,10},{3,19},{4,12},{5,21},{6,14},{7,23},{8,0},{9,25... | collective-permute-start | bytes 196616 | tf_op jit(solution)/shard_map/ppermute | solution.py:33
  27.3 0.6 %shard_map.75.a_ref = f32[64,512]{1,0:T(8,128)S(1)} custom-call(bf16[1024,1024]{1,0:T(8,128)(2,1)S(1)} %shard_map.64.refs_0_.refs_1_, bf16[128,1024]{1,0:T(8,128)(2,1)S(1)} %collective-permute-done.5.refs_2_.refs_1_, bf16[144,1024]{1,0:T(8,128)(2,1)S(1)} %collective-permute-done.6.refs_3_.refs_2_, f32[64,1024]{1,0:T(8,128)S(1)} %get-tuple-element.27.refs_5_.refs_3_), custom_call_target="tpu_custom_call" | custom-call | flops 335544320 | bytes 1572864 | tf_op jit(solution)/shard_map/pallas_call | solution.py:126
  28.5 2.2 %collective-permute-done.8.b_ref = bf16[64,512]{1,0:T(8,128)(2,1)S(1)} collective-permute-done((bf16[64,512]{1,0:T(8,128)(2,1)S(1)}, bf16[64,512]{1,0:T(8,128)(2,1)S(1)}, u32[]{:S(2)}, u32[]{:S(2)}) %collective-permute-start.8) | collective-permute-done | bytes 65568 | tf_op jit(solution)/shard_map/ppermute | solution.py:33
  30.7 2.0 %collective-permute-start.9 = (bf16[64,512]{1,0:T(8,128)(2,1)S(1)}, bf16[64,512]{1,0:T(8,128)(2,1)S(1)}, u32[]{:S(2)}, u32[]{:S(2)}) collective-permute-start(bf16[64,512]{1,0:T(8,128)(2,1)S(1)} %shard_map.74.refs_0_), channel_id=1, source_target_pairs={{0,16},{1,9},{2,18},{3,11},{4,20},{5,13},{6,22},{7,15},{8,24},{9,1... | collective-permute-start | bytes 196616 | tf_op jit(solution)/shard_map/ppermute | solution.py:33
  32.7 2.9 %collective-permute-start.12 = (bf16[64,512]{1,0:T(8,128)(2,1)S(1)}, bf16[64,512]{1,0:T(8,128)(2,1)S(1)}, u32[]{:S(2)}, u32[]{:S(2)}) collective-permute-start(bf16[64,512]{1,0:T(8,128)(2,1)S(1)} %shard_map.77.refs_2_), channel_id=1, source_target_pairs={{0,16},{1,9},{2,18},{3,11},{4,20},{5,13},{6,22},{7,15},{8,24},{9,1... | collective-permute-start | bytes 196616 | tf_op jit(solution)/shard_map/ppermute | solution.py:33
  35.9 2.0 %collective-permute-done.12.refs_3_ = bf16[64,512]{1,0:T(8,128)(2,1)S(1)} collective-permute-done((bf16[64,512]{1,0:T(8,128)(2,1)S(1)}, bf16[64,512]{1,0:T(8,128)(2,1)S(1)}, u32[]{:S(2)}, u32[]{:S(2)}) %collective-permute-start.12) | collective-permute-done | bytes 65568 | tf_op jit(solution)/shard_map/ppermute | solution.py:33
  37.9 0.8 %shard_map.78 = f32[64,1024]{1,0:T(8,128)} custom-call(bf16[64,512]{1,0:T(8,128)(2,1)S(1)} %shard_map.74.refs_0_, bf16[64,512]{1,0:T(8,128)(2,1)S(1)} %collective-permute-done.9.refs_1_, bf16[64,512]{1,0:T(8,128)(2,1)S(1)} %shard_map.77.refs_2_, bf16[64,512]{1,0:T(8,128)(2,1)S(1)} %collective-permute-done.12.refs_3_, f32[64,1]{1,0:T(8,128)S(1)} %copy.7.refs_4_), custom_call_target="tpu_custom_call" | custom-call | tf_op jit(solution)/shard_map/pallas_call | solution.py:155
  (23 shorter events, 3.5 us)
Async XLA Ops:
  1.0 15.5 %collective-permute-start = (bf16[1024,1024]{1,0:T(8,128)(2,1)}, bf16[1024,1024]{1,0:T(8,128)(2,1)S(1)}, u32[]{:S(2)}, u32[]{:S(2)}) collective-permute-start(bf16[1024,1024]{1,0:T(8,128)(2,1)} %in_ref.1), channel_id=1, source_target_pairs={{0,1},{1,0},{2,3},{3,2},{4,5},{5,4},{6,7},{7,6},{8,9},{9,8},{10,11... | collective-permute-start | bytes 6291464 | tf_op jit(solution)/shard_map/ppermute | solution.py:18
  1.5 12.3 %collective-permute-start.3 = (bf16[144,1024]{1,0:T(8,128)(2,1)S(1)}, bf16[144,1024]{1,0:T(8,128)(2,1)S(1)}, u32[]{:S(2)}, u32[]{:S(2)}) collective-permute-start(bf16[144,1024]{1,0:T(8,128)(2,1)S(1)} %slice.3.refs_2_), channel_id=1, source_target_pairs={{0,4},{1,3},{2,6},{3,1},{4,0},{5,7},{6,2},{7,5},{8,12},{9,11},{10,... | collective-permute-start | bytes 884744 | tf_op jit(solution)/shard_map/ppermute | solution.py:23
  5.1 8.7 %collective-permute-start.2 = (bf16[128,1024]{1,0:T(8,128)(2,1)S(1)}, bf16[128,1024]{1,0:T(8,128)(2,1)S(1)}, u32[]{:S(2)}, u32[]{:S(2)}) collective-permute-start(bf16[128,1024]{1,0:T(8,128)(2,1)S(1)} %shard_map.66.refs_1_), channel_id=1, source_target_pairs={{0,2},{1,5},{2,0},{3,7},{4,6},{5,1},{6,4},{7,3},{8,10},{9,13},{10,... | collective-permute-start | bytes 786440 | tf_op jit(solution)/shard_map/ppermute | solution.py:23
  6.7 13.0 %collective-permute-start.4 = (bf16[144,1024]{1,0:T(8,128)(2,1)S(1)}, bf16[144,1024]{1,0:T(8,128)(2,1)S(1)}, u32[]{:S(2)}, u32[]{:S(2)}) collective-permute-start(bf16[144,1024]{1,0:T(8,128)(2,1)S(1)} %slice.3.refs_2_), channel_id=1, source_target_pairs={{0,2},{1,5},{2,0},{3,7},{4,6},{5,1},{6,4},{7,3},{8,10},{9,13},{10,... | collective-permute-start | bytes 884744 | tf_op jit(solution)/shard_map/ppermute | solution.py:23
  7.2 14.0 %collective-permute-start.1 = (bf16[128,1024]{1,0:T(8,128)(2,1)S(1)}, bf16[128,1024]{1,0:T(8,128)(2,1)S(1)}, u32[]{:S(2)}, u32[]{:S(2)}) collective-permute-start(bf16[128,1024]{1,0:T(8,128)(2,1)S(1)} %shard_map.66.refs_1_), channel_id=1, source_target_pairs={{0,4},{1,3},{2,6},{3,1},{4,0},{5,7},{6,2},{7,5},{8,12},{9,11},{10,... | collective-permute-start | bytes 786440 | tf_op jit(solution)/shard_map/ppermute | solution.py:23
  7.3 1.6 %copy-start = (bf16[1024,1024]{1,0:T(8,128)(2,1)S(1)}, bf16[1024,1024]{1,0:T(8,128)(2,1)}, u32[]{:S(2)}) copy-start(bf16[1024,1024]{1,0:T(8,128)(2,1)} %in_ref.1) | copy-start | bytes 6291460
  13.8 9.2 %collective-permute-start.5 = (bf16[128,1024]{1,0:T(8,128)(2,1)S(1)}, bf16[128,1024]{1,0:T(8,128)(2,1)S(1)}, u32[]{:S(2)}, u32[]{:S(2)}) collective-permute-start(bf16[128,1024]{1,0:T(8,128)(2,1)S(1)} %collective-permute-done.2.refs_2_), channel_id=1, source_target_pairs={{0,4},{1,3},{2,6},{3,1},{4,0},{5,7},{6,2},{7,5},{8,12},{9,11},{10,... | collective-permute-start | bytes 786440 | tf_op jit(solution)/shard_map/ppermute | solution.py:23
  14.5 9.0 %collective-permute-start.6 = (bf16[144,1024]{1,0:T(8,128)(2,1)S(1)}, bf16[144,1024]{1,0:T(8,128)(2,1)S(1)}, u32[]{:S(2)}, u32[]{:S(2)}) collective-permute-start(bf16[144,1024]{1,0:T(8,128)(2,1)S(1)} %collective-permute-done.3.refs_3_), channel_id=1, source_target_pairs={{0,2},{1,5},{2,0},{3,7},{4,6},{5,1},{6,4},{7,3},{8,10},{9,13},{10,... | collective-permute-start | bytes 884744 | tf_op jit(solution)/shard_map/ppermute | solution.py:23
  24.1 1.5 %collective-permute-start.7 = (f32[64,512]{1,0:T(8,128)S(1)}, f32[64,512]{1,0:T(8,128)S(1)}, u32[]{:S(2)}, u32[]{:S(2)}) collective-permute-start(f32[64,512]{1,0:T(8,128)S(1)} %shard_map.72), channel_id=1, source_target_pairs={{0,1},{1,0},{2,3},{3,2},{4,5},{5,4},{6,7},{7,6},{8,9},{9,8},{10,11... | collective-permute-start | bytes 393224 | tf_op jit(solution)/shard_map/ppermute | solution.py:18
  25.1 10.5 %copy-start.1 = (f32[64]{0:T(128)S(1)}, f32[64]{0:T(128)}, u32[]{:S(2)}) copy-start(f32[64]{0:T(128)} %param.11) | copy-start | bytes 772
  25.1 2.7 %collective-permute-start.10 = (f32[64,512]{1,0:T(8,128)S(1)}, f32[64,512]{1,0:T(8,128)S(1)}, u32[]{:S(2)}, u32[]{:S(2)}) collective-permute-start(f32[64,512]{1,0:T(8,128)S(1)} %get-tuple-element.28), channel_id=1, source_target_pairs={{0,1},{1,0},{2,3},{3,2},{4,5},{5,4},{6,7},{7,6},{8,9},{9,8},{10,11... | collective-permute-start | bytes 393224 | tf_op jit(solution)/shard_map/ppermute | solution.py:18
  25.6 5.0 %collective-permute-start.8 = (bf16[64,512]{1,0:T(8,128)(2,1)S(1)}, bf16[64,512]{1,0:T(8,128)(2,1)S(1)}, u32[]{:S(2)}, u32[]{:S(2)}) collective-permute-start(bf16[64,512]{1,0:T(8,128)(2,1)S(1)} %shard_map.73.a_ref), channel_id=1, source_target_pairs={{0,8},{1,17},{2,10},{3,19},{4,12},{5,21},{6,14},{7,23},{8,0},{9,25... | collective-permute-start | bytes 196616 | tf_op jit(solution)/shard_map/ppermute | solution.py:33
  27.9 4.7 %collective-permute-start.11 = (bf16[64,512]{1,0:T(8,128)(2,1)S(1)}, bf16[64,512]{1,0:T(8,128)(2,1)S(1)}, u32[]{:S(2)}, u32[]{:S(2)}) collective-permute-start(bf16[64,512]{1,0:T(8,128)(2,1)S(1)} %shard_map.76.a_ref), channel_id=1, source_target_pairs={{0,8},{1,17},{2,10},{3,19},{4,12},{5,21},{6,14},{7,23},{8,0},{9,25... | collective-permute-start | bytes 196616 | tf_op jit(solution)/shard_map/ppermute | solution.py:33
  30.7 5.2 %collective-permute-start.9 = (bf16[64,512]{1,0:T(8,128)(2,1)S(1)}, bf16[64,512]{1,0:T(8,128)(2,1)S(1)}, u32[]{:S(2)}, u32[]{:S(2)}) collective-permute-start(bf16[64,512]{1,0:T(8,128)(2,1)S(1)} %shard_map.74.refs_0_), channel_id=1, source_target_pairs={{0,16},{1,9},{2,18},{3,11},{4,20},{5,13},{6,22},{7,15},{8,24},{9,1... | collective-permute-start | bytes 196616 | tf_op jit(solution)/shard_map/ppermute | solution.py:33
  32.7 5.2 %collective-permute-start.12 = (bf16[64,512]{1,0:T(8,128)(2,1)S(1)}, bf16[64,512]{1,0:T(8,128)(2,1)S(1)}, u32[]{:S(2)}, u32[]{:S(2)}) collective-permute-start(bf16[64,512]{1,0:T(8,128)(2,1)S(1)} %shard_map.77.refs_2_), channel_id=1, source_target_pairs={{0,16},{1,9},{2,18},{3,11},{4,20},{5,13},{6,22},{7,15},{8,24},{9,1... | collective-permute-start | bytes 196616 | tf_op jit(solution)/shard_map/ppermute | solution.py:33

commit v4 on v3

--- a/solution.py
+++ b/solution.py
@@ -122,15 +122,15 @@
     land = (first.shape[0] + second.shape[0]) * feat // (feat + ritz)
     count = len(slabs)
     spans = spans or [(0, rows)] * count
-    rows = spans[0][1] - spans[0][0]
+    widths = [stop - start for start, stop in spans]
     return pl.pallas_call(
         functools.partial(stage_kernel, count, coeff, ritz, accs is not None, spans),
-        out_shape=[jax.ShapeDtypeStruct((ritz, rows), jnp.float32)] * count,
+        out_shape=[jax.ShapeDtypeStruct((ritz, width), jnp.float32) for width in widths],
         compiler_params=pltpu.CompilerParams(vmem_limit_bytes=32 * MIB),
         cost_estimate=pl.CostEstimate(
-            flops=2 * count * rows * land * (feat + 4 * ritz),
-            bytes_accessed=2 * (count * rows + land) * feat,
-            transcendentals=count * rows * land,
+            flops=2 * sum(widths) * land * (feat + 4 * ritz),
+            bytes_accessed=2 * (sum(widths) + land) * feat,
+            transcendentals=sum(widths) * land,
         ),
     )(*slabs, first, second, *(accs or []))
 
@@ -199,21 +199,21 @@
     for t in range(1, (1 << ways) - 1):
         accs = stage([slab, other], *blocks[t], accs, coeff, cols)
     end = blocks[(1 << ways) - 1]
-    width = rows // 2
-    spans = [(0, width), (width, rows)]
-    half = jax.ShapeDtypeStruct((cols, width), jnp.bfloat16)
+    spans = [(0, rows * 5 // 8), (rows * 5 // 8, rows)]
+    pieces = [jax.ShapeDtypeStruct((cols, stop - start), jnp.bfloat16) for start, stop in spans]
     (early,) = stage([other], *end, accs[1:], coeff, cols, spans[:1])
     received = [core_send(early, n_sl)]
     late, mine = stage([other, slab], *end, accs[::-1], coeff, cols, spans[::-1])
     received.append(core_send(late, n_sl))
-    total = small_call(add_kernel, half, mine, received[0])
+    total = small_call(add_kernel, pieces[0], mine, received[0])
     acc, total = lax.optimization_barrier((accs[0], total))
     (mine,) = stage([slab], *end, [acc], coeff, cols, spans[1:])
-    totals = [total, small_call(add_kernel, half, mine, received[1])]
+    totals = [total, small_call(add_kernel, pieces[1], mine, received[1])]
     turns = n_lm.bit_length() - 1
     for k in range(turns - 1):
         arrived = [lm_send(total, k, n_lm, n_sl) for total in totals]
-        totals = [small_call(add_kernel, half, a, b) for a, b in zip(totals, arrived)]
+        arrived[0], _ = lax.optimization_barrier((arrived[0], totals[1]))
+        totals = [small_call(add_kernel, p, a, b) for p, a, b in zip(pieces, totals, arrived)]
     pairs = [(total, lm_send(total, turns - 1, n_lm, n_sl)) for total in totals]
     scale = functools.partial(scale_kernel, total_land=total_land)
     out = jax.ShapeDtypeStruct((cols, rows), jnp.float32)

time: 38.9 us -> 39.4 us (1.013)
  waiting for transfers between devices: 10.3 us -> 11.4 us
  starting transfers between devices: 15.6 us -> 14.8 us
    ppermute x4, waiting for transfers between devices: 4.39 us -> 5.45 us  [lm_send(): return lax.ppermute(value, ('lm', 'sl'), perm)]
    ppermute x4, starting transfers between devices: 7.11 us -> 6.34 us  [lm_send(): return lax.ppermute(value, ('lm', 'sl'), perm)]
  transfers between devices with their start and end apart: 13 -> 13, of which waited for: 7 -> 6; matrix products, arithmetic and copies ran while one was open for 0% -> 0% of each run, Pallas kernels for 22% -> 22%
where the time goes in v4:
time: 39.4 us; the launch traced here: 39.2 us
  starting transfers between devices  14.8 us (38%)
  waiting for transfers between devices  11.4 us (29%)
  Pallas kernels  10.2 us (26%)
  local copies, waits for them, and re-layouts  2.67 us (7%)
    ppermute x6, starting transfers between devices, chip_send(): lax.ppermute(value, 'sl', [(i, i ^ bits[(k + i % 2) % len(bits)]) for i i...  7.36 us
    pallas_call x7, Pallas kernels, stage(): pl.pallas_call(functools.partial(stage_kernel, count, coeff, ritz, accs i...  7.09 us
    ppermute x4, starting transfers between devices, lm_send(): return lax.ppermute(value, ('lm', 'sl'), perm)  6.34 us
    ppermute x6, waiting for transfers between devices, chip_send(): lax.ppermute(value, 'sl', [(i, i ^ bits[(k + i % 2) % len(bits)]) for i i...  5.93 us
    ppermute x4, waiting for transfers between devices, lm_send(): return lax.ppermute(value, ('lm', 'sl'), perm)  5.45 us
    pallas_call x7, Pallas kernels, small_call(): pl.pallas_call(kernel, out_shape=jax.ShapeDtypeStruct(out.shape, out.dtyp...  2.13 us
    unnamed x4, local copies, waits for them, and re-layouts  1.6 us
    ppermute x3, starting transfers between devices, core_send(): return lax.ppermute(value, 'sl', [(i, i ^ 1) for i in range(n)])  1.1 us
  transfers between devices with their start and end apart: 13, of which 6 were waited for; matrix products, arithmetic and copies ran while one was open for 0% of the time, Pallas kernels for 22%

profile of v4, /device:TPU:0, one launch (start us, length us, event | category | flops | bytes accessed | tf_op | source)
XLA Modules:
  0.0 39.2 jit_solution(8401596000558230734)
XLA Ops:
  0.0 1.0 %slice.3.refs_2_ = bf16[144,1024]{1,0:T(8,128)(2,1)S(1)} slice(bf16[256,1024]{1,0:T(8,128)(2,1)} %land_ref.1), slice={[112:256], [0:1024]} | slice | bytes 589824 | tf_op jit(solution)/shard_map/slice | solution.py:170
  1.5 2.6 %collective-permute-start.3 = (bf16[144,1024]{1,0:T(8,128)(2,1)S(1)}, bf16[144,1024]{1,0:T(8,128)(2,1)S(1)}, u32[]{:S(2)}, u32[]{:S(2)}) collective-permute-start(bf16[144,1024]{1,0:T(8,128)(2,1)S(1)} %slice.3.refs_2_), channel_id=1, source_target_pairs={{0,4},{1,3},{2,6},{3,1},{4,0},{5,7},{6,2},{7,5},{8,12},{9,11},{10,... | collective-permute-start | bytes 884744 | tf_op jit(solution)/shard_map/ppermute | solution.py:23
  4.1 1.0 %shard_map.66.refs_1_ = bf16[128,1024]{1,0:T(8,128)(2,1)S(1)} custom-call(bf16[256,1024]{1,0:T(8,128)(2,1)} %land_ref.1, bf16[96,256]{1,0:T(8,128)(2,1)} %bitcast.4, s32[2]{0:T(128)} %exponents_ref.1, bf16[64,96]{1,0:T(8,128)(2,1)} %bitcast.5), custom_call_target="tpu_custom_call" | custom-call | tf_op jit(solution)/shard_map/pallas_call | solution.py:70
  5.1 1.6 %collective-permute-start.2 = (bf16[128,1024]{1,0:T(8,128)(2,1)S(1)}, bf16[128,1024]{1,0:T(8,128)(2,1)S(1)}, u32[]{:S(2)}, u32[]{:S(2)}) collective-permute-start(bf16[128,1024]{1,0:T(8,128)(2,1)S(1)} %shard_map.66.refs_1_), channel_id=1, source_target_pairs={{0,2},{1,5},{2,0},{3,7},{4,6},{5,1},{6,4},{7,3},{8,10},{9,13},{10,... | collective-permute-start | bytes 786440 | tf_op jit(solution)/shard_map/ppermute | solution.py:23
  7.3 1.6 %copy-done = bf16[1024,1024]{1,0:T(8,128)(2,1)S(1)} copy-done((bf16[1024,1024]{1,0:T(8,128)(2,1)S(1)}, bf16[1024,1024]{1,0:T(8,128)(2,1)}, u32[]{:S(2)}) %copy-start) | copy-done | bytes 2097176
  8.9 0.6 %shard_map.64.refs_0_.refs_1_ = bf16[1024,1024]{1,0:T(8,128)(2,1)S(1)} custom-call(bf16[1024,1024]{1,0:T(8,128)(2,1)S(1)} %copy-done), custom_call_target="tpu_custom_call" | custom-call | tf_op jit(solution)/shard_map/pallas_call | solution.py:155
  9.5 0.9 %shard_map.67.refs_4_ = f32[64,1024]{1,0:T(8,128)S(1)} custom-call(bf16[1024,1024]{1,0:T(8,128)(2,1)S(1)} %shard_map.64.refs_0_.refs_1_, bf16[128,1024]{1,0:T(8,128)(2,1)S(1)} %shard_map.66.refs_1_, bf16[144,1024]{1,0:T(8,128)(2,1)S(1)} %slice.3.refs_2_), custom_call_target="tpu_custom_call" | custom-call | flops 671088640 | bytes 2621440 | tf_op jit(solution)/shard_map/pallas_call | solution.py:126
  10.4 3.4 %collective-permute-done.2.refs_2_ = bf16[128,1024]{1,0:T(8,128)(2,1)S(1)} collective-permute-done((bf16[128,1024]{1,0:T(8,128)(2,1)S(1)}, bf16[128,1024]{1,0:T(8,128)(2,1)S(1)}, u32[]{:S(2)}, u32[]{:S(2)}) %collective-permute-start.2) | collective-permute-done | bytes 262176 | tf_op jit(solution)/shard_map/ppermute | solution.py:23
  13.8 0.6 %collective-permute-start.5 = (bf16[128,1024]{1,0:T(8,128)(2,1)S(1)}, bf16[128,1024]{1,0:T(8,128)(2,1)S(1)}, u32[]{:S(2)}, u32[]{:S(2)}) collective-permute-start(bf16[128,1024]{1,0:T(8,128)(2,1)S(1)} %collective-permute-done.2.refs_2_), channel_id=1, source_target_pairs={{0,4},{1,3},{2,6},{3,1},{4,0},{5,7},{6,2},{7,5},{8,12},{9,11},{10,... | collective-permute-start | bytes 786440 | tf_op jit(solution)/shard_map/ppermute | solution.py:23
  14.5 2.0 %collective-permute-start.6 = (bf16[144,1024]{1,0:T(8,128)(2,1)S(1)}, bf16[144,1024]{1,0:T(8,128)(2,1)S(1)}, u32[]{:S(2)}, u32[]{:S(2)}) collective-permute-start(bf16[144,1024]{1,0:T(8,128)(2,1)S(1)} %collective-permute-done.3.refs_3_), channel_id=1, source_target_pairs={{0,2},{1,5},{2,0},{3,7},{4,6},{5,1},{6,4},{7,3},{8,10},{9,13},{10,... | collective-permute-start | bytes 884744 | tf_op jit(solution)/shard_map/ppermute | solution.py:23
  16.4 0.6 %shard_map.65.refs_0_.refs_1_ = bf16[1024,1024]{1,0:T(8,128)(2,1)S(1)} custom-call(bf16[1024,1024]{1,0:T(8,128)(2,1)S(1)} %collective-permute-done.in_ref), custom_call_target="tpu_custom_call" | custom-call | tf_op jit(solution)/shard_map/pallas_call | solution.py:155
  17.1 0.9 %shard_map.68.refs_5_ = f32[64,1024]{1,0:T(8,128)S(1)} custom-call(bf16[1024,1024]{1,0:T(8,128)(2,1)S(1)} %shard_map.65.refs_0_.refs_1_, bf16[128,1024]{1,0:T(8,128)(2,1)S(1)} %shard_map.66.refs_1_, bf16[144,1024]{1,0:T(8,128)(2,1)S(1)} %slice.3.refs_2_), custom_call_target="tpu_custom_call" | custom-call | flops 671088640 | bytes 2621440 | tf_op jit(solution)/shard_map/pallas_call | solution.py:126
  17.9 1.7 %collective-permute-done.4.refs_3_ = bf16[144,1024]{1,0:T(8,128)(2,1)S(1)} collective-permute-done((bf16[144,1024]{1,0:T(8,128)(2,1)S(1)}, bf16[144,1024]{1,0:T(8,128)(2,1)S(1)}, u32[]{:S(2)}, u32[]{:S(2)}) %collective-permute-start.4) | collective-permute-done | bytes 294944 | tf_op jit(solution)/shard_map/ppermute | solution.py:23
  19.7 1.5 %shard_map.69 = (f32[64,1024]{1,0:T(8,128)S(1)}, f32[64,1024]{1,0:T(8,128)S(1)}) custom-call(bf16[1024,1024]{1,0:T(8,128)(2,1)S(1)} %shard_map.64.refs_0_.refs_1_, bf16[1024,1024]{1,0:T(8,128)(2,1)S(1)} %shard_map.65.refs_0_.refs_1_, bf16[128,1024]{1,0:T(8,128)(2,1)S(1)} %collective-permute-done.2.refs_2_, ...), custom_call_target="tpu_custom_call" | custom-call | flops 1342177280 | bytes 4718592 | tf_op jit(solution)/shard_map/pallas_call | solution.py:126
  21.2 1.5 %shard_map.70 = (f32[64,1024]{1,0:T(8,128)S(1)}, f32[64,1024]{1,0:T(8,128)S(1)}) custom-call(bf16[1024,1024]{1,0:T(8,128)(2,1)S(1)} %shard_map.64.refs_0_.refs_1_, bf16[1024,1024]{1,0:T(8,128)(2,1)S(1)} %shard_map.65.refs_0_.refs_1_, bf16[128,1024]{1,0:T(8,128)(2,1)S(1)} %collective-permute-done.1.refs_2_, ...), custom_call_target="tpu_custom_call" | custom-call | flops 1342177280 | bytes 4718592 | tf_op jit(solution)/shard_map/pallas_call | solution.py:126
  23.5 0.7 %shard_map.72 = f32[64,640]{1,0:T(8,128)S(1)} custom-call(bf16[1024,1024]{1,0:T(8,128)(2,1)S(1)} %shard_map.65.refs_0_.refs_1_, bf16[128,1024]{1,0:T(8,128)(2,1)S(1)} %collective-permute-done.5.refs_2_.refs_1_, bf16[144,1024]{1,0:T(8,128)(2,1)S(1)} %collective-permute-done.6.refs_3_.refs_2_, f32[64,1024]{1,0:T(8,128)S(1)} %get-tuple-element.25.refs_4_.refs_3_), custom_call_target="tpu_custom_call" | custom-call | flops 419430400 | bytes 1835008 | tf_op jit(solution)/shard_map/pallas_call | solution.py:126
  24.3 1.0 %shard_map.71 = (f32[64,384]{1,0:T(8,128)S(1)}, f32[64,640]{1,0:T(8,128)S(1)}) custom-call(bf16[1024,1024]{1,0:T(8,128)(2,1)S(1)} %shard_map.65.refs_0_.refs_1_, bf16[1024,1024]{1,0:T(8,128)(2,1)S(1)} %shard_map.64.refs_0_.refs_1_, bf16[128,1024]{1,0:T(8,128)(2,1)S(1)} %collective-permute-done.5.refs_2_.refs_1_, ...), custom_call_target="tpu_custom_call" | custom-call | flops 671088640 | bytes 2621440 | tf_op jit(solution)/shard_map/pallas_call | solution.py:126
  25.9 1.6 %collective-permute-start.8 = (bf16[64,640]{1,0:T(8,128)(2,1)S(1)}, bf16[64,640]{1,0:T(8,128)(2,1)S(1)}, u32[]{:S(2)}, u32[]{:S(2)}) collective-permute-start(bf16[64,640]{1,0:T(8,128)(2,1)S(1)} %shard_map.73.a_ref), channel_id=1, source_target_pairs={{0,8},{1,17},{2,10},{3,19},{4,12},{5,21},{6,14},{7,23},{8,0},{9,25... | collective-permute-start | bytes 245768 | tf_op jit(solution)/shard_map/ppermute | solution.py:33
  27.5 0.6 %shard_map.74.a_ref = f32[64,384]{1,0:T(8,128)S(1)} custom-call(bf16[1024,1024]{1,0:T(8,128)(2,1)S(1)} %shard_map.64.refs_0_.refs_1_, bf16[128,1024]{1,0:T(8,128)(2,1)S(1)} %collective-permute-done.5.refs_2_.refs_1_, bf16[144,1024]{1,0:T(8,128)(2,1)S(1)} %collective-permute-done.6.refs_3_.refs_2_, f32[64,1024]{1,0:T(8,128)S(1)} %get-tuple-element.28.refs_5_.refs_3_), custom_call_target="tpu_custom_call" | custom-call | flops 251658240 | bytes 1310720 | tf_op jit(solution)/shard_map/pallas_call | solution.py:126
  28.6 2.6 %collective-permute-done.8.b_ref = bf16[64,640]{1,0:T(8,128)(2,1)S(1)} collective-permute-done((bf16[64,640]{1,0:T(8,128)(2,1)S(1)}, bf16[64,640]{1,0:T(8,128)(2,1)S(1)}, u32[]{:S(2)}, u32[]{:S(2)}) %collective-permute-start.8) | collective-permute-done | bytes 81952 | tf_op jit(solution)/shard_map/ppermute | solution.py:33
  31.3 1.9 %collective-permute-start.10 = (bf16[64,640]{1,0:T(8,128)(2,1)S(1)}, bf16[64,640]{1,0:T(8,128)(2,1)S(1)}, u32[]{:S(2)}, u32[]{:S(2)}) collective-permute-start(bf16[64,640]{1,0:T(8,128)(2,1)S(1)} %shard_map.76.refs_0_), channel_id=1, source_target_pairs={{0,16},{1,9},{2,18},{3,11},{4,20},{5,13},{6,22},{7,15},{8,24},{9,1... | collective-permute-start | bytes 245768 | tf_op jit(solution)/shard_map/ppermute | solution.py:33
  33.2 2.2 %collective-permute-start.12 = (bf16[64,384]{1,0:T(8,128)(2,1)S(1)}, bf16[64,384]{1,0:T(8,128)(2,1)S(1)}, u32[]{:S(2)}, u32[]{:S(2)}) collective-permute-start(bf16[64,384]{1,0:T(8,128)(2,1)S(1)} %shard_map.77.refs_2_), channel_id=1, source_target_pairs={{0,16},{1,9},{2,18},{3,11},{4,20},{5,13},{6,22},{7,15},{8,24},{9,1... | collective-permute-start | bytes 147464 | tf_op jit(solution)/shard_map/ppermute | solution.py:33
  35.6 2.9 %collective-permute-done.12.refs_3_ = bf16[64,384]{1,0:T(8,128)(2,1)S(1)} collective-permute-done((bf16[64,384]{1,0:T(8,128)(2,1)S(1)}, bf16[64,384]{1,0:T(8,128)(2,1)S(1)}, u32[]{:S(2)}, u32[]{:S(2)}) %collective-permute-start.12) | collective-permute-done | bytes 49184 | tf_op jit(solution)/shard_map/ppermute | solution.py:33
  38.4 0.8 %shard_map.78 = f32[64,1024]{1,0:T(8,128)} custom-call(bf16[64,640]{1,0:T(8,128)(2,1)S(1)} %shard_map.76.refs_0_, bf16[64,640]{1,0:T(8,128)(2,1)S(1)} %collective-permute-done.10.refs_1_, bf16[64,384]{1,0:T(8,128)(2,1)S(1)} %shard_map.77.refs_2_, bf16[64,384]{1,0:T(8,128)(2,1)S(1)} %collective-permute-done.12.refs_3_, f32[64,1]{1,0:T(8,128)S(1)} %copy.7.refs_4_), custom_call_target="tpu_custom_call" | custom-call | tf_op jit(solution)/shard_map/pallas_call | solution.py:155
  (23 shorter events, 3.2 us)
Async XLA Ops:
  1.0 15.5 %collective-permute-start = (bf16[1024,1024]{1,0:T(8,128)(2,1)}, bf16[1024,1024]{1,0:T(8,128)(2,1)S(1)}, u32[]{:S(2)}, u32[]{:S(2)}) collective-permute-start(bf16[1024,1024]{1,0:T(8,128)(2,1)} %in_ref.1), channel_id=1, source_target_pairs={{0,1},{1,0},{2,3},{3,2},{4,5},{5,4},{6,7},{7,6},{8,9},{9,8},{10,11... | collective-permute-start | bytes 6291464 | tf_op jit(solution)/shard_map/ppermute | solution.py:18
  1.5 12.3 %collective-permute-start.3 = (bf16[144,1024]{1,0:T(8,128)(2,1)S(1)}, bf16[144,1024]{1,0:T(8,128)(2,1)S(1)}, u32[]{:S(2)}, u32[]{:S(2)}) collective-permute-start(bf16[144,1024]{1,0:T(8,128)(2,1)S(1)} %slice.3.refs_2_), channel_id=1, source_target_pairs={{0,4},{1,3},{2,6},{3,1},{4,0},{5,7},{6,2},{7,5},{8,12},{9,11},{10,... | collective-permute-start | bytes 884744 | tf_op jit(solution)/shard_map/ppermute | solution.py:23
  5.1 8.7 %collective-permute-start.2 = (bf16[128,1024]{1,0:T(8,128)(2,1)S(1)}, bf16[128,1024]{1,0:T(8,128)(2,1)S(1)}, u32[]{:S(2)}, u32[]{:S(2)}) collective-permute-start(bf16[128,1024]{1,0:T(8,128)(2,1)S(1)} %shard_map.66.refs_1_), channel_id=1, source_target_pairs={{0,2},{1,5},{2,0},{3,7},{4,6},{5,1},{6,4},{7,3},{8,10},{9,13},{10,... | collective-permute-start | bytes 786440 | tf_op jit(solution)/shard_map/ppermute | solution.py:23
  6.7 13.0 %collective-permute-start.4 = (bf16[144,1024]{1,0:T(8,128)(2,1)S(1)}, bf16[144,1024]{1,0:T(8,128)(2,1)S(1)}, u32[]{:S(2)}, u32[]{:S(2)}) collective-permute-start(bf16[144,1024]{1,0:T(8,128)(2,1)S(1)} %slice.3.refs_2_), channel_id=1, source_target_pairs={{0,2},{1,5},{2,0},{3,7},{4,6},{5,1},{6,4},{7,3},{8,10},{9,13},{10,... | collective-permute-start | bytes 884744 | tf_op jit(solution)/shard_map/ppermute | solution.py:23
  7.2 14.0 %collective-permute-start.1 = (bf16[128,1024]{1,0:T(8,128)(2,1)S(1)}, bf16[128,1024]{1,0:T(8,128)(2,1)S(1)}, u32[]{:S(2)}, u32[]{:S(2)}) collective-permute-start(bf16[128,1024]{1,0:T(8,128)(2,1)S(1)} %shard_map.66.refs_1_), channel_id=1, source_target_pairs={{0,4},{1,3},{2,6},{3,1},{4,0},{5,7},{6,2},{7,5},{8,12},{9,11},{10,... | collective-permute-start | bytes 786440 | tf_op jit(solution)/shard_map/ppermute | solution.py:23
  7.3 1.6 %copy-start = (bf16[1024,1024]{1,0:T(8,128)(2,1)S(1)}, bf16[1024,1024]{1,0:T(8,128)(2,1)}, u32[]{:S(2)}) copy-start(bf16[1024,1024]{1,0:T(8,128)(2,1)} %in_ref.1) | copy-start | bytes 6291460
  13.8 9.2 %collective-permute-start.5 = (bf16[128,1024]{1,0:T(8,128)(2,1)S(1)}, bf16[128,1024]{1,0:T(8,128)(2,1)S(1)}, u32[]{:S(2)}, u32[]{:S(2)}) collective-permute-start(bf16[128,1024]{1,0:T(8,128)(2,1)S(1)} %collective-permute-done.2.refs_2_), channel_id=1, source_target_pairs={{0,4},{1,3},{2,6},{3,1},{4,0},{5,7},{6,2},{7,5},{8,12},{9,11},{10,... | collective-permute-start | bytes 786440 | tf_op jit(solution)/shard_map/ppermute | solution.py:23
  14.5 9.0 %collective-permute-start.6 = (bf16[144,1024]{1,0:T(8,128)(2,1)S(1)}, bf16[144,1024]{1,0:T(8,128)(2,1)S(1)}, u32[]{:S(2)}, u32[]{:S(2)}) collective-permute-start(bf16[144,1024]{1,0:T(8,128)(2,1)S(1)} %collective-permute-done.3.refs_3_), channel_id=1, source_target_pairs={{0,2},{1,5},{2,0},{3,7},{4,6},{5,1},{6,4},{7,3},{8,10},{9,13},{10,... | collective-permute-start | bytes 884744 | tf_op jit(solution)/shard_map/ppermute | solution.py:23
  24.2 1.6 %collective-permute-start.7 = (f32[64,640]{1,0:T(8,128)S(1)}, f32[64,640]{1,0:T(8,128)S(1)}, u32[]{:S(2)}, u32[]{:S(2)}) collective-permute-start(f32[64,640]{1,0:T(8,128)S(1)} %shard_map.72), channel_id=1, source_target_pairs={{0,1},{1,0},{2,3},{3,2},{4,5},{5,4},{6,7},{7,6},{8,9},{9,8},{10,11... | collective-permute-start | bytes 491528 | tf_op jit(solution)/shard_map/ppermute | solution.py:18
  25.4 10.1 %copy-start.1 = (f32[64]{0:T(128)S(1)}, f32[64]{0:T(128)}, u32[]{:S(2)}) copy-start(f32[64]{0:T(128)} %param.11) | copy-start | bytes 772
  25.4 2.7 %collective-permute-start.9 = (f32[64,384]{1,0:T(8,128)S(1)}, f32[64,384]{1,0:T(8,128)S(1)}, u32[]{:S(2)}, u32[]{:S(2)}) collective-permute-start(f32[64,384]{1,0:T(8,128)S(1)} %get-tuple-element.29), channel_id=1, source_target_pairs={{0,1},{1,0},{2,3},{3,2},{4,5},{5,4},{6,7},{7,6},{8,9},{9,8},{10,11... | collective-permute-start | bytes 294920 | tf_op jit(solution)/shard_map/ppermute | solution.py:18
  25.9 5.4 %collective-permute-start.8 = (bf16[64,640]{1,0:T(8,128)(2,1)S(1)}, bf16[64,640]{1,0:T(8,128)(2,1)S(1)}, u32[]{:S(2)}, u32[]{:S(2)}) collective-permute-start(bf16[64,640]{1,0:T(8,128)(2,1)S(1)} %shard_map.73.a_ref), channel_id=1, source_target_pairs={{0,8},{1,17},{2,10},{3,19},{4,12},{5,21},{6,14},{7,23},{8,0},{9,25... | collective-permute-start | bytes 245768 | tf_op jit(solution)/shard_map/ppermute | solution.py:33
  28.1 5.1 %collective-permute-start.11 = (bf16[64,384]{1,0:T(8,128)(2,1)S(1)}, bf16[64,384]{1,0:T(8,128)(2,1)S(1)}, u32[]{:S(2)}, u32[]{:S(2)}) collective-permute-start(bf16[64,384]{1,0:T(8,128)(2,1)S(1)} %shard_map.75.a_ref), channel_id=1, source_target_pairs={{0,8},{1,17},{2,10},{3,19},{4,12},{5,21},{6,14},{7,23},{8,0},{9,25... | collective-permute-start | bytes 147464 | tf_op jit(solution)/shard_map/ppermute | solution.py:33
  31.3 7.1 %collective-permute-start.10 = (bf16[64,640]{1,0:T(8,128)(2,1)S(1)}, bf16[64,640]{1,0:T(8,128)(2,1)S(1)}, u32[]{:S(2)}, u32[]{:S(2)}) collective-permute-start(bf16[64,640]{1,0:T(8,128)(2,1)S(1)} %shard_map.76.refs_0_), channel_id=1, source_target_pairs={{0,16},{1,9},{2,18},{3,11},{4,20},{5,13},{6,22},{7,15},{8,24},{9,1... | collective-permute-start | bytes 245768 | tf_op jit(solution)/shard_map/ppermute | solution.py:33
  33.2 5.2 %collective-permute-start.12 = (bf16[64,384]{1,0:T(8,128)(2,1)S(1)}, bf16[64,384]{1,0:T(8,128)(2,1)S(1)}, u32[]{:S(2)}, u32[]{:S(2)}) collective-permute-start(bf16[64,384]{1,0:T(8,128)(2,1)S(1)} %shard_map.77.refs_2_), channel_id=1, source_target_pairs={{0,16},{1,9},{2,18},{3,11},{4,20},{5,13},{6,22},{7,15},{8,24},{9,1... | collective-permute-start | bytes 147464 | tf_op jit(solution)/shard_map/ppermute | solution.py:33

commit v5 on v3

--- a/solution.py
+++ b/solution.py
@@ -87,15 +87,19 @@
         out_ref[:, rows] = in_ref[rows, :].T
 
 
-def stage_kernel(count, coeff, ritz, has_acc, spans, *refs):
-    slabs = refs[:count]
-    first_ref, second_ref = refs[count : count + 2]
-    accs = refs[count + 2 : 2 * count + 2] if has_acc else [None] * count
-    outs = refs[-count:]
-    tail, feat = second_ref.shape
-    rows = (first_ref.shape[0] + tail) * feat // (feat + ritz)
-    head = rows - tail
-    land = jnp.concatenate([first_ref[:head, :], second_ref[...]], axis=0)
+def stage_kernel(count, coeff, ritz, has_acc, spans, rows, use, *refs):
+    refs = list(refs)
+    slabs = [refs.pop(0) for _ in range(count)]
+    first_ref = refs.pop(0)
+    second_ref = refs.pop(0) if use[1] else None
+    accs = [refs.pop(0) for _ in range(count)] if has_acc else [None] * count
+    outs = refs
+    feat = first_ref.shape[1]
+    head = first_ref.shape[0] - ritz * rows // feat
+    lands = [first_ref[:head, :]] if use[0] else []
+    if second_ref is not None:
+        lands.append(second_ref[...])
+    land = jnp.concatenate(lands, axis=0) if len(lands) > 1 else lands[0]
     vec = jnp.concatenate(
         [first_ref[head:, c * rows : (c + 1) * rows] for c in range(feat // rows)], axis=0
     )
@@ -112,27 +116,36 @@
     for n, (k, cols) in enumerate(work):
         now, ahead = ahead, scores(*work[n + 1]) if n + 1 < len(work) else None
         affinity = jnp.exp(now * coeff).astype(jnp.bfloat16)
+        width = cols.stop - cols.start
+        if not use[0]:
+            affinity = jnp.concatenate([jnp.zeros((head, width), jnp.bfloat16), affinity], axis=0)
+        elif not use[1]:
+            blank = jnp.zeros((rows - head, width), jnp.bfloat16)
+            affinity = jnp.concatenate([affinity, blank], axis=0)
         term = jnp.dot(vec, affinity, preferred_element_type=jnp.float32)
         place = slice(cols.start - spans[k][0], cols.stop - spans[k][0])
         outs[k][:, place] = term if accs[k] is None else accs[k][:, cols] + term
 
 
-def stage(slabs, first, second, accs, coeff, ritz, spans=None):
+def stage(slabs, block, accs, coeff, ritz, size, use=(True, True), spans=None):
     feat, rows = slabs[0].shape
-    land = (first.shape[0] + second.shape[0]) * feat // (feat + ritz)
+    first, second = block
     count = len(slabs)
     spans = spans or [(0, rows)] * count
     rows = spans[0][1] - spans[0][0]
+    args = [*slabs, first]
+    if use[1]:
+        args.append(second)
     return pl.pallas_call(
-        functools.partial(stage_kernel, count, coeff, ritz, accs is not None, spans),
+        functools.partial(stage_kernel, count, coeff, ritz, accs is not None, spans, size, use),
         out_shape=[jax.ShapeDtypeStruct((ritz, rows), jnp.float32)] * count,
         compiler_params=pltpu.CompilerParams(vmem_limit_bytes=32 * MIB),
         cost_estimate=pl.CostEstimate(
-            flops=2 * count * rows * land * (feat + 4 * ritz),
-            bytes_accessed=2 * (count * rows + land) * feat,
-            transcendentals=count * rows * land,
+            flops=2 * count * rows * size * (feat + 4 * ritz),
+            bytes_accessed=2 * (count * rows + size) * feat,
+            transcendentals=count * rows * size,
         ),
-    )(*slabs, first, second, *(accs or []))
+    )(*args, *(accs or []))
 
 
 def add_kernel(a_ref, b_ref, out_ref):
@@ -166,6 +179,7 @@
     cols = ritz.shape[0]
     rows = slab.shape[0]
     ways = n_sl.bit_length() - 2
+    size = landmarks.shape[0]
 
     second = landmarks[landmarks.shape[0] // 2 - SHIFT :]
     first = prepare(landmarks, codes.T, exponents, eigvec.T)
@@ -180,12 +194,12 @@
     turned = jax.ShapeDtypeStruct(slab.shape[::-1], slab.dtype)
     other = small_call(transpose_kernel, turned, core_send(late_slab, n_sl))
     slab = small_call(transpose_kernel, turned, slab)
-    (acc,) = stage([slab], first, second, None, coeff, cols)
+    (acc,) = stage([slab], blocks[0], None, coeff, cols, size)
     held = [blocks[1 << k][k % 2] for k in range(ways)]
     held, acc = lax.optimization_barrier((held, acc))
     for k in range(ways):
         blocks[1 << k][k % 2] = held[k]
-    (other_acc,) = stage([other], first, second, None, coeff, cols)
+    (other_acc,) = stage([other], blocks[0], None, coeff, cols, size)
     accs = [acc, other_acc]
     for t in range(1, 1 << ways):
         if t in blocks:
@@ -197,18 +211,20 @@
         ]
 
     for t in range(1, (1 << ways) - 1):
-        accs = stage([slab, other], *blocks[t], accs, coeff, cols)
-    end = blocks[(1 << ways) - 1]
+        accs = stage([slab, other], blocks[t], accs, coeff, cols, size)
+    block = blocks[(1 << ways) - 1]
+    accs = stage([slab, other], block, accs, coeff, cols, size, (True, False))
+    end = functools.partial(stage, coeff=coeff, ritz=cols, size=size, use=(False, True))
     width = rows // 2
     spans = [(0, width), (width, rows)]
     half = jax.ShapeDtypeStruct((cols, width), jnp.bfloat16)
-    (early,) = stage([other], *end, accs[1:], coeff, cols, spans[:1])
+    (early,) = end([other], block, accs[1:], spans=spans[:1])
     received = [core_send(early, n_sl)]
-    late, mine = stage([other, slab], *end, accs[::-1], coeff, cols, spans[::-1])
+    late, mine = end([other, slab], block, accs[::-1], spans=spans[::-1])
     received.append(core_send(late, n_sl))
     total = small_call(add_kernel, half, mine, received[0])
     acc, total = lax.optimization_barrier((accs[0], total))
-    (mine,) = stage([slab], *end, [acc], coeff, cols, spans[1:])
+    (mine,) = end([slab], block, [acc], spans=spans[1:])
     totals = [total, small_call(add_kernel, half, mine, received[1])]
     turns = n_lm.bit_length() - 1
     for k in range(turns - 1):

time: 38.9 us -> 39.2 us (level)
  Pallas kernels: 9.97 us -> 10.6 us
  starting transfers between devices: 15.6 us -> 15.2 us
    pallas_call x7 -> x8, Pallas kernels: 6.82 us -> 7.41 us  [stage(): pl.pallas_call(functools.partial(stage_kernel, count, coeff, ritz, accs i...]
    ppermute x4, waiting for transfers between devices: 4.39 us -> 4.86 us  [lm_send(): return lax.ppermute(value, ('lm', 'sl'), perm)]
    ppermute x6, waiting for transfers between devices: 5.93 us -> 5.49 us  [chip_send(): lax.ppermute(value, 'sl', [(i, i ^ bits[(k + i % 2) % len(bits)]) for i i...]
  transfers between devices with their start and end apart: 13 -> 13, of which waited for: 7 -> 7; matrix products, arithmetic and copies ran while one was open for 0% -> 0% of each run, Pallas kernels for 22% -> 24%
where the time goes in v5:
time: 39.2 us; the launch traced here: 39 us
  starting transfers between devices  15.2 us (39%)
  Pallas kernels  10.6 us (27%)
  waiting for transfers between devices  10.5 us (27%)
  local copies, waits for them, and re-layouts  2.67 us (7%)
    pallas_call x8, Pallas kernels, stage(): pl.pallas_call(functools.partial(stage_kernel, count, coeff, ritz, accs i...  7.41 us
    ppermute x6, starting transfers between devices, chip_send(): lax.ppermute(value, 'sl', [(i, i ^ bits[(k + i % 2) % len(bits)]) for i i...  7.36 us
    ppermute x4, starting transfers between devices, lm_send(): return lax.ppermute(value, ('lm', 'sl'), perm)  6.75 us
    ppermute x6, waiting for transfers between devices, chip_send(): lax.ppermute(value, 'sl', [(i, i ^ bits[(k + i % 2) % len(bits)]) for i i...  5.49 us
    ppermute x4, waiting for transfers between devices, lm_send(): return lax.ppermute(value, ('lm', 'sl'), perm)  4.86 us
    pallas_call x7, Pallas kernels, small_call(): pl.pallas_call(kernel, out_shape=jax.ShapeDtypeStruct(out.shape, out.dtyp...  2.13 us
    unnamed x4, local copies, waits for them, and re-layouts  1.59 us
    ppermute x3, starting transfers between devices, core_send(): return lax.ppermute(value, 'sl', [(i, i ^ 1) for i in range(n)])  1.14 us
  transfers between devices with their start and end apart: 13, of which 7 were waited for; matrix products, arithmetic and copies ran while one was open for 0% of the time, Pallas kernels for 24%

profile of v5, /device:TPU:0, one launch (start us, length us, event | category | flops | bytes accessed | tf_op | source)
XLA Modules:
  0.0 39.0 jit_solution(16560605010661541315)
XLA Ops:
  0.0 1.0 %slice.3.refs_2_ = bf16[144,1024]{1,0:T(8,128)(2,1)S(1)} slice(bf16[256,1024]{1,0:T(8,128)(2,1)} %land_ref.1), slice={[112:256], [0:1024]} | slice | bytes 589824 | tf_op jit(solution)/shard_map/slice | solution.py:184
  1.5 2.6 %collective-permute-start.2 = (bf16[144,1024]{1,0:T(8,128)(2,1)S(1)}, bf16[144,1024]{1,0:T(8,128)(2,1)S(1)}, u32[]{:S(2)}, u32[]{:S(2)}) collective-permute-start(bf16[144,1024]{1,0:T(8,128)(2,1)S(1)} %slice.3.refs_2_), channel_id=1, source_target_pairs={{0,4},{1,3},{2,6},{3,1},{4,0},{5,7},{6,2},{7,5},{8,12},{9,11},{10,... | collective-permute-start | bytes 884744 | tf_op jit(solution)/shard_map/ppermute | solution.py:23
  4.1 1.0 %shard_map.66.refs_1_ = bf16[128,1024]{1,0:T(8,128)(2,1)S(1)} custom-call(bf16[256,1024]{1,0:T(8,128)(2,1)} %land_ref.1, bf16[96,256]{1,0:T(8,128)(2,1)} %bitcast.4, s32[2]{0:T(128)} %exponents_ref.1, bf16[64,96]{1,0:T(8,128)(2,1)} %bitcast.5), custom_call_target="tpu_custom_call" | custom-call | tf_op jit(solution)/shard_map/pallas_call | solution.py:70
  5.1 1.6 %collective-permute-start.1 = (bf16[128,1024]{1,0:T(8,128)(2,1)S(1)}, bf16[128,1024]{1,0:T(8,128)(2,1)S(1)}, u32[]{:S(2)}, u32[]{:S(2)}) collective-permute-start(bf16[128,1024]{1,0:T(8,128)(2,1)S(1)} %shard_map.66.refs_1_), channel_id=1, source_target_pairs={{0,2},{1,5},{2,0},{3,7},{4,6},{5,1},{6,4},{7,3},{8,10},{9,13},{10,... | collective-permute-start | bytes 786440 | tf_op jit(solution)/shard_map/ppermute | solution.py:23
  7.3 1.6 %copy-done = bf16[1024,1024]{1,0:T(8,128)(2,1)S(1)} copy-done((bf16[1024,1024]{1,0:T(8,128)(2,1)S(1)}, bf16[1024,1024]{1,0:T(8,128)(2,1)}, u32[]{:S(2)}) %copy-start) | copy-done | bytes 2097176
  8.9 0.6 %shard_map.64.refs_0_.refs_1_ = bf16[1024,1024]{1,0:T(8,128)(2,1)S(1)} custom-call(bf16[1024,1024]{1,0:T(8,128)(2,1)S(1)} %copy-done), custom_call_target="tpu_custom_call" | custom-call | tf_op jit(solution)/shard_map/pallas_call | solution.py:168
  9.5 0.9 %shard_map.67.refs_4_ = f32[64,1024]{1,0:T(8,128)S(1)} custom-call(bf16[1024,1024]{1,0:T(8,128)(2,1)S(1)} %shard_map.64.refs_0_.refs_1_, bf16[128,1024]{1,0:T(8,128)(2,1)S(1)} %shard_map.66.refs_1_, bf16[144,1024]{1,0:T(8,128)(2,1)S(1)} %slice.3.refs_2_), custom_call_target="tpu_custom_call" | custom-call | flops 671088640 | bytes 2621440 | tf_op jit(solution)/shard_map/pallas_call | solution.py:139
  10.4 3.4 %collective-permute-done.1.refs_2_ = bf16[128,1024]{1,0:T(8,128)(2,1)S(1)} collective-permute-done((bf16[128,1024]{1,0:T(8,128)(2,1)S(1)}, bf16[128,1024]{1,0:T(8,128)(2,1)S(1)}, u32[]{:S(2)}, u32[]{:S(2)}) %collective-permute-start.1) | collective-permute-done | bytes 262176 | tf_op jit(solution)/shard_map/ppermute | solution.py:23
  13.8 0.6 %collective-permute-start.3 = (bf16[128,1024]{1,0:T(8,128)(2,1)S(1)}, bf16[128,1024]{1,0:T(8,128)(2,1)S(1)}, u32[]{:S(2)}, u32[]{:S(2)}) collective-permute-start(bf16[128,1024]{1,0:T(8,128)(2,1)S(1)} %collective-permute-done.1.refs_2_), channel_id=1, source_target_pairs={{0,4},{1,3},{2,6},{3,1},{4,0},{5,7},{6,2},{7,5},{8,12},{9,11},{10,... | collective-permute-start | bytes 786440 | tf_op jit(solution)/shard_map/ppermute | solution.py:23
  14.5 2.0 %collective-permute-start.6 = (bf16[144,1024]{1,0:T(8,128)(2,1)S(1)}, bf16[144,1024]{1,0:T(8,128)(2,1)S(1)}, u32[]{:S(2)}, u32[]{:S(2)}) collective-permute-start(bf16[144,1024]{1,0:T(8,128)(2,1)S(1)} %collective-permute-done.2.refs_3_), channel_id=1, source_target_pairs={{0,2},{1,5},{2,0},{3,7},{4,6},{5,1},{6,4},{7,3},{8,10},{9,13},{10,... | collective-permute-start | bytes 884744 | tf_op jit(solution)/shard_map/ppermute | solution.py:23
  16.4 0.6 %shard_map.65.refs_0_.refs_1_ = bf16[1024,1024]{1,0:T(8,128)(2,1)S(1)} custom-call(bf16[1024,1024]{1,0:T(8,128)(2,1)S(1)} %collective-permute-done.in_ref), custom_call_target="tpu_custom_call" | custom-call | tf_op jit(solution)/shard_map/pallas_call | solution.py:168
  17.1 0.9 %shard_map.68.refs_5_ = f32[64,1024]{1,0:T(8,128)S(1)} custom-call(bf16[1024,1024]{1,0:T(8,128)(2,1)S(1)} %shard_map.65.refs_0_.refs_1_, bf16[128,1024]{1,0:T(8,128)(2,1)S(1)} %shard_map.66.refs_1_, bf16[144,1024]{1,0:T(8,128)(2,1)S(1)} %slice.3.refs_2_), custom_call_target="tpu_custom_call" | custom-call | flops 671088640 | bytes 2621440 | tf_op jit(solution)/shard_map/pallas_call | solution.py:139
  17.9 1.7 %collective-permute-done.5.refs_3_ = bf16[144,1024]{1,0:T(8,128)(2,1)S(1)} collective-permute-done((bf16[144,1024]{1,0:T(8,128)(2,1)S(1)}, bf16[144,1024]{1,0:T(8,128)(2,1)S(1)}, u32[]{:S(2)}, u32[]{:S(2)}) %collective-permute-start.5) | collective-permute-done | bytes 294944 | tf_op jit(solution)/shard_map/ppermute | solution.py:23
  19.7 1.5 %shard_map.69 = (f32[64,1024]{1,0:T(8,128)S(1)}, f32[64,1024]{1,0:T(8,128)S(1)}) custom-call(bf16[1024,1024]{1,0:T(8,128)(2,1)S(1)} %shard_map.64.refs_0_.refs_1_, bf16[1024,1024]{1,0:T(8,128)(2,1)S(1)} %shard_map.65.refs_0_.refs_1_, bf16[128,1024]{1,0:T(8,128)(2,1)S(1)} %collective-permute-done.1.refs_2_, ...), custom_call_target="tpu_custom_call" | custom-call | flops 1342177280 | bytes 4718592 | tf_op jit(solution)/shard_map/pallas_call | solution.py:139
  21.2 1.5 %shard_map.70 = (f32[64,1024]{1,0:T(8,128)S(1)}, f32[64,1024]{1,0:T(8,128)S(1)}) custom-call(bf16[1024,1024]{1,0:T(8,128)(2,1)S(1)} %shard_map.64.refs_0_.refs_1_, bf16[1024,1024]{1,0:T(8,128)(2,1)S(1)} %shard_map.65.refs_0_.refs_1_, bf16[128,1024]{1,0:T(8,128)(2,1)S(1)} %collective-permute-done.4.refs_2_, ...), custom_call_target="tpu_custom_call" | custom-call | flops 1342177280 | bytes 4718592 | tf_op jit(solution)/shard_map/pallas_call | solution.py:139
  23.1 1.0 %shard_map.71 = (f32[64,1024]{1,0:T(8,128)S(1)}, f32[64,1024]{1,0:T(8,128)S(1)}) custom-call(bf16[1024,1024]{1,0:T(8,128)(2,1)S(1)} %shard_map.64.refs_0_.refs_1_, bf16[1024,1024]{1,0:T(8,128)(2,1)S(1)} %shard_map.65.refs_0_.refs_1_, bf16[128,1024]{1,0:T(8,128)(2,1)S(1)} %collective-permute-done.3.refs_2_.refs_1_, f32[64,1024]{1,0:T(8,128)S(1)} %get-tuple-element.25.refs_3_, ...), custom_call_target="tpu_custom_call" | custom-call | flops 1342177280 | bytes 4718592 | tf_op jit(solution)/shard_map/pallas_call | solution.py:139
  24.6 0.7 %shard_map.72 = (f32[64,512]{1,0:T(8,128)S(1)}, f32[64,512]{1,0:T(8,128)S(1)}) custom-call(bf16[1024,1024]{1,0:T(8,128)(2,1)S(1)} %shard_map.65.refs_0_.refs_1_, bf16[1024,1024]{1,0:T(8,128)(2,1)S(1)} %shard_map.64.refs_0_.refs_1_, bf16[128,1024]{1,0:T(8,128)(2,1)S(1)} %collective-permute-done.3.refs_2_.refs_1_, ...), custom_call_target="tpu_custom_call" | custom-call | flops 671088640 | bytes 2621440 | tf_op jit(solution)/shard_map/pallas_call | solution.py:139
  25.3 0.6 %collective-permute-start.10 = (f32[64,512]{1,0:T(8,128)S(1)}, f32[64,512]{1,0:T(8,128)S(1)}, u32[]{:S(2)}, u32[]{:S(2)}) collective-permute-start(f32[64,512]{1,0:T(8,128)S(1)} %get-tuple-element.32), channel_id=1, source_target_pairs={{0,1},{1,0},{2,3},{3,2},{4,5},{5,4},{6,7},{7,6},{8,9},{9,8},{10,11... | collective-permute-start | bytes 393224 | tf_op jit(solution)/shard_map/ppermute | solution.py:18
  26.0 1.6 %collective-permute-start.8 = (bf16[64,512]{1,0:T(8,128)(2,1)S(1)}, bf16[64,512]{1,0:T(8,128)(2,1)S(1)}, u32[]{:S(2)}, u32[]{:S(2)}) collective-permute-start(bf16[64,512]{1,0:T(8,128)(2,1)S(1)} %shard_map.74.a_ref), channel_id=1, source_target_pairs={{0,8},{1,17},{2,10},{3,19},{4,12},{5,21},{6,14},{7,23},{8,0},{9,25... | collective-permute-start | bytes 196616 | tf_op jit(solution)/shard_map/ppermute | solution.py:33
  28.7 2.4 %collective-permute-done.8.b_ref = bf16[64,512]{1,0:T(8,128)(2,1)S(1)} collective-permute-done((bf16[64,512]{1,0:T(8,128)(2,1)S(1)}, bf16[64,512]{1,0:T(8,128)(2,1)S(1)}, u32[]{:S(2)}, u32[]{:S(2)}) %collective-permute-start.8) | collective-permute-done | bytes 65568 | tf_op jit(solution)/shard_map/ppermute | solution.py:33
  31.0 2.0 %collective-permute-start.9 = (bf16[64,512]{1,0:T(8,128)(2,1)S(1)}, bf16[64,512]{1,0:T(8,128)(2,1)S(1)}, u32[]{:S(2)}, u32[]{:S(2)}) collective-permute-start(bf16[64,512]{1,0:T(8,128)(2,1)S(1)} %shard_map.75.refs_0_), channel_id=1, source_target_pairs={{0,16},{1,9},{2,18},{3,11},{4,20},{5,13},{6,22},{7,15},{8,24},{9,1... | collective-permute-start | bytes 196616 | tf_op jit(solution)/shard_map/ppermute | solution.py:33
  33.0 2.6 %collective-permute-start.12 = (bf16[64,512]{1,0:T(8,128)(2,1)S(1)}, bf16[64,512]{1,0:T(8,128)(2,1)S(1)}, u32[]{:S(2)}, u32[]{:S(2)}) collective-permute-start(bf16[64,512]{1,0:T(8,128)(2,1)S(1)} %shard_map.78.refs_2_), channel_id=1, source_target_pairs={{0,16},{1,9},{2,18},{3,11},{4,20},{5,13},{6,22},{7,15},{8,24},{9,1... | collective-permute-start | bytes 196616 | tf_op jit(solution)/shard_map/ppermute | solution.py:33
  36.3 2.0 %collective-permute-done.12.refs_3_ = bf16[64,512]{1,0:T(8,128)(2,1)S(1)} collective-permute-done((bf16[64,512]{1,0:T(8,128)(2,1)S(1)}, bf16[64,512]{1,0:T(8,128)(2,1)S(1)}, u32[]{:S(2)}, u32[]{:S(2)}) %collective-permute-start.12) | collective-permute-done | bytes 65568 | tf_op jit(solution)/shard_map/ppermute | solution.py:33
  38.3 0.8 %shard_map.79 = f32[64,1024]{1,0:T(8,128)} custom-call(bf16[64,512]{1,0:T(8,128)(2,1)S(1)} %shard_map.75.refs_0_, bf16[64,512]{1,0:T(8,128)(2,1)S(1)} %collective-permute-done.9.refs_1_, bf16[64,512]{1,0:T(8,128)(2,1)S(1)} %shard_map.78.refs_2_, bf16[64,512]{1,0:T(8,128)(2,1)S(1)} %collective-permute-done.12.refs_3_, f32[64,1]{1,0:T(8,128)S(1)} %copy.7.refs_4_), custom_call_target="tpu_custom_call" | custom-call | tf_op jit(solution)/shard_map/pallas_call | solution.py:168
  (24 shorter events, 3.8 us)
Async XLA Ops:
  1.0 15.5 %collective-permute-start = (bf16[1024,1024]{1,0:T(8,128)(2,1)}, bf16[1024,1024]{1,0:T(8,128)(2,1)S(1)}, u32[]{:S(2)}, u32[]{:S(2)}) collective-permute-start(bf16[1024,1024]{1,0:T(8,128)(2,1)} %in_ref.1), channel_id=1, source_target_pairs={{0,1},{1,0},{2,3},{3,2},{4,5},{5,4},{6,7},{7,6},{8,9},{9,8},{10,11... | collective-permute-start | bytes 6291464 | tf_op jit(solution)/shard_map/ppermute | solution.py:18
  1.5 12.3 %collective-permute-start.2 = (bf16[144,1024]{1,0:T(8,128)(2,1)S(1)}, bf16[144,1024]{1,0:T(8,128)(2,1)S(1)}, u32[]{:S(2)}, u32[]{:S(2)}) collective-permute-start(bf16[144,1024]{1,0:T(8,128)(2,1)S(1)} %slice.3.refs_2_), channel_id=1, source_target_pairs={{0,4},{1,3},{2,6},{3,1},{4,0},{5,7},{6,2},{7,5},{8,12},{9,11},{10,... | collective-permute-start | bytes 884744 | tf_op jit(solution)/shard_map/ppermute | solution.py:23
  5.1 8.7 %collective-permute-start.1 = (bf16[128,1024]{1,0:T(8,128)(2,1)S(1)}, bf16[128,1024]{1,0:T(8,128)(2,1)S(1)}, u32[]{:S(2)}, u32[]{:S(2)}) collective-permute-start(bf16[128,1024]{1,0:T(8,128)(2,1)S(1)} %shard_map.66.refs_1_), channel_id=1, source_target_pairs={{0,2},{1,5},{2,0},{3,7},{4,6},{5,1},{6,4},{7,3},{8,10},{9,13},{10,... | collective-permute-start | bytes 786440 | tf_op jit(solution)/shard_map/ppermute | solution.py:23
  6.7 13.0 %collective-permute-start.5 = (bf16[144,1024]{1,0:T(8,128)(2,1)S(1)}, bf16[144,1024]{1,0:T(8,128)(2,1)S(1)}, u32[]{:S(2)}, u32[]{:S(2)}) collective-permute-start(bf16[144,1024]{1,0:T(8,128)(2,1)S(1)} %slice.3.refs_2_), channel_id=1, source_target_pairs={{0,2},{1,5},{2,0},{3,7},{4,6},{5,1},{6,4},{7,3},{8,10},{9,13},{10,... | collective-permute-start | bytes 884744 | tf_op jit(solution)/shard_map/ppermute | solution.py:23
  7.2 14.0 %collective-permute-start.4 = (bf16[128,1024]{1,0:T(8,128)(2,1)S(1)}, bf16[128,1024]{1,0:T(8,128)(2,1)S(1)}, u32[]{:S(2)}, u32[]{:S(2)}) collective-permute-start(bf16[128,1024]{1,0:T(8,128)(2,1)S(1)} %shard_map.66.refs_1_), channel_id=1, source_target_pairs={{0,4},{1,3},{2,6},{3,1},{4,0},{5,7},{6,2},{7,5},{8,12},{9,11},{10,... | collective-permute-start | bytes 786440 | tf_op jit(solution)/shard_map/ppermute | solution.py:23
  7.3 1.6 %copy-start = (bf16[1024,1024]{1,0:T(8,128)(2,1)S(1)}, bf16[1024,1024]{1,0:T(8,128)(2,1)}, u32[]{:S(2)}) copy-start(bf16[1024,1024]{1,0:T(8,128)(2,1)} %in_ref.1) | copy-start | bytes 6291460
  13.8 9.2 %collective-permute-start.3 = (bf16[128,1024]{1,0:T(8,128)(2,1)S(1)}, bf16[128,1024]{1,0:T(8,128)(2,1)S(1)}, u32[]{:S(2)}, u32[]{:S(2)}) collective-permute-start(bf16[128,1024]{1,0:T(8,128)(2,1)S(1)} %collective-permute-done.1.refs_2_), channel_id=1, source_target_pairs={{0,4},{1,3},{2,6},{3,1},{4,0},{5,7},{6,2},{7,5},{8,12},{9,11},{10,... | collective-permute-start | bytes 786440 | tf_op jit(solution)/shard_map/ppermute | solution.py:23
  14.5 9.6 %collective-permute-start.6 = (bf16[144,1024]{1,0:T(8,128)(2,1)S(1)}, bf16[144,1024]{1,0:T(8,128)(2,1)S(1)}, u32[]{:S(2)}, u32[]{:S(2)}) collective-permute-start(bf16[144,1024]{1,0:T(8,128)(2,1)S(1)} %collective-permute-done.2.refs_3_), channel_id=1, source_target_pairs={{0,2},{1,5},{2,0},{3,7},{4,6},{5,1},{6,4},{7,3},{8,10},{9,13},{10,... | collective-permute-start | bytes 884744 | tf_op jit(solution)/shard_map/ppermute | solution.py:23
  24.6 1.4 %collective-permute-start.7 = (f32[64,512]{1,0:T(8,128)S(1)}, f32[64,512]{1,0:T(8,128)S(1)}, u32[]{:S(2)}, u32[]{:S(2)}) collective-permute-start(f32[64,512]{1,0:T(8,128)S(1)} %shard_map.73), channel_id=1, source_target_pairs={{0,1},{1,0},{2,3},{3,2},{4,5},{5,4},{6,7},{7,6},{8,9},{9,8},{10,11... | collective-permute-start | bytes 393224 | tf_op jit(solution)/shard_map/ppermute | solution.py:18
  25.3 10.4 %copy-start.1 = (f32[64]{0:T(128)S(1)}, f32[64]{0:T(128)}, u32[]{:S(2)}) copy-start(f32[64]{0:T(128)} %param.11) | copy-start | bytes 772
  25.3 2.8 %collective-permute-start.10 = (f32[64,512]{1,0:T(8,128)S(1)}, f32[64,512]{1,0:T(8,128)S(1)}, u32[]{:S(2)}, u32[]{:S(2)}) collective-permute-start(f32[64,512]{1,0:T(8,128)S(1)} %get-tuple-element.32), channel_id=1, source_target_pairs={{0,1},{1,0},{2,3},{3,2},{4,5},{5,4},{6,7},{7,6},{8,9},{9,8},{10,11... | collective-permute-start | bytes 393224 | tf_op jit(solution)/shard_map/ppermute | solution.py:18
  26.0 5.0 %collective-permute-start.8 = (bf16[64,512]{1,0:T(8,128)(2,1)S(1)}, bf16[64,512]{1,0:T(8,128)(2,1)S(1)}, u32[]{:S(2)}, u32[]{:S(2)}) collective-permute-start(bf16[64,512]{1,0:T(8,128)(2,1)S(1)} %shard_map.74.a_ref), channel_id=1, source_target_pairs={{0,8},{1,17},{2,10},{3,19},{4,12},{5,21},{6,14},{7,23},{8,0},{9,25... | collective-permute-start | bytes 196616 | tf_op jit(solution)/shard_map/ppermute | solution.py:33
  28.1 4.9 %collective-permute-start.11 = (bf16[64,512]{1,0:T(8,128)(2,1)S(1)}, bf16[64,512]{1,0:T(8,128)(2,1)S(1)}, u32[]{:S(2)}, u32[]{:S(2)}) collective-permute-start(bf16[64,512]{1,0:T(8,128)(2,1)S(1)} %shard_map.77.a_ref), channel_id=1, source_target_pairs={{0,8},{1,17},{2,10},{3,19},{4,12},{5,21},{6,14},{7,23},{8,0},{9,25... | collective-permute-start | bytes 196616 | tf_op jit(solution)/shard_map/ppermute | solution.py:33
  31.0 5.2 %collective-permute-start.9 = (bf16[64,512]{1,0:T(8,128)(2,1)S(1)}, bf16[64,512]{1,0:T(8,128)(2,1)S(1)}, u32[]{:S(2)}, u32[]{:S(2)}) collective-permute-start(bf16[64,512]{1,0:T(8,128)(2,1)S(1)} %shard_map.75.refs_0_), channel_id=1, source_target_pairs={{0,16},{1,9},{2,18},{3,11},{4,20},{5,13},{6,22},{7,15},{8,24},{9,1... | collective-permute-start | bytes 196616 | tf_op jit(solution)/shard_map/ppermute | solution.py:33
  33.0 5.2 %collective-permute-start.12 = (bf16[64,512]{1,0:T(8,128)(2,1)S(1)}, bf16[64,512]{1,0:T(8,128)(2,1)S(1)}, u32[]{:S(2)}, u32[]{:S(2)}) collective-permute-start(bf16[64,512]{1,0:T(8,128)(2,1)S(1)} %shard_map.78.refs_2_), channel_id=1, source_target_pairs={{0,16},{1,9},{2,18},{3,11},{4,20},{5,13},{6,22},{7,15},{8,24},{9,1... | collective-permute-start | bytes 196616 | tf_op jit(solution)/shard_map/ppermute | solution.py:33

commit v6 on v3

--- a/solution.py
+++ b/solution.py
@@ -34,7 +34,7 @@
 
 
 def prepare_kernel(
-    land_ref, codes_ref, exponents_ref, eig_ref, first_ref, codes, eig, exponents, sems
+    land_ref, codes_ref, exponents_ref, eig_ref, first_ref, vec_ref, codes, eig, exponents, sems
 ):
     rows, feat = land_ref.shape
     half = rows // 2 - SHIFT
@@ -59,7 +59,9 @@
     chunks = feat // rows
     depth = ritz // chunks
     for c in range(chunks):
-        first_ref[half:, c * rows : (c + 1) * rows] = vectors[c * depth : (c + 1) * depth, :]
+        part = vectors[c * depth : (c + 1) * depth, :]
+        first_ref[half:, c * rows : (c + 1) * rows] = part
+        vec_ref[:, c * rows : (c + 1) * rows] = part
     for copy in copies[3:]:
         copy.wait()
 
@@ -69,7 +71,10 @@
     extra = eig_t.shape[0] * rows // feat
     return pl.pallas_call(
         prepare_kernel,
-        out_shape=jax.ShapeDtypeStruct((rows // 2 - SHIFT + extra, feat), jnp.bfloat16),
+        out_shape=[
+            jax.ShapeDtypeStruct((rows // 2 - SHIFT + extra, feat), jnp.bfloat16),
+            jax.ShapeDtypeStruct((extra, feat), jnp.bfloat16),
+        ],
         in_specs=[pl.BlockSpec(memory_space=pltpu.HBM)] * 4,
         scratch_shapes=[
             pltpu.VMEM(codes_t.shape, codes_t.dtype),
@@ -81,6 +86,16 @@
     )(*(pltpu.with_memory_space_constraint(x, pltpu.HBM) for x in (landmarks, codes_t, exponents, eig_t)))
 
 
+def cut_first_kernel(land_ref, vec_ref, out_ref):
+    head = out_ref.shape[0] - vec_ref.shape[0]
+    out_ref[:head, :] = land_ref[:head, :]
+    out_ref[head:, :] = vec_ref[...]
+
+
+def cut_second_kernel(land_ref, out_ref):
+    out_ref[...] = land_ref[land_ref.shape[0] - out_ref.shape[0] :, :]
+
+
 def transpose_kernel(in_ref, out_ref):
     for k in range(in_ref.shape[0] // CHUNK):
         rows = slice(k * CHUNK, (k + 1) * CHUNK)
@@ -95,7 +110,9 @@
     tail, feat = second_ref.shape
     rows = (first_ref.shape[0] + tail) * feat // (feat + ritz)
     head = rows - tail
-    land = jnp.concatenate([first_ref[:head, :], second_ref[...]], axis=0)
+    land = second_ref[...]
+    if head:
+        land = jnp.concatenate([first_ref[:head, :], land], axis=0)
     vec = jnp.concatenate(
         [first_ref[head:, c * rows : (c + 1) * rows] for c in range(feat // rows)], axis=0
     )
@@ -167,24 +184,30 @@
     rows = slab.shape[0]
     ways = n_sl.bit_length() - 2
 
+    first, vectors = prepare(landmarks, codes.T, exponents, eigvec.T)
     second = landmarks[landmarks.shape[0] // 2 - SHIFT :]
-    first = prepare(landmarks, codes.T, exponents, eigvec.T)
-    blocks = {0: [first, second]}
-    for k in range(ways):
-        blocks[1 << k] = [None, None]
-    for turn in (0, 1):
-        for k in range(ways):
-            piece = (k + turn) % 2
-            blocks[1 << k][piece] = chip_send(blocks[0][piece], k, n_sl)
-    late_slab, _ = lax.optimization_barrier((slab, second))
+    whole = {k: chip_send(landmarks, k, n_sl) for k in range(1, ways, 2)}
+    other = core_send(slab, n_sl)
+    blocks, parts = {}, {}
+    for k in range(0, ways, 2):
+        blocks[1 << k] = [chip_send(first, k, n_sl), None]
+    for k in range(0, ways, 2):
+        blocks[1 << k][1] = chip_send(second, k, n_sl)
     turned = jax.ShapeDtypeStruct(slab.shape[::-1], slab.dtype)
-    other = small_call(transpose_kernel, turned, core_send(late_slab, n_sl))
+    other = small_call(transpose_kernel, turned, other)
     slab = small_call(transpose_kernel, turned, slab)
     (acc,) = stage([slab], first, second, None, coeff, cols)
-    held = [blocks[1 << k][k % 2] for k in range(ways)]
-    held, acc = lax.optimization_barrier((held, acc))
-    for k in range(ways):
-        blocks[1 << k][k % 2] = held[k]
+    heads = [blocks[1 << k][0] for k in range(0, ways, 2)]
+    heads, whole, acc = lax.optimization_barrier((heads, whole, acc))
+    for k in range(0, ways, 2):
+        blocks[1 << k][0] = heads[k // 2]
+    for k in range(1, ways, 2):
+        vec = chip_send(vectors, k, n_sl)
+        parts[1 << k] = [vec, whole[k]]
+        blocks[1 << k] = [
+            small_call(cut_first_kernel, first, whole[k], vec),
+            small_call(cut_second_kernel, second, whole[k]),
+        ]
     (other_acc,) = stage([other], first, second, None, coeff, cols)
     accs = [acc, other_acc]
     for t in range(1, 1 << ways):
@@ -197,7 +220,7 @@
         ]
 
     for t in range(1, (1 << ways) - 1):
-        accs = stage([slab, other], *blocks[t], accs, coeff, cols)
+        accs = stage([slab, other], *parts.get(t, blocks[t]), accs, coeff, cols)
     end = blocks[(1 << ways) - 1]
     width = rows // 2
     spans = [(0, width), (width, rows)]

time: 38.9 us -> 39.2 us (level)
  starting transfers between devices: 15.6 us -> 17.9 us
  waiting for transfers between devices: 10.3 us -> 8.33 us
    ppermute x6, starting transfers between devices: 7.36 us -> 9.72 us  [chip_send(): lax.ppermute(value, 'sl', [(i, i ^ bits[(k + i % 2) % len(bits)]) for i i...]
    ppermute x6, waiting for transfers between devices: 5.93 us -> 3.66 us  [chip_send(): lax.ppermute(value, 'sl', [(i, i ^ bits[(k + i % 2) % len(bits)]) for i i...]
    pallas_call x7 -> x8, Pallas kernels: 2.13 us -> 2.15 us  [small_call(): pl.pallas_call(kernel, out_shape=jax.ShapeDtypeStruct(out.shape, out.dtyp...]
  transfers between devices with their start and end apart: 13 -> 13, of which waited for: 7 -> 6; matrix products, arithmetic and copies ran while one was open for 0% -> 3% of each run, Pallas kernels for 22% -> 22%
where the time goes in v6:
time: 39.2 us; the launch traced here: 39 us
  starting transfers between devices  17.9 us (46%)
  Pallas kernels  10 us (26%)
  waiting for transfers between devices  8.33 us (21%)
  local copies, waits for them, and re-layouts  2.67 us (7%)
    ppermute x6, starting transfers between devices, chip_send(): lax.ppermute(value, 'sl', [(i, i ^ bits[(k + i % 2) % len(bits)]) for i i...  9.72 us
    ppermute x4, starting transfers between devices, lm_send(): return lax.ppermute(value, ('lm', 'sl'), perm)  7.04 us
    pallas_call x7, Pallas kernels, stage(): pl.pallas_call(functools.partial(stage_kernel, count, coeff, ritz, accs i...  6.83 us
    ppermute x4, waiting for transfers between devices, lm_send(): return lax.ppermute(value, ('lm', 'sl'), perm)  4.67 us
    ppermute x6, waiting for transfers between devices, chip_send(): lax.ppermute(value, 'sl', [(i, i ^ bits[(k + i % 2) % len(bits)]) for i i...  3.66 us
    pallas_call x8, Pallas kernels, small_call(): pl.pallas_call(kernel, out_shape=jax.ShapeDtypeStruct(out.shape, out.dtyp...  2.15 us
    unnamed x4, local copies, waits for them, and re-layouts  1.59 us
    ppermute x3, starting transfers between devices, core_send(): return lax.ppermute(value, 'sl', [(i, i ^ 1) for i in range(n)])  1.09 us
  transfers between devices with their start and end apart: 13, of which 6 were waited for; matrix products, arithmetic and copies ran while one was open for 3% of the time, Pallas kernels for 22%

profile of v6, /device:TPU:0, one launch (start us, length us, event | category | flops | bytes accessed | tf_op | source)
XLA Modules:
  0.0 39.0 jit_solution(7942988841467750597)
XLA Ops:
  0.5 2.5 %collective-permute-start.3 = (bf16[256,1024]{1,0:T(8,128)(2,1)}, bf16[256,1024]{1,0:T(8,128)(2,1)S(1)}, u32[]{:S(2)}, u32[]{:S(2)}) collective-permute-start(bf16[256,1024]{1,0:T(8,128)(2,1)} %land_ref.1), channel_id=1, source_target_pairs={{0,4},{1,3},{2,6},{3,1},{4,0},{5,7},{6,2},{7,5},{8,12},{9,11},{10,... | collective-permute-start | bytes 1572872 | tf_op jit(solution)/shard_map/ppermute | solution.py:23
  3.0 1.1 %shard_map.66 = (bf16[128,1024]{1,0:T(8,128)(2,1)S(1)}, bf16[16,1024]{1,0:T(8,128)(2,1)S(1)}) custom-call(bf16[256,1024]{1,0:T(8,128)(2,1)} %land_ref.1, bf16[96,256]{1,0:T(8,128)(2,1)} %bitcast.4, s32[2]{0:T(128)} %exponents_ref.1, bf16[64,96]{1,0:T(8,128)(2,1)} %bitcast.5), custom_call_target="tpu_custom_call" | custom-call | tf_op jit(solution)/shard_map/pallas_call | solution.py:72
  4.0 1.6 %collective-permute-start.2 = (bf16[128,1024]{1,0:T(8,128)(2,1)S(1)}, bf16[128,1024]{1,0:T(8,128)(2,1)S(1)}, u32[]{:S(2)}, u32[]{:S(2)}) collective-permute-start(bf16[128,1024]{1,0:T(8,128)(2,1)S(1)} %get-tuple-element.19.refs_1_), channel_id=1, source_target_pairs={{0,2},{1,5},{2,0},{3,7},{4,6},{5,1},{6,4},{7,3},{8,10},{9,13},{10,... | collective-permute-start | bytes 786440 | tf_op jit(solution)/shard_map/ppermute | solution.py:23
  5.6 1.0 %slice.3.refs_2_ = bf16[144,1024]{1,0:T(8,128)(2,1)S(1)} slice(bf16[256,1024]{1,0:T(8,128)(2,1)} %land_ref.1), slice={[112:256], [0:1024]} | slice | bytes 589824 | tf_op jit(solution)/shard_map/slice | solution.py:188
  6.6 0.6 %collective-permute-start.4 = (bf16[144,1024]{1,0:T(8,128)(2,1)S(1)}, bf16[144,1024]{1,0:T(8,128)(2,1)S(1)}, u32[]{:S(2)}, u32[]{:S(2)}) collective-permute-start(bf16[144,1024]{1,0:T(8,128)(2,1)S(1)} %slice.3.refs_2_), channel_id=1, source_target_pairs={{0,2},{1,5},{2,0},{3,7},{4,6},{5,1},{6,4},{7,3},{8,10},{9,13},{10,... | collective-permute-start | bytes 884744 | tf_op jit(solution)/shard_map/ppermute | solution.py:23
  7.2 1.6 %copy-done = bf16[1024,1024]{1,0:T(8,128)(2,1)S(1)} copy-done((bf16[1024,1024]{1,0:T(8,128)(2,1)S(1)}, bf16[1024,1024]{1,0:T(8,128)(2,1)}, u32[]{:S(2)}) %copy-start) | copy-done | bytes 2097176
  8.8 0.6 %shard_map.64.refs_0_.refs_1_ = bf16[1024,1024]{1,0:T(8,128)(2,1)S(1)} custom-call(bf16[1024,1024]{1,0:T(8,128)(2,1)S(1)} %copy-done), custom_call_target="tpu_custom_call" | custom-call | tf_op jit(solution)/shard_map/pallas_call | solution.py:172
  9.5 0.9 %shard_map.67.refs_4_ = f32[64,1024]{1,0:T(8,128)S(1)} custom-call(bf16[1024,1024]{1,0:T(8,128)(2,1)S(1)} %shard_map.64.refs_0_.refs_1_, bf16[128,1024]{1,0:T(8,128)(2,1)S(1)} %get-tuple-element.19.refs_1_, bf16[144,1024]{1,0:T(8,128)(2,1)S(1)} %slice.3.refs_2_), custom_call_target="tpu_custom_call" | custom-call | flops 671088640 | bytes 2621440 | tf_op jit(solution)/shard_map/pallas_call | solution.py:143
  10.3 3.0 %collective-permute-done.2.refs_2_ = bf16[128,1024]{1,0:T(8,128)(2,1)S(1)} collective-permute-done((bf16[128,1024]{1,0:T(8,128)(2,1)S(1)}, bf16[128,1024]{1,0:T(8,128)(2,1)S(1)}, u32[]{:S(2)}, u32[]{:S(2)}) %collective-permute-start.2) | collective-permute-done | bytes 262176 | tf_op jit(solution)/shard_map/ppermute | solution.py:23
  13.9 2.4 %collective-permute-start.5 = (bf16[128,1024]{1,0:T(8,128)(2,1)S(1)}, bf16[128,1024]{1,0:T(8,128)(2,1)S(1)}, u32[]{:S(2)}, u32[]{:S(2)}) collective-permute-start(bf16[128,1024]{1,0:T(8,128)(2,1)S(1)} %collective-permute-done.2.refs_2_), channel_id=1, source_target_pairs={{0,4},{1,3},{2,6},{3,1},{4,0},{5,7},{6,2},{7,5},{8,12},{9,11},{10,... | collective-permute-start | bytes 786440 | tf_op jit(solution)/shard_map/ppermute | solution.py:23
  16.3 2.6 %collective-permute-start.6 = (bf16[144,1024]{1,0:T(8,128)(2,1)S(1)}, bf16[144,1024]{1,0:T(8,128)(2,1)S(1)}, u32[]{:S(2)}, u32[]{:S(2)}) collective-permute-start(bf16[144,1024]{1,0:T(8,128)(2,1)S(1)} %shard_map.71), channel_id=1, source_target_pairs={{0,2},{1,5},{2,0},{3,7},{4,6},{5,1},{6,4},{7,3},{8,10},{9,13},{10,... | collective-permute-start | bytes 884744 | tf_op jit(solution)/shard_map/ppermute | solution.py:23
  18.9 0.6 %shard_map.65.refs_0_.refs_1_ = bf16[1024,1024]{1,0:T(8,128)(2,1)S(1)} custom-call(bf16[1024,1024]{1,0:T(8,128)(2,1)S(1)} %collective-permute-done.in_ref), custom_call_target="tpu_custom_call" | custom-call | tf_op jit(solution)/shard_map/pallas_call | solution.py:172
  19.5 0.9 %shard_map.68.refs_5_ = f32[64,1024]{1,0:T(8,128)S(1)} custom-call(bf16[1024,1024]{1,0:T(8,128)(2,1)S(1)} %shard_map.65.refs_0_.refs_1_, bf16[128,1024]{1,0:T(8,128)(2,1)S(1)} %get-tuple-element.19.refs_1_, bf16[144,1024]{1,0:T(8,128)(2,1)S(1)} %slice.3.refs_2_), custom_call_target="tpu_custom_call" | custom-call | flops 671088640 | bytes 2621440 | tf_op jit(solution)/shard_map/pallas_call | solution.py:143
  20.4 1.5 %shard_map.69 = (f32[64,1024]{1,0:T(8,128)S(1)}, f32[64,1024]{1,0:T(8,128)S(1)}) custom-call(bf16[1024,1024]{1,0:T(8,128)(2,1)S(1)} %shard_map.64.refs_0_.refs_1_, bf16[1024,1024]{1,0:T(8,128)(2,1)S(1)} %shard_map.65.refs_0_.refs_1_, bf16[128,1024]{1,0:T(8,128)(2,1)S(1)} %collective-permute-done.2.refs_2_, ...), custom_call_target="tpu_custom_call" | custom-call | flops 1342177280 | bytes 4718592 | tf_op jit(solution)/shard_map/pallas_call | solution.py:143
  22.0 1.5 %shard_map.70 = (f32[64,1024]{1,0:T(8,128)S(1)}, f32[64,1024]{1,0:T(8,128)S(1)}) custom-call(bf16[1024,1024]{1,0:T(8,128)(2,1)S(1)} %shard_map.64.refs_0_.refs_1_, bf16[1024,1024]{1,0:T(8,128)(2,1)S(1)} %shard_map.65.refs_0_.refs_1_, bf16[16,1024]{1,0:T(8,128)(2,1)S(1)} %collective-permute-done.1.refs_2_, ...), custom_call_target="tpu_custom_call" | custom-call | flops 1342177280 | bytes 4718592 | tf_op jit(solution)/shard_map/pallas_call | solution.py:143
  23.6 0.6 %shard_map.73 = f32[64,512]{1,0:T(8,128)S(1)} custom-call(bf16[1024,1024]{1,0:T(8,128)(2,1)S(1)} %shard_map.65.refs_0_.refs_1_, bf16[128,1024]{1,0:T(8,128)(2,1)S(1)} %collective-permute-done.5.refs_2_.refs_1_, bf16[144,1024]{1,0:T(8,128)(2,1)S(1)} %collective-permute-done.6.refs_3_.refs_2_, f32[64,1024]{1,0:T(8,128)S(1)} %get-tuple-element.26.refs_4_.refs_3_), custom_call_target="tpu_custom_call" | custom-call | flops 335544320 | bytes 1572864 | tf_op jit(solution)/shard_map/pallas_call | solution.py:143
  24.4 0.9 %shard_map.72 = (f32[64,512]{1,0:T(8,128)S(1)}, f32[64,512]{1,0:T(8,128)S(1)}) custom-call(bf16[1024,1024]{1,0:T(8,128)(2,1)S(1)} %shard_map.65.refs_0_.refs_1_, bf16[1024,1024]{1,0:T(8,128)(2,1)S(1)} %shard_map.64.refs_0_.refs_1_, bf16[128,1024]{1,0:T(8,128)(2,1)S(1)} %collective-permute-done.5.refs_2_.refs_1_, ...), custom_call_target="tpu_custom_call" | custom-call | flops 671088640 | bytes 2621440 | tf_op jit(solution)/shard_map/pallas_call | solution.py:143
  25.7 1.8 %collective-permute-start.8 = (bf16[64,512]{1,0:T(8,128)(2,1)S(1)}, bf16[64,512]{1,0:T(8,128)(2,1)S(1)}, u32[]{:S(2)}, u32[]{:S(2)}) collective-permute-start(bf16[64,512]{1,0:T(8,128)(2,1)S(1)} %shard_map.74.a_ref), channel_id=1, source_target_pairs={{0,8},{1,17},{2,10},{3,19},{4,12},{5,21},{6,14},{7,23},{8,0},{9,25... | collective-permute-start | bytes 196616 | tf_op jit(solution)/shard_map/ppermute | solution.py:33
  27.6 0.6 %shard_map.76.a_ref = f32[64,512]{1,0:T(8,128)S(1)} custom-call(bf16[1024,1024]{1,0:T(8,128)(2,1)S(1)} %shard_map.64.refs_0_.refs_1_, bf16[128,1024]{1,0:T(8,128)(2,1)S(1)} %collective-permute-done.5.refs_2_.refs_1_, bf16[144,1024]{1,0:T(8,128)(2,1)S(1)} %collective-permute-done.6.refs_3_.refs_2_, f32[64,1024]{1,0:T(8,128)S(1)} %get-tuple-element.29.refs_5_.refs_3_), custom_call_target="tpu_custom_call" | custom-call | flops 335544320 | bytes 1572864 | tf_op jit(solution)/shard_map/pallas_call | solution.py:143
  28.6 2.2 %collective-permute-done.8.b_ref = bf16[64,512]{1,0:T(8,128)(2,1)S(1)} collective-permute-done((bf16[64,512]{1,0:T(8,128)(2,1)S(1)}, bf16[64,512]{1,0:T(8,128)(2,1)S(1)}, u32[]{:S(2)}, u32[]{:S(2)}) %collective-permute-start.8) | collective-permute-done | bytes 65568 | tf_op jit(solution)/shard_map/ppermute | solution.py:33
  30.8 2.2 %collective-permute-start.9 = (bf16[64,512]{1,0:T(8,128)(2,1)S(1)}, bf16[64,512]{1,0:T(8,128)(2,1)S(1)}, u32[]{:S(2)}, u32[]{:S(2)}) collective-permute-start(bf16[64,512]{1,0:T(8,128)(2,1)S(1)} %shard_map.75.refs_0_), channel_id=1, source_target_pairs={{0,16},{1,9},{2,18},{3,11},{4,20},{5,13},{6,22},{7,15},{8,24},{9,1... | collective-permute-start | bytes 196616 | tf_op jit(solution)/shard_map/ppermute | solution.py:33
  33.0 2.7 %collective-permute-start.12 = (bf16[64,512]{1,0:T(8,128)(2,1)S(1)}, bf16[64,512]{1,0:T(8,128)(2,1)S(1)}, u32[]{:S(2)}, u32[]{:S(2)}) collective-permute-start(bf16[64,512]{1,0:T(8,128)(2,1)S(1)} %shard_map.78.refs_2_), channel_id=1, source_target_pairs={{0,16},{1,9},{2,18},{3,11},{4,20},{5,13},{6,22},{7,15},{8,24},{9,1... | collective-permute-start | bytes 196616 | tf_op jit(solution)/shard_map/ppermute | solution.py:33
  36.0 2.2 %collective-permute-done.12.refs_3_ = bf16[64,512]{1,0:T(8,128)(2,1)S(1)} collective-permute-done((bf16[64,512]{1,0:T(8,128)(2,1)S(1)}, bf16[64,512]{1,0:T(8,128)(2,1)S(1)}, u32[]{:S(2)}, u32[]{:S(2)}) %collective-permute-start.12) | collective-permute-done | bytes 65568 | tf_op jit(solution)/shard_map/ppermute | solution.py:33
  38.2 0.8 %shard_map.79 = f32[64,1024]{1,0:T(8,128)} custom-call(bf16[64,512]{1,0:T(8,128)(2,1)S(1)} %shard_map.75.refs_0_, bf16[64,512]{1,0:T(8,128)(2,1)S(1)} %collective-permute-done.9.refs_1_, bf16[64,512]{1,0:T(8,128)(2,1)S(1)} %shard_map.78.refs_2_, bf16[64,512]{1,0:T(8,128)(2,1)S(1)} %collective-permute-done.12.refs_3_, f32[64,1]{1,0:T(8,128)S(1)} %copy.7.refs_4_), custom_call_target="tpu_custom_call" | custom-call | tf_op jit(solution)/shard_map/pallas_call | solution.py:172
  (24 shorter events, 2.7 us)
Async XLA Ops:
  0.0 18.9 %collective-permute-start = (bf16[1024,1024]{1,0:T(8,128)(2,1)}, bf16[1024,1024]{1,0:T(8,128)(2,1)S(1)}, u32[]{:S(2)}, u32[]{:S(2)}) collective-permute-start(bf16[1024,1024]{1,0:T(8,128)(2,1)} %in_ref.1), channel_id=1, source_target_pairs={{0,1},{1,0},{2,3},{3,2},{4,5},{5,4},{6,7},{7,6},{8,9},{9,8},{10,11... | collective-permute-start | bytes 6291464 | tf_op jit(solution)/shard_map/ppermute | solution.py:18
  0.5 13.4 %collective-permute-start.3 = (bf16[256,1024]{1,0:T(8,128)(2,1)}, bf16[256,1024]{1,0:T(8,128)(2,1)S(1)}, u32[]{:S(2)}, u32[]{:S(2)}) collective-permute-start(bf16[256,1024]{1,0:T(8,128)(2,1)} %land_ref.1), channel_id=1, source_target_pairs={{0,4},{1,3},{2,6},{3,1},{4,0},{5,7},{6,2},{7,5},{8,12},{9,11},{10,... | collective-permute-start | bytes 1572872 | tf_op jit(solution)/shard_map/ppermute | solution.py:23
  4.0 9.3 %collective-permute-start.2 = (bf16[128,1024]{1,0:T(8,128)(2,1)S(1)}, bf16[128,1024]{1,0:T(8,128)(2,1)S(1)}, u32[]{:S(2)}, u32[]{:S(2)}) collective-permute-start(bf16[128,1024]{1,0:T(8,128)(2,1)S(1)} %get-tuple-element.19.refs_1_), channel_id=1, source_target_pairs={{0,2},{1,5},{2,0},{3,7},{4,6},{5,1},{6,4},{7,3},{8,10},{9,13},{10,... | collective-permute-start | bytes 786440 | tf_op jit(solution)/shard_map/ppermute | solution.py:23
  6.6 13.8 %collective-permute-start.4 = (bf16[144,1024]{1,0:T(8,128)(2,1)S(1)}, bf16[144,1024]{1,0:T(8,128)(2,1)S(1)}, u32[]{:S(2)}, u32[]{:S(2)}) collective-permute-start(bf16[144,1024]{1,0:T(8,128)(2,1)S(1)} %slice.3.refs_2_), channel_id=1, source_target_pairs={{0,2},{1,5},{2,0},{3,7},{4,6},{5,1},{6,4},{7,3},{8,10},{9,13},{10,... | collective-permute-start | bytes 884744 | tf_op jit(solution)/shard_map/ppermute | solution.py:23
  7.2 14.8 %collective-permute-start.1 = (bf16[16,1024]{1,0:T(8,128)(2,1)S(1)}, bf16[16,1024]{1,0:T(8,128)(2,1)S(1)}, u32[]{:S(2)}, u32[]{:S(2)}) collective-permute-start(bf16[16,1024]{1,0:T(8,128)(2,1)S(1)} %get-tuple-element.18), channel_id=1, source_target_pairs={{0,4},{1,3},{2,6},{3,1},{4,0},{5,7},{6,2},{7,5},{8,12},{9,11},{10,... | collective-permute-start | bytes 98312 | tf_op jit(solution)/shard_map/ppermute | solution.py:23
  7.2 1.6 %copy-start = (bf16[1024,1024]{1,0:T(8,128)(2,1)S(1)}, bf16[1024,1024]{1,0:T(8,128)(2,1)}, u32[]{:S(2)}) copy-start(bf16[1024,1024]{1,0:T(8,128)(2,1)} %in_ref.1) | copy-start | bytes 6291460
  13.9 9.6 %collective-permute-start.5 = (bf16[128,1024]{1,0:T(8,128)(2,1)S(1)}, bf16[128,1024]{1,0:T(8,128)(2,1)S(1)}, u32[]{:S(2)}, u32[]{:S(2)}) collective-permute-start(bf16[128,1024]{1,0:T(8,128)(2,1)S(1)} %collective-permute-done.2.refs_2_), channel_id=1, source_target_pairs={{0,4},{1,3},{2,6},{3,1},{4,0},{5,7},{6,2},{7,5},{8,12},{9,11},{10,... | collective-permute-start | bytes 786440 | tf_op jit(solution)/shard_map/ppermute | solution.py:23
  16.3 7.3 %collective-permute-start.6 = (bf16[144,1024]{1,0:T(8,128)(2,1)S(1)}, bf16[144,1024]{1,0:T(8,128)(2,1)S(1)}, u32[]{:S(2)}, u32[]{:S(2)}) collective-permute-start(bf16[144,1024]{1,0:T(8,128)(2,1)S(1)} %shard_map.71), channel_id=1, source_target_pairs={{0,2},{1,5},{2,0},{3,7},{4,6},{5,1},{6,4},{7,3},{8,10},{9,13},{10,... | collective-permute-start | bytes 884744 | tf_op jit(solution)/shard_map/ppermute | solution.py:23
  24.2 1.5 %collective-permute-start.7 = (f32[64,512]{1,0:T(8,128)S(1)}, f32[64,512]{1,0:T(8,128)S(1)}, u32[]{:S(2)}, u32[]{:S(2)}) collective-permute-start(f32[64,512]{1,0:T(8,128)S(1)} %shard_map.73), channel_id=1, source_target_pairs={{0,1},{1,0},{2,3},{3,2},{4,5},{5,4},{6,7},{7,6},{8,9},{9,8},{10,11... | collective-permute-start | bytes 393224 | tf_op jit(solution)/shard_map/ppermute | solution.py:18
  25.2 10.4 %copy-start.1 = (f32[64]{0:T(128)S(1)}, f32[64]{0:T(128)}, u32[]{:S(2)}) copy-start(f32[64]{0:T(128)} %param.11) | copy-start | bytes 772
  25.2 2.9 %collective-permute-start.10 = (f32[64,512]{1,0:T(8,128)S(1)}, f32[64,512]{1,0:T(8,128)S(1)}, u32[]{:S(2)}, u32[]{:S(2)}) collective-permute-start(f32[64,512]{1,0:T(8,128)S(1)} %get-tuple-element.30), channel_id=1, source_target_pairs={{0,1},{1,0},{2,3},{3,2},{4,5},{5,4},{6,7},{7,6},{8,9},{9,8},{10,11... | collective-permute-start | bytes 393224 | tf_op jit(solution)/shard_map/ppermute | solution.py:18
  25.7 5.0 %collective-permute-start.8 = (bf16[64,512]{1,0:T(8,128)(2,1)S(1)}, bf16[64,512]{1,0:T(8,128)(2,1)S(1)}, u32[]{:S(2)}, u32[]{:S(2)}) collective-permute-start(bf16[64,512]{1,0:T(8,128)(2,1)S(1)} %shard_map.74.a_ref), channel_id=1, source_target_pairs={{0,8},{1,17},{2,10},{3,19},{4,12},{5,21},{6,14},{7,23},{8,0},{9,25... | collective-permute-start | bytes 196616 | tf_op jit(solution)/shard_map/ppermute | solution.py:33
  28.2 4.7 %collective-permute-start.11 = (bf16[64,512]{1,0:T(8,128)(2,1)S(1)}, bf16[64,512]{1,0:T(8,128)(2,1)S(1)}, u32[]{:S(2)}, u32[]{:S(2)}) collective-permute-start(bf16[64,512]{1,0:T(8,128)(2,1)S(1)} %shard_map.77.a_ref), channel_id=1, source_target_pairs={{0,8},{1,17},{2,10},{3,19},{4,12},{5,21},{6,14},{7,23},{8,0},{9,25... | collective-permute-start | bytes 196616 | tf_op jit(solution)/shard_map/ppermute | solution.py:33
  30.8 5.2 %collective-permute-start.9 = (bf16[64,512]{1,0:T(8,128)(2,1)S(1)}, bf16[64,512]{1,0:T(8,128)(2,1)S(1)}, u32[]{:S(2)}, u32[]{:S(2)}) collective-permute-start(bf16[64,512]{1,0:T(8,128)(2,1)S(1)} %shard_map.75.refs_0_), channel_id=1, source_target_pairs={{0,16},{1,9},{2,18},{3,11},{4,20},{5,13},{6,22},{7,15},{8,24},{9,1... | collective-permute-start | bytes 196616 | tf_op jit(solution)/shard_map/ppermute | solution.py:33
  33.0 5.2 %collective-permute-start.12 = (bf16[64,512]{1,0:T(8,128)(2,1)S(1)}, bf16[64,512]{1,0:T(8,128)(2,1)S(1)}, u32[]{:S(2)}, u32[]{:S(2)}) collective-permute-start(bf16[64,512]{1,0:T(8,128)(2,1)S(1)} %shard_map.78.refs_2_), channel_id=1, source_target_pairs={{0,16},{1,9},{2,18},{3,11},{4,20},{5,13},{6,22},{7,15},{8,24},{9,1... | collective-permute-start | bytes 196616 | tf_op jit(solution)/shard_map/ppermute | solution.py:33

commit v7 on v3

--- a/solution.py
+++ b/solution.py
@@ -212,9 +212,10 @@
     totals = [total, small_call(add_kernel, half, mine, received[1])]
     turns = n_lm.bit_length() - 1
     for k in range(turns - 1):
-        arrived = [lm_send(total, k, n_lm, n_sl) for total in totals]
+        arrived = [lm_send(total, k + h, n_lm, n_sl) for h, total in enumerate(totals)]
         totals = [small_call(add_kernel, half, a, b) for a, b in zip(totals, arrived)]
-    pairs = [(total, lm_send(total, turns - 1, n_lm, n_sl)) for total in totals]
+    last = [lm_send(total, turns - 1 + h, n_lm, n_sl) for h, total in enumerate(totals)]
+    pairs = list(zip(totals, last))
     scale = functools.partial(scale_kernel, total_land=total_land)
     out = jax.ShapeDtypeStruct((cols, rows), jnp.float32)
     return small_call(scale, out, *(x for pair in pairs for x in pair), ritz[:, None]).T

time: 38.9 us -> 39.4 us (1.013)
  starting transfers between devices: 15.6 us -> 16.7 us
  waiting for transfers between devices: 10.3 us -> 9.82 us
    ppermute x4, starting transfers between devices: 7.11 us -> 8.18 us  [lm_send(): return lax.ppermute(value, ('lm', 'sl'), perm)]
    ppermute x4, waiting for transfers between devices: 4.39 us -> 3.88 us  [lm_send(): return lax.ppermute(value, ('lm', 'sl'), perm)]
  transfers between devices with their start and end apart: 13 -> 13, of which waited for: 7 -> 8; matrix products, arithmetic and copies ran while one was open for 0% -> 0% of each run, Pallas kernels for 22% -> 22%
where the time goes in v7:
time: 39.4 us; the launch traced here: 39.2 us
  starting transfers between devices  16.7 us (42%)
  Pallas kernels  9.97 us (25%)
  waiting for transfers between devices  9.82 us (25%)
  local copies, waits for them, and re-layouts  2.67 us (7%)
    ppermute x4, starting transfers between devices, lm_send(): return lax.ppermute(value, ('lm', 'sl'), perm)  8.18 us
    ppermute x6, starting transfers between devices, chip_send(): lax.ppermute(value, 'sl', [(i, i ^ bits[(k + i % 2) % len(bits)]) for i i...  7.36 us
    pallas_call x7, Pallas kernels, stage(): pl.pallas_call(functools.partial(stage_kernel, count, coeff, ritz, accs i...  6.82 us
    ppermute x6, waiting for transfers between devices, chip_send(): lax.ppermute(value, 'sl', [(i, i ^ bits[(k + i % 2) % len(bits)]) for i i...  5.93 us
    ppermute x4, waiting for transfers between devices, lm_send(): return lax.ppermute(value, ('lm', 'sl'), perm)  3.88 us
    pallas_call x7, Pallas kernels, small_call(): pl.pallas_call(kernel, out_shape=jax.ShapeDtypeStruct(out.shape, out.dtyp...  2.13 us
    unnamed x4, local copies, waits for them, and re-layouts  1.59 us
    ppermute x3, starting transfers between devices, core_send(): return lax.ppermute(value, 'sl', [(i, i ^ 1) for i in range(n)])  1.16 us
  transfers between devices with their start and end apart: 13, of which 8 were waited for; matrix products, arithmetic and copies ran while one was open for 0% of the time, Pallas kernels for 22%

profile of v7, /device:TPU:0, one launch (start us, length us, event | category | flops | bytes accessed | tf_op | source)
XLA Modules:
  0.0 39.2 jit_solution(14370511161748896186)
XLA Ops:
  0.0 1.0 %slice.3.refs_2_ = bf16[144,1024]{1,0:T(8,128)(2,1)S(1)} slice(bf16[256,1024]{1,0:T(8,128)(2,1)} %land_ref.1), slice={[112:256], [0:1024]} | slice | bytes 589824 | tf_op jit(solution)/shard_map/slice | solution.py:170
  1.5 2.6 %collective-permute-start.3 = (bf16[144,1024]{1,0:T(8,128)(2,1)S(1)}, bf16[144,1024]{1,0:T(8,128)(2,1)S(1)}, u32[]{:S(2)}, u32[]{:S(2)}) collective-permute-start(bf16[144,1024]{1,0:T(8,128)(2,1)S(1)} %slice.3.refs_2_), channel_id=1, source_target_pairs={{0,4},{1,3},{2,6},{3,1},{4,0},{5,7},{6,2},{7,5},{8,12},{9,11},{10,... | collective-permute-start | bytes 884744 | tf_op jit(solution)/shard_map/ppermute | solution.py:23
  4.1 1.0 %shard_map.66.refs_1_ = bf16[128,1024]{1,0:T(8,128)(2,1)S(1)} custom-call(bf16[256,1024]{1,0:T(8,128)(2,1)} %land_ref.1, bf16[96,256]{1,0:T(8,128)(2,1)} %bitcast.4, s32[2]{0:T(128)} %exponents_ref.1, bf16[64,96]{1,0:T(8,128)(2,1)} %bitcast.5), custom_call_target="tpu_custom_call" | custom-call | tf_op jit(solution)/shard_map/pallas_call | solution.py:70
  5.1 1.6 %collective-permute-start.2 = (bf16[128,1024]{1,0:T(8,128)(2,1)S(1)}, bf16[128,1024]{1,0:T(8,128)(2,1)S(1)}, u32[]{:S(2)}, u32[]{:S(2)}) collective-permute-start(bf16[128,1024]{1,0:T(8,128)(2,1)S(1)} %shard_map.66.refs_1_), channel_id=1, source_target_pairs={{0,2},{1,5},{2,0},{3,7},{4,6},{5,1},{6,4},{7,3},{8,10},{9,13},{10,... | collective-permute-start | bytes 786440 | tf_op jit(solution)/shard_map/ppermute | solution.py:23
  7.3 1.6 %copy-done = bf16[1024,1024]{1,0:T(8,128)(2,1)S(1)} copy-done((bf16[1024,1024]{1,0:T(8,128)(2,1)S(1)}, bf16[1024,1024]{1,0:T(8,128)(2,1)}, u32[]{:S(2)}) %copy-start) | copy-done | bytes 2097176
  8.9 0.6 %shard_map.64.refs_0_.refs_1_ = bf16[1024,1024]{1,0:T(8,128)(2,1)S(1)} custom-call(bf16[1024,1024]{1,0:T(8,128)(2,1)S(1)} %copy-done), custom_call_target="tpu_custom_call" | custom-call | tf_op jit(solution)/shard_map/pallas_call | solution.py:155
  9.5 0.9 %shard_map.67.refs_4_ = f32[64,1024]{1,0:T(8,128)S(1)} custom-call(bf16[1024,1024]{1,0:T(8,128)(2,1)S(1)} %shard_map.64.refs_0_.refs_1_, bf16[128,1024]{1,0:T(8,128)(2,1)S(1)} %shard_map.66.refs_1_, bf16[144,1024]{1,0:T(8,128)(2,1)S(1)} %slice.3.refs_2_), custom_call_target="tpu_custom_call" | custom-call | flops 671088640 | bytes 2621440 | tf_op jit(solution)/shard_map/pallas_call | solution.py:126
  10.4 3.4 %collective-permute-done.2.refs_2_ = bf16[128,1024]{1,0:T(8,128)(2,1)S(1)} collective-permute-done((bf16[128,1024]{1,0:T(8,128)(2,1)S(1)}, bf16[128,1024]{1,0:T(8,128)(2,1)S(1)}, u32[]{:S(2)}, u32[]{:S(2)}) %collective-permute-start.2) | collective-permute-done | bytes 262176 | tf_op jit(solution)/shard_map/ppermute | solution.py:23
  13.8 0.6 %collective-permute-start.5 = (bf16[128,1024]{1,0:T(8,128)(2,1)S(1)}, bf16[128,1024]{1,0:T(8,128)(2,1)S(1)}, u32[]{:S(2)}, u32[]{:S(2)}) collective-permute-start(bf16[128,1024]{1,0:T(8,128)(2,1)S(1)} %collective-permute-done.2.refs_2_), channel_id=1, source_target_pairs={{0,4},{1,3},{2,6},{3,1},{4,0},{5,7},{6,2},{7,5},{8,12},{9,11},{10,... | collective-permute-start | bytes 786440 | tf_op jit(solution)/shard_map/ppermute | solution.py:23
  14.5 2.0 %collective-permute-start.6 = (bf16[144,1024]{1,0:T(8,128)(2,1)S(1)}, bf16[144,1024]{1,0:T(8,128)(2,1)S(1)}, u32[]{:S(2)}, u32[]{:S(2)}) collective-permute-start(bf16[144,1024]{1,0:T(8,128)(2,1)S(1)} %collective-permute-done.3.refs_3_), channel_id=1, source_target_pairs={{0,2},{1,5},{2,0},{3,7},{4,6},{5,1},{6,4},{7,3},{8,10},{9,13},{10,... | collective-permute-start | bytes 884744 | tf_op jit(solution)/shard_map/ppermute | solution.py:23
  16.4 0.6 %shard_map.65.refs_0_.refs_1_ = bf16[1024,1024]{1,0:T(8,128)(2,1)S(1)} custom-call(bf16[1024,1024]{1,0:T(8,128)(2,1)S(1)} %collective-permute-done.in_ref), custom_call_target="tpu_custom_call" | custom-call | tf_op jit(solution)/shard_map/pallas_call | solution.py:155
  17.1 0.9 %shard_map.68.refs_5_ = f32[64,1024]{1,0:T(8,128)S(1)} custom-call(bf16[1024,1024]{1,0:T(8,128)(2,1)S(1)} %shard_map.65.refs_0_.refs_1_, bf16[128,1024]{1,0:T(8,128)(2,1)S(1)} %shard_map.66.refs_1_, bf16[144,1024]{1,0:T(8,128)(2,1)S(1)} %slice.3.refs_2_), custom_call_target="tpu_custom_call" | custom-call | flops 671088640 | bytes 2621440 | tf_op jit(solution)/shard_map/pallas_call | solution.py:126
  17.9 1.7 %collective-permute-done.4.refs_3_ = bf16[144,1024]{1,0:T(8,128)(2,1)S(1)} collective-permute-done((bf16[144,1024]{1,0:T(8,128)(2,1)S(1)}, bf16[144,1024]{1,0:T(8,128)(2,1)S(1)}, u32[]{:S(2)}, u32[]{:S(2)}) %collective-permute-start.4) | collective-permute-done | bytes 294944 | tf_op jit(solution)/shard_map/ppermute | solution.py:23
  19.7 1.5 %shard_map.69 = (f32[64,1024]{1,0:T(8,128)S(1)}, f32[64,1024]{1,0:T(8,128)S(1)}) custom-call(bf16[1024,1024]{1,0:T(8,128)(2,1)S(1)} %shard_map.64.refs_0_.refs_1_, bf16[1024,1024]{1,0:T(8,128)(2,1)S(1)} %shard_map.65.refs_0_.refs_1_, bf16[128,1024]{1,0:T(8,128)(2,1)S(1)} %collective-permute-done.2.refs_2_, ...), custom_call_target="tpu_custom_call" | custom-call | flops 1342177280 | bytes 4718592 | tf_op jit(solution)/shard_map/pallas_call | solution.py:126
  21.2 1.5 %shard_map.70 = (f32[64,1024]{1,0:T(8,128)S(1)}, f32[64,1024]{1,0:T(8,128)S(1)}) custom-call(bf16[1024,1024]{1,0:T(8,128)(2,1)S(1)} %shard_map.64.refs_0_.refs_1_, bf16[1024,1024]{1,0:T(8,128)(2,1)S(1)} %shard_map.65.refs_0_.refs_1_, bf16[128,1024]{1,0:T(8,128)(2,1)S(1)} %collective-permute-done.1.refs_2_, ...), custom_call_target="tpu_custom_call" | custom-call | flops 1342177280 | bytes 4718592 | tf_op jit(solution)/shard_map/pallas_call | solution.py:126
  24.3 0.9 %shard_map.71 = (f32[64,512]{1,0:T(8,128)S(1)}, f32[64,512]{1,0:T(8,128)S(1)}) custom-call(bf16[1024,1024]{1,0:T(8,128)(2,1)S(1)} %shard_map.65.refs_0_.refs_1_, bf16[1024,1024]{1,0:T(8,128)(2,1)S(1)} %shard_map.64.refs_0_.refs_1_, bf16[128,1024]{1,0:T(8,128)(2,1)S(1)} %collective-permute-done.5.refs_2_.refs_1_, ...), custom_call_target="tpu_custom_call" | custom-call | flops 671088640 | bytes 2621440 | tf_op jit(solution)/shard_map/pallas_call | solution.py:126
  25.6 1.6 %collective-permute-start.8 = (bf16[64,512]{1,0:T(8,128)(2,1)S(1)}, bf16[64,512]{1,0:T(8,128)(2,1)S(1)}, u32[]{:S(2)}, u32[]{:S(2)}) collective-permute-start(bf16[64,512]{1,0:T(8,128)(2,1)S(1)} %shard_map.73.a_ref), channel_id=1, source_target_pairs={{0,8},{1,17},{2,10},{3,19},{4,12},{5,21},{6,14},{7,23},{8,0},{9,25... | collective-permute-start | bytes 196616 | tf_op jit(solution)/shard_map/ppermute | solution.py:33
  27.9 2.7 %collective-permute-start.11 = (bf16[64,512]{1,0:T(8,128)(2,1)S(1)}, bf16[64,512]{1,0:T(8,128)(2,1)S(1)}, u32[]{:S(2)}, u32[]{:S(2)}) collective-permute-start(bf16[64,512]{1,0:T(8,128)(2,1)S(1)} %shard_map.76.a_ref), channel_id=1, source_target_pairs={{0,16},{1,9},{2,18},{3,11},{4,20},{5,13},{6,22},{7,15},{8,24},{9,1... | collective-permute-start | bytes 196616 | tf_op jit(solution)/shard_map/ppermute | solution.py:33
  30.7 2.4 %collective-permute-start.9 = (bf16[64,512]{1,0:T(8,128)(2,1)S(1)}, bf16[64,512]{1,0:T(8,128)(2,1)S(1)}, u32[]{:S(2)}, u32[]{:S(2)}) collective-permute-start(bf16[64,512]{1,0:T(8,128)(2,1)S(1)} %shard_map.74.refs_0_), channel_id=1, source_target_pairs={{0,16},{1,9},{2,18},{3,11},{4,20},{5,13},{6,22},{7,15},{8,24},{9,1... | collective-permute-start | bytes 196616 | tf_op jit(solution)/shard_map/ppermute | solution.py:33
  33.0 0.8 %collective-permute-done.11.b_ref = bf16[64,512]{1,0:T(8,128)(2,1)S(1)} collective-permute-done((bf16[64,512]{1,0:T(8,128)(2,1)S(1)}, bf16[64,512]{1,0:T(8,128)(2,1)S(1)}, u32[]{:S(2)}, u32[]{:S(2)}) %collective-permute-start.11) | collective-permute-done | bytes 65568 | tf_op jit(solution)/shard_map/ppermute | solution.py:33
  33.9 1.5 %collective-permute-start.12 = (bf16[64,512]{1,0:T(8,128)(2,1)S(1)}, bf16[64,512]{1,0:T(8,128)(2,1)S(1)}, u32[]{:S(2)}, u32[]{:S(2)}) collective-permute-start(bf16[64,512]{1,0:T(8,128)(2,1)S(1)} %shard_map.77.refs_2_), channel_id=1, source_target_pairs={{0,8},{1,17},{2,10},{3,19},{4,12},{5,21},{6,14},{7,23},{8,0},{9,25... | collective-permute-start | bytes 196616 | tf_op jit(solution)/shard_map/ppermute | solution.py:33
  35.5 0.7 %collective-permute-done.9.refs_1_ = bf16[64,512]{1,0:T(8,128)(2,1)S(1)} collective-permute-done((bf16[64,512]{1,0:T(8,128)(2,1)S(1)}, bf16[64,512]{1,0:T(8,128)(2,1)S(1)}, u32[]{:S(2)}, u32[]{:S(2)}) %collective-permute-start.9) | collective-permute-done | bytes 65568 | tf_op jit(solution)/shard_map/ppermute | solution.py:33
  36.1 2.3 %collective-permute-done.12.refs_3_ = bf16[64,512]{1,0:T(8,128)(2,1)S(1)} collective-permute-done((bf16[64,512]{1,0:T(8,128)(2,1)S(1)}, bf16[64,512]{1,0:T(8,128)(2,1)S(1)}, u32[]{:S(2)}, u32[]{:S(2)}) %collective-permute-start.12) | collective-permute-done | bytes 65568 | tf_op jit(solution)/shard_map/ppermute | solution.py:33
  38.4 0.8 %shard_map.78 = f32[64,1024]{1,0:T(8,128)} custom-call(bf16[64,512]{1,0:T(8,128)(2,1)S(1)} %shard_map.74.refs_0_, bf16[64,512]{1,0:T(8,128)(2,1)S(1)} %collective-permute-done.9.refs_1_, bf16[64,512]{1,0:T(8,128)(2,1)S(1)} %shard_map.77.refs_2_, bf16[64,512]{1,0:T(8,128)(2,1)S(1)} %collective-permute-done.12.refs_3_, f32[64,1]{1,0:T(8,128)S(1)} %copy.7.refs_4_), custom_call_target="tpu_custom_call" | custom-call | tf_op jit(solution)/shard_map/pallas_call | solution.py:155
  (23 shorter events, 4.0 us)
Async XLA Ops:
  1.0 15.5 %collective-permute-start = (bf16[1024,1024]{1,0:T(8,128)(2,1)}, bf16[1024,1024]{1,0:T(8,128)(2,1)S(1)}, u32[]{:S(2)}, u32[]{:S(2)}) collective-permute-start(bf16[1024,1024]{1,0:T(8,128)(2,1)} %in_ref.1), channel_id=1, source_target_pairs={{0,1},{1,0},{2,3},{3,2},{4,5},{5,4},{6,7},{7,6},{8,9},{9,8},{10,11... | collective-permute-start | bytes 6291464 | tf_op jit(solution)/shard_map/ppermute | solution.py:18
  1.5 12.3 %collective-permute-start.3 = (bf16[144,1024]{1,0:T(8,128)(2,1)S(1)}, bf16[144,1024]{1,0:T(8,128)(2,1)S(1)}, u32[]{:S(2)}, u32[]{:S(2)}) collective-permute-start(bf16[144,1024]{1,0:T(8,128)(2,1)S(1)} %slice.3.refs_2_), channel_id=1, source_target_pairs={{0,4},{1,3},{2,6},{3,1},{4,0},{5,7},{6,2},{7,5},{8,12},{9,11},{10,... | collective-permute-start | bytes 884744 | tf_op jit(solution)/shard_map/ppermute | solution.py:23
  5.1 8.7 %collective-permute-start.2 = (bf16[128,1024]{1,0:T(8,128)(2,1)S(1)}, bf16[128,1024]{1,0:T(8,128)(2,1)S(1)}, u32[]{:S(2)}, u32[]{:S(2)}) collective-permute-start(bf16[128,1024]{1,0:T(8,128)(2,1)S(1)} %shard_map.66.refs_1_), channel_id=1, source_target_pairs={{0,2},{1,5},{2,0},{3,7},{4,6},{5,1},{6,4},{7,3},{8,10},{9,13},{10,... | collective-permute-start | bytes 786440 | tf_op jit(solution)/shard_map/ppermute | solution.py:23
  6.7 13.0 %collective-permute-start.4 = (bf16[144,1024]{1,0:T(8,128)(2,1)S(1)}, bf16[144,1024]{1,0:T(8,128)(2,1)S(1)}, u32[]{:S(2)}, u32[]{:S(2)}) collective-permute-start(bf16[144,1024]{1,0:T(8,128)(2,1)S(1)} %slice.3.refs_2_), channel_id=1, source_target_pairs={{0,2},{1,5},{2,0},{3,7},{4,6},{5,1},{6,4},{7,3},{8,10},{9,13},{10,... | collective-permute-start | bytes 884744 | tf_op jit(solution)/shard_map/ppermute | solution.py:23
  7.2 14.0 %collective-permute-start.1 = (bf16[128,1024]{1,0:T(8,128)(2,1)S(1)}, bf16[128,1024]{1,0:T(8,128)(2,1)S(1)}, u32[]{:S(2)}, u32[]{:S(2)}) collective-permute-start(bf16[128,1024]{1,0:T(8,128)(2,1)S(1)} %shard_map.66.refs_1_), channel_id=1, source_target_pairs={{0,4},{1,3},{2,6},{3,1},{4,0},{5,7},{6,2},{7,5},{8,12},{9,11},{10,... | collective-permute-start | bytes 786440 | tf_op jit(solution)/shard_map/ppermute | solution.py:23
  7.3 1.6 %copy-start = (bf16[1024,1024]{1,0:T(8,128)(2,1)S(1)}, bf16[1024,1024]{1,0:T(8,128)(2,1)}, u32[]{:S(2)}) copy-start(bf16[1024,1024]{1,0:T(8,128)(2,1)} %in_ref.1) | copy-start | bytes 6291460
  13.8 9.2 %collective-permute-start.5 = (bf16[128,1024]{1,0:T(8,128)(2,1)S(1)}, bf16[128,1024]{1,0:T(8,128)(2,1)S(1)}, u32[]{:S(2)}, u32[]{:S(2)}) collective-permute-start(bf16[128,1024]{1,0:T(8,128)(2,1)S(1)} %collective-permute-done.2.refs_2_), channel_id=1, source_target_pairs={{0,4},{1,3},{2,6},{3,1},{4,0},{5,7},{6,2},{7,5},{8,12},{9,11},{10,... | collective-permute-start | bytes 786440 | tf_op jit(solution)/shard_map/ppermute | solution.py:23
  14.5 9.0 %collective-permute-start.6 = (bf16[144,1024]{1,0:T(8,128)(2,1)S(1)}, bf16[144,1024]{1,0:T(8,128)(2,1)S(1)}, u32[]{:S(2)}, u32[]{:S(2)}) collective-permute-start(bf16[144,1024]{1,0:T(8,128)(2,1)S(1)} %collective-permute-done.3.refs_3_), channel_id=1, source_target_pairs={{0,2},{1,5},{2,0},{3,7},{4,6},{5,1},{6,4},{7,3},{8,10},{9,13},{10,... | collective-permute-start | bytes 884744 | tf_op jit(solution)/shard_map/ppermute | solution.py:23
  24.1 1.5 %collective-permute-start.7 = (f32[64,512]{1,0:T(8,128)S(1)}, f32[64,512]{1,0:T(8,128)S(1)}, u32[]{:S(2)}, u32[]{:S(2)}) collective-permute-start(f32[64,512]{1,0:T(8,128)S(1)} %shard_map.72), channel_id=1, source_target_pairs={{0,1},{1,0},{2,3},{3,2},{4,5},{5,4},{6,7},{7,6},{8,9},{9,8},{10,11... | collective-permute-start | bytes 393224 | tf_op jit(solution)/shard_map/ppermute | solution.py:18
  25.1 10.2 %copy-start.1 = (f32[64]{0:T(128)S(1)}, f32[64]{0:T(128)}, u32[]{:S(2)}) copy-start(f32[64]{0:T(128)} %param.11) | copy-start | bytes 772
  25.1 2.7 %collective-permute-start.10 = (f32[64,512]{1,0:T(8,128)S(1)}, f32[64,512]{1,0:T(8,128)S(1)}, u32[]{:S(2)}, u32[]{:S(2)}) collective-permute-start(f32[64,512]{1,0:T(8,128)S(1)} %get-tuple-element.28), channel_id=1, source_target_pairs={{0,1},{1,0},{2,3},{3,2},{4,5},{5,4},{6,7},{7,6},{8,9},{9,8},{10,11... | collective-permute-start | bytes 393224 | tf_op jit(solution)/shard_map/ppermute | solution.py:18
  25.6 5.0 %collective-permute-start.8 = (bf16[64,512]{1,0:T(8,128)(2,1)S(1)}, bf16[64,512]{1,0:T(8,128)(2,1)S(1)}, u32[]{:S(2)}, u32[]{:S(2)}) collective-permute-start(bf16[64,512]{1,0:T(8,128)(2,1)S(1)} %shard_map.73.a_ref), channel_id=1, source_target_pairs={{0,8},{1,17},{2,10},{3,19},{4,12},{5,21},{6,14},{7,23},{8,0},{9,25... | collective-permute-start | bytes 196616 | tf_op jit(solution)/shard_map/ppermute | solution.py:33
  27.9 6.0 %collective-permute-start.11 = (bf16[64,512]{1,0:T(8,128)(2,1)S(1)}, bf16[64,512]{1,0:T(8,128)(2,1)S(1)}, u32[]{:S(2)}, u32[]{:S(2)}) collective-permute-start(bf16[64,512]{1,0:T(8,128)(2,1)S(1)} %shard_map.76.a_ref), channel_id=1, source_target_pairs={{0,16},{1,9},{2,18},{3,11},{4,20},{5,13},{6,22},{7,15},{8,24},{9,1... | collective-permute-start | bytes 196616 | tf_op jit(solution)/shard_map/ppermute | solution.py:33
  30.7 5.5 %collective-permute-start.9 = (bf16[64,512]{1,0:T(8,128)(2,1)S(1)}, bf16[64,512]{1,0:T(8,128)(2,1)S(1)}, u32[]{:S(2)}, u32[]{:S(2)}) collective-permute-start(bf16[64,512]{1,0:T(8,128)(2,1)S(1)} %shard_map.74.refs_0_), channel_id=1, source_target_pairs={{0,16},{1,9},{2,18},{3,11},{4,20},{5,13},{6,22},{7,15},{8,24},{9,1... | collective-permute-start | bytes 196616 | tf_op jit(solution)/shard_map/ppermute | solution.py:33
  33.9 4.6 %collective-permute-start.12 = (bf16[64,512]{1,0:T(8,128)(2,1)S(1)}, bf16[64,512]{1,0:T(8,128)(2,1)S(1)}, u32[]{:S(2)}, u32[]{:S(2)}) collective-permute-start(bf16[64,512]{1,0:T(8,128)(2,1)S(1)} %shard_map.77.refs_2_), channel_id=1, source_target_pairs={{0,8},{1,17},{2,10},{3,19},{4,12},{5,21},{6,14},{7,23},{8,0},{9,25... | collective-permute-start | bytes 196616 | tf_op jit(solution)/shard_map/ppermute | solution.py:33

commit v8 on v1

--- a/solution.py
+++ b/solution.py
@@ -221,12 +221,11 @@
     half = jax.ShapeDtypeStruct((cols, width), jnp.bfloat16)
     (early,) = stage([other], *end, accs[1:], coeff, cols, spans[:1])
     received = [core_send(early, n_sl)]
-    late, mine = stage([other, slab], *end, accs[::-1], coeff, cols, spans[::-1])
+    late, *mine = stage(
+        [other, slab, slab], *end, [accs[1], accs[0], accs[0]], coeff, cols, [spans[1], *spans]
+    )
     received.append(core_send(late, n_sl))
-    total = small_call(add_kernel, half, mine, received[0])
-    acc, total = lax.optimization_barrier((accs[0], total))
-    (mine,) = stage([slab], *end, [acc], coeff, cols, spans[1:])
-    totals = [total, small_call(add_kernel, half, mine, received[1])]
+    totals = [small_call(add_kernel, half, a, b) for a, b in zip(mine, received)]
     turns = n_lm.bit_length() - 1
     for k in range(turns - 1):
         arrived = [lm_send(total, k, n_lm, n_sl) for total in totals]

time: 38.9 us -> 39.2 us (level)
  waiting for transfers between devices: 10.3 us -> 10.9 us
    ppermute x4, waiting for transfers between devices: 4.4 us -> 4.99 us  [lm_send(): return lax.ppermute(value, ('lm', 'sl'), perm)]
    pallas_call x7 -> x6, Pallas kernels: 6.83 us -> 6.58 us  [stage(): pl.pallas_call(functools.partial(stage_kernel, count, coeff, ritz, accs i...]
  transfers between devices with their start and end apart: 13 -> 13, of which waited for: 7 -> 7; matrix products, arithmetic and copies ran while one was open for 0% -> 0% of each run, Pallas kernels for 22% -> 21%
where the time goes in v8:
time: 39.2 us; the launch traced here: 39 us
  starting transfers between devices  15.6 us (40%)
  waiting for transfers between devices  10.9 us (28%)
  Pallas kernels  10.7 us (27%)
  local copies, waits for them, and re-layouts  1.69 us (4%)
    ppermute x6, starting transfers between devices, chip_send(): lax.ppermute(value, 'sl', [(i, i ^ bits[(k + i % 2) % len(bits)]) for i i...  7.36 us
    ppermute x4, starting transfers between devices, lm_send(): return lax.ppermute(value, ('lm', 'sl'), perm)  7.11 us
    pallas_call x6, Pallas kernels, stage(): pl.pallas_call(functools.partial(stage_kernel, count, coeff, ritz, accs i...  6.58 us
    ppermute x6, waiting for transfers between devices, chip_send(): lax.ppermute(value, 'sl', [(i, i ^ bits[(k + i % 2) % len(bits)]) for i i...  5.92 us
    ppermute x4, waiting for transfers between devices, lm_send(): return lax.ppermute(value, ('lm', 'sl'), perm)  4.99 us
    pallas_call x7, Pallas kernels, small_call(): pl.pallas_call(kernel, out_shape=jax.ShapeDtypeStruct(out.shape, out.dtyp...  2.13 us
    unnamed x4, local copies, waits for them, and re-layouts  1.59 us
    ppermute x3, starting transfers between devices, core_send(): return lax.ppermute(value, 'sl', [(i, i ^ 1) for i in range(n)])  1.15 us
  transfers between devices with their start and end apart: 13, of which 7 were waited for; matrix products, arithmetic and copies ran while one was open for 0% of the time, Pallas kernels for 21%

profile of v8, /device:TPU:0, one launch (start us, length us, event | category | flops | bytes accessed | tf_op | source)
XLA Modules:
  0.0 39.0 jit_solution(5305379178775195958)
XLA Ops:
  0.0 1.0 %shard_map.64.refs_2_ = bf16[144,1024]{1,0:T(8,128)(2,1)S(1)} custom-call(bf16[256,1024]{1,0:T(8,128)(2,1)} %land_ref.3), custom_call_target="tpu_custom_call" | custom-call | tf_op jit(solution)/shard_map/pallas_call | solution.py:75
  1.5 2.6 %collective-permute-start.2 = (bf16[144,1024]{1,0:T(8,128)(2,1)S(1)}, bf16[144,1024]{1,0:T(8,128)(2,1)S(1)}, u32[]{:S(2)}, u32[]{:S(2)}) collective-permute-start(bf16[144,1024]{1,0:T(8,128)(2,1)S(1)} %shard_map.64.refs_2_), channel_id=1, source_target_pairs={{0,4},{1,3},{2,6},{3,1},{4,0},{5,7},{6,2},{7,5},{8,12},{9,11},{10,... | collective-permute-start | bytes 884744 | tf_op jit(solution)/shard_map/ppermute | solution.py:23
  4.1 1.0 %shard_map.67.refs_1_ = bf16[128,1024]{1,0:T(8,128)(2,1)S(1)} custom-call(bf16[256,1024]{1,0:T(8,128)(2,1)} %land_ref.3, bf16[96,256]{1,0:T(8,128)(2,1)} %bitcast.4, s32[2]{0:T(128)} %exponents_ref.1, bf16[64,96]{1,0:T(8,128)(2,1)} %bitcast.5), custom_call_target="tpu_custom_call" | custom-call | tf_op jit(solution)/shard_map/pallas_call | solution.py:87
  5.1 1.6 %collective-permute-start.1 = (bf16[128,1024]{1,0:T(8,128)(2,1)S(1)}, bf16[128,1024]{1,0:T(8,128)(2,1)S(1)}, u32[]{:S(2)}, u32[]{:S(2)}) collective-permute-start(bf16[128,1024]{1,0:T(8,128)(2,1)S(1)} %shard_map.67.refs_1_), channel_id=1, source_target_pairs={{0,2},{1,5},{2,0},{3,7},{4,6},{5,1},{6,4},{7,3},{8,10},{9,13},{10,... | collective-permute-start | bytes 786440 | tf_op jit(solution)/shard_map/ppermute | solution.py:23
  7.3 1.6 %copy-done = bf16[1024,1024]{1,0:T(8,128)(2,1)S(1)} copy-done((bf16[1024,1024]{1,0:T(8,128)(2,1)S(1)}, bf16[1024,1024]{1,0:T(8,128)(2,1)}, u32[]{:S(2)}) %copy-start) | copy-done | bytes 2097176
  8.9 0.6 %shard_map.66.refs_0_.refs_1_.refs_2_ = bf16[1024,1024]{1,0:T(8,128)(2,1)S(1)} custom-call(bf16[1024,1024]{1,0:T(8,128)(2,1)S(1)} %copy-done), custom_call_target="tpu_custom_call" | custom-call | tf_op jit(solution)/shard_map/pallas_call | solution.py:172
  9.5 0.9 %shard_map.68.refs_4_ = f32[64,1024]{1,0:T(8,128)S(1)} custom-call(bf16[1024,1024]{1,0:T(8,128)(2,1)S(1)} %shard_map.66.refs_0_.refs_1_.refs_2_, bf16[128,1024]{1,0:T(8,128)(2,1)S(1)} %shard_map.67.refs_1_, bf16[144,1024]{1,0:T(8,128)(2,1)S(1)} %shard_map.64.refs_2_), custom_call_target="tpu_custom_call" | custom-call | flops 671088640 | bytes 2621440 | tf_op jit(solution)/shard_map/pallas_call | solution.py:143
  10.4 3.4 %collective-permute-done.1.refs_2_ = bf16[128,1024]{1,0:T(8,128)(2,1)S(1)} collective-permute-done((bf16[128,1024]{1,0:T(8,128)(2,1)S(1)}, bf16[128,1024]{1,0:T(8,128)(2,1)S(1)}, u32[]{:S(2)}, u32[]{:S(2)}) %collective-permute-start.1) | collective-permute-done | bytes 262176 | tf_op jit(solution)/shard_map/ppermute | solution.py:23
  13.8 0.6 %collective-permute-start.3 = (bf16[128,1024]{1,0:T(8,128)(2,1)S(1)}, bf16[128,1024]{1,0:T(8,128)(2,1)S(1)}, u32[]{:S(2)}, u32[]{:S(2)}) collective-permute-start(bf16[128,1024]{1,0:T(8,128)(2,1)S(1)} %collective-permute-done.1.refs_2_), channel_id=1, source_target_pairs={{0,4},{1,3},{2,6},{3,1},{4,0},{5,7},{6,2},{7,5},{8,12},{9,11},{10,... | collective-permute-start | bytes 786440 | tf_op jit(solution)/shard_map/ppermute | solution.py:23
  14.4 2.0 %collective-permute-start.4 = (bf16[144,1024]{1,0:T(8,128)(2,1)S(1)}, bf16[144,1024]{1,0:T(8,128)(2,1)S(1)}, u32[]{:S(2)}, u32[]{:S(2)}) collective-permute-start(bf16[144,1024]{1,0:T(8,128)(2,1)S(1)} %collective-permute-done.2.refs_3_), channel_id=1, source_target_pairs={{0,2},{1,5},{2,0},{3,7},{4,6},{5,1},{6,4},{7,3},{8,10},{9,13},{10,... | collective-permute-start | bytes 884744 | tf_op jit(solution)/shard_map/ppermute | solution.py:23
  16.4 0.6 %shard_map.65.refs_0_.refs_1_ = bf16[1024,1024]{1,0:T(8,128)(2,1)S(1)} custom-call(bf16[1024,1024]{1,0:T(8,128)(2,1)S(1)} %collective-permute-done.in_ref), custom_call_target="tpu_custom_call" | custom-call | tf_op jit(solution)/shard_map/pallas_call | solution.py:172
  17.1 0.9 %shard_map.69.refs_5_ = f32[64,1024]{1,0:T(8,128)S(1)} custom-call(bf16[1024,1024]{1,0:T(8,128)(2,1)S(1)} %shard_map.65.refs_0_.refs_1_, bf16[128,1024]{1,0:T(8,128)(2,1)S(1)} %shard_map.67.refs_1_, bf16[144,1024]{1,0:T(8,128)(2,1)S(1)} %shard_map.64.refs_2_), custom_call_target="tpu_custom_call" | custom-call | flops 671088640 | bytes 2621440 | tf_op jit(solution)/shard_map/pallas_call | solution.py:143
  17.9 1.7 %collective-permute-done.6.refs_3_ = bf16[144,1024]{1,0:T(8,128)(2,1)S(1)} collective-permute-done((bf16[144,1024]{1,0:T(8,128)(2,1)S(1)}, bf16[144,1024]{1,0:T(8,128)(2,1)S(1)}, u32[]{:S(2)}, u32[]{:S(2)}) %collective-permute-start.6) | collective-permute-done | bytes 294944 | tf_op jit(solution)/shard_map/ppermute | solution.py:23
  19.6 1.5 %shard_map.70 = (f32[64,1024]{1,0:T(8,128)S(1)}, f32[64,1024]{1,0:T(8,128)S(1)}) custom-call(bf16[1024,1024]{1,0:T(8,128)(2,1)S(1)} %shard_map.66.refs_0_.refs_1_.refs_2_, bf16[1024,1024]{1,0:T(8,128)(2,1)S(1)} %shard_map.65.refs_0_.refs_1_, bf16[128,1024]{1,0:T(8,128)(2,1)S(1)} %collective-permute-done.1.refs_2_, ...), custom_call_target="tpu_custom_call" | custom-call | flops 1342177280 | bytes 4718592 | tf_op jit(solution)/shard_map/pallas_call | solution.py:143
  21.2 1.5 %shard_map.71 = (f32[64,1024]{1,0:T(8,128)S(1)}, f32[64,1024]{1,0:T(8,128)S(1)}) custom-call(bf16[1024,1024]{1,0:T(8,128)(2,1)S(1)} %shard_map.66.refs_0_.refs_1_.refs_2_, bf16[1024,1024]{1,0:T(8,128)(2,1)S(1)} %shard_map.65.refs_0_.refs_1_, bf16[128,1024]{1,0:T(8,128)(2,1)S(1)} %collective-permute-done.5.refs_2_, ...), custom_call_target="tpu_custom_call" | custom-call | flops 1342177280 | bytes 4718592 | tf_op jit(solution)/shard_map/pallas_call | solution.py:143
  24.3 1.2 %shard_map.72 = (f32[64,512]{1,0:T(8,128)S(1)}, f32[64,512]{1,0:T(8,128)S(1)}, f32[64,512]{1,0:T(8,128)S(1)}) custom-call(bf16[1024,1024]{1,0:T(8,128)(2,1)S(1)} %shard_map.65.refs_0_.refs_1_, bf16[1024,1024]{1,0:T(8,128)(2,1)S(1)} %shard_map.66.refs_0_.refs_1_.refs_2_, bf16[1024,1024]{1,0:T(8,128)(2,1)S(1)} %shard_map.66.refs_0_.refs_1_.refs_2_, ...), custom_call_target="tpu_custom_call" | custom-call | flops 1006632960 | bytes 3670016 | tf_op jit(solution)/shard_map/pallas_call | solution.py:143
  25.9 1.6 %collective-permute-start.8 = (bf16[64,512]{1,0:T(8,128)(2,1)S(1)}, bf16[64,512]{1,0:T(8,128)(2,1)S(1)}, u32[]{:S(2)}, u32[]{:S(2)}) collective-permute-start(bf16[64,512]{1,0:T(8,128)(2,1)S(1)} %shard_map.74.a_ref), channel_id=1, source_target_pairs={{0,8},{1,17},{2,10},{3,19},{4,12},{5,21},{6,14},{7,23},{8,0},{9,25... | collective-permute-start | bytes 196616 | tf_op jit(solution)/shard_map/ppermute | solution.py:33
  27.6 1.2 %collective-permute-start.11 = (bf16[64,512]{1,0:T(8,128)(2,1)S(1)}, bf16[64,512]{1,0:T(8,128)(2,1)S(1)}, u32[]{:S(2)}, u32[]{:S(2)}) collective-permute-start(bf16[64,512]{1,0:T(8,128)(2,1)S(1)} %shard_map.76.a_ref), channel_id=1, source_target_pairs={{0,8},{1,17},{2,10},{3,19},{4,12},{5,21},{6,14},{7,23},{8,0},{9,25... | collective-permute-start | bytes 196616 | tf_op jit(solution)/shard_map/ppermute | solution.py:33
  28.8 2.2 %collective-permute-done.8.b_ref = bf16[64,512]{1,0:T(8,128)(2,1)S(1)} collective-permute-done((bf16[64,512]{1,0:T(8,128)(2,1)S(1)}, bf16[64,512]{1,0:T(8,128)(2,1)S(1)}, u32[]{:S(2)}, u32[]{:S(2)}) %collective-permute-start.8) | collective-permute-done | bytes 65568 | tf_op jit(solution)/shard_map/ppermute | solution.py:33
  31.0 2.0 %collective-permute-start.9 = (bf16[64,512]{1,0:T(8,128)(2,1)S(1)}, bf16[64,512]{1,0:T(8,128)(2,1)S(1)}, u32[]{:S(2)}, u32[]{:S(2)}) collective-permute-start(bf16[64,512]{1,0:T(8,128)(2,1)S(1)} %shard_map.75.refs_0_), channel_id=1, source_target_pairs={{0,16},{1,9},{2,18},{3,11},{4,20},{5,13},{6,22},{7,15},{8,24},{9,1... | collective-permute-start | bytes 196616 | tf_op jit(solution)/shard_map/ppermute | solution.py:33
  33.0 2.3 %collective-permute-start.12 = (bf16[64,512]{1,0:T(8,128)(2,1)S(1)}, bf16[64,512]{1,0:T(8,128)(2,1)S(1)}, u32[]{:S(2)}, u32[]{:S(2)}) collective-permute-start(bf16[64,512]{1,0:T(8,128)(2,1)S(1)} %shard_map.77.refs_2_), channel_id=1, source_target_pairs={{0,16},{1,9},{2,18},{3,11},{4,20},{5,13},{6,22},{7,15},{8,24},{9,1... | collective-permute-start | bytes 196616 | tf_op jit(solution)/shard_map/ppermute | solution.py:33
  35.4 0.8 %collective-permute-done.9.refs_1_ = bf16[64,512]{1,0:T(8,128)(2,1)S(1)} collective-permute-done((bf16[64,512]{1,0:T(8,128)(2,1)S(1)}, bf16[64,512]{1,0:T(8,128)(2,1)S(1)}, u32[]{:S(2)}, u32[]{:S(2)}) %collective-permute-start.9) | collective-permute-done | bytes 65568 | tf_op jit(solution)/shard_map/ppermute | solution.py:33
  36.2 2.0 %collective-permute-done.12.refs_3_ = bf16[64,512]{1,0:T(8,128)(2,1)S(1)} collective-permute-done((bf16[64,512]{1,0:T(8,128)(2,1)S(1)}, bf16[64,512]{1,0:T(8,128)(2,1)S(1)}, u32[]{:S(2)}, u32[]{:S(2)}) %collective-permute-start.12) | collective-permute-done | bytes 65568 | tf_op jit(solution)/shard_map/ppermute | solution.py:33
  38.2 0.8 %shard_map.78 = f32[64,1024]{1,0:T(8,128)} custom-call(bf16[64,512]{1,0:T(8,128)(2,1)S(1)} %shard_map.75.refs_0_, bf16[64,512]{1,0:T(8,128)(2,1)S(1)} %collective-permute-done.9.refs_1_, bf16[64,512]{1,0:T(8,128)(2,1)S(1)} %shard_map.77.refs_2_, bf16[64,512]{1,0:T(8,128)(2,1)S(1)} %collective-permute-done.12.refs_3_, f32[64,1]{1,0:T(8,128)S(1)} %copy.7.refs_4_), custom_call_target="tpu_custom_call" | custom-call | tf_op jit(solution)/shard_map/pallas_call | solution.py:172
  (22 shorter events, 3.3 us)
Async XLA Ops:
  1.0 15.5 %collective-permute-start = (bf16[1024,1024]{1,0:T(8,128)(2,1)}, bf16[1024,1024]{1,0:T(8,128)(2,1)S(1)}, u32[]{:S(2)}, u32[]{:S(2)}) collective-permute-start(bf16[1024,1024]{1,0:T(8,128)(2,1)} %in_ref.1), channel_id=1, source_target_pairs={{0,1},{1,0},{2,3},{3,2},{4,5},{5,4},{6,7},{7,6},{8,9},{9,8},{10,11... | collective-permute-start | bytes 6291464 | tf_op jit(solution)/shard_map/ppermute | solution.py:18
  1.5 12.3 %collective-permute-start.2 = (bf16[144,1024]{1,0:T(8,128)(2,1)S(1)}, bf16[144,1024]{1,0:T(8,128)(2,1)S(1)}, u32[]{:S(2)}, u32[]{:S(2)}) collective-permute-start(bf16[144,1024]{1,0:T(8,128)(2,1)S(1)} %shard_map.64.refs_2_), channel_id=1, source_target_pairs={{0,4},{1,3},{2,6},{3,1},{4,0},{5,7},{6,2},{7,5},{8,12},{9,11},{10,... | collective-permute-start | bytes 884744 | tf_op jit(solution)/shard_map/ppermute | solution.py:23
  5.1 8.7 %collective-permute-start.1 = (bf16[128,1024]{1,0:T(8,128)(2,1)S(1)}, bf16[128,1024]{1,0:T(8,128)(2,1)S(1)}, u32[]{:S(2)}, u32[]{:S(2)}) collective-permute-start(bf16[128,1024]{1,0:T(8,128)(2,1)S(1)} %shard_map.67.refs_1_), channel_id=1, source_target_pairs={{0,2},{1,5},{2,0},{3,7},{4,6},{5,1},{6,4},{7,3},{8,10},{9,13},{10,... | collective-permute-start | bytes 786440 | tf_op jit(solution)/shard_map/ppermute | solution.py:23
  6.7 13.0 %collective-permute-start.6 = (bf16[144,1024]{1,0:T(8,128)(2,1)S(1)}, bf16[144,1024]{1,0:T(8,128)(2,1)S(1)}, u32[]{:S(2)}, u32[]{:S(2)}) collective-permute-start(bf16[144,1024]{1,0:T(8,128)(2,1)S(1)} %shard_map.64.refs_2_), channel_id=1, source_target_pairs={{0,2},{1,5},{2,0},{3,7},{4,6},{5,1},{6,4},{7,3},{8,10},{9,13},{10,... | collective-permute-start | bytes 884744 | tf_op jit(solution)/shard_map/ppermute | solution.py:23
  7.2 14.0 %collective-permute-start.5 = (bf16[128,1024]{1,0:T(8,128)(2,1)S(1)}, bf16[128,1024]{1,0:T(8,128)(2,1)S(1)}, u32[]{:S(2)}, u32[]{:S(2)}) collective-permute-start(bf16[128,1024]{1,0:T(8,128)(2,1)S(1)} %shard_map.67.refs_1_), channel_id=1, source_target_pairs={{0,4},{1,3},{2,6},{3,1},{4,0},{5,7},{6,2},{7,5},{8,12},{9,11},{10,... | collective-permute-start | bytes 786440 | tf_op jit(solution)/shard_map/ppermute | solution.py:23
  7.3 1.6 %copy-start = (bf16[1024,1024]{1,0:T(8,128)(2,1)S(1)}, bf16[1024,1024]{1,0:T(8,128)(2,1)}, u32[]{:S(2)}) copy-start(bf16[1024,1024]{1,0:T(8,128)(2,1)} %in_ref.1) | copy-start | bytes 6291460
  13.8 9.2 %collective-permute-start.3 = (bf16[128,1024]{1,0:T(8,128)(2,1)S(1)}, bf16[128,1024]{1,0:T(8,128)(2,1)S(1)}, u32[]{:S(2)}, u32[]{:S(2)}) collective-permute-start(bf16[128,1024]{1,0:T(8,128)(2,1)S(1)} %collective-permute-done.1.refs_2_), channel_id=1, source_target_pairs={{0,4},{1,3},{2,6},{3,1},{4,0},{5,7},{6,2},{7,5},{8,12},{9,11},{10,... | collective-permute-start | bytes 786440 | tf_op jit(solution)/shard_map/ppermute | solution.py:23
  14.4 9.0 %collective-permute-start.4 = (bf16[144,1024]{1,0:T(8,128)(2,1)S(1)}, bf16[144,1024]{1,0:T(8,128)(2,1)S(1)}, u32[]{:S(2)}, u32[]{:S(2)}) collective-permute-start(bf16[144,1024]{1,0:T(8,128)(2,1)S(1)} %collective-permute-done.2.refs_3_), channel_id=1, source_target_pairs={{0,2},{1,5},{2,0},{3,7},{4,6},{5,1},{6,4},{7,3},{8,10},{9,13},{10,... | collective-permute-start | bytes 884744 | tf_op jit(solution)/shard_map/ppermute | solution.py:23
  24.1 1.8 %collective-permute-start.7 = (f32[64,512]{1,0:T(8,128)S(1)}, f32[64,512]{1,0:T(8,128)S(1)}, u32[]{:S(2)}, u32[]{:S(2)}) collective-permute-start(f32[64,512]{1,0:T(8,128)S(1)} %shard_map.73), channel_id=1, source_target_pairs={{0,1},{1,0},{2,3},{3,2},{4,5},{5,4},{6,7},{7,6},{8,9},{9,8},{10,11... | collective-permute-start | bytes 393224 | tf_op jit(solution)/shard_map/ppermute | solution.py:18
  24.3 11.1 %copy-start.1 = (f32[64]{0:T(128)S(1)}, f32[64]{0:T(128)}, u32[]{:S(2)}) copy-start(f32[64]{0:T(128)} %param.11) | copy-start | bytes 772
  25.5 2.1 %collective-permute-start.10 = (f32[64,512]{1,0:T(8,128)S(1)}, f32[64,512]{1,0:T(8,128)S(1)}, u32[]{:S(2)}, u32[]{:S(2)}) collective-permute-start(f32[64,512]{1,0:T(8,128)S(1)} %get-tuple-element.26), channel_id=1, source_target_pairs={{0,1},{1,0},{2,3},{3,2},{4,5},{5,4},{6,7},{7,6},{8,9},{9,8},{10,11... | collective-permute-start | bytes 393224 | tf_op jit(solution)/shard_map/ppermute | solution.py:18
  25.9 5.0 %collective-permute-start.8 = (bf16[64,512]{1,0:T(8,128)(2,1)S(1)}, bf16[64,512]{1,0:T(8,128)(2,1)S(1)}, u32[]{:S(2)}, u32[]{:S(2)}) collective-permute-start(bf16[64,512]{1,0:T(8,128)(2,1)S(1)} %shard_map.74.a_ref), channel_id=1, source_target_pairs={{0,8},{1,17},{2,10},{3,19},{4,12},{5,21},{6,14},{7,23},{8,0},{9,25... | collective-permute-start | bytes 196616 | tf_op jit(solution)/shard_map/ppermute | solution.py:33
  27.6 5.3 %collective-permute-start.11 = (bf16[64,512]{1,0:T(8,128)(2,1)S(1)}, bf16[64,512]{1,0:T(8,128)(2,1)S(1)}, u32[]{:S(2)}, u32[]{:S(2)}) collective-permute-start(bf16[64,512]{1,0:T(8,128)(2,1)S(1)} %shard_map.76.a_ref), channel_id=1, source_target_pairs={{0,8},{1,17},{2,10},{3,19},{4,12},{5,21},{6,14},{7,23},{8,0},{9,25... | collective-permute-start | bytes 196616 | tf_op jit(solution)/shard_map/ppermute | solution.py:33
  31.0 5.3 %collective-permute-start.9 = (bf16[64,512]{1,0:T(8,128)(2,1)S(1)}, bf16[64,512]{1,0:T(8,128)(2,1)S(1)}, u32[]{:S(2)}, u32[]{:S(2)}) collective-permute-start(bf16[64,512]{1,0:T(8,128)(2,1)S(1)} %shard_map.75.refs_0_), channel_id=1, source_target_pairs={{0,16},{1,9},{2,18},{3,11},{4,20},{5,13},{6,22},{7,15},{8,24},{9,1... | collective-permute-start | bytes 196616 | tf_op jit(solution)/shard_map/ppermute | solution.py:33
  33.0 5.2 %collective-permute-start.12 = (bf16[64,512]{1,0:T(8,128)(2,1)S(1)}, bf16[64,512]{1,0:T(8,128)(2,1)S(1)}, u32[]{:S(2)}, u32[]{:S(2)}) collective-permute-start(bf16[64,512]{1,0:T(8,128)(2,1)S(1)} %shard_map.77.refs_2_), channel_id=1, source_target_pairs={{0,16},{1,9},{2,18},{3,11},{4,20},{5,13},{6,22},{7,15},{8,24},{9,1... | collective-permute-start | bytes 196616 | tf_op jit(solution)/shard_map/ppermute | solution.py:33

commit v9 on v1

--- a/solution.py
+++ b/solution.py
@@ -193,9 +193,8 @@
         for k in range(ways):
             piece = (k + turn) % 2
             blocks[1 << k][piece] = chip_send(blocks[0][piece], k, n_sl)
-    late_slab, _ = lax.optimization_barrier((slab, second))
     turned = jax.ShapeDtypeStruct(slab.shape[::-1], slab.dtype)
-    other = small_call(transpose_kernel, turned, core_send(late_slab, n_sl))
+    other = small_call(transpose_kernel, turned, core_send(slab, n_sl))
     slab = small_call(transpose_kernel, turned, slab)
     (acc,) = stage([slab], first, second, None, coeff, cols)
     held = [blocks[1 << k][k % 2] for k in range(ways)]

time: 38.9 us -> 38.9 us (level)
  transfers between devices with their start and end apart: 13 -> 13, of which waited for: 7 -> 7; matrix products, arithmetic and copies ran while one was open for 0% -> 0% of each run, Pallas kernels for 22% -> 25%
where the time goes in v9:
time: 38.9 us; the launch traced here: 38.7 us
  starting transfers between devices  15.7 us (40%)
  Pallas kernels  10.9 us (28%)
  waiting for transfers between devices  10.3 us (26%)
  local copies, waits for them, and re-layouts  1.69 us (4%)
    ppermute x6, starting transfers between devices, chip_send(): lax.ppermute(value, 'sl', [(i, i ^ bits[(k + i % 2) % len(bits)]) for i i...  7.44 us
    ppermute x4, starting transfers between devices, lm_send(): return lax.ppermute(value, ('lm', 'sl'), perm)  7.13 us
    pallas_call x7, Pallas kernels, stage(): pl.pallas_call(functools.partial(stage_kernel, count, coeff, ritz, accs i...  6.83 us
    ppermute x6, waiting for transfers between devices, chip_send(): lax.ppermute(value, 'sl', [(i, i ^ bits[(k + i % 2) % len(bits)]) for i i...  5.84 us
    ppermute x4, waiting for transfers between devices, lm_send(): return lax.ppermute(value, ('lm', 'sl'), perm)  4.45 us
    pallas_call x7, Pallas kernels, small_call(): pl.pallas_call(kernel, out_shape=jax.ShapeDtypeStruct(out.shape, out.dtyp...  2.13 us
    unnamed x4, local copies, waits for them, and re-layouts  1.59 us
    ppermute x3, starting transfers between devices, core_send(): return lax.ppermute(value, 'sl', [(i, i ^ 1) for i in range(n)])  1.09 us
  transfers between devices with their start and end apart: 13, of which 7 were waited for; matrix products, arithmetic and copies ran while one was open for 0% of the time, Pallas kernels for 25%

profile of v9, /device:TPU:0, one launch (start us, length us, event | category | flops | bytes accessed | tf_op | source)
XLA Modules:
  0.0 38.7 jit_solution(7252564210106414976)
XLA Ops:
  0.5 1.0 %shard_map.67.refs_2_ = bf16[144,1024]{1,0:T(8,128)(2,1)S(1)} custom-call(bf16[256,1024]{1,0:T(8,128)(2,1)} %land_ref.3), custom_call_target="tpu_custom_call" | custom-call | tf_op jit(solution)/shard_map/pallas_call | solution.py:75
  1.4 2.6 %collective-permute-start.3 = (bf16[144,1024]{1,0:T(8,128)(2,1)S(1)}, bf16[144,1024]{1,0:T(8,128)(2,1)S(1)}, u32[]{:S(2)}, u32[]{:S(2)}) collective-permute-start(bf16[144,1024]{1,0:T(8,128)(2,1)S(1)} %shard_map.67.refs_2_), channel_id=1, source_target_pairs={{0,4},{1,3},{2,6},{3,1},{4,0},{5,7},{6,2},{7,5},{8,12},{9,11},{10,... | collective-permute-start | bytes 884744 | tf_op jit(solution)/shard_map/ppermute | solution.py:23
  4.0 1.0 %shard_map.66.refs_1_ = bf16[128,1024]{1,0:T(8,128)(2,1)S(1)} custom-call(bf16[256,1024]{1,0:T(8,128)(2,1)} %land_ref.3, bf16[96,256]{1,0:T(8,128)(2,1)} %bitcast.4, s32[2]{0:T(128)} %exponents_ref.1, bf16[64,96]{1,0:T(8,128)(2,1)} %bitcast.5), custom_call_target="tpu_custom_call" | custom-call | tf_op jit(solution)/shard_map/pallas_call | solution.py:87
  5.0 1.6 %collective-permute-start.2 = (bf16[128,1024]{1,0:T(8,128)(2,1)S(1)}, bf16[128,1024]{1,0:T(8,128)(2,1)S(1)}, u32[]{:S(2)}, u32[]{:S(2)}) collective-permute-start(bf16[128,1024]{1,0:T(8,128)(2,1)S(1)} %shard_map.66.refs_1_), channel_id=1, source_target_pairs={{0,2},{1,5},{2,0},{3,7},{4,6},{5,1},{6,4},{7,3},{8,10},{9,13},{10,... | collective-permute-start | bytes 786440 | tf_op jit(solution)/shard_map/ppermute | solution.py:23
  7.2 1.6 %copy-done = bf16[1024,1024]{1,0:T(8,128)(2,1)S(1)} copy-done((bf16[1024,1024]{1,0:T(8,128)(2,1)S(1)}, bf16[1024,1024]{1,0:T(8,128)(2,1)}, u32[]{:S(2)}) %copy-start) | copy-done | bytes 2097176
  8.8 0.6 %shard_map.64.refs_0_.refs_1_ = bf16[1024,1024]{1,0:T(8,128)(2,1)S(1)} custom-call(bf16[1024,1024]{1,0:T(8,128)(2,1)S(1)} %copy-done), custom_call_target="tpu_custom_call" | custom-call | tf_op jit(solution)/shard_map/pallas_call | solution.py:172
  9.4 0.9 %shard_map.68.refs_4_ = f32[64,1024]{1,0:T(8,128)S(1)} custom-call(bf16[1024,1024]{1,0:T(8,128)(2,1)S(1)} %shard_map.64.refs_0_.refs_1_, bf16[128,1024]{1,0:T(8,128)(2,1)S(1)} %shard_map.66.refs_1_, bf16[144,1024]{1,0:T(8,128)(2,1)S(1)} %shard_map.67.refs_2_), custom_call_target="tpu_custom_call" | custom-call | flops 671088640 | bytes 2621440 | tf_op jit(solution)/shard_map/pallas_call | solution.py:143
  10.3 3.4 %collective-permute-done.2.refs_2_ = bf16[128,1024]{1,0:T(8,128)(2,1)S(1)} collective-permute-done((bf16[128,1024]{1,0:T(8,128)(2,1)S(1)}, bf16[128,1024]{1,0:T(8,128)(2,1)S(1)}, u32[]{:S(2)}, u32[]{:S(2)}) %collective-permute-start.2) | collective-permute-done | bytes 262176 | tf_op jit(solution)/shard_map/ppermute | solution.py:23
  13.6 0.7 %collective-permute-start.5 = (bf16[128,1024]{1,0:T(8,128)(2,1)S(1)}, bf16[128,1024]{1,0:T(8,128)(2,1)S(1)}, u32[]{:S(2)}, u32[]{:S(2)}) collective-permute-start(bf16[128,1024]{1,0:T(8,128)(2,1)S(1)} %collective-permute-done.2.refs_2_), channel_id=1, source_target_pairs={{0,4},{1,3},{2,6},{3,1},{4,0},{5,7},{6,2},{7,5},{8,12},{9,11},{10,... | collective-permute-start | bytes 786440 | tf_op jit(solution)/shard_map/ppermute | solution.py:23
  14.4 2.0 %collective-permute-start.6 = (bf16[144,1024]{1,0:T(8,128)(2,1)S(1)}, bf16[144,1024]{1,0:T(8,128)(2,1)S(1)}, u32[]{:S(2)}, u32[]{:S(2)}) collective-permute-start(bf16[144,1024]{1,0:T(8,128)(2,1)S(1)} %collective-permute-done.3.refs_3_), channel_id=1, source_target_pairs={{0,2},{1,5},{2,0},{3,7},{4,6},{5,1},{6,4},{7,3},{8,10},{9,13},{10,... | collective-permute-start | bytes 884744 | tf_op jit(solution)/shard_map/ppermute | solution.py:23
  16.4 0.6 %shard_map.65.refs_0_.refs_1_ = bf16[1024,1024]{1,0:T(8,128)(2,1)S(1)} custom-call(bf16[1024,1024]{1,0:T(8,128)(2,1)S(1)} %collective-permute-done.in_ref), custom_call_target="tpu_custom_call" | custom-call | tf_op jit(solution)/shard_map/pallas_call | solution.py:172
  17.0 0.9 %shard_map.69.refs_5_ = f32[64,1024]{1,0:T(8,128)S(1)} custom-call(bf16[1024,1024]{1,0:T(8,128)(2,1)S(1)} %shard_map.65.refs_0_.refs_1_, bf16[128,1024]{1,0:T(8,128)(2,1)S(1)} %shard_map.66.refs_1_, bf16[144,1024]{1,0:T(8,128)(2,1)S(1)} %shard_map.67.refs_2_), custom_call_target="tpu_custom_call" | custom-call | flops 671088640 | bytes 2621440 | tf_op jit(solution)/shard_map/pallas_call | solution.py:143
  17.9 1.6 %collective-permute-done.4.refs_3_ = bf16[144,1024]{1,0:T(8,128)(2,1)S(1)} collective-permute-done((bf16[144,1024]{1,0:T(8,128)(2,1)S(1)}, bf16[144,1024]{1,0:T(8,128)(2,1)S(1)}, u32[]{:S(2)}, u32[]{:S(2)}) %collective-permute-start.4) | collective-permute-done | bytes 294944 | tf_op jit(solution)/shard_map/ppermute | solution.py:23
  19.5 1.5 %shard_map.70 = (f32[64,1024]{1,0:T(8,128)S(1)}, f32[64,1024]{1,0:T(8,128)S(1)}) custom-call(bf16[1024,1024]{1,0:T(8,128)(2,1)S(1)} %shard_map.64.refs_0_.refs_1_, bf16[1024,1024]{1,0:T(8,128)(2,1)S(1)} %shard_map.65.refs_0_.refs_1_, bf16[128,1024]{1,0:T(8,128)(2,1)S(1)} %collective-permute-done.2.refs_2_, ...), custom_call_target="tpu_custom_call" | custom-call | flops 1342177280 | bytes 4718592 | tf_op jit(solution)/shard_map/pallas_call | solution.py:143
  21.0 1.5 %shard_map.71 = (f32[64,1024]{1,0:T(8,128)S(1)}, f32[64,1024]{1,0:T(8,128)S(1)}) custom-call(bf16[1024,1024]{1,0:T(8,128)(2,1)S(1)} %shard_map.64.refs_0_.refs_1_, bf16[1024,1024]{1,0:T(8,128)(2,1)S(1)} %shard_map.65.refs_0_.refs_1_, bf16[128,1024]{1,0:T(8,128)(2,1)S(1)} %collective-permute-done.1.refs_2_, ...), custom_call_target="tpu_custom_call" | custom-call | flops 1342177280 | bytes 4718592 | tf_op jit(solution)/shard_map/pallas_call | solution.py:143
  23.4 0.6 %shard_map.73 = f32[64,512]{1,0:T(8,128)S(1)} custom-call(bf16[1024,1024]{1,0:T(8,128)(2,1)S(1)} %shard_map.65.refs_0_.refs_1_, bf16[128,1024]{1,0:T(8,128)(2,1)S(1)} %collective-permute-done.5.refs_2_.refs_1_, bf16[144,1024]{1,0:T(8,128)(2,1)S(1)} %collective-permute-done.6.refs_3_.refs_2_, f32[64,1024]{1,0:T(8,128)S(1)} %get-tuple-element.22.refs_4_.refs_3_), custom_call_target="tpu_custom_call" | custom-call | flops 335544320 | bytes 1572864 | tf_op jit(solution)/shard_map/pallas_call | solution.py:143
  24.2 0.9 %shard_map.72 = (f32[64,512]{1,0:T(8,128)S(1)}, f32[64,512]{1,0:T(8,128)S(1)}) custom-call(bf16[1024,1024]{1,0:T(8,128)(2,1)S(1)} %shard_map.65.refs_0_.refs_1_, bf16[1024,1024]{1,0:T(8,128)(2,1)S(1)} %shard_map.64.refs_0_.refs_1_, bf16[128,1024]{1,0:T(8,128)(2,1)S(1)} %collective-permute-done.5.refs_2_.refs_1_, ...), custom_call_target="tpu_custom_call" | custom-call | flops 671088640 | bytes 2621440 | tf_op jit(solution)/shard_map/pallas_call | solution.py:143
  25.5 1.7 %collective-permute-start.8 = (bf16[64,512]{1,0:T(8,128)(2,1)S(1)}, bf16[64,512]{1,0:T(8,128)(2,1)S(1)}, u32[]{:S(2)}, u32[]{:S(2)}) collective-permute-start(bf16[64,512]{1,0:T(8,128)(2,1)S(1)} %shard_map.74.a_ref), channel_id=1, source_target_pairs={{0,8},{1,17},{2,10},{3,19},{4,12},{5,21},{6,14},{7,23},{8,0},{9,25... | collective-permute-start | bytes 196616 | tf_op jit(solution)/shard_map/ppermute | solution.py:33
  27.3 0.6 %shard_map.76.a_ref = f32[64,512]{1,0:T(8,128)S(1)} custom-call(bf16[1024,1024]{1,0:T(8,128)(2,1)S(1)} %shard_map.64.refs_0_.refs_1_, bf16[128,1024]{1,0:T(8,128)(2,1)S(1)} %collective-permute-done.5.refs_2_.refs_1_, bf16[144,1024]{1,0:T(8,128)(2,1)S(1)} %collective-permute-done.6.refs_3_.refs_2_, f32[64,1024]{1,0:T(8,128)S(1)} %get-tuple-element.25.refs_5_.refs_3_), custom_call_target="tpu_custom_call" | custom-call | flops 335544320 | bytes 1572864 | tf_op jit(solution)/shard_map/pallas_call | solution.py:143
  28.4 2.2 %collective-permute-done.8.b_ref = bf16[64,512]{1,0:T(8,128)(2,1)S(1)} collective-permute-done((bf16[64,512]{1,0:T(8,128)(2,1)S(1)}, bf16[64,512]{1,0:T(8,128)(2,1)S(1)}, u32[]{:S(2)}, u32[]{:S(2)}) %collective-permute-start.8) | collective-permute-done | bytes 65568 | tf_op jit(solution)/shard_map/ppermute | solution.py:33
  30.6 2.0 %collective-permute-start.9 = (bf16[64,512]{1,0:T(8,128)(2,1)S(1)}, bf16[64,512]{1,0:T(8,128)(2,1)S(1)}, u32[]{:S(2)}, u32[]{:S(2)}) collective-permute-start(bf16[64,512]{1,0:T(8,128)(2,1)S(1)} %shard_map.75.refs_0_), channel_id=1, source_target_pairs={{0,16},{1,9},{2,18},{3,11},{4,20},{5,13},{6,22},{7,15},{8,24},{9,1... | collective-permute-start | bytes 196616 | tf_op jit(solution)/shard_map/ppermute | solution.py:33
  32.7 2.9 %collective-permute-start.12 = (bf16[64,512]{1,0:T(8,128)(2,1)S(1)}, bf16[64,512]{1,0:T(8,128)(2,1)S(1)}, u32[]{:S(2)}, u32[]{:S(2)}) collective-permute-start(bf16[64,512]{1,0:T(8,128)(2,1)S(1)} %shard_map.78.refs_2_), channel_id=1, source_target_pairs={{0,16},{1,9},{2,18},{3,11},{4,20},{5,13},{6,22},{7,15},{8,24},{9,1... | collective-permute-start | bytes 196616 | tf_op jit(solution)/shard_map/ppermute | solution.py:33
  35.8 2.1 %collective-permute-done.12.refs_3_ = bf16[64,512]{1,0:T(8,128)(2,1)S(1)} collective-permute-done((bf16[64,512]{1,0:T(8,128)(2,1)S(1)}, bf16[64,512]{1,0:T(8,128)(2,1)S(1)}, u32[]{:S(2)}, u32[]{:S(2)}) %collective-permute-start.12) | collective-permute-done | bytes 65568 | tf_op jit(solution)/shard_map/ppermute | solution.py:33
  37.9 0.8 %shard_map.79 = f32[64,1024]{1,0:T(8,128)} custom-call(bf16[64,512]{1,0:T(8,128)(2,1)S(1)} %shard_map.75.refs_0_, bf16[64,512]{1,0:T(8,128)(2,1)S(1)} %collective-permute-done.9.refs_1_, bf16[64,512]{1,0:T(8,128)(2,1)S(1)} %shard_map.78.refs_2_, bf16[64,512]{1,0:T(8,128)(2,1)S(1)} %collective-permute-done.12.refs_3_, f32[64,1]{1,0:T(8,128)S(1)} %copy.7.refs_4_), custom_call_target="tpu_custom_call" | custom-call | tf_op jit(solution)/shard_map/pallas_call | solution.py:172
  (23 shorter events, 3.4 us)
Async XLA Ops:
  0.0 16.4 %collective-permute-start = (bf16[1024,1024]{1,0:T(8,128)(2,1)}, bf16[1024,1024]{1,0:T(8,128)(2,1)S(1)}, u32[]{:S(2)}, u32[]{:S(2)}) collective-permute-start(bf16[1024,1024]{1,0:T(8,128)(2,1)} %in_ref.1), channel_id=1, source_target_pairs={{0,1},{1,0},{2,3},{3,2},{4,5},{5,4},{6,7},{7,6},{8,9},{9,8},{10,11... | collective-permute-start | bytes 6291464 | tf_op jit(solution)/shard_map/ppermute | solution.py:18
  1.4 12.2 %collective-permute-start.3 = (bf16[144,1024]{1,0:T(8,128)(2,1)S(1)}, bf16[144,1024]{1,0:T(8,128)(2,1)S(1)}, u32[]{:S(2)}, u32[]{:S(2)}) collective-permute-start(bf16[144,1024]{1,0:T(8,128)(2,1)S(1)} %shard_map.67.refs_2_), channel_id=1, source_target_pairs={{0,4},{1,3},{2,6},{3,1},{4,0},{5,7},{6,2},{7,5},{8,12},{9,11},{10,... | collective-permute-start | bytes 884744 | tf_op jit(solution)/shard_map/ppermute | solution.py:23
  5.0 8.6 %collective-permute-start.2 = (bf16[128,1024]{1,0:T(8,128)(2,1)S(1)}, bf16[128,1024]{1,0:T(8,128)(2,1)S(1)}, u32[]{:S(2)}, u32[]{:S(2)}) collective-permute-start(bf16[128,1024]{1,0:T(8,128)(2,1)S(1)} %shard_map.66.refs_1_), channel_id=1, source_target_pairs={{0,2},{1,5},{2,0},{3,7},{4,6},{5,1},{6,4},{7,3},{8,10},{9,13},{10,... | collective-permute-start | bytes 786440 | tf_op jit(solution)/shard_map/ppermute | solution.py:23
  6.6 12.9 %collective-permute-start.4 = (bf16[144,1024]{1,0:T(8,128)(2,1)S(1)}, bf16[144,1024]{1,0:T(8,128)(2,1)S(1)}, u32[]{:S(2)}, u32[]{:S(2)}) collective-permute-start(bf16[144,1024]{1,0:T(8,128)(2,1)S(1)} %shard_map.67.refs_2_), channel_id=1, source_target_pairs={{0,2},{1,5},{2,0},{3,7},{4,6},{5,1},{6,4},{7,3},{8,10},{9,13},{10,... | collective-permute-start | bytes 884744 | tf_op jit(solution)/shard_map/ppermute | solution.py:23
  7.1 13.9 %collective-permute-start.1 = (bf16[128,1024]{1,0:T(8,128)(2,1)S(1)}, bf16[128,1024]{1,0:T(8,128)(2,1)S(1)}, u32[]{:S(2)}, u32[]{:S(2)}) collective-permute-start(bf16[128,1024]{1,0:T(8,128)(2,1)S(1)} %shard_map.66.refs_1_), channel_id=1, source_target_pairs={{0,4},{1,3},{2,6},{3,1},{4,0},{5,7},{6,2},{7,5},{8,12},{9,11},{10,... | collective-permute-start | bytes 786440 | tf_op jit(solution)/shard_map/ppermute | solution.py:23
  7.2 1.6 %copy-start = (bf16[1024,1024]{1,0:T(8,128)(2,1)S(1)}, bf16[1024,1024]{1,0:T(8,128)(2,1)}, u32[]{:S(2)}) copy-start(bf16[1024,1024]{1,0:T(8,128)(2,1)} %in_ref.1) | copy-start | bytes 6291460
  13.6 9.2 %collective-permute-start.5 = (bf16[128,1024]{1,0:T(8,128)(2,1)S(1)}, bf16[128,1024]{1,0:T(8,128)(2,1)S(1)}, u32[]{:S(2)}, u32[]{:S(2)}) collective-permute-start(bf16[128,1024]{1,0:T(8,128)(2,1)S(1)} %collective-permute-done.2.refs_2_), channel_id=1, source_target_pairs={{0,4},{1,3},{2,6},{3,1},{4,0},{5,7},{6,2},{7,5},{8,12},{9,11},{10,... | collective-permute-start | bytes 786440 | tf_op jit(solution)/shard_map/ppermute | solution.py:23
  14.4 9.0 %collective-permute-start.6 = (bf16[144,1024]{1,0:T(8,128)(2,1)S(1)}, bf16[144,1024]{1,0:T(8,128)(2,1)S(1)}, u32[]{:S(2)}, u32[]{:S(2)}) collective-permute-start(bf16[144,1024]{1,0:T(8,128)(2,1)S(1)} %collective-permute-done.3.refs_3_), channel_id=1, source_target_pairs={{0,2},{1,5},{2,0},{3,7},{4,6},{5,1},{6,4},{7,3},{8,10},{9,13},{10,... | collective-permute-start | bytes 884744 | tf_op jit(solution)/shard_map/ppermute | solution.py:23
  24.0 1.5 %collective-permute-start.7 = (f32[64,512]{1,0:T(8,128)S(1)}, f32[64,512]{1,0:T(8,128)S(1)}, u32[]{:S(2)}, u32[]{:S(2)}) collective-permute-start(f32[64,512]{1,0:T(8,128)S(1)} %shard_map.73), channel_id=1, source_target_pairs={{0,1},{1,0},{2,3},{3,2},{4,5},{5,4},{6,7},{7,6},{8,9},{9,8},{10,11... | collective-permute-start | bytes 393224 | tf_op jit(solution)/shard_map/ppermute | solution.py:18
  25.0 10.5 %copy-start.1 = (f32[64]{0:T(128)S(1)}, f32[64]{0:T(128)}, u32[]{:S(2)}) copy-start(f32[64]{0:T(128)} %param.11) | copy-start | bytes 772
  25.1 2.8 %collective-permute-start.10 = (f32[64,512]{1,0:T(8,128)S(1)}, f32[64,512]{1,0:T(8,128)S(1)}, u32[]{:S(2)}, u32[]{:S(2)}) collective-permute-start(f32[64,512]{1,0:T(8,128)S(1)} %get-tuple-element.26), channel_id=1, source_target_pairs={{0,1},{1,0},{2,3},{3,2},{4,5},{5,4},{6,7},{7,6},{8,9},{9,8},{10,11... | collective-permute-start | bytes 393224 | tf_op jit(solution)/shard_map/ppermute | solution.py:18
  25.5 5.0 %collective-permute-start.8 = (bf16[64,512]{1,0:T(8,128)(2,1)S(1)}, bf16[64,512]{1,0:T(8,128)(2,1)S(1)}, u32[]{:S(2)}, u32[]{:S(2)}) collective-permute-start(bf16[64,512]{1,0:T(8,128)(2,1)S(1)} %shard_map.74.a_ref), channel_id=1, source_target_pairs={{0,8},{1,17},{2,10},{3,19},{4,12},{5,21},{6,14},{7,23},{8,0},{9,25... | collective-permute-start | bytes 196616 | tf_op jit(solution)/shard_map/ppermute | solution.py:33
  27.9 4.7 %collective-permute-start.11 = (bf16[64,512]{1,0:T(8,128)(2,1)S(1)}, bf16[64,512]{1,0:T(8,128)(2,1)S(1)}, u32[]{:S(2)}, u32[]{:S(2)}) collective-permute-start(bf16[64,512]{1,0:T(8,128)(2,1)S(1)} %shard_map.77.a_ref), channel_id=1, source_target_pairs={{0,8},{1,17},{2,10},{3,19},{4,12},{5,21},{6,14},{7,23},{8,0},{9,25... | collective-permute-start | bytes 196616 | tf_op jit(solution)/shard_map/ppermute | solution.py:33
  30.6 5.2 %collective-permute-start.9 = (bf16[64,512]{1,0:T(8,128)(2,1)S(1)}, bf16[64,512]{1,0:T(8,128)(2,1)S(1)}, u32[]{:S(2)}, u32[]{:S(2)}) collective-permute-start(bf16[64,512]{1,0:T(8,128)(2,1)S(1)} %shard_map.75.refs_0_), channel_id=1, source_target_pairs={{0,16},{1,9},{2,18},{3,11},{4,20},{5,13},{6,22},{7,15},{8,24},{9,1... | collective-permute-start | bytes 196616 | tf_op jit(solution)/shard_map/ppermute | solution.py:33
  32.7 5.2 %collective-permute-start.12 = (bf16[64,512]{1,0:T(8,128)(2,1)S(1)}, bf16[64,512]{1,0:T(8,128)(2,1)S(1)}, u32[]{:S(2)}, u32[]{:S(2)}) collective-permute-start(bf16[64,512]{1,0:T(8,128)(2,1)S(1)} %shard_map.78.refs_2_), channel_id=1, source_target_pairs={{0,16},{1,9},{2,18},{3,11},{4,20},{5,13},{6,22},{7,15},{8,24},{9,1... | collective-permute-start | bytes 196616 | tf_op jit(solution)/shard_map/ppermute | solution.py:33

commit v10 on v3

--- a/solution.py
+++ b/solution.py
@@ -34,7 +34,7 @@
 
 
 def prepare_kernel(
-    land_ref, codes_ref, exponents_ref, eig_ref, first_ref, codes, eig, exponents, sems
+    land_ref, codes_ref, exponents_ref, eig_ref, first_ref, second_ref, codes, eig, exponents, sems
 ):
     rows, feat = land_ref.shape
     half = rows // 2 - SHIFT
@@ -44,6 +44,7 @@
         (eig_ref, eig),
         (exponents_ref, exponents),
         (land_ref.at[:half], first_ref.at[:half]),
+        (land_ref.at[half:], second_ref),
     ]
     copies = [pltpu.make_async_copy(src, dst, sems.at[k]) for k, (src, dst) in enumerate(pairs)]
     for copy in copies:
@@ -69,13 +70,16 @@
     extra = eig_t.shape[0] * rows // feat
     return pl.pallas_call(
         prepare_kernel,
-        out_shape=jax.ShapeDtypeStruct((rows // 2 - SHIFT + extra, feat), jnp.bfloat16),
+        out_shape=[
+            jax.ShapeDtypeStruct((rows // 2 - SHIFT + extra, feat), jnp.bfloat16),
+            jax.ShapeDtypeStruct((rows // 2 + SHIFT, feat), jnp.bfloat16),
+        ],
         in_specs=[pl.BlockSpec(memory_space=pltpu.HBM)] * 4,
         scratch_shapes=[
             pltpu.VMEM(codes_t.shape, codes_t.dtype),
             pltpu.VMEM(eig_t.shape, eig_t.dtype),
             pltpu.SMEM(exponents.shape, exponents.dtype),
-            pltpu.SemaphoreType.DMA((4,)),
+            pltpu.SemaphoreType.DMA((5,)),
         ],
         compiler_params=pltpu.CompilerParams(vmem_limit_bytes=8 * MIB),
     )(*(pltpu.with_memory_space_constraint(x, pltpu.HBM) for x in (landmarks, codes_t, exponents, eig_t)))
@@ -167,8 +171,7 @@
     rows = slab.shape[0]
     ways = n_sl.bit_length() - 2
 
-    second = landmarks[landmarks.shape[0] // 2 - SHIFT :]
-    first = prepare(landmarks, codes.T, exponents, eigvec.T)
+    first, second = prepare(landmarks, codes.T, exponents, eigvec.T)
     blocks = {0: [first, second]}
     for k in range(ways):
         blocks[1 << k] = [None, None]
@@ -176,9 +179,8 @@
         for k in range(ways):
             piece = (k + turn) % 2
             blocks[1 << k][piece] = chip_send(blocks[0][piece], k, n_sl)
-    late_slab, _ = lax.optimization_barrier((slab, second))
     turned = jax.ShapeDtypeStruct(slab.shape[::-1], slab.dtype)
-    other = small_call(transpose_kernel, turned, core_send(late_slab, n_sl))
+    other = small_call(transpose_kernel, turned, core_send(slab, n_sl))
     slab = small_call(transpose_kernel, turned, slab)
     (acc,) = stage([slab], first, second, None, coeff, cols)
     held = [blocks[1 << k][k % 2] for k in range(ways)]

time: 38.9 us -> 39 us (level)
  waiting for transfers between devices: 10.3 us -> 11.6 us
  local copies, waits for them, and re-layouts: 2.67 us -> 1.69 us
    ppermute x6, waiting for transfers between devices: 5.93 us -> 7.3 us  [chip_send(): lax.ppermute(value, 'sl', [(i, i ^ bits[(k + i % 2) % len(bits)]) for i i...]
    slice x1 -> x0, local copies, waits for them, and re-layouts: 0.98 us -> none  [local(): second = landmarks[landmarks.shape[0] // 2 - SHIFT:]]
    ppermute x6, starting transfers between devices: 7.36 us -> 6.83 us  [chip_send(): lax.ppermute(value, 'sl', [(i, i ^ bits[(k + i % 2) % len(bits)]) for i i...]
  transfers between devices with their start and end apart: 13 -> 13, of which waited for: 7 -> 6; matrix products, arithmetic and copies ran while one was open for 0% -> 0% of each run, Pallas kernels for 22% -> 22%
where the time goes in v10:
time: 39 us; the launch traced here: 38.9 us
  starting transfers between devices  15.4 us (39%)
  waiting for transfers between devices  11.6 us (30%)
  Pallas kernels  10.1 us (26%)
  local copies, waits for them, and re-layouts  1.69 us (4%)
    ppermute x4, starting transfers between devices, lm_send(): return lax.ppermute(value, ('lm', 'sl'), perm)  7.46 us
    ppermute x6, waiting for transfers between devices, chip_send(): lax.ppermute(value, 'sl', [(i, i ^ bits[(k + i % 2) % len(bits)]) for i i...  7.3 us
    ppermute x6, starting transfers between devices, chip_send(): lax.ppermute(value, 'sl', [(i, i ^ bits[(k + i % 2) % len(bits)]) for i i...  6.83 us
    pallas_call x7, Pallas kernels, stage(): pl.pallas_call(functools.partial(stage_kernel, count, coeff, ritz, accs i...  6.83 us
    ppermute x4, waiting for transfers between devices, lm_send(): return lax.ppermute(value, ('lm', 'sl'), perm)  4.29 us
    pallas_call x7, Pallas kernels, small_call(): pl.pallas_call(kernel, out_shape=jax.ShapeDtypeStruct(out.shape, out.dtyp...  2.13 us
    unnamed x4, local copies, waits for them, and re-layouts  1.59 us
    pallas_call x1, Pallas kernels, prepare(): pl.pallas_call(prepare_kernel, out_shape=[jax.ShapeDtypeStruct((rows // 2...  1.16 us
  transfers between devices with their start and end apart: 13, of which 6 were waited for; matrix products, arithmetic and copies ran while one was open for 0% of the time, Pallas kernels for 22%

profile of v10, /device:TPU:0, one launch (start us, length us, event | category | flops | bytes accessed | tf_op | source)
XLA Modules:
  0.0 38.9 jit_solution(6568958212766324119)
XLA Ops:
  0.5 1.2 %shard_map.66 = (bf16[128,1024]{1,0:T(8,128)(2,1)S(1)}, bf16[144,1024]{1,0:T(8,128)(2,1)S(1)}) custom-call(bf16[256,1024]{1,0:T(8,128)(2,1)} %land_ref.1, bf16[96,256]{1,0:T(8,128)(2,1)} %bitcast.4, s32[2]{0:T(128)} %exponents_ref.1, bf16[64,96]{1,0:T(8,128)(2,1)} %bitcast.5), custom_call_target="tpu_custom_call" | custom-call | tf_op jit(solution)/shard_map/pallas_call | solution.py:71
  1.6 2.6 %collective-permute-start.3 = (bf16[144,1024]{1,0:T(8,128)(2,1)S(1)}, bf16[144,1024]{1,0:T(8,128)(2,1)S(1)}, u32[]{:S(2)}, u32[]{:S(2)}) collective-permute-start(bf16[144,1024]{1,0:T(8,128)(2,1)S(1)} %get-tuple-element.19.refs_2_), channel_id=1, source_target_pairs={{0,4},{1,3},{2,6},{3,1},{4,0},{5,7},{6,2},{7,5},{8,12},{9,11},{10,... | collective-permute-start | bytes 884744 | tf_op jit(solution)/shard_map/ppermute | solution.py:23
  4.2 1.5 %collective-permute-start.2 = (bf16[128,1024]{1,0:T(8,128)(2,1)S(1)}, bf16[128,1024]{1,0:T(8,128)(2,1)S(1)}, u32[]{:S(2)}, u32[]{:S(2)}) collective-permute-start(bf16[128,1024]{1,0:T(8,128)(2,1)S(1)} %get-tuple-element.18.refs_1_), channel_id=1, source_target_pairs={{0,2},{1,5},{2,0},{3,7},{4,6},{5,1},{6,4},{7,3},{8,10},{9,13},{10,... | collective-permute-start | bytes 786440 | tf_op jit(solution)/shard_map/ppermute | solution.py:23
  5.7 0.5 %collective-permute-start.4 = (bf16[144,1024]{1,0:T(8,128)(2,1)S(1)}, bf16[144,1024]{1,0:T(8,128)(2,1)S(1)}, u32[]{:S(2)}, u32[]{:S(2)}) collective-permute-start(bf16[144,1024]{1,0:T(8,128)(2,1)S(1)} %get-tuple-element.19.refs_2_), channel_id=1, source_target_pairs={{0,2},{1,5},{2,0},{3,7},{4,6},{5,1},{6,4},{7,3},{8,10},{9,13},{10,... | collective-permute-start | bytes 884744 | tf_op jit(solution)/shard_map/ppermute | solution.py:23
  6.3 1.6 %copy-done = bf16[1024,1024]{1,0:T(8,128)(2,1)S(1)} copy-done((bf16[1024,1024]{1,0:T(8,128)(2,1)S(1)}, bf16[1024,1024]{1,0:T(8,128)(2,1)}, u32[]{:S(2)}) %copy-start) | copy-done | bytes 2097176
  7.9 0.6 %shard_map.64.refs_0_.refs_1_ = bf16[1024,1024]{1,0:T(8,128)(2,1)S(1)} custom-call(bf16[1024,1024]{1,0:T(8,128)(2,1)S(1)} %copy-done), custom_call_target="tpu_custom_call" | custom-call | tf_op jit(solution)/shard_map/pallas_call | solution.py:159
  8.5 0.9 %shard_map.67.refs_4_ = f32[64,1024]{1,0:T(8,128)S(1)} custom-call(bf16[1024,1024]{1,0:T(8,128)(2,1)S(1)} %shard_map.64.refs_0_.refs_1_, bf16[128,1024]{1,0:T(8,128)(2,1)S(1)} %get-tuple-element.18.refs_1_, bf16[144,1024]{1,0:T(8,128)(2,1)S(1)} %get-tuple-element.19.refs_2_), custom_call_target="tpu_custom_call" | custom-call | flops 671088640 | bytes 2621440 | tf_op jit(solution)/shard_map/pallas_call | solution.py:130
  9.4 4.0 %collective-permute-done.2.refs_2_ = bf16[128,1024]{1,0:T(8,128)(2,1)S(1)} collective-permute-done((bf16[128,1024]{1,0:T(8,128)(2,1)S(1)}, bf16[128,1024]{1,0:T(8,128)(2,1)S(1)}, u32[]{:S(2)}, u32[]{:S(2)}) %collective-permute-start.2) | collective-permute-done | bytes 262176 | tf_op jit(solution)/shard_map/ppermute | solution.py:23
  13.5 2.1 %collective-permute-start.6 = (bf16[144,1024]{1,0:T(8,128)(2,1)S(1)}, bf16[144,1024]{1,0:T(8,128)(2,1)S(1)}, u32[]{:S(2)}, u32[]{:S(2)}) collective-permute-start(bf16[144,1024]{1,0:T(8,128)(2,1)S(1)} %collective-permute-done.3.refs_3_), channel_id=1, source_target_pairs={{0,2},{1,5},{2,0},{3,7},{4,6},{5,1},{6,4},{7,3},{8,10},{9,13},{10,... | collective-permute-start | bytes 884744 | tf_op jit(solution)/shard_map/ppermute | solution.py:23
  15.6 0.6 %shard_map.65.refs_0_.refs_1_ = bf16[1024,1024]{1,0:T(8,128)(2,1)S(1)} custom-call(bf16[1024,1024]{1,0:T(8,128)(2,1)S(1)} %collective-permute-done.in_ref), custom_call_target="tpu_custom_call" | custom-call | tf_op jit(solution)/shard_map/pallas_call | solution.py:159
  16.2 0.9 %shard_map.68.refs_5_ = f32[64,1024]{1,0:T(8,128)S(1)} custom-call(bf16[1024,1024]{1,0:T(8,128)(2,1)S(1)} %shard_map.65.refs_0_.refs_1_, bf16[128,1024]{1,0:T(8,128)(2,1)S(1)} %get-tuple-element.18.refs_1_, bf16[144,1024]{1,0:T(8,128)(2,1)S(1)} %get-tuple-element.19.refs_2_), custom_call_target="tpu_custom_call" | custom-call | flops 671088640 | bytes 2621440 | tf_op jit(solution)/shard_map/pallas_call | solution.py:130
  17.1 2.4 %collective-permute-done.4.refs_3_ = bf16[144,1024]{1,0:T(8,128)(2,1)S(1)} collective-permute-done((bf16[144,1024]{1,0:T(8,128)(2,1)S(1)}, bf16[144,1024]{1,0:T(8,128)(2,1)S(1)}, u32[]{:S(2)}, u32[]{:S(2)}) %collective-permute-start.4) | collective-permute-done | bytes 294944 | tf_op jit(solution)/shard_map/ppermute | solution.py:23
  19.5 1.5 %shard_map.69 = (f32[64,1024]{1,0:T(8,128)S(1)}, f32[64,1024]{1,0:T(8,128)S(1)}) custom-call(bf16[1024,1024]{1,0:T(8,128)(2,1)S(1)} %shard_map.64.refs_0_.refs_1_, bf16[1024,1024]{1,0:T(8,128)(2,1)S(1)} %shard_map.65.refs_0_.refs_1_, bf16[128,1024]{1,0:T(8,128)(2,1)S(1)} %collective-permute-done.2.refs_2_, ...), custom_call_target="tpu_custom_call" | custom-call | flops 1342177280 | bytes 4718592 | tf_op jit(solution)/shard_map/pallas_call | solution.py:130
  21.1 1.5 %shard_map.70 = (f32[64,1024]{1,0:T(8,128)S(1)}, f32[64,1024]{1,0:T(8,128)S(1)}) custom-call(bf16[1024,1024]{1,0:T(8,128)(2,1)S(1)} %shard_map.64.refs_0_.refs_1_, bf16[1024,1024]{1,0:T(8,128)(2,1)S(1)} %shard_map.65.refs_0_.refs_1_, bf16[128,1024]{1,0:T(8,128)(2,1)S(1)} %collective-permute-done.1.refs_2_, ...), custom_call_target="tpu_custom_call" | custom-call | flops 1342177280 | bytes 4718592 | tf_op jit(solution)/shard_map/pallas_call | solution.py:130
  22.7 0.7 %collective-permute-done.6.refs_3_.refs_2_ = bf16[144,1024]{1,0:T(8,128)(2,1)S(1)} collective-permute-done((bf16[144,1024]{1,0:T(8,128)(2,1)S(1)}, bf16[144,1024]{1,0:T(8,128)(2,1)S(1)}, u32[]{:S(2)}, u32[]{:S(2)}) %collective-permute-start.6) | collective-permute-done | bytes 294944 | tf_op jit(solution)/shard_map/ppermute | solution.py:23
  23.4 0.6 %shard_map.72 = f32[64,512]{1,0:T(8,128)S(1)} custom-call(bf16[1024,1024]{1,0:T(8,128)(2,1)S(1)} %shard_map.65.refs_0_.refs_1_, bf16[128,1024]{1,0:T(8,128)(2,1)S(1)} %collective-permute-done.5.refs_2_.refs_1_, bf16[144,1024]{1,0:T(8,128)(2,1)S(1)} %collective-permute-done.6.refs_3_.refs_2_, f32[64,1024]{1,0:T(8,128)S(1)} %get-tuple-element.26.refs_4_.refs_3_), custom_call_target="tpu_custom_call" | custom-call | flops 335544320 | bytes 1572864 | tf_op jit(solution)/shard_map/pallas_call | solution.py:130
  24.2 0.9 %shard_map.71 = (f32[64,512]{1,0:T(8,128)S(1)}, f32[64,512]{1,0:T(8,128)S(1)}) custom-call(bf16[1024,1024]{1,0:T(8,128)(2,1)S(1)} %shard_map.65.refs_0_.refs_1_, bf16[1024,1024]{1,0:T(8,128)(2,1)S(1)} %shard_map.64.refs_0_.refs_1_, bf16[128,1024]{1,0:T(8,128)(2,1)S(1)} %collective-permute-done.5.refs_2_.refs_1_, ...), custom_call_target="tpu_custom_call" | custom-call | flops 671088640 | bytes 2621440 | tf_op jit(solution)/shard_map/pallas_call | solution.py:130
  25.6 1.9 %collective-permute-start.8 = (bf16[64,512]{1,0:T(8,128)(2,1)S(1)}, bf16[64,512]{1,0:T(8,128)(2,1)S(1)}, u32[]{:S(2)}, u32[]{:S(2)}) collective-permute-start(bf16[64,512]{1,0:T(8,128)(2,1)S(1)} %shard_map.73.a_ref), channel_id=1, source_target_pairs={{0,8},{1,17},{2,10},{3,19},{4,12},{5,21},{6,14},{7,23},{8,0},{9,25... | collective-permute-start | bytes 196616 | tf_op jit(solution)/shard_map/ppermute | solution.py:33
  27.5 0.6 %shard_map.75.a_ref = f32[64,512]{1,0:T(8,128)S(1)} custom-call(bf16[1024,1024]{1,0:T(8,128)(2,1)S(1)} %shard_map.64.refs_0_.refs_1_, bf16[128,1024]{1,0:T(8,128)(2,1)S(1)} %collective-permute-done.5.refs_2_.refs_1_, bf16[144,1024]{1,0:T(8,128)(2,1)S(1)} %collective-permute-done.6.refs_3_.refs_2_, f32[64,1024]{1,0:T(8,128)S(1)} %get-tuple-element.29.refs_5_.refs_3_), custom_call_target="tpu_custom_call" | custom-call | flops 335544320 | bytes 1572864 | tf_op jit(solution)/shard_map/pallas_call | solution.py:130
  28.6 2.0 %collective-permute-done.8.b_ref = bf16[64,512]{1,0:T(8,128)(2,1)S(1)} collective-permute-done((bf16[64,512]{1,0:T(8,128)(2,1)S(1)}, bf16[64,512]{1,0:T(8,128)(2,1)S(1)}, u32[]{:S(2)}, u32[]{:S(2)}) %collective-permute-start.8) | collective-permute-done | bytes 65568 | tf_op jit(solution)/shard_map/ppermute | solution.py:33
  30.6 2.2 %collective-permute-start.9 = (bf16[64,512]{1,0:T(8,128)(2,1)S(1)}, bf16[64,512]{1,0:T(8,128)(2,1)S(1)}, u32[]{:S(2)}, u32[]{:S(2)}) collective-permute-start(bf16[64,512]{1,0:T(8,128)(2,1)S(1)} %shard_map.74.refs_0_), channel_id=1, source_target_pairs={{0,16},{1,9},{2,18},{3,11},{4,20},{5,13},{6,22},{7,15},{8,24},{9,1... | collective-permute-start | bytes 196616 | tf_op jit(solution)/shard_map/ppermute | solution.py:33
  32.8 2.9 %collective-permute-start.12 = (bf16[64,512]{1,0:T(8,128)(2,1)S(1)}, bf16[64,512]{1,0:T(8,128)(2,1)S(1)}, u32[]{:S(2)}, u32[]{:S(2)}) collective-permute-start(bf16[64,512]{1,0:T(8,128)(2,1)S(1)} %shard_map.77.refs_2_), channel_id=1, source_target_pairs={{0,16},{1,9},{2,18},{3,11},{4,20},{5,13},{6,22},{7,15},{8,24},{9,1... | collective-permute-start | bytes 196616 | tf_op jit(solution)/shard_map/ppermute | solution.py:33
  35.9 2.2 %collective-permute-done.12.refs_3_ = bf16[64,512]{1,0:T(8,128)(2,1)S(1)} collective-permute-done((bf16[64,512]{1,0:T(8,128)(2,1)S(1)}, bf16[64,512]{1,0:T(8,128)(2,1)S(1)}, u32[]{:S(2)}, u32[]{:S(2)}) %collective-permute-start.12) | collective-permute-done | bytes 65568 | tf_op jit(solution)/shard_map/ppermute | solution.py:33
  38.1 0.8 %shard_map.78 = f32[64,1024]{1,0:T(8,128)} custom-call(bf16[64,512]{1,0:T(8,128)(2,1)S(1)} %shard_map.74.refs_0_, bf16[64,512]{1,0:T(8,128)(2,1)S(1)} %collective-permute-done.9.refs_1_, bf16[64,512]{1,0:T(8,128)(2,1)S(1)} %shard_map.77.refs_2_, bf16[64,512]{1,0:T(8,128)(2,1)S(1)} %collective-permute-done.12.refs_3_, f32[64,1]{1,0:T(8,128)S(1)} %copy.7.refs_4_), custom_call_target="tpu_custom_call" | custom-call | tf_op jit(solution)/shard_map/pallas_call | solution.py:159
  (22 shorter events, 2.0 us)
Async XLA Ops:
  0.0 15.6 %collective-permute-start = (bf16[1024,1024]{1,0:T(8,128)(2,1)}, bf16[1024,1024]{1,0:T(8,128)(2,1)S(1)}, u32[]{:S(2)}, u32[]{:S(2)}) collective-permute-start(bf16[1024,1024]{1,0:T(8,128)(2,1)} %in_ref.1), channel_id=1, source_target_pairs={{0,1},{1,0},{2,3},{3,2},{4,5},{5,4},{6,7},{7,6},{8,9},{9,8},{10,11... | collective-permute-start | bytes 6291464 | tf_op jit(solution)/shard_map/ppermute | solution.py:18
  1.6 11.8 %collective-permute-start.3 = (bf16[144,1024]{1,0:T(8,128)(2,1)S(1)}, bf16[144,1024]{1,0:T(8,128)(2,1)S(1)}, u32[]{:S(2)}, u32[]{:S(2)}) collective-permute-start(bf16[144,1024]{1,0:T(8,128)(2,1)S(1)} %get-tuple-element.19.refs_2_), channel_id=1, source_target_pairs={{0,4},{1,3},{2,6},{3,1},{4,0},{5,7},{6,2},{7,5},{8,12},{9,11},{10,... | collective-permute-start | bytes 884744 | tf_op jit(solution)/shard_map/ppermute | solution.py:23
  4.2 9.2 %collective-permute-start.2 = (bf16[128,1024]{1,0:T(8,128)(2,1)S(1)}, bf16[128,1024]{1,0:T(8,128)(2,1)S(1)}, u32[]{:S(2)}, u32[]{:S(2)}) collective-permute-start(bf16[128,1024]{1,0:T(8,128)(2,1)S(1)} %get-tuple-element.18.refs_1_), channel_id=1, source_target_pairs={{0,2},{1,5},{2,0},{3,7},{4,6},{5,1},{6,4},{7,3},{8,10},{9,13},{10,... | collective-permute-start | bytes 786440 | tf_op jit(solution)/shard_map/ppermute | solution.py:23
  5.7 13.8 %collective-permute-start.4 = (bf16[144,1024]{1,0:T(8,128)(2,1)S(1)}, bf16[144,1024]{1,0:T(8,128)(2,1)S(1)}, u32[]{:S(2)}, u32[]{:S(2)}) collective-permute-start(bf16[144,1024]{1,0:T(8,128)(2,1)S(1)} %get-tuple-element.19.refs_2_), channel_id=1, source_target_pairs={{0,2},{1,5},{2,0},{3,7},{4,6},{5,1},{6,4},{7,3},{8,10},{9,13},{10,... | collective-permute-start | bytes 884744 | tf_op jit(solution)/shard_map/ppermute | solution.py:23
  6.2 14.8 %collective-permute-start.1 = (bf16[128,1024]{1,0:T(8,128)(2,1)S(1)}, bf16[128,1024]{1,0:T(8,128)(2,1)S(1)}, u32[]{:S(2)}, u32[]{:S(2)}) collective-permute-start(bf16[128,1024]{1,0:T(8,128)(2,1)S(1)} %get-tuple-element.18.refs_1_), channel_id=1, source_target_pairs={{0,4},{1,3},{2,6},{3,1},{4,0},{5,7},{6,2},{7,5},{8,12},{9,11},{10,... | collective-permute-start | bytes 786440 | tf_op jit(solution)/shard_map/ppermute | solution.py:23
  6.3 1.6 %copy-start = (bf16[1024,1024]{1,0:T(8,128)(2,1)S(1)}, bf16[1024,1024]{1,0:T(8,128)(2,1)}, u32[]{:S(2)}) copy-start(bf16[1024,1024]{1,0:T(8,128)(2,1)} %in_ref.1) | copy-start | bytes 6291460
  13.5 9.2 %collective-permute-start.5 = (bf16[128,1024]{1,0:T(8,128)(2,1)S(1)}, bf16[128,1024]{1,0:T(8,128)(2,1)S(1)}, u32[]{:S(2)}, u32[]{:S(2)}) collective-permute-start(bf16[128,1024]{1,0:T(8,128)(2,1)S(1)} %collective-permute-done.2.refs_2_), channel_id=1, source_target_pairs={{0,4},{1,3},{2,6},{3,1},{4,0},{5,7},{6,2},{7,5},{8,12},{9,11},{10,... | collective-permute-start | bytes 786440 | tf_op jit(solution)/shard_map/ppermute | solution.py:23
  13.5 10.0 %collective-permute-start.6 = (bf16[144,1024]{1,0:T(8,128)(2,1)S(1)}, bf16[144,1024]{1,0:T(8,128)(2,1)S(1)}, u32[]{:S(2)}, u32[]{:S(2)}) collective-permute-start(bf16[144,1024]{1,0:T(8,128)(2,1)S(1)} %collective-permute-done.3.refs_3_), channel_id=1, source_target_pairs={{0,2},{1,5},{2,0},{3,7},{4,6},{5,1},{6,4},{7,3},{8,10},{9,13},{10,... | collective-permute-start | bytes 884744 | tf_op jit(solution)/shard_map/ppermute | solution.py:23
  24.0 1.5 %collective-permute-start.7 = (f32[64,512]{1,0:T(8,128)S(1)}, f32[64,512]{1,0:T(8,128)S(1)}, u32[]{:S(2)}, u32[]{:S(2)}) collective-permute-start(f32[64,512]{1,0:T(8,128)S(1)} %shard_map.72), channel_id=1, source_target_pairs={{0,1},{1,0},{2,3},{3,2},{4,5},{5,4},{6,7},{7,6},{8,9},{9,8},{10,11... | collective-permute-start | bytes 393224 | tf_op jit(solution)/shard_map/ppermute | solution.py:18
  25.1 10.6 %copy-start.1 = (f32[64]{0:T(128)S(1)}, f32[64]{0:T(128)}, u32[]{:S(2)}) copy-start(f32[64]{0:T(128)} %param.11) | copy-start | bytes 772
  25.1 3.0 %collective-permute-start.10 = (f32[64,512]{1,0:T(8,128)S(1)}, f32[64,512]{1,0:T(8,128)S(1)}, u32[]{:S(2)}, u32[]{:S(2)}) collective-permute-start(f32[64,512]{1,0:T(8,128)S(1)} %get-tuple-element.30), channel_id=1, source_target_pairs={{0,1},{1,0},{2,3},{3,2},{4,5},{5,4},{6,7},{7,6},{8,9},{9,8},{10,11... | collective-permute-start | bytes 393224 | tf_op jit(solution)/shard_map/ppermute | solution.py:18
  25.6 5.0 %collective-permute-start.8 = (bf16[64,512]{1,0:T(8,128)(2,1)S(1)}, bf16[64,512]{1,0:T(8,128)(2,1)S(1)}, u32[]{:S(2)}, u32[]{:S(2)}) collective-permute-start(bf16[64,512]{1,0:T(8,128)(2,1)S(1)} %shard_map.73.a_ref), channel_id=1, source_target_pairs={{0,8},{1,17},{2,10},{3,19},{4,12},{5,21},{6,14},{7,23},{8,0},{9,25... | collective-permute-start | bytes 196616 | tf_op jit(solution)/shard_map/ppermute | solution.py:33
  28.1 4.8 %collective-permute-start.11 = (bf16[64,512]{1,0:T(8,128)(2,1)S(1)}, bf16[64,512]{1,0:T(8,128)(2,1)S(1)}, u32[]{:S(2)}, u32[]{:S(2)}) collective-permute-start(bf16[64,512]{1,0:T(8,128)(2,1)S(1)} %shard_map.76.a_ref), channel_id=1, source_target_pairs={{0,8},{1,17},{2,10},{3,19},{4,12},{5,21},{6,14},{7,23},{8,0},{9,25... | collective-permute-start | bytes 196616 | tf_op jit(solution)/shard_map/ppermute | solution.py:33
  30.6 5.2 %collective-permute-start.9 = (bf16[64,512]{1,0:T(8,128)(2,1)S(1)}, bf16[64,512]{1,0:T(8,128)(2,1)S(1)}, u32[]{:S(2)}, u32[]{:S(2)}) collective-permute-start(bf16[64,512]{1,0:T(8,128)(2,1)S(1)} %shard_map.74.refs_0_), channel_id=1, source_target_pairs={{0,16},{1,9},{2,18},{3,11},{4,20},{5,13},{6,22},{7,15},{8,24},{9,1... | collective-permute-start | bytes 196616 | tf_op jit(solution)/shard_map/ppermute | solution.py:33
  32.8 5.2 %collective-permute-start.12 = (bf16[64,512]{1,0:T(8,128)(2,1)S(1)}, bf16[64,512]{1,0:T(8,128)(2,1)S(1)}, u32[]{:S(2)}, u32[]{:S(2)}) collective-permute-start(bf16[64,512]{1,0:T(8,128)(2,1)S(1)} %shard_map.77.refs_2_), channel_id=1, source_target_pairs={{0,16},{1,9},{2,18},{3,11},{4,20},{5,13},{6,22},{7,15},{8,24},{9,1... | collective-permute-start | bytes 196616 | tf_op jit(solution)/shard_map/ppermute | solution.py:33

commit v11 on v9

--- a/solution.py
+++ b/solution.py
@@ -189,13 +189,14 @@
     blocks = {0: [first, second]}
     for k in range(ways):
         blocks[1 << k] = [None, None]
-    for turn in (0, 1):
-        for k in range(ways):
-            piece = (k + turn) % 2
-            blocks[1 << k][piece] = chip_send(blocks[0][piece], k, n_sl)
+    for k in range(ways):
+        blocks[1 << k][k % 2] = chip_send(blocks[0][k % 2], k, n_sl)
     turned = jax.ShapeDtypeStruct(slab.shape[::-1], slab.dtype)
     other = small_call(transpose_kernel, turned, core_send(slab, n_sl))
     slab = small_call(transpose_kernel, turned, slab)
+    later, slab = lax.optimization_barrier((blocks[0], slab))
+    for k in range(ways):
+        blocks[1 << k][1 - k % 2] = chip_send(later[1 - k % 2], k, n_sl)
     (acc,) = stage([slab], first, second, None, coeff, cols)
     held = [blocks[1 << k][k % 2] for k in range(ways)]
     held, acc = lax.optimization_barrier((held, acc))

time: 38.9 us -> 39.3 us (1.010)
  starting transfers between devices: 15.7 us -> 17 us
  waiting for transfers between devices: 10.3 us -> 9.37 us
    ppermute x6, starting transfers between devices: 7.44 us -> 8.64 us  [chip_send(): lax.ppermute(value, 'sl', [(i, i ^ bits[(k + i % 2) % len(bits)]) for i i...]
    ppermute x6, waiting for transfers between devices: 5.84 us -> 4.82 us  [chip_send(): lax.ppermute(value, 'sl', [(i, i ^ bits[(k + i % 2) % len(bits)]) for i i...]
  transfers between devices with their start and end apart: 13 -> 13, of which waited for: 7 -> 7; matrix products, arithmetic and copies ran while one was open for 0% -> 0% of each run, Pallas kernels for 25% -> 24%
where the time goes in v11:
time: 39.3 us; the launch traced here: 39.1 us
  starting transfers between devices  17 us (43%)
  Pallas kernels  10.9 us (28%)
  waiting for transfers between devices  9.37 us (24%)
  local copies, waits for them, and re-layouts  1.69 us (4%)
    ppermute x6, starting transfers between devices, chip_send(): lax.ppermute(value, 'sl', [(i, i ^ bits[(k + i % 2) % len(bits)]) for i i...  8.64 us
    ppermute x4, starting transfers between devices, lm_send(): return lax.ppermute(value, ('lm', 'sl'), perm)  7.32 us
    pallas_call x7, Pallas kernels, stage(): pl.pallas_call(functools.partial(stage_kernel, count, coeff, ritz, accs i...  6.83 us
    ppermute x6, waiting for transfers between devices, chip_send(): lax.ppermute(value, 'sl', [(i, i ^ bits[(k + i % 2) % len(bits)]) for i i...  4.82 us
    ppermute x4, waiting for transfers between devices, lm_send(): return lax.ppermute(value, ('lm', 'sl'), perm)  4.54 us
    pallas_call x7, Pallas kernels, small_call(): pl.pallas_call(kernel, out_shape=jax.ShapeDtypeStruct(out.shape, out.dtyp...  2.13 us
    unnamed x4, local copies, waits for them, and re-layouts  1.59 us
    ppermute x3, starting transfers between devices, core_send(): return lax.ppermute(value, 'sl', [(i, i ^ 1) for i in range(n)])  1.08 us
  transfers between devices with their start and end apart: 13, of which 7 were waited for; matrix products, arithmetic and copies ran while one was open for 0% of the time, Pallas kernels for 24%

profile of v11, /device:TPU:0, one launch (start us, length us, event | category | flops | bytes accessed | tf_op | source)
XLA Modules:
  0.0 39.1 jit_solution(9186429450710309643)
XLA Ops:
  0.5 1.0 %shard_map.65.refs_2_ = bf16[144,1024]{1,0:T(8,128)(2,1)S(1)} custom-call(bf16[256,1024]{1,0:T(8,128)(2,1)} %land_ref.3), custom_call_target="tpu_custom_call" | custom-call | tf_op jit(solution)/shard_map/pallas_call | solution.py:75
  1.4 2.6 %collective-permute-start.3 = (bf16[144,1024]{1,0:T(8,128)(2,1)S(1)}, bf16[144,1024]{1,0:T(8,128)(2,1)S(1)}, u32[]{:S(2)}, u32[]{:S(2)}) collective-permute-start(bf16[144,1024]{1,0:T(8,128)(2,1)S(1)} %shard_map.65.refs_2_), channel_id=1, source_target_pairs={{0,4},{1,3},{2,6},{3,1},{4,0},{5,7},{6,2},{7,5},{8,12},{9,11},{10,... | collective-permute-start | bytes 884744 | tf_op jit(solution)/shard_map/ppermute | solution.py:23
  4.0 1.0 %shard_map.64.refs_1_ = bf16[128,1024]{1,0:T(8,128)(2,1)S(1)} custom-call(bf16[256,1024]{1,0:T(8,128)(2,1)} %land_ref.3, bf16[96,256]{1,0:T(8,128)(2,1)} %bitcast.4, s32[2]{0:T(128)} %exponents_ref.1, bf16[64,96]{1,0:T(8,128)(2,1)} %bitcast.5), custom_call_target="tpu_custom_call" | custom-call | tf_op jit(solution)/shard_map/pallas_call | solution.py:87
  5.0 1.6 %collective-permute-start.2 = (bf16[128,1024]{1,0:T(8,128)(2,1)S(1)}, bf16[128,1024]{1,0:T(8,128)(2,1)S(1)}, u32[]{:S(2)}, u32[]{:S(2)}) collective-permute-start(bf16[128,1024]{1,0:T(8,128)(2,1)S(1)} %shard_map.64.refs_1_), channel_id=1, source_target_pairs={{0,2},{1,5},{2,0},{3,7},{4,6},{5,1},{6,4},{7,3},{8,10},{9,13},{10,... | collective-permute-start | bytes 786440 | tf_op jit(solution)/shard_map/ppermute | solution.py:23
  6.6 1.6 %copy-done = bf16[1024,1024]{1,0:T(8,128)(2,1)S(1)} copy-done((bf16[1024,1024]{1,0:T(8,128)(2,1)S(1)}, bf16[1024,1024]{1,0:T(8,128)(2,1)}, u32[]{:S(2)}) %copy-start) | copy-done | bytes 2097176
  8.2 0.6 %shard_map.66.refs_0_.refs_1_ = bf16[1024,1024]{1,0:T(8,128)(2,1)S(1)} custom-call(bf16[1024,1024]{1,0:T(8,128)(2,1)S(1)} %copy-done), custom_call_target="tpu_custom_call" | custom-call | tf_op jit(solution)/shard_map/pallas_call | solution.py:172
  8.8 0.6 %collective-permute-start.4 = (bf16[144,1024]{1,0:T(8,128)(2,1)S(1)}, bf16[144,1024]{1,0:T(8,128)(2,1)S(1)}, u32[]{:S(2)}, u32[]{:S(2)}) collective-permute-start(bf16[144,1024]{1,0:T(8,128)(2,1)S(1)} %shard_map.65.refs_2_), channel_id=1, source_target_pairs={{0,2},{1,5},{2,0},{3,7},{4,6},{5,1},{6,4},{7,3},{8,10},{9,13},{10,... | collective-permute-start | bytes 884744 | tf_op jit(solution)/shard_map/ppermute | solution.py:23
  9.5 0.9 %shard_map.68.refs_4_ = f32[64,1024]{1,0:T(8,128)S(1)} custom-call(bf16[1024,1024]{1,0:T(8,128)(2,1)S(1)} %shard_map.66.refs_0_.refs_1_, bf16[128,1024]{1,0:T(8,128)(2,1)S(1)} %shard_map.64.refs_1_, bf16[144,1024]{1,0:T(8,128)(2,1)S(1)} %shard_map.65.refs_2_), custom_call_target="tpu_custom_call" | custom-call | flops 671088640 | bytes 2621440 | tf_op jit(solution)/shard_map/pallas_call | solution.py:143
  10.3 1.2 %collective-permute-done.2.refs_2_ = bf16[128,1024]{1,0:T(8,128)(2,1)S(1)} collective-permute-done((bf16[128,1024]{1,0:T(8,128)(2,1)S(1)}, bf16[128,1024]{1,0:T(8,128)(2,1)S(1)}, u32[]{:S(2)}, u32[]{:S(2)}) %collective-permute-start.2) | collective-permute-done | bytes 262176 | tf_op jit(solution)/shard_map/ppermute | solution.py:23
  11.5 1.6 %collective-permute-start.5 = (bf16[128,1024]{1,0:T(8,128)(2,1)S(1)}, bf16[128,1024]{1,0:T(8,128)(2,1)S(1)}, u32[]{:S(2)}, u32[]{:S(2)}) collective-permute-start(bf16[128,1024]{1,0:T(8,128)(2,1)S(1)} %collective-permute-done.2.refs_2_), channel_id=1, source_target_pairs={{0,4},{1,3},{2,6},{3,1},{4,0},{5,7},{6,2},{7,5},{8,12},{9,11},{10,... | collective-permute-start | bytes 786440 | tf_op jit(solution)/shard_map/ppermute | solution.py:23
  13.1 2.3 %collective-permute-start.6 = (bf16[144,1024]{1,0:T(8,128)(2,1)S(1)}, bf16[144,1024]{1,0:T(8,128)(2,1)S(1)}, u32[]{:S(2)}, u32[]{:S(2)}) collective-permute-start(bf16[144,1024]{1,0:T(8,128)(2,1)S(1)} %collective-permute-done.3.refs_3_), channel_id=1, source_target_pairs={{0,2},{1,5},{2,0},{3,7},{4,6},{5,1},{6,4},{7,3},{8,10},{9,13},{10,... | collective-permute-start | bytes 884744 | tf_op jit(solution)/shard_map/ppermute | solution.py:23
  15.4 0.6 %shard_map.67.refs_0_.refs_1_ = bf16[1024,1024]{1,0:T(8,128)(2,1)S(1)} custom-call(bf16[1024,1024]{1,0:T(8,128)(2,1)S(1)} %collective-permute-done.in_ref), custom_call_target="tpu_custom_call" | custom-call | tf_op jit(solution)/shard_map/pallas_call | solution.py:172
  16.0 0.9 %shard_map.69.refs_5_ = f32[64,1024]{1,0:T(8,128)S(1)} custom-call(bf16[1024,1024]{1,0:T(8,128)(2,1)S(1)} %shard_map.67.refs_0_.refs_1_, bf16[128,1024]{1,0:T(8,128)(2,1)S(1)} %shard_map.64.refs_1_, bf16[144,1024]{1,0:T(8,128)(2,1)S(1)} %shard_map.65.refs_2_), custom_call_target="tpu_custom_call" | custom-call | flops 671088640 | bytes 2621440 | tf_op jit(solution)/shard_map/pallas_call | solution.py:143
  16.9 1.9 %collective-permute-done.4.refs_3_ = bf16[144,1024]{1,0:T(8,128)(2,1)S(1)} collective-permute-done((bf16[144,1024]{1,0:T(8,128)(2,1)S(1)}, bf16[144,1024]{1,0:T(8,128)(2,1)S(1)}, u32[]{:S(2)}, u32[]{:S(2)}) %collective-permute-start.4) | collective-permute-done | bytes 294944 | tf_op jit(solution)/shard_map/ppermute | solution.py:23
  18.7 1.5 %shard_map.70 = (f32[64,1024]{1,0:T(8,128)S(1)}, f32[64,1024]{1,0:T(8,128)S(1)}) custom-call(bf16[1024,1024]{1,0:T(8,128)(2,1)S(1)} %shard_map.66.refs_0_.refs_1_, bf16[1024,1024]{1,0:T(8,128)(2,1)S(1)} %shard_map.67.refs_0_.refs_1_, bf16[128,1024]{1,0:T(8,128)(2,1)S(1)} %collective-permute-done.2.refs_2_, ...), custom_call_target="tpu_custom_call" | custom-call | flops 1342177280 | bytes 4718592 | tf_op jit(solution)/shard_map/pallas_call | solution.py:143
  20.3 1.5 %shard_map.71 = (f32[64,1024]{1,0:T(8,128)S(1)}, f32[64,1024]{1,0:T(8,128)S(1)}) custom-call(bf16[1024,1024]{1,0:T(8,128)(2,1)S(1)} %shard_map.66.refs_0_.refs_1_, bf16[1024,1024]{1,0:T(8,128)(2,1)S(1)} %shard_map.67.refs_0_.refs_1_, bf16[128,1024]{1,0:T(8,128)(2,1)S(1)} %collective-permute-done.1.refs_2_, ...), custom_call_target="tpu_custom_call" | custom-call | flops 1342177280 | bytes 4718592 | tf_op jit(solution)/shard_map/pallas_call | solution.py:143
  21.8 1.6 %collective-permute-done.5.refs_2_.refs_1_ = bf16[128,1024]{1,0:T(8,128)(2,1)S(1)} collective-permute-done((bf16[128,1024]{1,0:T(8,128)(2,1)S(1)}, bf16[128,1024]{1,0:T(8,128)(2,1)S(1)}, u32[]{:S(2)}, u32[]{:S(2)}) %collective-permute-start.5) | collective-permute-done | bytes 262176 | tf_op jit(solution)/shard_map/ppermute | solution.py:23
  24.3 0.9 %shard_map.72 = (f32[64,512]{1,0:T(8,128)S(1)}, f32[64,512]{1,0:T(8,128)S(1)}) custom-call(bf16[1024,1024]{1,0:T(8,128)(2,1)S(1)} %shard_map.67.refs_0_.refs_1_, bf16[1024,1024]{1,0:T(8,128)(2,1)S(1)} %shard_map.66.refs_0_.refs_1_, bf16[128,1024]{1,0:T(8,128)(2,1)S(1)} %collective-permute-done.5.refs_2_.refs_1_, ...), custom_call_target="tpu_custom_call" | custom-call | flops 671088640 | bytes 2621440 | tf_op jit(solution)/shard_map/pallas_call | solution.py:143
  25.7 2.0 %collective-permute-start.8 = (bf16[64,512]{1,0:T(8,128)(2,1)S(1)}, bf16[64,512]{1,0:T(8,128)(2,1)S(1)}, u32[]{:S(2)}, u32[]{:S(2)}) collective-permute-start(bf16[64,512]{1,0:T(8,128)(2,1)S(1)} %shard_map.74.a_ref), channel_id=1, source_target_pairs={{0,8},{1,17},{2,10},{3,19},{4,12},{5,21},{6,14},{7,23},{8,0},{9,25... | collective-permute-start | bytes 196616 | tf_op jit(solution)/shard_map/ppermute | solution.py:33
  28.7 2.0 %collective-permute-done.8.b_ref = bf16[64,512]{1,0:T(8,128)(2,1)S(1)} collective-permute-done((bf16[64,512]{1,0:T(8,128)(2,1)S(1)}, bf16[64,512]{1,0:T(8,128)(2,1)S(1)}, u32[]{:S(2)}, u32[]{:S(2)}) %collective-permute-start.8) | collective-permute-done | bytes 65568 | tf_op jit(solution)/shard_map/ppermute | solution.py:33
  30.8 2.3 %collective-permute-start.9 = (bf16[64,512]{1,0:T(8,128)(2,1)S(1)}, bf16[64,512]{1,0:T(8,128)(2,1)S(1)}, u32[]{:S(2)}, u32[]{:S(2)}) collective-permute-start(bf16[64,512]{1,0:T(8,128)(2,1)S(1)} %shard_map.75.refs_0_), channel_id=1, source_target_pairs={{0,16},{1,9},{2,18},{3,11},{4,20},{5,13},{6,22},{7,15},{8,24},{9,1... | collective-permute-start | bytes 196616 | tf_op jit(solution)/shard_map/ppermute | solution.py:33
  33.1 2.6 %collective-permute-start.12 = (bf16[64,512]{1,0:T(8,128)(2,1)S(1)}, bf16[64,512]{1,0:T(8,128)(2,1)S(1)}, u32[]{:S(2)}, u32[]{:S(2)}) collective-permute-start(bf16[64,512]{1,0:T(8,128)(2,1)S(1)} %shard_map.78.refs_2_), channel_id=1, source_target_pairs={{0,16},{1,9},{2,18},{3,11},{4,20},{5,13},{6,22},{7,15},{8,24},{9,1... | collective-permute-start | bytes 196616 | tf_op jit(solution)/shard_map/ppermute | solution.py:33
  36.0 2.3 %collective-permute-done.12.refs_3_ = bf16[64,512]{1,0:T(8,128)(2,1)S(1)} collective-permute-done((bf16[64,512]{1,0:T(8,128)(2,1)S(1)}, bf16[64,512]{1,0:T(8,128)(2,1)S(1)}, u32[]{:S(2)}, u32[]{:S(2)}) %collective-permute-start.12) | collective-permute-done | bytes 65568 | tf_op jit(solution)/shard_map/ppermute | solution.py:33
  38.4 0.8 %shard_map.79 = f32[64,1024]{1,0:T(8,128)} custom-call(bf16[64,512]{1,0:T(8,128)(2,1)S(1)} %shard_map.75.refs_0_, bf16[64,512]{1,0:T(8,128)(2,1)S(1)} %collective-permute-done.9.refs_1_, bf16[64,512]{1,0:T(8,128)(2,1)S(1)} %shard_map.78.refs_2_, bf16[64,512]{1,0:T(8,128)(2,1)S(1)} %collective-permute-done.12.refs_3_, f32[64,1]{1,0:T(8,128)S(1)} %copy.7.refs_4_), custom_call_target="tpu_custom_call" | custom-call | tf_op jit(solution)/shard_map/pallas_call | solution.py:172
  (23 shorter events, 3.1 us)
Async XLA Ops:
  0.0 15.4 %collective-permute-start = (bf16[1024,1024]{1,0:T(8,128)(2,1)}, bf16[1024,1024]{1,0:T(8,128)(2,1)S(1)}, u32[]{:S(2)}, u32[]{:S(2)}) collective-permute-start(bf16[1024,1024]{1,0:T(8,128)(2,1)} %in_ref.1), channel_id=1, source_target_pairs={{0,1},{1,0},{2,3},{3,2},{4,5},{5,4},{6,7},{7,6},{8,9},{9,8},{10,11... | collective-permute-start | bytes 6291464 | tf_op jit(solution)/shard_map/ppermute | solution.py:18
  1.4 10.1 %collective-permute-start.3 = (bf16[144,1024]{1,0:T(8,128)(2,1)S(1)}, bf16[144,1024]{1,0:T(8,128)(2,1)S(1)}, u32[]{:S(2)}, u32[]{:S(2)}) collective-permute-start(bf16[144,1024]{1,0:T(8,128)(2,1)S(1)} %shard_map.65.refs_2_), channel_id=1, source_target_pairs={{0,4},{1,3},{2,6},{3,1},{4,0},{5,7},{6,2},{7,5},{8,12},{9,11},{10,... | collective-permute-start | bytes 884744 | tf_op jit(solution)/shard_map/ppermute | solution.py:23
  5.0 6.5 %collective-permute-start.2 = (bf16[128,1024]{1,0:T(8,128)(2,1)S(1)}, bf16[128,1024]{1,0:T(8,128)(2,1)S(1)}, u32[]{:S(2)}, u32[]{:S(2)}) collective-permute-start(bf16[128,1024]{1,0:T(8,128)(2,1)S(1)} %shard_map.64.refs_1_), channel_id=1, source_target_pairs={{0,2},{1,5},{2,0},{3,7},{4,6},{5,1},{6,4},{7,3},{8,10},{9,13},{10,... | collective-permute-start | bytes 786440 | tf_op jit(solution)/shard_map/ppermute | solution.py:23
  6.6 1.6 %copy-start = (bf16[1024,1024]{1,0:T(8,128)(2,1)S(1)}, bf16[1024,1024]{1,0:T(8,128)(2,1)}, u32[]{:S(2)}) copy-start(bf16[1024,1024]{1,0:T(8,128)(2,1)} %in_ref.1) | copy-start | bytes 6291460
  8.8 9.9 %collective-permute-start.4 = (bf16[144,1024]{1,0:T(8,128)(2,1)S(1)}, bf16[144,1024]{1,0:T(8,128)(2,1)S(1)}, u32[]{:S(2)}, u32[]{:S(2)}) collective-permute-start(bf16[144,1024]{1,0:T(8,128)(2,1)S(1)} %shard_map.65.refs_2_), channel_id=1, source_target_pairs={{0,2},{1,5},{2,0},{3,7},{4,6},{5,1},{6,4},{7,3},{8,10},{9,13},{10,... | collective-permute-start | bytes 884744 | tf_op jit(solution)/shard_map/ppermute | solution.py:23
  9.4 10.9 %collective-permute-start.1 = (bf16[128,1024]{1,0:T(8,128)(2,1)S(1)}, bf16[128,1024]{1,0:T(8,128)(2,1)S(1)}, u32[]{:S(2)}, u32[]{:S(2)}) collective-permute-start(bf16[128,1024]{1,0:T(8,128)(2,1)S(1)} %shard_map.64.refs_1_), channel_id=1, source_target_pairs={{0,4},{1,3},{2,6},{3,1},{4,0},{5,7},{6,2},{7,5},{8,12},{9,11},{10,... | collective-permute-start | bytes 786440 | tf_op jit(solution)/shard_map/ppermute | solution.py:23
  11.5 11.9 %collective-permute-start.5 = (bf16[128,1024]{1,0:T(8,128)(2,1)S(1)}, bf16[128,1024]{1,0:T(8,128)(2,1)S(1)}, u32[]{:S(2)}, u32[]{:S(2)}) collective-permute-start(bf16[128,1024]{1,0:T(8,128)(2,1)S(1)} %collective-permute-done.2.refs_2_), channel_id=1, source_target_pairs={{0,4},{1,3},{2,6},{3,1},{4,0},{5,7},{6,2},{7,5},{8,12},{9,11},{10,... | collective-permute-start | bytes 786440 | tf_op jit(solution)/shard_map/ppermute | solution.py:23
  13.1 10.5 %collective-permute-start.6 = (bf16[144,1024]{1,0:T(8,128)(2,1)S(1)}, bf16[144,1024]{1,0:T(8,128)(2,1)S(1)}, u32[]{:S(2)}, u32[]{:S(2)}) collective-permute-start(bf16[144,1024]{1,0:T(8,128)(2,1)S(1)} %collective-permute-done.3.refs_3_), channel_id=1, source_target_pairs={{0,2},{1,5},{2,0},{3,7},{4,6},{5,1},{6,4},{7,3},{8,10},{9,13},{10,... | collective-permute-start | bytes 884744 | tf_op jit(solution)/shard_map/ppermute | solution.py:23
  24.2 1.5 %collective-permute-start.7 = (f32[64,512]{1,0:T(8,128)S(1)}, f32[64,512]{1,0:T(8,128)S(1)}, u32[]{:S(2)}, u32[]{:S(2)}) collective-permute-start(f32[64,512]{1,0:T(8,128)S(1)} %shard_map.73), channel_id=1, source_target_pairs={{0,1},{1,0},{2,3},{3,2},{4,5},{5,4},{6,7},{7,6},{8,9},{9,8},{10,11... | collective-permute-start | bytes 393224 | tf_op jit(solution)/shard_map/ppermute | solution.py:18
  25.1 10.6 %copy-start.1 = (f32[64]{0:T(128)S(1)}, f32[64]{0:T(128)}, u32[]{:S(2)}) copy-start(f32[64]{0:T(128)} %param.11) | copy-start | bytes 772
  25.1 3.2 %collective-permute-start.10 = (f32[64,512]{1,0:T(8,128)S(1)}, f32[64,512]{1,0:T(8,128)S(1)}, u32[]{:S(2)}, u32[]{:S(2)}) collective-permute-start(f32[64,512]{1,0:T(8,128)S(1)} %get-tuple-element.32), channel_id=1, source_target_pairs={{0,1},{1,0},{2,3},{3,2},{4,5},{5,4},{6,7},{7,6},{8,9},{9,8},{10,11... | collective-permute-start | bytes 393224 | tf_op jit(solution)/shard_map/ppermute | solution.py:18
  25.7 5.0 %collective-permute-start.8 = (bf16[64,512]{1,0:T(8,128)(2,1)S(1)}, bf16[64,512]{1,0:T(8,128)(2,1)S(1)}, u32[]{:S(2)}, u32[]{:S(2)}) collective-permute-start(bf16[64,512]{1,0:T(8,128)(2,1)S(1)} %shard_map.74.a_ref), channel_id=1, source_target_pairs={{0,8},{1,17},{2,10},{3,19},{4,12},{5,21},{6,14},{7,23},{8,0},{9,25... | collective-permute-start | bytes 196616 | tf_op jit(solution)/shard_map/ppermute | solution.py:33
  28.4 4.7 %collective-permute-start.11 = (bf16[64,512]{1,0:T(8,128)(2,1)S(1)}, bf16[64,512]{1,0:T(8,128)(2,1)S(1)}, u32[]{:S(2)}, u32[]{:S(2)}) collective-permute-start(bf16[64,512]{1,0:T(8,128)(2,1)S(1)} %shard_map.77.a_ref), channel_id=1, source_target_pairs={{0,8},{1,17},{2,10},{3,19},{4,12},{5,21},{6,14},{7,23},{8,0},{9,25... | collective-permute-start | bytes 196616 | tf_op jit(solution)/shard_map/ppermute | solution.py:33
  30.8 5.2 %collective-permute-start.9 = (bf16[64,512]{1,0:T(8,128)(2,1)S(1)}, bf16[64,512]{1,0:T(8,128)(2,1)S(1)}, u32[]{:S(2)}, u32[]{:S(2)}) collective-permute-start(bf16[64,512]{1,0:T(8,128)(2,1)S(1)} %shard_map.75.refs_0_), channel_id=1, source_target_pairs={{0,16},{1,9},{2,18},{3,11},{4,20},{5,13},{6,22},{7,15},{8,24},{9,1... | collective-permute-start | bytes 196616 | tf_op jit(solution)/shard_map/ppermute | solution.py:33
  33.1 5.2 %collective-permute-start.12 = (bf16[64,512]{1,0:T(8,128)(2,1)S(1)}, bf16[64,512]{1,0:T(8,128)(2,1)S(1)}, u32[]{:S(2)}, u32[]{:S(2)}) collective-permute-start(bf16[64,512]{1,0:T(8,128)(2,1)S(1)} %shard_map.78.refs_2_), channel_id=1, source_target_pairs={{0,16},{1,9},{2,18},{3,11},{4,20},{5,13},{6,22},{7,15},{8,24},{9,1... | collective-permute-start | bytes 196616 | tf_op jit(solution)/shard_map/ppermute | solution.py:33

commit v12 on v1

--- a/solution.py
+++ b/solution.py
@@ -20,7 +20,7 @@
 
 def chip_send(value, k, n):
     bits = [1 << b for b in range(1, n.bit_length() - 1)]
-    return lax.ppermute(value, "sl", [(i, i ^ bits[(k + i % 2) % len(bits)]) for i in range(n)])
+    return lax.ppermute(value, "sl", [(i, i ^ bits[(k + 1 - i % 2) % len(bits)]) for i in range(n)])
 
 
 def lm_send(value, k, n_lm, n_sl):

time: 38.9 us -> 38.9 us (level)
  no operation moved by 1% of the time
where the time goes in v12:
time: 38.9 us; the launch traced here: 38.7 us
  starting transfers between devices  15.8 us (41%)
  Pallas kernels  10.9 us (28%)
  waiting for transfers between devices  10.1 us (26%)
  local copies, waits for them, and re-layouts  1.69 us (4%)
    ppermute x6, starting transfers between devices, chip_send(): lax.ppermute(value, 'sl', [(i, i ^ bits[(k + 1 - i % 2) % len(bits)]) for...  7.51 us
    ppermute x4, starting transfers between devices, lm_send(): return lax.ppermute(value, ('lm', 'sl'), perm)  7.16 us
    pallas_call x7, Pallas kernels, stage(): pl.pallas_call(functools.partial(stage_kernel, count, coeff, ritz, accs i...  6.82 us
    ppermute x6, waiting for transfers between devices, chip_send(): lax.ppermute(value, 'sl', [(i, i ^ bits[(k + 1 - i % 2) % len(bits)]) for...  5.75 us
    ppermute x4, waiting for transfers between devices, lm_send(): return lax.ppermute(value, ('lm', 'sl'), perm)  4.37 us
    pallas_call x7, Pallas kernels, small_call(): pl.pallas_call(kernel, out_shape=jax.ShapeDtypeStruct(out.shape, out.dtyp...  2.13 us
    unnamed x4, local copies, waits for them, and re-layouts  1.59 us
    ppermute x3, starting transfers between devices, core_send(): return lax.ppermute(value, 'sl', [(i, i ^ 1) for i in range(n)])  1.15 us
  transfers between devices with their start and end apart: 13, of which 7 were waited for; matrix products, arithmetic and copies ran while one was open for 0% of the time, Pallas kernels for 22%

profile of v12, /device:TPU:0, one launch (start us, length us, event | category | flops | bytes accessed | tf_op | source)
XLA Modules:
  0.0 38.7 jit_solution(6344773502512400665)
XLA Ops:
  0.0 1.0 %shard_map.65.refs_2_ = bf16[144,1024]{1,0:T(8,128)(2,1)S(1)} custom-call(bf16[256,1024]{1,0:T(8,128)(2,1)} %land_ref.3), custom_call_target="tpu_custom_call" | custom-call | tf_op jit(solution)/shard_map/pallas_call | solution.py:75
  1.5 2.6 %collective-permute-start.3 = (bf16[144,1024]{1,0:T(8,128)(2,1)S(1)}, bf16[144,1024]{1,0:T(8,128)(2,1)S(1)}, u32[]{:S(2)}, u32[]{:S(2)}) collective-permute-start(bf16[144,1024]{1,0:T(8,128)(2,1)S(1)} %shard_map.65.refs_2_), channel_id=1, source_target_pairs={{0,2},{1,5},{2,0},{3,7},{4,6},{5,1},{6,4},{7,3},{8,10},{9,13},{10,... | collective-permute-start | bytes 884744 | tf_op jit(solution)/shard_map/ppermute | solution.py:23
  4.1 1.0 %shard_map.67.refs_1_ = bf16[128,1024]{1,0:T(8,128)(2,1)S(1)} custom-call(bf16[256,1024]{1,0:T(8,128)(2,1)} %land_ref.3, bf16[96,256]{1,0:T(8,128)(2,1)} %bitcast.4, s32[2]{0:T(128)} %exponents_ref.1, bf16[64,96]{1,0:T(8,128)(2,1)} %bitcast.5), custom_call_target="tpu_custom_call" | custom-call | tf_op jit(solution)/shard_map/pallas_call | solution.py:87
  5.1 1.6 %collective-permute-start.2 = (bf16[128,1024]{1,0:T(8,128)(2,1)S(1)}, bf16[128,1024]{1,0:T(8,128)(2,1)S(1)}, u32[]{:S(2)}, u32[]{:S(2)}) collective-permute-start(bf16[128,1024]{1,0:T(8,128)(2,1)S(1)} %shard_map.67.refs_1_), channel_id=1, source_target_pairs={{0,4},{1,3},{2,6},{3,1},{4,0},{5,7},{6,2},{7,5},{8,12},{9,11},{10,... | collective-permute-start | bytes 786440 | tf_op jit(solution)/shard_map/ppermute | solution.py:23
  7.3 1.6 %copy-done = bf16[1024,1024]{1,0:T(8,128)(2,1)S(1)} copy-done((bf16[1024,1024]{1,0:T(8,128)(2,1)S(1)}, bf16[1024,1024]{1,0:T(8,128)(2,1)}, u32[]{:S(2)}) %copy-start) | copy-done | bytes 2097176
  8.9 0.6 %shard_map.64.refs_0_.refs_1_ = bf16[1024,1024]{1,0:T(8,128)(2,1)S(1)} custom-call(bf16[1024,1024]{1,0:T(8,128)(2,1)S(1)} %copy-done), custom_call_target="tpu_custom_call" | custom-call | tf_op jit(solution)/shard_map/pallas_call | solution.py:172
  9.5 0.9 %shard_map.68.refs_4_ = f32[64,1024]{1,0:T(8,128)S(1)} custom-call(bf16[1024,1024]{1,0:T(8,128)(2,1)S(1)} %shard_map.64.refs_0_.refs_1_, bf16[128,1024]{1,0:T(8,128)(2,1)S(1)} %shard_map.67.refs_1_, bf16[144,1024]{1,0:T(8,128)(2,1)S(1)} %shard_map.65.refs_2_), custom_call_target="tpu_custom_call" | custom-call | flops 671088640 | bytes 2621440 | tf_op jit(solution)/shard_map/pallas_call | solution.py:143
  10.4 3.3 %collective-permute-done.2.refs_2_ = bf16[128,1024]{1,0:T(8,128)(2,1)S(1)} collective-permute-done((bf16[128,1024]{1,0:T(8,128)(2,1)S(1)}, bf16[128,1024]{1,0:T(8,128)(2,1)S(1)}, u32[]{:S(2)}, u32[]{:S(2)}) %collective-permute-start.2) | collective-permute-done | bytes 262176 | tf_op jit(solution)/shard_map/ppermute | solution.py:23
  13.7 0.7 %collective-permute-start.5 = (bf16[128,1024]{1,0:T(8,128)(2,1)S(1)}, bf16[128,1024]{1,0:T(8,128)(2,1)S(1)}, u32[]{:S(2)}, u32[]{:S(2)}) collective-permute-start(bf16[128,1024]{1,0:T(8,128)(2,1)S(1)} %collective-permute-done.2.refs_2_), channel_id=1, source_target_pairs={{0,2},{1,5},{2,0},{3,7},{4,6},{5,1},{6,4},{7,3},{8,10},{9,13},{10,... | collective-permute-start | bytes 786440 | tf_op jit(solution)/shard_map/ppermute | solution.py:23
  14.4 2.0 %collective-permute-start.6 = (bf16[144,1024]{1,0:T(8,128)(2,1)S(1)}, bf16[144,1024]{1,0:T(8,128)(2,1)S(1)}, u32[]{:S(2)}, u32[]{:S(2)}) collective-permute-start(bf16[144,1024]{1,0:T(8,128)(2,1)S(1)} %collective-permute-done.3.refs_3_), channel_id=1, source_target_pairs={{0,4},{1,3},{2,6},{3,1},{4,0},{5,7},{6,2},{7,5},{8,12},{9,11},{10,... | collective-permute-start | bytes 884744 | tf_op jit(solution)/shard_map/ppermute | solution.py:23
  16.5 0.6 %shard_map.66.refs_0_.refs_1_ = bf16[1024,1024]{1,0:T(8,128)(2,1)S(1)} custom-call(bf16[1024,1024]{1,0:T(8,128)(2,1)S(1)} %collective-permute-done.in_ref), custom_call_target="tpu_custom_call" | custom-call | tf_op jit(solution)/shard_map/pallas_call | solution.py:172
  17.1 0.9 %shard_map.69.refs_5_ = f32[64,1024]{1,0:T(8,128)S(1)} custom-call(bf16[1024,1024]{1,0:T(8,128)(2,1)S(1)} %shard_map.66.refs_0_.refs_1_, bf16[128,1024]{1,0:T(8,128)(2,1)S(1)} %shard_map.67.refs_1_, bf16[144,1024]{1,0:T(8,128)(2,1)S(1)} %shard_map.65.refs_2_), custom_call_target="tpu_custom_call" | custom-call | flops 671088640 | bytes 2621440 | tf_op jit(solution)/shard_map/pallas_call | solution.py:143
  18.0 1.6 %collective-permute-done.4.refs_3_ = bf16[144,1024]{1,0:T(8,128)(2,1)S(1)} collective-permute-done((bf16[144,1024]{1,0:T(8,128)(2,1)S(1)}, bf16[144,1024]{1,0:T(8,128)(2,1)S(1)}, u32[]{:S(2)}, u32[]{:S(2)}) %collective-permute-start.4) | collective-permute-done | bytes 294944 | tf_op jit(solution)/shard_map/ppermute | solution.py:23
  19.6 1.5 %shard_map.70 = (f32[64,1024]{1,0:T(8,128)S(1)}, f32[64,1024]{1,0:T(8,128)S(1)}) custom-call(bf16[1024,1024]{1,0:T(8,128)(2,1)S(1)} %shard_map.64.refs_0_.refs_1_, bf16[1024,1024]{1,0:T(8,128)(2,1)S(1)} %shard_map.66.refs_0_.refs_1_, bf16[128,1024]{1,0:T(8,128)(2,1)S(1)} %collective-permute-done.2.refs_2_, ...), custom_call_target="tpu_custom_call" | custom-call | flops 1342177280 | bytes 4718592 | tf_op jit(solution)/shard_map/pallas_call | solution.py:143
  21.1 1.5 %shard_map.71 = (f32[64,1024]{1,0:T(8,128)S(1)}, f32[64,1024]{1,0:T(8,128)S(1)}) custom-call(bf16[1024,1024]{1,0:T(8,128)(2,1)S(1)} %shard_map.64.refs_0_.refs_1_, bf16[1024,1024]{1,0:T(8,128)(2,1)S(1)} %shard_map.66.refs_0_.refs_1_, bf16[128,1024]{1,0:T(8,128)(2,1)S(1)} %collective-permute-done.1.refs_2_, ...), custom_call_target="tpu_custom_call" | custom-call | flops 1342177280 | bytes 4718592 | tf_op jit(solution)/shard_map/pallas_call | solution.py:143
  23.5 0.6 %shard_map.73 = f32[64,512]{1,0:T(8,128)S(1)} custom-call(bf16[1024,1024]{1,0:T(8,128)(2,1)S(1)} %shard_map.66.refs_0_.refs_1_, bf16[128,1024]{1,0:T(8,128)(2,1)S(1)} %collective-permute-done.5.refs_2_.refs_1_, bf16[144,1024]{1,0:T(8,128)(2,1)S(1)} %collective-permute-done.6.refs_3_.refs_2_, f32[64,1024]{1,0:T(8,128)S(1)} %get-tuple-element.24.refs_4_.refs_3_), custom_call_target="tpu_custom_call" | custom-call | flops 335544320 | bytes 1572864 | tf_op jit(solution)/shard_map/pallas_call | solution.py:143
  24.2 0.9 %shard_map.72 = (f32[64,512]{1,0:T(8,128)S(1)}, f32[64,512]{1,0:T(8,128)S(1)}) custom-call(bf16[1024,1024]{1,0:T(8,128)(2,1)S(1)} %shard_map.66.refs_0_.refs_1_, bf16[1024,1024]{1,0:T(8,128)(2,1)S(1)} %shard_map.64.refs_0_.refs_1_, bf16[128,1024]{1,0:T(8,128)(2,1)S(1)} %collective-permute-done.5.refs_2_.refs_1_, ...), custom_call_target="tpu_custom_call" | custom-call | flops 671088640 | bytes 2621440 | tf_op jit(solution)/shard_map/pallas_call | solution.py:143
  25.6 1.7 %collective-permute-start.8 = (bf16[64,512]{1,0:T(8,128)(2,1)S(1)}, bf16[64,512]{1,0:T(8,128)(2,1)S(1)}, u32[]{:S(2)}, u32[]{:S(2)}) collective-permute-start(bf16[64,512]{1,0:T(8,128)(2,1)S(1)} %shard_map.74.a_ref), channel_id=1, source_target_pairs={{0,8},{1,17},{2,10},{3,19},{4,12},{5,21},{6,14},{7,23},{8,0},{9,25... | collective-permute-start | bytes 196616 | tf_op jit(solution)/shard_map/ppermute | solution.py:33
  27.3 0.6 %shard_map.76.a_ref = f32[64,512]{1,0:T(8,128)S(1)} custom-call(bf16[1024,1024]{1,0:T(8,128)(2,1)S(1)} %shard_map.64.refs_0_.refs_1_, bf16[128,1024]{1,0:T(8,128)(2,1)S(1)} %collective-permute-done.5.refs_2_.refs_1_, bf16[144,1024]{1,0:T(8,128)(2,1)S(1)} %collective-permute-done.6.refs_3_.refs_2_, f32[64,1024]{1,0:T(8,128)S(1)} %get-tuple-element.27.refs_5_.refs_3_), custom_call_target="tpu_custom_call" | custom-call | flops 335544320 | bytes 1572864 | tf_op jit(solution)/shard_map/pallas_call | solution.py:143
  28.5 2.2 %collective-permute-done.8.b_ref = bf16[64,512]{1,0:T(8,128)(2,1)S(1)} collective-permute-done((bf16[64,512]{1,0:T(8,128)(2,1)S(1)}, bf16[64,512]{1,0:T(8,128)(2,1)S(1)}, u32[]{:S(2)}, u32[]{:S(2)}) %collective-permute-start.8) | collective-permute-done | bytes 65568 | tf_op jit(solution)/shard_map/ppermute | solution.py:33
  30.6 2.0 %collective-permute-start.9 = (bf16[64,512]{1,0:T(8,128)(2,1)S(1)}, bf16[64,512]{1,0:T(8,128)(2,1)S(1)}, u32[]{:S(2)}, u32[]{:S(2)}) collective-permute-start(bf16[64,512]{1,0:T(8,128)(2,1)S(1)} %shard_map.75.refs_0_), channel_id=1, source_target_pairs={{0,16},{1,9},{2,18},{3,11},{4,20},{5,13},{6,22},{7,15},{8,24},{9,1... | collective-permute-start | bytes 196616 | tf_op jit(solution)/shard_map/ppermute | solution.py:33
  32.7 2.9 %collective-permute-start.12 = (bf16[64,512]{1,0:T(8,128)(2,1)S(1)}, bf16[64,512]{1,0:T(8,128)(2,1)S(1)}, u32[]{:S(2)}, u32[]{:S(2)}) collective-permute-start(bf16[64,512]{1,0:T(8,128)(2,1)S(1)} %shard_map.78.refs_2_), channel_id=1, source_target_pairs={{0,16},{1,9},{2,18},{3,11},{4,20},{5,13},{6,22},{7,15},{8,24},{9,1... | collective-permute-start | bytes 196616 | tf_op jit(solution)/shard_map/ppermute | solution.py:33
  35.9 2.0 %collective-permute-done.12.refs_3_ = bf16[64,512]{1,0:T(8,128)(2,1)S(1)} collective-permute-done((bf16[64,512]{1,0:T(8,128)(2,1)S(1)}, bf16[64,512]{1,0:T(8,128)(2,1)S(1)}, u32[]{:S(2)}, u32[]{:S(2)}) %collective-permute-start.12) | collective-permute-done | bytes 65568 | tf_op jit(solution)/shard_map/ppermute | solution.py:33
  37.9 0.8 %shard_map.79 = f32[64,1024]{1,0:T(8,128)} custom-call(bf16[64,512]{1,0:T(8,128)(2,1)S(1)} %shard_map.75.refs_0_, bf16[64,512]{1,0:T(8,128)(2,1)S(1)} %collective-permute-done.9.refs_1_, bf16[64,512]{1,0:T(8,128)(2,1)S(1)} %shard_map.78.refs_2_, bf16[64,512]{1,0:T(8,128)(2,1)S(1)} %collective-permute-done.12.refs_3_, f32[64,1]{1,0:T(8,128)S(1)} %copy.7.refs_4_), custom_call_target="tpu_custom_call" | custom-call | tf_op jit(solution)/shard_map/pallas_call | solution.py:172
  (23 shorter events, 3.5 us)
Async XLA Ops:
  1.0 15.5 %collective-permute-start = (bf16[1024,1024]{1,0:T(8,128)(2,1)}, bf16[1024,1024]{1,0:T(8,128)(2,1)S(1)}, u32[]{:S(2)}, u32[]{:S(2)}) collective-permute-start(bf16[1024,1024]{1,0:T(8,128)(2,1)} %in_ref.1), channel_id=1, source_target_pairs={{0,1},{1,0},{2,3},{3,2},{4,5},{5,4},{6,7},{7,6},{8,9},{9,8},{10,11... | collective-permute-start | bytes 6291464 | tf_op jit(solution)/shard_map/ppermute | solution.py:18
  1.5 12.2 %collective-permute-start.3 = (bf16[144,1024]{1,0:T(8,128)(2,1)S(1)}, bf16[144,1024]{1,0:T(8,128)(2,1)S(1)}, u32[]{:S(2)}, u32[]{:S(2)}) collective-permute-start(bf16[144,1024]{1,0:T(8,128)(2,1)S(1)} %shard_map.65.refs_2_), channel_id=1, source_target_pairs={{0,2},{1,5},{2,0},{3,7},{4,6},{5,1},{6,4},{7,3},{8,10},{9,13},{10,... | collective-permute-start | bytes 884744 | tf_op jit(solution)/shard_map/ppermute | solution.py:23
  5.1 8.6 %collective-permute-start.2 = (bf16[128,1024]{1,0:T(8,128)(2,1)S(1)}, bf16[128,1024]{1,0:T(8,128)(2,1)S(1)}, u32[]{:S(2)}, u32[]{:S(2)}) collective-permute-start(bf16[128,1024]{1,0:T(8,128)(2,1)S(1)} %shard_map.67.refs_1_), channel_id=1, source_target_pairs={{0,4},{1,3},{2,6},{3,1},{4,0},{5,7},{6,2},{7,5},{8,12},{9,11},{10,... | collective-permute-start | bytes 786440 | tf_op jit(solution)/shard_map/ppermute | solution.py:23
  6.7 12.9 %collective-permute-start.4 = (bf16[144,1024]{1,0:T(8,128)(2,1)S(1)}, bf16[144,1024]{1,0:T(8,128)(2,1)S(1)}, u32[]{:S(2)}, u32[]{:S(2)}) collective-permute-start(bf16[144,1024]{1,0:T(8,128)(2,1)S(1)} %shard_map.65.refs_2_), channel_id=1, source_target_pairs={{0,4},{1,3},{2,6},{3,1},{4,0},{5,7},{6,2},{7,5},{8,12},{9,11},{10,... | collective-permute-start | bytes 884744 | tf_op jit(solution)/shard_map/ppermute | solution.py:23
  7.2 13.9 %collective-permute-start.1 = (bf16[128,1024]{1,0:T(8,128)(2,1)S(1)}, bf16[128,1024]{1,0:T(8,128)(2,1)S(1)}, u32[]{:S(2)}, u32[]{:S(2)}) collective-permute-start(bf16[128,1024]{1,0:T(8,128)(2,1)S(1)} %shard_map.67.refs_1_), channel_id=1, source_target_pairs={{0,2},{1,5},{2,0},{3,7},{4,6},{5,1},{6,4},{7,3},{8,10},{9,13},{10,... | collective-permute-start | bytes 786440 | tf_op jit(solution)/shard_map/ppermute | solution.py:23
  7.3 1.6 %copy-start = (bf16[1024,1024]{1,0:T(8,128)(2,1)S(1)}, bf16[1024,1024]{1,0:T(8,128)(2,1)}, u32[]{:S(2)}) copy-start(bf16[1024,1024]{1,0:T(8,128)(2,1)} %in_ref.1) | copy-start | bytes 6291460
  13.7 9.2 %collective-permute-start.5 = (bf16[128,1024]{1,0:T(8,128)(2,1)S(1)}, bf16[128,1024]{1,0:T(8,128)(2,1)S(1)}, u32[]{:S(2)}, u32[]{:S(2)}) collective-permute-start(bf16[128,1024]{1,0:T(8,128)(2,1)S(1)} %collective-permute-done.2.refs_2_), channel_id=1, source_target_pairs={{0,2},{1,5},{2,0},{3,7},{4,6},{5,1},{6,4},{7,3},{8,10},{9,13},{10,... | collective-permute-start | bytes 786440 | tf_op jit(solution)/shard_map/ppermute | solution.py:23
  14.4 9.0 %collective-permute-start.6 = (bf16[144,1024]{1,0:T(8,128)(2,1)S(1)}, bf16[144,1024]{1,0:T(8,128)(2,1)S(1)}, u32[]{:S(2)}, u32[]{:S(2)}) collective-permute-start(bf16[144,1024]{1,0:T(8,128)(2,1)S(1)} %collective-permute-done.3.refs_3_), channel_id=1, source_target_pairs={{0,4},{1,3},{2,6},{3,1},{4,0},{5,7},{6,2},{7,5},{8,12},{9,11},{10,... | collective-permute-start | bytes 884744 | tf_op jit(solution)/shard_map/ppermute | solution.py:23
  24.1 1.5 %collective-permute-start.7 = (f32[64,512]{1,0:T(8,128)S(1)}, f32[64,512]{1,0:T(8,128)S(1)}, u32[]{:S(2)}, u32[]{:S(2)}) collective-permute-start(f32[64,512]{1,0:T(8,128)S(1)} %shard_map.73), channel_id=1, source_target_pairs={{0,1},{1,0},{2,3},{3,2},{4,5},{5,4},{6,7},{7,6},{8,9},{9,8},{10,11... | collective-permute-start | bytes 393224 | tf_op jit(solution)/shard_map/ppermute | solution.py:18
  25.1 10.5 %copy-start.1 = (f32[64]{0:T(128)S(1)}, f32[64]{0:T(128)}, u32[]{:S(2)}) copy-start(f32[64]{0:T(128)} %param.11) | copy-start | bytes 772
  25.1 2.8 %collective-permute-start.10 = (f32[64,512]{1,0:T(8,128)S(1)}, f32[64,512]{1,0:T(8,128)S(1)}, u32[]{:S(2)}, u32[]{:S(2)}) collective-permute-start(f32[64,512]{1,0:T(8,128)S(1)} %get-tuple-element.28), channel_id=1, source_target_pairs={{0,1},{1,0},{2,3},{3,2},{4,5},{5,4},{6,7},{7,6},{8,9},{9,8},{10,11... | collective-permute-start | bytes 393224 | tf_op jit(solution)/shard_map/ppermute | solution.py:18
  25.6 5.0 %collective-permute-start.8 = (bf16[64,512]{1,0:T(8,128)(2,1)S(1)}, bf16[64,512]{1,0:T(8,128)(2,1)S(1)}, u32[]{:S(2)}, u32[]{:S(2)}) collective-permute-start(bf16[64,512]{1,0:T(8,128)(2,1)S(1)} %shard_map.74.a_ref), channel_id=1, source_target_pairs={{0,8},{1,17},{2,10},{3,19},{4,12},{5,21},{6,14},{7,23},{8,0},{9,25... | collective-permute-start | bytes 196616 | tf_op jit(solution)/shard_map/ppermute | solution.py:33
  27.9 4.7 %collective-permute-start.11 = (bf16[64,512]{1,0:T(8,128)(2,1)S(1)}, bf16[64,512]{1,0:T(8,128)(2,1)S(1)}, u32[]{:S(2)}, u32[]{:S(2)}) collective-permute-start(bf16[64,512]{1,0:T(8,128)(2,1)S(1)} %shard_map.77.a_ref), channel_id=1, source_target_pairs={{0,8},{1,17},{2,10},{3,19},{4,12},{5,21},{6,14},{7,23},{8,0},{9,25... | collective-permute-start | bytes 196616 | tf_op jit(solution)/shard_map/ppermute | solution.py:33
  30.6 5.2 %collective-permute-start.9 = (bf16[64,512]{1,0:T(8,128)(2,1)S(1)}, bf16[64,512]{1,0:T(8,128)(2,1)S(1)}, u32[]{:S(2)}, u32[]{:S(2)}) collective-permute-start(bf16[64,512]{1,0:T(8,128)(2,1)S(1)} %shard_map.75.refs_0_), channel_id=1, source_target_pairs={{0,16},{1,9},{2,18},{3,11},{4,20},{5,13},{6,22},{7,15},{8,24},{9,1... | collective-permute-start | bytes 196616 | tf_op jit(solution)/shard_map/ppermute | solution.py:33
  32.7 5.2 %collective-permute-start.12 = (bf16[64,512]{1,0:T(8,128)(2,1)S(1)}, bf16[64,512]{1,0:T(8,128)(2,1)S(1)}, u32[]{:S(2)}, u32[]{:S(2)}) collective-permute-start(bf16[64,512]{1,0:T(8,128)(2,1)S(1)} %shard_map.78.refs_2_), channel_id=1, source_target_pairs={{0,16},{1,9},{2,18},{3,11},{4,20},{5,13},{6,22},{7,15},{8,24},{9,1... | collective-permute-start | bytes 196616 | tf_op jit(solution)/shard_map/ppermute | solution.py:33

commit v13 on v9

--- a/solution.py
+++ b/solution.py
@@ -20,7 +20,7 @@
 
 def chip_send(value, k, n):
     bits = [1 << b for b in range(1, n.bit_length() - 1)]
-    return lax.ppermute(value, "sl", [(i, i ^ bits[(k + i % 2) % len(bits)]) for i in range(n)])
+    return lax.ppermute(value, "sl", [(i, i ^ bits[(k + 1 - i % 2) % len(bits)]) for i in range(n)])
 
 
 def lm_send(value, k, n_lm, n_sl):

time: 38.9 us -> 38.9 us (level)
  no operation moved by 1% of the time
where the time goes in v13:
time: 38.9 us; the launch traced here: 38.7 us
  starting transfers between devices  15.9 us (41%)
  Pallas kernels  10.9 us (28%)
  waiting for transfers between devices  10.1 us (26%)
  local copies, waits for them, and re-layouts  1.69 us (4%)
    ppermute x6, starting transfers between devices, chip_send(): lax.ppermute(value, 'sl', [(i, i ^ bits[(k + 1 - i % 2) % len(bits)]) for...  7.59 us
    ppermute x4, starting transfers between devices, lm_send(): return lax.ppermute(value, ('lm', 'sl'), perm)  7.19 us
    pallas_call x7, Pallas kernels, stage(): pl.pallas_call(functools.partial(stage_kernel, count, coeff, ritz, accs i...  6.83 us
    ppermute x6, waiting for transfers between devices, chip_send(): lax.ppermute(value, 'sl', [(i, i ^ bits[(k + 1 - i % 2) % len(bits)]) for...  5.65 us
    ppermute x4, waiting for transfers between devices, lm_send(): return lax.ppermute(value, ('lm', 'sl'), perm)  4.42 us
    pallas_call x7, Pallas kernels, small_call(): pl.pallas_call(kernel, out_shape=jax.ShapeDtypeStruct(out.shape, out.dtyp...  2.13 us
    unnamed x4, local copies, waits for them, and re-layouts  1.59 us
    ppermute x3, starting transfers between devices, core_send(): return lax.ppermute(value, 'sl', [(i, i ^ 1) for i in range(n)])  1.09 us
  transfers between devices with their start and end apart: 13, of which 7 were waited for; matrix products, arithmetic and copies ran while one was open for 0% of the time, Pallas kernels for 25%

profile of v13, /device:TPU:0, one launch (start us, length us, event | category | flops | bytes accessed | tf_op | source)
XLA Modules:
  0.0 38.7 jit_solution(8484491793890197580)
XLA Ops:
  0.5 1.0 %shard_map.67.refs_2_ = bf16[144,1024]{1,0:T(8,128)(2,1)S(1)} custom-call(bf16[256,1024]{1,0:T(8,128)(2,1)} %land_ref.3), custom_call_target="tpu_custom_call" | custom-call | tf_op jit(solution)/shard_map/pallas_call | solution.py:75
  1.4 2.6 %collective-permute-start.3 = (bf16[144,1024]{1,0:T(8,128)(2,1)S(1)}, bf16[144,1024]{1,0:T(8,128)(2,1)S(1)}, u32[]{:S(2)}, u32[]{:S(2)}) collective-permute-start(bf16[144,1024]{1,0:T(8,128)(2,1)S(1)} %shard_map.67.refs_2_), channel_id=1, source_target_pairs={{0,2},{1,5},{2,0},{3,7},{4,6},{5,1},{6,4},{7,3},{8,10},{9,13},{10,... | collective-permute-start | bytes 884744 | tf_op jit(solution)/shard_map/ppermute | solution.py:23
  4.0 1.0 %shard_map.66.refs_1_ = bf16[128,1024]{1,0:T(8,128)(2,1)S(1)} custom-call(bf16[256,1024]{1,0:T(8,128)(2,1)} %land_ref.3, bf16[96,256]{1,0:T(8,128)(2,1)} %bitcast.4, s32[2]{0:T(128)} %exponents_ref.1, bf16[64,96]{1,0:T(8,128)(2,1)} %bitcast.5), custom_call_target="tpu_custom_call" | custom-call | tf_op jit(solution)/shard_map/pallas_call | solution.py:87
  5.0 1.6 %collective-permute-start.2 = (bf16[128,1024]{1,0:T(8,128)(2,1)S(1)}, bf16[128,1024]{1,0:T(8,128)(2,1)S(1)}, u32[]{:S(2)}, u32[]{:S(2)}) collective-permute-start(bf16[128,1024]{1,0:T(8,128)(2,1)S(1)} %shard_map.66.refs_1_), channel_id=1, source_target_pairs={{0,4},{1,3},{2,6},{3,1},{4,0},{5,7},{6,2},{7,5},{8,12},{9,11},{10,... | collective-permute-start | bytes 786440 | tf_op jit(solution)/shard_map/ppermute | solution.py:23
  7.2 1.6 %copy-done = bf16[1024,1024]{1,0:T(8,128)(2,1)S(1)} copy-done((bf16[1024,1024]{1,0:T(8,128)(2,1)S(1)}, bf16[1024,1024]{1,0:T(8,128)(2,1)}, u32[]{:S(2)}) %copy-start) | copy-done | bytes 2097176
  8.8 0.6 %shard_map.64.refs_0_.refs_1_ = bf16[1024,1024]{1,0:T(8,128)(2,1)S(1)} custom-call(bf16[1024,1024]{1,0:T(8,128)(2,1)S(1)} %copy-done), custom_call_target="tpu_custom_call" | custom-call | tf_op jit(solution)/shard_map/pallas_call | solution.py:172
  9.4 0.9 %shard_map.68.refs_4_ = f32[64,1024]{1,0:T(8,128)S(1)} custom-call(bf16[1024,1024]{1,0:T(8,128)(2,1)S(1)} %shard_map.64.refs_0_.refs_1_, bf16[128,1024]{1,0:T(8,128)(2,1)S(1)} %shard_map.66.refs_1_, bf16[144,1024]{1,0:T(8,128)(2,1)S(1)} %shard_map.67.refs_2_), custom_call_target="tpu_custom_call" | custom-call | flops 671088640 | bytes 2621440 | tf_op jit(solution)/shard_map/pallas_call | solution.py:143
  10.3 3.2 %collective-permute-done.2.refs_2_ = bf16[128,1024]{1,0:T(8,128)(2,1)S(1)} collective-permute-done((bf16[128,1024]{1,0:T(8,128)(2,1)S(1)}, bf16[128,1024]{1,0:T(8,128)(2,1)S(1)}, u32[]{:S(2)}, u32[]{:S(2)}) %collective-permute-start.2) | collective-permute-done | bytes 262176 | tf_op jit(solution)/shard_map/ppermute | solution.py:23
  13.5 0.8 %collective-permute-start.5 = (bf16[128,1024]{1,0:T(8,128)(2,1)S(1)}, bf16[128,1024]{1,0:T(8,128)(2,1)S(1)}, u32[]{:S(2)}, u32[]{:S(2)}) collective-permute-start(bf16[128,1024]{1,0:T(8,128)(2,1)S(1)} %collective-permute-done.2.refs_2_), channel_id=1, source_target_pairs={{0,2},{1,5},{2,0},{3,7},{4,6},{5,1},{6,4},{7,3},{8,10},{9,13},{10,... | collective-permute-start | bytes 786440 | tf_op jit(solution)/shard_map/ppermute | solution.py:23
  14.4 2.0 %collective-permute-start.6 = (bf16[144,1024]{1,0:T(8,128)(2,1)S(1)}, bf16[144,1024]{1,0:T(8,128)(2,1)S(1)}, u32[]{:S(2)}, u32[]{:S(2)}) collective-permute-start(bf16[144,1024]{1,0:T(8,128)(2,1)S(1)} %collective-permute-done.3.refs_3_), channel_id=1, source_target_pairs={{0,4},{1,3},{2,6},{3,1},{4,0},{5,7},{6,2},{7,5},{8,12},{9,11},{10,... | collective-permute-start | bytes 884744 | tf_op jit(solution)/shard_map/ppermute | solution.py:23
  16.4 0.6 %shard_map.65.refs_0_.refs_1_ = bf16[1024,1024]{1,0:T(8,128)(2,1)S(1)} custom-call(bf16[1024,1024]{1,0:T(8,128)(2,1)S(1)} %collective-permute-done.in_ref), custom_call_target="tpu_custom_call" | custom-call | tf_op jit(solution)/shard_map/pallas_call | solution.py:172
  17.0 0.9 %shard_map.69.refs_5_ = f32[64,1024]{1,0:T(8,128)S(1)} custom-call(bf16[1024,1024]{1,0:T(8,128)(2,1)S(1)} %shard_map.65.refs_0_.refs_1_, bf16[128,1024]{1,0:T(8,128)(2,1)S(1)} %shard_map.66.refs_1_, bf16[144,1024]{1,0:T(8,128)(2,1)S(1)} %shard_map.67.refs_2_), custom_call_target="tpu_custom_call" | custom-call | flops 671088640 | bytes 2621440 | tf_op jit(solution)/shard_map/pallas_call | solution.py:143
  17.9 1.6 %collective-permute-done.4.refs_3_ = bf16[144,1024]{1,0:T(8,128)(2,1)S(1)} collective-permute-done((bf16[144,1024]{1,0:T(8,128)(2,1)S(1)}, bf16[144,1024]{1,0:T(8,128)(2,1)S(1)}, u32[]{:S(2)}, u32[]{:S(2)}) %collective-permute-start.4) | collective-permute-done | bytes 294944 | tf_op jit(solution)/shard_map/ppermute | solution.py:23
  19.4 1.5 %shard_map.70 = (f32[64,1024]{1,0:T(8,128)S(1)}, f32[64,1024]{1,0:T(8,128)S(1)}) custom-call(bf16[1024,1024]{1,0:T(8,128)(2,1)S(1)} %shard_map.64.refs_0_.refs_1_, bf16[1024,1024]{1,0:T(8,128)(2,1)S(1)} %shard_map.65.refs_0_.refs_1_, bf16[128,1024]{1,0:T(8,128)(2,1)S(1)} %collective-permute-done.2.refs_2_, ...), custom_call_target="tpu_custom_call" | custom-call | flops 1342177280 | bytes 4718592 | tf_op jit(solution)/shard_map/pallas_call | solution.py:143
  21.0 1.5 %shard_map.71 = (f32[64,1024]{1,0:T(8,128)S(1)}, f32[64,1024]{1,0:T(8,128)S(1)}) custom-call(bf16[1024,1024]{1,0:T(8,128)(2,1)S(1)} %shard_map.64.refs_0_.refs_1_, bf16[1024,1024]{1,0:T(8,128)(2,1)S(1)} %shard_map.65.refs_0_.refs_1_, bf16[128,1024]{1,0:T(8,128)(2,1)S(1)} %collective-permute-done.1.refs_2_, ...), custom_call_target="tpu_custom_call" | custom-call | flops 1342177280 | bytes 4718592 | tf_op jit(solution)/shard_map/pallas_call | solution.py:143
  22.8 0.6 %collective-permute-done.6.refs_3_.refs_2_ = bf16[144,1024]{1,0:T(8,128)(2,1)S(1)} collective-permute-done((bf16[144,1024]{1,0:T(8,128)(2,1)S(1)}, bf16[144,1024]{1,0:T(8,128)(2,1)S(1)}, u32[]{:S(2)}, u32[]{:S(2)}) %collective-permute-start.6) | collective-permute-done | bytes 294944 | tf_op jit(solution)/shard_map/ppermute | solution.py:23
  23.4 0.6 %shard_map.73 = f32[64,512]{1,0:T(8,128)S(1)} custom-call(bf16[1024,1024]{1,0:T(8,128)(2,1)S(1)} %shard_map.65.refs_0_.refs_1_, bf16[128,1024]{1,0:T(8,128)(2,1)S(1)} %collective-permute-done.5.refs_2_.refs_1_, bf16[144,1024]{1,0:T(8,128)(2,1)S(1)} %collective-permute-done.6.refs_3_.refs_2_, f32[64,1024]{1,0:T(8,128)S(1)} %get-tuple-element.22.refs_4_.refs_3_), custom_call_target="tpu_custom_call" | custom-call | flops 335544320 | bytes 1572864 | tf_op jit(solution)/shard_map/pallas_call | solution.py:143
  24.2 0.9 %shard_map.72 = (f32[64,512]{1,0:T(8,128)S(1)}, f32[64,512]{1,0:T(8,128)S(1)}) custom-call(bf16[1024,1024]{1,0:T(8,128)(2,1)S(1)} %shard_map.65.refs_0_.refs_1_, bf16[1024,1024]{1,0:T(8,128)(2,1)S(1)} %shard_map.64.refs_0_.refs_1_, bf16[128,1024]{1,0:T(8,128)(2,1)S(1)} %collective-permute-done.5.refs_2_.refs_1_, ...), custom_call_target="tpu_custom_call" | custom-call | flops 671088640 | bytes 2621440 | tf_op jit(solution)/shard_map/pallas_call | solution.py:143
  25.5 1.8 %collective-permute-start.8 = (bf16[64,512]{1,0:T(8,128)(2,1)S(1)}, bf16[64,512]{1,0:T(8,128)(2,1)S(1)}, u32[]{:S(2)}, u32[]{:S(2)}) collective-permute-start(bf16[64,512]{1,0:T(8,128)(2,1)S(1)} %shard_map.74.a_ref), channel_id=1, source_target_pairs={{0,8},{1,17},{2,10},{3,19},{4,12},{5,21},{6,14},{7,23},{8,0},{9,25... | collective-permute-start | bytes 196616 | tf_op jit(solution)/shard_map/ppermute | solution.py:33
  28.4 2.2 %collective-permute-done.8.b_ref = bf16[64,512]{1,0:T(8,128)(2,1)S(1)} collective-permute-done((bf16[64,512]{1,0:T(8,128)(2,1)S(1)}, bf16[64,512]{1,0:T(8,128)(2,1)S(1)}, u32[]{:S(2)}, u32[]{:S(2)}) %collective-permute-start.8) | collective-permute-done | bytes 65568 | tf_op jit(solution)/shard_map/ppermute | solution.py:33
  30.6 2.1 %collective-permute-start.9 = (bf16[64,512]{1,0:T(8,128)(2,1)S(1)}, bf16[64,512]{1,0:T(8,128)(2,1)S(1)}, u32[]{:S(2)}, u32[]{:S(2)}) collective-permute-start(bf16[64,512]{1,0:T(8,128)(2,1)S(1)} %shard_map.75.refs_0_), channel_id=1, source_target_pairs={{0,16},{1,9},{2,18},{3,11},{4,20},{5,13},{6,22},{7,15},{8,24},{9,1... | collective-permute-start | bytes 196616 | tf_op jit(solution)/shard_map/ppermute | solution.py:33
  32.7 2.9 %collective-permute-start.12 = (bf16[64,512]{1,0:T(8,128)(2,1)S(1)}, bf16[64,512]{1,0:T(8,128)(2,1)S(1)}, u32[]{:S(2)}, u32[]{:S(2)}) collective-permute-start(bf16[64,512]{1,0:T(8,128)(2,1)S(1)} %shard_map.78.refs_2_), channel_id=1, source_target_pairs={{0,16},{1,9},{2,18},{3,11},{4,20},{5,13},{6,22},{7,15},{8,24},{9,1... | collective-permute-start | bytes 196616 | tf_op jit(solution)/shard_map/ppermute | solution.py:33
  35.8 2.1 %collective-permute-done.12.refs_3_ = bf16[64,512]{1,0:T(8,128)(2,1)S(1)} collective-permute-done((bf16[64,512]{1,0:T(8,128)(2,1)S(1)}, bf16[64,512]{1,0:T(8,128)(2,1)S(1)}, u32[]{:S(2)}, u32[]{:S(2)}) %collective-permute-start.12) | collective-permute-done | bytes 65568 | tf_op jit(solution)/shard_map/ppermute | solution.py:33
  37.9 0.8 %shard_map.79 = f32[64,1024]{1,0:T(8,128)} custom-call(bf16[64,512]{1,0:T(8,128)(2,1)S(1)} %shard_map.75.refs_0_, bf16[64,512]{1,0:T(8,128)(2,1)S(1)} %collective-permute-done.9.refs_1_, bf16[64,512]{1,0:T(8,128)(2,1)S(1)} %shard_map.78.refs_2_, bf16[64,512]{1,0:T(8,128)(2,1)S(1)} %collective-permute-done.12.refs_3_, f32[64,1]{1,0:T(8,128)S(1)} %copy.7.refs_4_), custom_call_target="tpu_custom_call" | custom-call | tf_op jit(solution)/shard_map/pallas_call | solution.py:172
  (23 shorter events, 3.4 us)
Async XLA Ops:
  0.0 16.4 %collective-permute-start = (bf16[1024,1024]{1,0:T(8,128)(2,1)}, bf16[1024,1024]{1,0:T(8,128)(2,1)S(1)}, u32[]{:S(2)}, u32[]{:S(2)}) collective-permute-start(bf16[1024,1024]{1,0:T(8,128)(2,1)} %in_ref.1), channel_id=1, source_target_pairs={{0,1},{1,0},{2,3},{3,2},{4,5},{5,4},{6,7},{7,6},{8,9},{9,8},{10,11... | collective-permute-start | bytes 6291464 | tf_op jit(solution)/shard_map/ppermute | solution.py:18
  1.4 12.1 %collective-permute-start.3 = (bf16[144,1024]{1,0:T(8,128)(2,1)S(1)}, bf16[144,1024]{1,0:T(8,128)(2,1)S(1)}, u32[]{:S(2)}, u32[]{:S(2)}) collective-permute-start(bf16[144,1024]{1,0:T(8,128)(2,1)S(1)} %shard_map.67.refs_2_), channel_id=1, source_target_pairs={{0,2},{1,5},{2,0},{3,7},{4,6},{5,1},{6,4},{7,3},{8,10},{9,13},{10,... | collective-permute-start | bytes 884744 | tf_op jit(solution)/shard_map/ppermute | solution.py:23
  5.0 8.5 %collective-permute-start.2 = (bf16[128,1024]{1,0:T(8,128)(2,1)S(1)}, bf16[128,1024]{1,0:T(8,128)(2,1)S(1)}, u32[]{:S(2)}, u32[]{:S(2)}) collective-permute-start(bf16[128,1024]{1,0:T(8,128)(2,1)S(1)} %shard_map.66.refs_1_), channel_id=1, source_target_pairs={{0,4},{1,3},{2,6},{3,1},{4,0},{5,7},{6,2},{7,5},{8,12},{9,11},{10,... | collective-permute-start | bytes 786440 | tf_op jit(solution)/shard_map/ppermute | solution.py:23
  6.6 12.8 %collective-permute-start.4 = (bf16[144,1024]{1,0:T(8,128)(2,1)S(1)}, bf16[144,1024]{1,0:T(8,128)(2,1)S(1)}, u32[]{:S(2)}, u32[]{:S(2)}) collective-permute-start(bf16[144,1024]{1,0:T(8,128)(2,1)S(1)} %shard_map.67.refs_2_), channel_id=1, source_target_pairs={{0,4},{1,3},{2,6},{3,1},{4,0},{5,7},{6,2},{7,5},{8,12},{9,11},{10,... | collective-permute-start | bytes 884744 | tf_op jit(solution)/shard_map/ppermute | solution.py:23
  7.1 13.9 %collective-permute-start.1 = (bf16[128,1024]{1,0:T(8,128)(2,1)S(1)}, bf16[128,1024]{1,0:T(8,128)(2,1)S(1)}, u32[]{:S(2)}, u32[]{:S(2)}) collective-permute-start(bf16[128,1024]{1,0:T(8,128)(2,1)S(1)} %shard_map.66.refs_1_), channel_id=1, source_target_pairs={{0,2},{1,5},{2,0},{3,7},{4,6},{5,1},{6,4},{7,3},{8,10},{9,13},{10,... | collective-permute-start | bytes 786440 | tf_op jit(solution)/shard_map/ppermute | solution.py:23
  7.2 1.6 %copy-start = (bf16[1024,1024]{1,0:T(8,128)(2,1)S(1)}, bf16[1024,1024]{1,0:T(8,128)(2,1)}, u32[]{:S(2)}) copy-start(bf16[1024,1024]{1,0:T(8,128)(2,1)} %in_ref.1) | copy-start | bytes 6291460
  13.5 9.2 %collective-permute-start.5 = (bf16[128,1024]{1,0:T(8,128)(2,1)S(1)}, bf16[128,1024]{1,0:T(8,128)(2,1)S(1)}, u32[]{:S(2)}, u32[]{:S(2)}) collective-permute-start(bf16[128,1024]{1,0:T(8,128)(2,1)S(1)} %collective-permute-done.2.refs_2_), channel_id=1, source_target_pairs={{0,2},{1,5},{2,0},{3,7},{4,6},{5,1},{6,4},{7,3},{8,10},{9,13},{10,... | collective-permute-start | bytes 786440 | tf_op jit(solution)/shard_map/ppermute | solution.py:23
  14.4 9.0 %collective-permute-start.6 = (bf16[144,1024]{1,0:T(8,128)(2,1)S(1)}, bf16[144,1024]{1,0:T(8,128)(2,1)S(1)}, u32[]{:S(2)}, u32[]{:S(2)}) collective-permute-start(bf16[144,1024]{1,0:T(8,128)(2,1)S(1)} %collective-permute-done.3.refs_3_), channel_id=1, source_target_pairs={{0,4},{1,3},{2,6},{3,1},{4,0},{5,7},{6,2},{7,5},{8,12},{9,11},{10,... | collective-permute-start | bytes 884744 | tf_op jit(solution)/shard_map/ppermute | solution.py:23
  24.0 1.5 %collective-permute-start.7 = (f32[64,512]{1,0:T(8,128)S(1)}, f32[64,512]{1,0:T(8,128)S(1)}, u32[]{:S(2)}, u32[]{:S(2)}) collective-permute-start(f32[64,512]{1,0:T(8,128)S(1)} %shard_map.73), channel_id=1, source_target_pairs={{0,1},{1,0},{2,3},{3,2},{4,5},{5,4},{6,7},{7,6},{8,9},{9,8},{10,11... | collective-permute-start | bytes 393224 | tf_op jit(solution)/shard_map/ppermute | solution.py:18
  25.0 10.5 %copy-start.1 = (f32[64]{0:T(128)S(1)}, f32[64]{0:T(128)}, u32[]{:S(2)}) copy-start(f32[64]{0:T(128)} %param.11) | copy-start | bytes 772
  25.0 2.8 %collective-permute-start.10 = (f32[64,512]{1,0:T(8,128)S(1)}, f32[64,512]{1,0:T(8,128)S(1)}, u32[]{:S(2)}, u32[]{:S(2)}) collective-permute-start(f32[64,512]{1,0:T(8,128)S(1)} %get-tuple-element.26), channel_id=1, source_target_pairs={{0,1},{1,0},{2,3},{3,2},{4,5},{5,4},{6,7},{7,6},{8,9},{9,8},{10,11... | collective-permute-start | bytes 393224 | tf_op jit(solution)/shard_map/ppermute | solution.py:18
  25.5 5.0 %collective-permute-start.8 = (bf16[64,512]{1,0:T(8,128)(2,1)S(1)}, bf16[64,512]{1,0:T(8,128)(2,1)S(1)}, u32[]{:S(2)}, u32[]{:S(2)}) collective-permute-start(bf16[64,512]{1,0:T(8,128)(2,1)S(1)} %shard_map.74.a_ref), channel_id=1, source_target_pairs={{0,8},{1,17},{2,10},{3,19},{4,12},{5,21},{6,14},{7,23},{8,0},{9,25... | collective-permute-start | bytes 196616 | tf_op jit(solution)/shard_map/ppermute | solution.py:33
  27.9 4.7 %collective-permute-start.11 = (bf16[64,512]{1,0:T(8,128)(2,1)S(1)}, bf16[64,512]{1,0:T(8,128)(2,1)S(1)}, u32[]{:S(2)}, u32[]{:S(2)}) collective-permute-start(bf16[64,512]{1,0:T(8,128)(2,1)S(1)} %shard_map.77.a_ref), channel_id=1, source_target_pairs={{0,8},{1,17},{2,10},{3,19},{4,12},{5,21},{6,14},{7,23},{8,0},{9,25... | collective-permute-start | bytes 196616 | tf_op jit(solution)/shard_map/ppermute | solution.py:33
  30.6 5.2 %collective-permute-start.9 = (bf16[64,512]{1,0:T(8,128)(2,1)S(1)}, bf16[64,512]{1,0:T(8,128)(2,1)S(1)}, u32[]{:S(2)}, u32[]{:S(2)}) collective-permute-start(bf16[64,512]{1,0:T(8,128)(2,1)S(1)} %shard_map.75.refs_0_), channel_id=1, source_target_pairs={{0,16},{1,9},{2,18},{3,11},{4,20},{5,13},{6,22},{7,15},{8,24},{9,1... | collective-permute-start | bytes 196616 | tf_op jit(solution)/shard_map/ppermute | solution.py:33
  32.7 5.2 %collective-permute-start.12 = (bf16[64,512]{1,0:T(8,128)(2,1)S(1)}, bf16[64,512]{1,0:T(8,128)(2,1)S(1)}, u32[]{:S(2)}, u32[]{:S(2)}) collective-permute-start(bf16[64,512]{1,0:T(8,128)(2,1)S(1)} %shard_map.78.refs_2_), channel_id=1, source_target_pairs={{0,16},{1,9},{2,18},{3,11},{4,20},{5,13},{6,22},{7,15},{8,24},{9,1... | collective-permute-start | bytes 196616 | tf_op jit(solution)/shard_map/ppermute | solution.py:33

commit v14 on v12

--- a/solution.py
+++ b/solution.py
@@ -128,7 +128,7 @@
     ahead = scores(*work[0])
     for n, (k, cols) in enumerate(work):
         now, ahead = ahead, scores(*work[n + 1]) if n + 1 < len(work) else None
-        affinity = jnp.exp(now * coeff).astype(jnp.bfloat16)
+        affinity = jnp.exp2(now * coeff).astype(jnp.bfloat16)
         term = jnp.dot(vec, affinity, preferred_element_type=jnp.float32)
         place = slice(cols.start - spans[k][0], cols.stop - spans[k][0])
         outs[k][:, place] = term if accs[k] is None else accs[k][:, cols] + term
@@ -179,7 +179,7 @@
 def local(slab, landmarks, codes, exponents, eigvec, ritz):
     n_lm, n_sl = lax.axis_size("lm"), lax.axis_size("sl")
     total_land = codes.shape[0] * n_lm * n_sl
-    coeff = 1.0 / math.sqrt(slab.shape[1])
+    coeff = math.log2(math.e) / math.sqrt(slab.shape[1])
     cols = ritz.shape[0]
     rows = slab.shape[0]
     ways = n_sl.bit_length() - 2

time: 38.9 us -> 38.9 us (level)
  no operation moved by 1% of the time
where the time goes in v14:
time: 38.9 us; the launch traced here: 38.7 us
  starting transfers between devices  15.8 us (41%)
  Pallas kernels  10.9 us (28%)
  waiting for transfers between devices  10.1 us (26%)
  local copies, waits for them, and re-layouts  1.69 us (4%)
    ppermute x6, starting transfers between devices, chip_send(): lax.ppermute(value, 'sl', [(i, i ^ bits[(k + 1 - i % 2) % len(bits)]) for...  7.51 us
    ppermute x4, starting transfers between devices, lm_send(): return lax.ppermute(value, ('lm', 'sl'), perm)  7.16 us
    pallas_call x7, Pallas kernels, stage(): pl.pallas_call(functools.partial(stage_kernel, count, coeff, ritz, accs i...  6.82 us
    ppermute x6, waiting for transfers between devices, chip_send(): lax.ppermute(value, 'sl', [(i, i ^ bits[(k + 1 - i % 2) % len(bits)]) for...  5.74 us
    ppermute x4, waiting for transfers between devices, lm_send(): return lax.ppermute(value, ('lm', 'sl'), perm)  4.37 us
    pallas_call x7, Pallas kernels, small_call(): pl.pallas_call(kernel, out_shape=jax.ShapeDtypeStruct(out.shape, out.dtyp...  2.13 us
    unnamed x4, local copies, waits for them, and re-layouts  1.59 us
    ppermute x3, starting transfers between devices, core_send(): return lax.ppermute(value, 'sl', [(i, i ^ 1) for i in range(n)])  1.15 us
  transfers between devices with their start and end apart: 13, of which 7 were waited for; matrix products, arithmetic and copies ran while one was open for 0% of the time, Pallas kernels for 22%

profile of v14, /device:TPU:0, one launch (start us, length us, event | category | flops | bytes accessed | tf_op | source)
XLA Modules:
  0.0 38.7 jit_solution(15589424316884825574)
XLA Ops:
  0.0 1.0 %shard_map.65.refs_2_ = bf16[144,1024]{1,0:T(8,128)(2,1)S(1)} custom-call(bf16[256,1024]{1,0:T(8,128)(2,1)} %land_ref.3), custom_call_target="tpu_custom_call" | custom-call | tf_op jit(solution)/shard_map/pallas_call | solution.py:75
  1.5 2.6 %collective-permute-start.3 = (bf16[144,1024]{1,0:T(8,128)(2,1)S(1)}, bf16[144,1024]{1,0:T(8,128)(2,1)S(1)}, u32[]{:S(2)}, u32[]{:S(2)}) collective-permute-start(bf16[144,1024]{1,0:T(8,128)(2,1)S(1)} %shard_map.65.refs_2_), channel_id=1, source_target_pairs={{0,2},{1,5},{2,0},{3,7},{4,6},{5,1},{6,4},{7,3},{8,10},{9,13},{10,... | collective-permute-start | bytes 884744 | tf_op jit(solution)/shard_map/ppermute | solution.py:23
  4.1 1.0 %shard_map.67.refs_1_ = bf16[128,1024]{1,0:T(8,128)(2,1)S(1)} custom-call(bf16[256,1024]{1,0:T(8,128)(2,1)} %land_ref.3, bf16[96,256]{1,0:T(8,128)(2,1)} %bitcast.4, s32[2]{0:T(128)} %exponents_ref.1, bf16[64,96]{1,0:T(8,128)(2,1)} %bitcast.5), custom_call_target="tpu_custom_call" | custom-call | tf_op jit(solution)/shard_map/pallas_call | solution.py:87
  5.1 1.6 %collective-permute-start.2 = (bf16[128,1024]{1,0:T(8,128)(2,1)S(1)}, bf16[128,1024]{1,0:T(8,128)(2,1)S(1)}, u32[]{:S(2)}, u32[]{:S(2)}) collective-permute-start(bf16[128,1024]{1,0:T(8,128)(2,1)S(1)} %shard_map.67.refs_1_), channel_id=1, source_target_pairs={{0,4},{1,3},{2,6},{3,1},{4,0},{5,7},{6,2},{7,5},{8,12},{9,11},{10,... | collective-permute-start | bytes 786440 | tf_op jit(solution)/shard_map/ppermute | solution.py:23
  7.3 1.6 %copy-done = bf16[1024,1024]{1,0:T(8,128)(2,1)S(1)} copy-done((bf16[1024,1024]{1,0:T(8,128)(2,1)S(1)}, bf16[1024,1024]{1,0:T(8,128)(2,1)}, u32[]{:S(2)}) %copy-start) | copy-done | bytes 2097176
  8.9 0.6 %shard_map.64.refs_0_.refs_1_ = bf16[1024,1024]{1,0:T(8,128)(2,1)S(1)} custom-call(bf16[1024,1024]{1,0:T(8,128)(2,1)S(1)} %copy-done), custom_call_target="tpu_custom_call" | custom-call | tf_op jit(solution)/shard_map/pallas_call | solution.py:172
  9.5 0.8 %shard_map.68.refs_4_ = f32[64,1024]{1,0:T(8,128)S(1)} custom-call(bf16[1024,1024]{1,0:T(8,128)(2,1)S(1)} %shard_map.64.refs_0_.refs_1_, bf16[128,1024]{1,0:T(8,128)(2,1)S(1)} %shard_map.67.refs_1_, bf16[144,1024]{1,0:T(8,128)(2,1)S(1)} %shard_map.65.refs_2_), custom_call_target="tpu_custom_call" | custom-call | flops 671088640 | bytes 2621440 | tf_op jit(solution)/shard_map/pallas_call | solution.py:143
  10.4 3.3 %collective-permute-done.2.refs_2_ = bf16[128,1024]{1,0:T(8,128)(2,1)S(1)} collective-permute-done((bf16[128,1024]{1,0:T(8,128)(2,1)S(1)}, bf16[128,1024]{1,0:T(8,128)(2,1)S(1)}, u32[]{:S(2)}, u32[]{:S(2)}) %collective-permute-start.2) | collective-permute-done | bytes 262176 | tf_op jit(solution)/shard_map/ppermute | solution.py:23
  13.7 0.7 %collective-permute-start.5 = (bf16[128,1024]{1,0:T(8,128)(2,1)S(1)}, bf16[128,1024]{1,0:T(8,128)(2,1)S(1)}, u32[]{:S(2)}, u32[]{:S(2)}) collective-permute-start(bf16[128,1024]{1,0:T(8,128)(2,1)S(1)} %collective-permute-done.2.refs_2_), channel_id=1, source_target_pairs={{0,2},{1,5},{2,0},{3,7},{4,6},{5,1},{6,4},{7,3},{8,10},{9,13},{10,... | collective-permute-start | bytes 786440 | tf_op jit(solution)/shard_map/ppermute | solution.py:23
  14.4 2.0 %collective-permute-start.6 = (bf16[144,1024]{1,0:T(8,128)(2,1)S(1)}, bf16[144,1024]{1,0:T(8,128)(2,1)S(1)}, u32[]{:S(2)}, u32[]{:S(2)}) collective-permute-start(bf16[144,1024]{1,0:T(8,128)(2,1)S(1)} %collective-permute-done.3.refs_3_), channel_id=1, source_target_pairs={{0,4},{1,3},{2,6},{3,1},{4,0},{5,7},{6,2},{7,5},{8,12},{9,11},{10,... | collective-permute-start | bytes 884744 | tf_op jit(solution)/shard_map/ppermute | solution.py:23
  16.5 0.6 %shard_map.66.refs_0_.refs_1_ = bf16[1024,1024]{1,0:T(8,128)(2,1)S(1)} custom-call(bf16[1024,1024]{1,0:T(8,128)(2,1)S(1)} %collective-permute-done.in_ref), custom_call_target="tpu_custom_call" | custom-call | tf_op jit(solution)/shard_map/pallas_call | solution.py:172
  17.1 0.8 %shard_map.69.refs_5_ = f32[64,1024]{1,0:T(8,128)S(1)} custom-call(bf16[1024,1024]{1,0:T(8,128)(2,1)S(1)} %shard_map.66.refs_0_.refs_1_, bf16[128,1024]{1,0:T(8,128)(2,1)S(1)} %shard_map.67.refs_1_, bf16[144,1024]{1,0:T(8,128)(2,1)S(1)} %shard_map.65.refs_2_), custom_call_target="tpu_custom_call" | custom-call | flops 671088640 | bytes 2621440 | tf_op jit(solution)/shard_map/pallas_call | solution.py:143
  18.0 1.6 %collective-permute-done.4.refs_3_ = bf16[144,1024]{1,0:T(8,128)(2,1)S(1)} collective-permute-done((bf16[144,1024]{1,0:T(8,128)(2,1)S(1)}, bf16[144,1024]{1,0:T(8,128)(2,1)S(1)}, u32[]{:S(2)}, u32[]{:S(2)}) %collective-permute-start.4) | collective-permute-done | bytes 294944 | tf_op jit(solution)/shard_map/ppermute | solution.py:23
  19.6 1.5 %shard_map.70 = (f32[64,1024]{1,0:T(8,128)S(1)}, f32[64,1024]{1,0:T(8,128)S(1)}) custom-call(bf16[1024,1024]{1,0:T(8,128)(2,1)S(1)} %shard_map.64.refs_0_.refs_1_, bf16[1024,1024]{1,0:T(8,128)(2,1)S(1)} %shard_map.66.refs_0_.refs_1_, bf16[128,1024]{1,0:T(8,128)(2,1)S(1)} %collective-permute-done.2.refs_2_, ...), custom_call_target="tpu_custom_call" | custom-call | flops 1342177280 | bytes 4718592 | tf_op jit(solution)/shard_map/pallas_call | solution.py:143
  21.1 1.5 %shard_map.71 = (f32[64,1024]{1,0:T(8,128)S(1)}, f32[64,1024]{1,0:T(8,128)S(1)}) custom-call(bf16[1024,1024]{1,0:T(8,128)(2,1)S(1)} %shard_map.64.refs_0_.refs_1_, bf16[1024,1024]{1,0:T(8,128)(2,1)S(1)} %shard_map.66.refs_0_.refs_1_, bf16[128,1024]{1,0:T(8,128)(2,1)S(1)} %collective-permute-done.1.refs_2_, ...), custom_call_target="tpu_custom_call" | custom-call | flops 1342177280 | bytes 4718592 | tf_op jit(solution)/shard_map/pallas_call | solution.py:143
  23.5 0.6 %shard_map.73 = f32[64,512]{1,0:T(8,128)S(1)} custom-call(bf16[1024,1024]{1,0:T(8,128)(2,1)S(1)} %shard_map.66.refs_0_.refs_1_, bf16[128,1024]{1,0:T(8,128)(2,1)S(1)} %collective-permute-done.5.refs_2_.refs_1_, bf16[144,1024]{1,0:T(8,128)(2,1)S(1)} %collective-permute-done.6.refs_3_.refs_2_, f32[64,1024]{1,0:T(8,128)S(1)} %get-tuple-element.24.refs_4_.refs_3_), custom_call_target="tpu_custom_call" | custom-call | flops 335544320 | bytes 1572864 | tf_op jit(solution)/shard_map/pallas_call | solution.py:143
  24.2 0.9 %shard_map.72 = (f32[64,512]{1,0:T(8,128)S(1)}, f32[64,512]{1,0:T(8,128)S(1)}) custom-call(bf16[1024,1024]{1,0:T(8,128)(2,1)S(1)} %shard_map.66.refs_0_.refs_1_, bf16[1024,1024]{1,0:T(8,128)(2,1)S(1)} %shard_map.64.refs_0_.refs_1_, bf16[128,1024]{1,0:T(8,128)(2,1)S(1)} %collective-permute-done.5.refs_2_.refs_1_, ...), custom_call_target="tpu_custom_call" | custom-call | flops 671088640 | bytes 2621440 | tf_op jit(solution)/shard_map/pallas_call | solution.py:143
  25.6 1.7 %collective-permute-start.8 = (bf16[64,512]{1,0:T(8,128)(2,1)S(1)}, bf16[64,512]{1,0:T(8,128)(2,1)S(1)}, u32[]{:S(2)}, u32[]{:S(2)}) collective-permute-start(bf16[64,512]{1,0:T(8,128)(2,1)S(1)} %shard_map.74.a_ref), channel_id=1, source_target_pairs={{0,8},{1,17},{2,10},{3,19},{4,12},{5,21},{6,14},{7,23},{8,0},{9,25... | collective-permute-start | bytes 196616 | tf_op jit(solution)/shard_map/ppermute | solution.py:33
  27.3 0.6 %shard_map.76.a_ref = f32[64,512]{1,0:T(8,128)S(1)} custom-call(bf16[1024,1024]{1,0:T(8,128)(2,1)S(1)} %shard_map.64.refs_0_.refs_1_, bf16[128,1024]{1,0:T(8,128)(2,1)S(1)} %collective-permute-done.5.refs_2_.refs_1_, bf16[144,1024]{1,0:T(8,128)(2,1)S(1)} %collective-permute-done.6.refs_3_.refs_2_, f32[64,1024]{1,0:T(8,128)S(1)} %get-tuple-element.27.refs_5_.refs_3_), custom_call_target="tpu_custom_call" | custom-call | flops 335544320 | bytes 1572864 | tf_op jit(solution)/shard_map/pallas_call | solution.py:143
  28.5 2.2 %collective-permute-done.8.b_ref = bf16[64,512]{1,0:T(8,128)(2,1)S(1)} collective-permute-done((bf16[64,512]{1,0:T(8,128)(2,1)S(1)}, bf16[64,512]{1,0:T(8,128)(2,1)S(1)}, u32[]{:S(2)}, u32[]{:S(2)}) %collective-permute-start.8) | collective-permute-done | bytes 65568 | tf_op jit(solution)/shard_map/ppermute | solution.py:33
  30.6 2.0 %collective-permute-start.9 = (bf16[64,512]{1,0:T(8,128)(2,1)S(1)}, bf16[64,512]{1,0:T(8,128)(2,1)S(1)}, u32[]{:S(2)}, u32[]{:S(2)}) collective-permute-start(bf16[64,512]{1,0:T(8,128)(2,1)S(1)} %shard_map.75.refs_0_), channel_id=1, source_target_pairs={{0,16},{1,9},{2,18},{3,11},{4,20},{5,13},{6,22},{7,15},{8,24},{9,1... | collective-permute-start | bytes 196616 | tf_op jit(solution)/shard_map/ppermute | solution.py:33
  32.6 2.9 %collective-permute-start.12 = (bf16[64,512]{1,0:T(8,128)(2,1)S(1)}, bf16[64,512]{1,0:T(8,128)(2,1)S(1)}, u32[]{:S(2)}, u32[]{:S(2)}) collective-permute-start(bf16[64,512]{1,0:T(8,128)(2,1)S(1)} %shard_map.78.refs_2_), channel_id=1, source_target_pairs={{0,16},{1,9},{2,18},{3,11},{4,20},{5,13},{6,22},{7,15},{8,24},{9,1... | collective-permute-start | bytes 196616 | tf_op jit(solution)/shard_map/ppermute | solution.py:33
  35.9 2.0 %collective-permute-done.12.refs_3_ = bf16[64,512]{1,0:T(8,128)(2,1)S(1)} collective-permute-done((bf16[64,512]{1,0:T(8,128)(2,1)S(1)}, bf16[64,512]{1,0:T(8,128)(2,1)S(1)}, u32[]{:S(2)}, u32[]{:S(2)}) %collective-permute-start.12) | collective-permute-done | bytes 65568 | tf_op jit(solution)/shard_map/ppermute | solution.py:33
  37.9 0.8 %shard_map.79 = f32[64,1024]{1,0:T(8,128)} custom-call(bf16[64,512]{1,0:T(8,128)(2,1)S(1)} %shard_map.75.refs_0_, bf16[64,512]{1,0:T(8,128)(2,1)S(1)} %collective-permute-done.9.refs_1_, bf16[64,512]{1,0:T(8,128)(2,1)S(1)} %shard_map.78.refs_2_, bf16[64,512]{1,0:T(8,128)(2,1)S(1)} %collective-permute-done.12.refs_3_, f32[64,1]{1,0:T(8,128)S(1)} %copy.7.refs_4_), custom_call_target="tpu_custom_call" | custom-call | tf_op jit(solution)/shard_map/pallas_call | solution.py:172
  (23 shorter events, 3.5 us)
Async XLA Ops:
  1.0 15.5 %collective-permute-start = (bf16[1024,1024]{1,0:T(8,128)(2,1)}, bf16[1024,1024]{1,0:T(8,128)(2,1)S(1)}, u32[]{:S(2)}, u32[]{:S(2)}) collective-permute-start(bf16[1024,1024]{1,0:T(8,128)(2,1)} %in_ref.1), channel_id=1, source_target_pairs={{0,1},{1,0},{2,3},{3,2},{4,5},{5,4},{6,7},{7,6},{8,9},{9,8},{10,11... | collective-permute-start | bytes 6291464 | tf_op jit(solution)/shard_map/ppermute | solution.py:18
  1.5 12.2 %collective-permute-start.3 = (bf16[144,1024]{1,0:T(8,128)(2,1)S(1)}, bf16[144,1024]{1,0:T(8,128)(2,1)S(1)}, u32[]{:S(2)}, u32[]{:S(2)}) collective-permute-start(bf16[144,1024]{1,0:T(8,128)(2,1)S(1)} %shard_map.65.refs_2_), channel_id=1, source_target_pairs={{0,2},{1,5},{2,0},{3,7},{4,6},{5,1},{6,4},{7,3},{8,10},{9,13},{10,... | collective-permute-start | bytes 884744 | tf_op jit(solution)/shard_map/ppermute | solution.py:23
  5.1 8.6 %collective-permute-start.2 = (bf16[128,1024]{1,0:T(8,128)(2,1)S(1)}, bf16[128,1024]{1,0:T(8,128)(2,1)S(1)}, u32[]{:S(2)}, u32[]{:S(2)}) collective-permute-start(bf16[128,1024]{1,0:T(8,128)(2,1)S(1)} %shard_map.67.refs_1_), channel_id=1, source_target_pairs={{0,4},{1,3},{2,6},{3,1},{4,0},{5,7},{6,2},{7,5},{8,12},{9,11},{10,... | collective-permute-start | bytes 786440 | tf_op jit(solution)/shard_map/ppermute | solution.py:23
  6.7 12.9 %collective-permute-start.4 = (bf16[144,1024]{1,0:T(8,128)(2,1)S(1)}, bf16[144,1024]{1,0:T(8,128)(2,1)S(1)}, u32[]{:S(2)}, u32[]{:S(2)}) collective-permute-start(bf16[144,1024]{1,0:T(8,128)(2,1)S(1)} %shard_map.65.refs_2_), channel_id=1, source_target_pairs={{0,4},{1,3},{2,6},{3,1},{4,0},{5,7},{6,2},{7,5},{8,12},{9,11},{10,... | collective-permute-start | bytes 884744 | tf_op jit(solution)/shard_map/ppermute | solution.py:23
  7.2 14.0 %collective-permute-start.1 = (bf16[128,1024]{1,0:T(8,128)(2,1)S(1)}, bf16[128,1024]{1,0:T(8,128)(2,1)S(1)}, u32[]{:S(2)}, u32[]{:S(2)}) collective-permute-start(bf16[128,1024]{1,0:T(8,128)(2,1)S(1)} %shard_map.67.refs_1_), channel_id=1, source_target_pairs={{0,2},{1,5},{2,0},{3,7},{4,6},{5,1},{6,4},{7,3},{8,10},{9,13},{10,... | collective-permute-start | bytes 786440 | tf_op jit(solution)/shard_map/ppermute | solution.py:23
  7.3 1.6 %copy-start = (bf16[1024,1024]{1,0:T(8,128)(2,1)S(1)}, bf16[1024,1024]{1,0:T(8,128)(2,1)}, u32[]{:S(2)}) copy-start(bf16[1024,1024]{1,0:T(8,128)(2,1)} %in_ref.1) | copy-start | bytes 6291460
  13.7 9.2 %collective-permute-start.5 = (bf16[128,1024]{1,0:T(8,128)(2,1)S(1)}, bf16[128,1024]{1,0:T(8,128)(2,1)S(1)}, u32[]{:S(2)}, u32[]{:S(2)}) collective-permute-start(bf16[128,1024]{1,0:T(8,128)(2,1)S(1)} %collective-permute-done.2.refs_2_), channel_id=1, source_target_pairs={{0,2},{1,5},{2,0},{3,7},{4,6},{5,1},{6,4},{7,3},{8,10},{9,13},{10,... | collective-permute-start | bytes 786440 | tf_op jit(solution)/shard_map/ppermute | solution.py:23
  14.4 9.0 %collective-permute-start.6 = (bf16[144,1024]{1,0:T(8,128)(2,1)S(1)}, bf16[144,1024]{1,0:T(8,128)(2,1)S(1)}, u32[]{:S(2)}, u32[]{:S(2)}) collective-permute-start(bf16[144,1024]{1,0:T(8,128)(2,1)S(1)} %collective-permute-done.3.refs_3_), channel_id=1, source_target_pairs={{0,4},{1,3},{2,6},{3,1},{4,0},{5,7},{6,2},{7,5},{8,12},{9,11},{10,... | collective-permute-start | bytes 884744 | tf_op jit(solution)/shard_map/ppermute | solution.py:23
  24.1 1.5 %collective-permute-start.7 = (f32[64,512]{1,0:T(8,128)S(1)}, f32[64,512]{1,0:T(8,128)S(1)}, u32[]{:S(2)}, u32[]{:S(2)}) collective-permute-start(f32[64,512]{1,0:T(8,128)S(1)} %shard_map.73), channel_id=1, source_target_pairs={{0,1},{1,0},{2,3},{3,2},{4,5},{5,4},{6,7},{7,6},{8,9},{9,8},{10,11... | collective-permute-start | bytes 393224 | tf_op jit(solution)/shard_map/ppermute | solution.py:18
  25.1 10.5 %copy-start.1 = (f32[64]{0:T(128)S(1)}, f32[64]{0:T(128)}, u32[]{:S(2)}) copy-start(f32[64]{0:T(128)} %param.11) | copy-start | bytes 772
  25.1 2.8 %collective-permute-start.10 = (f32[64,512]{1,0:T(8,128)S(1)}, f32[64,512]{1,0:T(8,128)S(1)}, u32[]{:S(2)}, u32[]{:S(2)}) collective-permute-start(f32[64,512]{1,0:T(8,128)S(1)} %get-tuple-element.28), channel_id=1, source_target_pairs={{0,1},{1,0},{2,3},{3,2},{4,5},{5,4},{6,7},{7,6},{8,9},{9,8},{10,11... | collective-permute-start | bytes 393224 | tf_op jit(solution)/shard_map/ppermute | solution.py:18
  25.6 5.0 %collective-permute-start.8 = (bf16[64,512]{1,0:T(8,128)(2,1)S(1)}, bf16[64,512]{1,0:T(8,128)(2,1)S(1)}, u32[]{:S(2)}, u32[]{:S(2)}) collective-permute-start(bf16[64,512]{1,0:T(8,128)(2,1)S(1)} %shard_map.74.a_ref), channel_id=1, source_target_pairs={{0,8},{1,17},{2,10},{3,19},{4,12},{5,21},{6,14},{7,23},{8,0},{9,25... | collective-permute-start | bytes 196616 | tf_op jit(solution)/shard_map/ppermute | solution.py:33
  27.9 4.7 %collective-permute-start.11 = (bf16[64,512]{1,0:T(8,128)(2,1)S(1)}, bf16[64,512]{1,0:T(8,128)(2,1)S(1)}, u32[]{:S(2)}, u32[]{:S(2)}) collective-permute-start(bf16[64,512]{1,0:T(8,128)(2,1)S(1)} %shard_map.77.a_ref), channel_id=1, source_target_pairs={{0,8},{1,17},{2,10},{3,19},{4,12},{5,21},{6,14},{7,23},{8,0},{9,25... | collective-permute-start | bytes 196616 | tf_op jit(solution)/shard_map/ppermute | solution.py:33
  30.6 5.2 %collective-permute-start.9 = (bf16[64,512]{1,0:T(8,128)(2,1)S(1)}, bf16[64,512]{1,0:T(8,128)(2,1)S(1)}, u32[]{:S(2)}, u32[]{:S(2)}) collective-permute-start(bf16[64,512]{1,0:T(8,128)(2,1)S(1)} %shard_map.75.refs_0_), channel_id=1, source_target_pairs={{0,16},{1,9},{2,18},{3,11},{4,20},{5,13},{6,22},{7,15},{8,24},{9,1... | collective-permute-start | bytes 196616 | tf_op jit(solution)/shard_map/ppermute | solution.py:33
  32.6 5.2 %collective-permute-start.12 = (bf16[64,512]{1,0:T(8,128)(2,1)S(1)}, bf16[64,512]{1,0:T(8,128)(2,1)S(1)}, u32[]{:S(2)}, u32[]{:S(2)}) collective-permute-start(bf16[64,512]{1,0:T(8,128)(2,1)S(1)} %shard_map.78.refs_2_), channel_id=1, source_target_pairs={{0,16},{1,9},{2,18},{3,11},{4,20},{5,13},{6,22},{7,15},{8,24},{9,1... | collective-permute-start | bytes 196616 | tf_op jit(solution)/shard_map/ppermute | solution.py:33

commit v15 on v12

--- a/solution.py
+++ b/solution.py
@@ -198,10 +198,8 @@
     other = small_call(transpose_kernel, turned, core_send(late_slab, n_sl))
     slab = small_call(transpose_kernel, turned, slab)
     (acc,) = stage([slab], first, second, None, coeff, cols)
-    held = [blocks[1 << k][k % 2] for k in range(ways)]
-    held, acc = lax.optimization_barrier((held, acc))
-    for k in range(ways):
-        blocks[1 << k][k % 2] = held[k]
+    for k in reversed(range(ways)):
+        blocks[1 << k][k % 2], acc = lax.optimization_barrier((blocks[1 << k][k % 2], acc))
     (other_acc,) = stage([other], first, second, None, coeff, cols)
     accs = [acc, other_acc]
     for t in range(1, 1 << ways):

time: 38.9 us -> 38.9 us (level)
  no operation moved by 1% of the time
where the time goes in v15:
time: 38.9 us; the launch traced here: 38.7 us
  starting transfers between devices  15.8 us (41%)
  Pallas kernels  11 us (28%)
  waiting for transfers between devices  10.1 us (26%)
  local copies, waits for them, and re-layouts  1.69 us (4%)
    ppermute x6, starting transfers between devices, chip_send(): lax.ppermute(value, 'sl', [(i, i ^ bits[(k + 1 - i % 2) % len(bits)]) for...  7.51 us
    ppermute x4, starting transfers between devices, lm_send(): return lax.ppermute(value, ('lm', 'sl'), perm)  7.16 us
    pallas_call x7, Pallas kernels, stage(): pl.pallas_call(functools.partial(stage_kernel, count, coeff, ritz, accs i...  6.83 us
    ppermute x6, waiting for transfers between devices, chip_send(): lax.ppermute(value, 'sl', [(i, i ^ bits[(k + 1 - i % 2) % len(bits)]) for...  5.74 us
    ppermute x4, waiting for transfers between devices, lm_send(): return lax.ppermute(value, ('lm', 'sl'), perm)  4.37 us
    pallas_call x7, Pallas kernels, small_call(): pl.pallas_call(kernel, out_shape=jax.ShapeDtypeStruct(out.shape, out.dtyp...  2.13 us
    unnamed x4, local copies, waits for them, and re-layouts  1.59 us
    ppermute x3, starting transfers between devices, core_send(): return lax.ppermute(value, 'sl', [(i, i ^ 1) for i in range(n)])  1.15 us
  transfers between devices with their start and end apart: 13, of which 7 were waited for; matrix products, arithmetic and copies ran while one was open for 0% of the time, Pallas kernels for 22%

profile of v15, /device:TPU:0, one launch (start us, length us, event | category | flops | bytes accessed | tf_op | source)
XLA Modules:
  0.0 38.7 jit_solution(18355218011723830169)
XLA Ops:
  0.0 1.0 %shard_map.65.refs_2_ = bf16[144,1024]{1,0:T(8,128)(2,1)S(1)} custom-call(bf16[256,1024]{1,0:T(8,128)(2,1)} %land_ref.3), custom_call_target="tpu_custom_call" | custom-call | tf_op jit(solution)/shard_map/pallas_call | solution.py:75
  1.5 2.6 %collective-permute-start.2 = (bf16[144,1024]{1,0:T(8,128)(2,1)S(1)}, bf16[144,1024]{1,0:T(8,128)(2,1)S(1)}, u32[]{:S(2)}, u32[]{:S(2)}) collective-permute-start(bf16[144,1024]{1,0:T(8,128)(2,1)S(1)} %shard_map.65.refs_2_), channel_id=1, source_target_pairs={{0,2},{1,5},{2,0},{3,7},{4,6},{5,1},{6,4},{7,3},{8,10},{9,13},{10,... | collective-permute-start | bytes 884744 | tf_op jit(solution)/shard_map/ppermute | solution.py:23
  4.1 1.0 %shard_map.67.refs_1_ = bf16[128,1024]{1,0:T(8,128)(2,1)S(1)} custom-call(bf16[256,1024]{1,0:T(8,128)(2,1)} %land_ref.3, bf16[96,256]{1,0:T(8,128)(2,1)} %bitcast.4, s32[2]{0:T(128)} %exponents_ref.1, bf16[64,96]{1,0:T(8,128)(2,1)} %bitcast.5), custom_call_target="tpu_custom_call" | custom-call | tf_op jit(solution)/shard_map/pallas_call | solution.py:87
  5.1 1.6 %collective-permute-start.3 = (bf16[128,1024]{1,0:T(8,128)(2,1)S(1)}, bf16[128,1024]{1,0:T(8,128)(2,1)S(1)}, u32[]{:S(2)}, u32[]{:S(2)}) collective-permute-start(bf16[128,1024]{1,0:T(8,128)(2,1)S(1)} %shard_map.67.refs_1_), channel_id=1, source_target_pairs={{0,4},{1,3},{2,6},{3,1},{4,0},{5,7},{6,2},{7,5},{8,12},{9,11},{10,... | collective-permute-start | bytes 786440 | tf_op jit(solution)/shard_map/ppermute | solution.py:23
  7.3 1.6 %copy-done = bf16[1024,1024]{1,0:T(8,128)(2,1)S(1)} copy-done((bf16[1024,1024]{1,0:T(8,128)(2,1)S(1)}, bf16[1024,1024]{1,0:T(8,128)(2,1)}, u32[]{:S(2)}) %copy-start) | copy-done | bytes 2097176
  8.9 0.6 %shard_map.64.refs_0_.refs_1_ = bf16[1024,1024]{1,0:T(8,128)(2,1)S(1)} custom-call(bf16[1024,1024]{1,0:T(8,128)(2,1)S(1)} %copy-done), custom_call_target="tpu_custom_call" | custom-call | tf_op jit(solution)/shard_map/pallas_call | solution.py:172
  9.5 0.9 %shard_map.68.refs_4_ = f32[64,1024]{1,0:T(8,128)S(1)} custom-call(bf16[1024,1024]{1,0:T(8,128)(2,1)S(1)} %shard_map.64.refs_0_.refs_1_, bf16[128,1024]{1,0:T(8,128)(2,1)S(1)} %shard_map.67.refs_1_, bf16[144,1024]{1,0:T(8,128)(2,1)S(1)} %shard_map.65.refs_2_), custom_call_target="tpu_custom_call" | custom-call | flops 671088640 | bytes 2621440 | tf_op jit(solution)/shard_map/pallas_call | solution.py:143
  10.4 3.3 %collective-permute-done.3.refs_2_ = bf16[128,1024]{1,0:T(8,128)(2,1)S(1)} collective-permute-done((bf16[128,1024]{1,0:T(8,128)(2,1)S(1)}, bf16[128,1024]{1,0:T(8,128)(2,1)S(1)}, u32[]{:S(2)}, u32[]{:S(2)}) %collective-permute-start.3) | collective-permute-done | bytes 262176 | tf_op jit(solution)/shard_map/ppermute | solution.py:23
  13.7 0.7 %collective-permute-start.5 = (bf16[128,1024]{1,0:T(8,128)(2,1)S(1)}, bf16[128,1024]{1,0:T(8,128)(2,1)S(1)}, u32[]{:S(2)}, u32[]{:S(2)}) collective-permute-start(bf16[128,1024]{1,0:T(8,128)(2,1)S(1)} %collective-permute-done.3.refs_2_), channel_id=1, source_target_pairs={{0,2},{1,5},{2,0},{3,7},{4,6},{5,1},{6,4},{7,3},{8,10},{9,13},{10,... | collective-permute-start | bytes 786440 | tf_op jit(solution)/shard_map/ppermute | solution.py:23
  14.4 2.0 %collective-permute-start.6 = (bf16[144,1024]{1,0:T(8,128)(2,1)S(1)}, bf16[144,1024]{1,0:T(8,128)(2,1)S(1)}, u32[]{:S(2)}, u32[]{:S(2)}) collective-permute-start(bf16[144,1024]{1,0:T(8,128)(2,1)S(1)} %collective-permute-done.2.refs_3_), channel_id=1, source_target_pairs={{0,4},{1,3},{2,6},{3,1},{4,0},{5,7},{6,2},{7,5},{8,12},{9,11},{10,... | collective-permute-start | bytes 884744 | tf_op jit(solution)/shard_map/ppermute | solution.py:23
  16.5 0.6 %shard_map.66.refs_0_.refs_1_ = bf16[1024,1024]{1,0:T(8,128)(2,1)S(1)} custom-call(bf16[1024,1024]{1,0:T(8,128)(2,1)S(1)} %collective-permute-done.in_ref), custom_call_target="tpu_custom_call" | custom-call | tf_op jit(solution)/shard_map/pallas_call | solution.py:172
  17.1 0.9 %shard_map.69.refs_5_ = f32[64,1024]{1,0:T(8,128)S(1)} custom-call(bf16[1024,1024]{1,0:T(8,128)(2,1)S(1)} %shard_map.66.refs_0_.refs_1_, bf16[128,1024]{1,0:T(8,128)(2,1)S(1)} %shard_map.67.refs_1_, bf16[144,1024]{1,0:T(8,128)(2,1)S(1)} %shard_map.65.refs_2_), custom_call_target="tpu_custom_call" | custom-call | flops 671088640 | bytes 2621440 | tf_op jit(solution)/shard_map/pallas_call | solution.py:143
  18.0 1.6 %collective-permute-done.4.refs_3_ = bf16[144,1024]{1,0:T(8,128)(2,1)S(1)} collective-permute-done((bf16[144,1024]{1,0:T(8,128)(2,1)S(1)}, bf16[144,1024]{1,0:T(8,128)(2,1)S(1)}, u32[]{:S(2)}, u32[]{:S(2)}) %collective-permute-start.4) | collective-permute-done | bytes 294944 | tf_op jit(solution)/shard_map/ppermute | solution.py:23
  19.6 1.5 %shard_map.70 = (f32[64,1024]{1,0:T(8,128)S(1)}, f32[64,1024]{1,0:T(8,128)S(1)}) custom-call(bf16[1024,1024]{1,0:T(8,128)(2,1)S(1)} %shard_map.64.refs_0_.refs_1_, bf16[1024,1024]{1,0:T(8,128)(2,1)S(1)} %shard_map.66.refs_0_.refs_1_, bf16[128,1024]{1,0:T(8,128)(2,1)S(1)} %collective-permute-done.3.refs_2_, ...), custom_call_target="tpu_custom_call" | custom-call | flops 1342177280 | bytes 4718592 | tf_op jit(solution)/shard_map/pallas_call | solution.py:143
  21.1 1.5 %shard_map.71 = (f32[64,1024]{1,0:T(8,128)S(1)}, f32[64,1024]{1,0:T(8,128)S(1)}) custom-call(bf16[1024,1024]{1,0:T(8,128)(2,1)S(1)} %shard_map.64.refs_0_.refs_1_, bf16[1024,1024]{1,0:T(8,128)(2,1)S(1)} %shard_map.66.refs_0_.refs_1_, bf16[128,1024]{1,0:T(8,128)(2,1)S(1)} %collective-permute-done.1.refs_2_, ...), custom_call_target="tpu_custom_call" | custom-call | flops 1342177280 | bytes 4718592 | tf_op jit(solution)/shard_map/pallas_call | solution.py:143
  23.5 0.6 %shard_map.73 = f32[64,512]{1,0:T(8,128)S(1)} custom-call(bf16[1024,1024]{1,0:T(8,128)(2,1)S(1)} %shard_map.66.refs_0_.refs_1_, bf16[128,1024]{1,0:T(8,128)(2,1)S(1)} %collective-permute-done.5.refs_2_.refs_1_, bf16[144,1024]{1,0:T(8,128)(2,1)S(1)} %collective-permute-done.6.refs_3_.refs_2_, f32[64,1024]{1,0:T(8,128)S(1)} %get-tuple-element.26.refs_4_.refs_3_), custom_call_target="tpu_custom_call" | custom-call | flops 335544320 | bytes 1572864 | tf_op jit(solution)/shard_map/pallas_call | solution.py:143
  24.2 0.9 %shard_map.72 = (f32[64,512]{1,0:T(8,128)S(1)}, f32[64,512]{1,0:T(8,128)S(1)}) custom-call(bf16[1024,1024]{1,0:T(8,128)(2,1)S(1)} %shard_map.66.refs_0_.refs_1_, bf16[1024,1024]{1,0:T(8,128)(2,1)S(1)} %shard_map.64.refs_0_.refs_1_, bf16[128,1024]{1,0:T(8,128)(2,1)S(1)} %collective-permute-done.5.refs_2_.refs_1_, ...), custom_call_target="tpu_custom_call" | custom-call | flops 671088640 | bytes 2621440 | tf_op jit(solution)/shard_map/pallas_call | solution.py:143
  25.6 1.7 %collective-permute-start.8 = (bf16[64,512]{1,0:T(8,128)(2,1)S(1)}, bf16[64,512]{1,0:T(8,128)(2,1)S(1)}, u32[]{:S(2)}, u32[]{:S(2)}) collective-permute-start(bf16[64,512]{1,0:T(8,128)(2,1)S(1)} %shard_map.74.a_ref), channel_id=1, source_target_pairs={{0,8},{1,17},{2,10},{3,19},{4,12},{5,21},{6,14},{7,23},{8,0},{9,25... | collective-permute-start | bytes 196616 | tf_op jit(solution)/shard_map/ppermute | solution.py:33
  27.3 0.6 %shard_map.76.a_ref = f32[64,512]{1,0:T(8,128)S(1)} custom-call(bf16[1024,1024]{1,0:T(8,128)(2,1)S(1)} %shard_map.64.refs_0_.refs_1_, bf16[128,1024]{1,0:T(8,128)(2,1)S(1)} %collective-permute-done.5.refs_2_.refs_1_, bf16[144,1024]{1,0:T(8,128)(2,1)S(1)} %collective-permute-done.6.refs_3_.refs_2_, f32[64,1024]{1,0:T(8,128)S(1)} %get-tuple-element.29.refs_5_.refs_3_), custom_call_target="tpu_custom_call" | custom-call | flops 335544320 | bytes 1572864 | tf_op jit(solution)/shard_map/pallas_call | solution.py:143
  28.5 2.2 %collective-permute-done.8.b_ref = bf16[64,512]{1,0:T(8,128)(2,1)S(1)} collective-permute-done((bf16[64,512]{1,0:T(8,128)(2,1)S(1)}, bf16[64,512]{1,0:T(8,128)(2,1)S(1)}, u32[]{:S(2)}, u32[]{:S(2)}) %collective-permute-start.8) | collective-permute-done | bytes 65568 | tf_op jit(solution)/shard_map/ppermute | solution.py:33
  30.6 2.0 %collective-permute-start.9 = (bf16[64,512]{1,0:T(8,128)(2,1)S(1)}, bf16[64,512]{1,0:T(8,128)(2,1)S(1)}, u32[]{:S(2)}, u32[]{:S(2)}) collective-permute-start(bf16[64,512]{1,0:T(8,128)(2,1)S(1)} %shard_map.75.refs_0_), channel_id=1, source_target_pairs={{0,16},{1,9},{2,18},{3,11},{4,20},{5,13},{6,22},{7,15},{8,24},{9,1... | collective-permute-start | bytes 196616 | tf_op jit(solution)/shard_map/ppermute | solution.py:33
  32.7 2.9 %collective-permute-start.12 = (bf16[64,512]{1,0:T(8,128)(2,1)S(1)}, bf16[64,512]{1,0:T(8,128)(2,1)S(1)}, u32[]{:S(2)}, u32[]{:S(2)}) collective-permute-start(bf16[64,512]{1,0:T(8,128)(2,1)S(1)} %shard_map.78.refs_2_), channel_id=1, source_target_pairs={{0,16},{1,9},{2,18},{3,11},{4,20},{5,13},{6,22},{7,15},{8,24},{9,1... | collective-permute-start | bytes 196616 | tf_op jit(solution)/shard_map/ppermute | solution.py:33
  35.9 2.0 %collective-permute-done.12.refs_3_ = bf16[64,512]{1,0:T(8,128)(2,1)S(1)} collective-permute-done((bf16[64,512]{1,0:T(8,128)(2,1)S(1)}, bf16[64,512]{1,0:T(8,128)(2,1)S(1)}, u32[]{:S(2)}, u32[]{:S(2)}) %collective-permute-start.12) | collective-permute-done | bytes 65568 | tf_op jit(solution)/shard_map/ppermute | solution.py:33
  37.9 0.8 %shard_map.79 = f32[64,1024]{1,0:T(8,128)} custom-call(bf16[64,512]{1,0:T(8,128)(2,1)S(1)} %shard_map.75.refs_0_, bf16[64,512]{1,0:T(8,128)(2,1)S(1)} %collective-permute-done.9.refs_1_, bf16[64,512]{1,0:T(8,128)(2,1)S(1)} %shard_map.78.refs_2_, bf16[64,512]{1,0:T(8,128)(2,1)S(1)} %collective-permute-done.12.refs_3_, f32[64,1]{1,0:T(8,128)S(1)} %copy.7.refs_4_), custom_call_target="tpu_custom_call" | custom-call | tf_op jit(solution)/shard_map/pallas_call | solution.py:172
  (23 shorter events, 3.5 us)
Async XLA Ops:
  1.0 15.5 %collective-permute-start = (bf16[1024,1024]{1,0:T(8,128)(2,1)}, bf16[1024,1024]{1,0:T(8,128)(2,1)S(1)}, u32[]{:S(2)}, u32[]{:S(2)}) collective-permute-start(bf16[1024,1024]{1,0:T(8,128)(2,1)} %in_ref.1), channel_id=1, source_target_pairs={{0,1},{1,0},{2,3},{3,2},{4,5},{5,4},{6,7},{7,6},{8,9},{9,8},{10,11... | collective-permute-start | bytes 6291464 | tf_op jit(solution)/shard_map/ppermute | solution.py:18
  1.5 8.9 %collective-permute-start.2 = (bf16[144,1024]{1,0:T(8,128)(2,1)S(1)}, bf16[144,1024]{1,0:T(8,128)(2,1)S(1)}, u32[]{:S(2)}, u32[]{:S(2)}) collective-permute-start(bf16[144,1024]{1,0:T(8,128)(2,1)S(1)} %shard_map.65.refs_2_), channel_id=1, source_target_pairs={{0,2},{1,5},{2,0},{3,7},{4,6},{5,1},{6,4},{7,3},{8,10},{9,13},{10,... | collective-permute-start | bytes 884744 | tf_op jit(solution)/shard_map/ppermute | solution.py:23
  5.1 8.6 %collective-permute-start.3 = (bf16[128,1024]{1,0:T(8,128)(2,1)S(1)}, bf16[128,1024]{1,0:T(8,128)(2,1)S(1)}, u32[]{:S(2)}, u32[]{:S(2)}) collective-permute-start(bf16[128,1024]{1,0:T(8,128)(2,1)S(1)} %shard_map.67.refs_1_), channel_id=1, source_target_pairs={{0,4},{1,3},{2,6},{3,1},{4,0},{5,7},{6,2},{7,5},{8,12},{9,11},{10,... | collective-permute-start | bytes 786440 | tf_op jit(solution)/shard_map/ppermute | solution.py:23
  6.7 12.9 %collective-permute-start.4 = (bf16[144,1024]{1,0:T(8,128)(2,1)S(1)}, bf16[144,1024]{1,0:T(8,128)(2,1)S(1)}, u32[]{:S(2)}, u32[]{:S(2)}) collective-permute-start(bf16[144,1024]{1,0:T(8,128)(2,1)S(1)} %shard_map.65.refs_2_), channel_id=1, source_target_pairs={{0,4},{1,3},{2,6},{3,1},{4,0},{5,7},{6,2},{7,5},{8,12},{9,11},{10,... | collective-permute-start | bytes 884744 | tf_op jit(solution)/shard_map/ppermute | solution.py:23
  7.2 14.0 %collective-permute-start.1 = (bf16[128,1024]{1,0:T(8,128)(2,1)S(1)}, bf16[128,1024]{1,0:T(8,128)(2,1)S(1)}, u32[]{:S(2)}, u32[]{:S(2)}) collective-permute-start(bf16[128,1024]{1,0:T(8,128)(2,1)S(1)} %shard_map.67.refs_1_), channel_id=1, source_target_pairs={{0,2},{1,5},{2,0},{3,7},{4,6},{5,1},{6,4},{7,3},{8,10},{9,13},{10,... | collective-permute-start | bytes 786440 | tf_op jit(solution)/shard_map/ppermute | solution.py:23
  7.3 1.6 %copy-start = (bf16[1024,1024]{1,0:T(8,128)(2,1)S(1)}, bf16[1024,1024]{1,0:T(8,128)(2,1)}, u32[]{:S(2)}) copy-start(bf16[1024,1024]{1,0:T(8,128)(2,1)} %in_ref.1) | copy-start | bytes 6291460
  13.7 9.2 %collective-permute-start.5 = (bf16[128,1024]{1,0:T(8,128)(2,1)S(1)}, bf16[128,1024]{1,0:T(8,128)(2,1)S(1)}, u32[]{:S(2)}, u32[]{:S(2)}) collective-permute-start(bf16[128,1024]{1,0:T(8,128)(2,1)S(1)} %collective-permute-done.3.refs_2_), channel_id=1, source_target_pairs={{0,2},{1,5},{2,0},{3,7},{4,6},{5,1},{6,4},{7,3},{8,10},{9,13},{10,... | collective-permute-start | bytes 786440 | tf_op jit(solution)/shard_map/ppermute | solution.py:23
  14.4 9.0 %collective-permute-start.6 = (bf16[144,1024]{1,0:T(8,128)(2,1)S(1)}, bf16[144,1024]{1,0:T(8,128)(2,1)S(1)}, u32[]{:S(2)}, u32[]{:S(2)}) collective-permute-start(bf16[144,1024]{1,0:T(8,128)(2,1)S(1)} %collective-permute-done.2.refs_3_), channel_id=1, source_target_pairs={{0,4},{1,3},{2,6},{3,1},{4,0},{5,7},{6,2},{7,5},{8,12},{9,11},{10,... | collective-permute-start | bytes 884744 | tf_op jit(solution)/shard_map/ppermute | solution.py:23
  24.1 1.5 %collective-permute-start.7 = (f32[64,512]{1,0:T(8,128)S(1)}, f32[64,512]{1,0:T(8,128)S(1)}, u32[]{:S(2)}, u32[]{:S(2)}) collective-permute-start(f32[64,512]{1,0:T(8,128)S(1)} %shard_map.73), channel_id=1, source_target_pairs={{0,1},{1,0},{2,3},{3,2},{4,5},{5,4},{6,7},{7,6},{8,9},{9,8},{10,11... | collective-permute-start | bytes 393224 | tf_op jit(solution)/shard_map/ppermute | solution.py:18
  25.1 10.5 %copy-start.1 = (f32[64]{0:T(128)S(1)}, f32[64]{0:T(128)}, u32[]{:S(2)}) copy-start(f32[64]{0:T(128)} %param.11) | copy-start | bytes 772
  25.1 2.8 %collective-permute-start.10 = (f32[64,512]{1,0:T(8,128)S(1)}, f32[64,512]{1,0:T(8,128)S(1)}, u32[]{:S(2)}, u32[]{:S(2)}) collective-permute-start(f32[64,512]{1,0:T(8,128)S(1)} %get-tuple-element.30), channel_id=1, source_target_pairs={{0,1},{1,0},{2,3},{3,2},{4,5},{5,4},{6,7},{7,6},{8,9},{9,8},{10,11... | collective-permute-start | bytes 393224 | tf_op jit(solution)/shard_map/ppermute | solution.py:18
  25.6 5.0 %collective-permute-start.8 = (bf16[64,512]{1,0:T(8,128)(2,1)S(1)}, bf16[64,512]{1,0:T(8,128)(2,1)S(1)}, u32[]{:S(2)}, u32[]{:S(2)}) collective-permute-start(bf16[64,512]{1,0:T(8,128)(2,1)S(1)} %shard_map.74.a_ref), channel_id=1, source_target_pairs={{0,8},{1,17},{2,10},{3,19},{4,12},{5,21},{6,14},{7,23},{8,0},{9,25... | collective-permute-start | bytes 196616 | tf_op jit(solution)/shard_map/ppermute | solution.py:33
  27.9 4.7 %collective-permute-start.11 = (bf16[64,512]{1,0:T(8,128)(2,1)S(1)}, bf16[64,512]{1,0:T(8,128)(2,1)S(1)}, u32[]{:S(2)}, u32[]{:S(2)}) collective-permute-start(bf16[64,512]{1,0:T(8,128)(2,1)S(1)} %shard_map.77.a_ref), channel_id=1, source_target_pairs={{0,8},{1,17},{2,10},{3,19},{4,12},{5,21},{6,14},{7,23},{8,0},{9,25... | collective-permute-start | bytes 196616 | tf_op jit(solution)/shard_map/ppermute | solution.py:33
  30.6 5.2 %collective-permute-start.9 = (bf16[64,512]{1,0:T(8,128)(2,1)S(1)}, bf16[64,512]{1,0:T(8,128)(2,1)S(1)}, u32[]{:S(2)}, u32[]{:S(2)}) collective-permute-start(bf16[64,512]{1,0:T(8,128)(2,1)S(1)} %shard_map.75.refs_0_), channel_id=1, source_target_pairs={{0,16},{1,9},{2,18},{3,11},{4,20},{5,13},{6,22},{7,15},{8,24},{9,1... | collective-permute-start | bytes 196616 | tf_op jit(solution)/shard_map/ppermute | solution.py:33
  32.7 5.2 %collective-permute-start.12 = (bf16[64,512]{1,0:T(8,128)(2,1)S(1)}, bf16[64,512]{1,0:T(8,128)(2,1)S(1)}, u32[]{:S(2)}, u32[]{:S(2)}) collective-permute-start(bf16[64,512]{1,0:T(8,128)(2,1)S(1)} %shard_map.78.refs_2_), channel_id=1, source_target_pairs={{0,16},{1,9},{2,18},{3,11},{4,20},{5,13},{6,22},{7,15},{8,24},{9,1... | collective-permute-start | bytes 196616 | tf_op jit(solution)/shard_map/ppermute | solution.py:33
